TPU v7x, 32 devices: a whole 2x2x4 slice. The times are simulated.
32 devices in a mesh: dp: 8 (over z, y), state: 4 (over x, core).
Axes of the slice: x: 2, y: 2, z: 4, core: 2. Of those that a mesh axis runs over, the one named last changes fastest.
Arguments:
- inputs: float32 [8, 512, 1024], P('dp', 'state'), may hold values from -50 to 50
- lengths: int32 [8], P('dp'), may hold values from 1 to 1024, 6144 in all
- cotangent: float32 [8, 512, 1024], P('dp', 'state'), may hold values from -6 to 6
- bn_gain: float32 [2, 512], P(None, 'state'), may hold values from 0.25 to 1.75
- bn_bias: float32 [2, 512], P(None, 'state'), may hold values from -3 to 3
- b_weight: bfloat16 [2, 2, 256, 512], P(None, None, 'state'), may hold values from -0.1875 to 0.1875
- c_weight: bfloat16 [2, 2, 256, 512], P(None, None, 'state'), may hold values from -0.375 to 0.375
- nu_log: float32 [2, 256], P(None, 'state'), may hold values from -9 to -3
- theta_log: float32 [2, 256], P(None, 'state'), may hold values from -4.6 to 1.1
- gamma_log: float32 [2, 256], P(None, 'state'), may hold values from -5 to 0
- skip_weight: float32 [2, 512], P(None, 'state'), may hold values from -4 to 4
- glu_weight: bfloat16 [2, 2, 512, 512], P(None, None, 'state'), may hold values from -0.5 to 0.5
- glu_bias: float32 [2, 2, 512], P(None, None, 'state'), may hold values from -2 to 2
Outputs:
- result: float32 [8, 512, 1024], P('dp', 'state')
- grad_inputs: float32 [8, 512, 1024], P('dp', 'state')
- grad_bn_gain: float32 [2, 512], P(None, 'state')
- grad_bn_bias: float32 [2, 512], P(None, 'state')
- grad_b: float32 [2, 2, 256, 512], P(None, None, 'state')
- grad_c: float32 [2, 2, 256, 512], P(None, None, 'state')
- grad_nu: float32 [2, 256], P(None, 'state')
- grad_theta: float32 [2, 256], P(None, 'state')
- grad_gamma: float32 [2, 256], P(None, 'state')
- grad_skip: float32 [2, 512], P(None, 'state')
- grad_glu_weight: float32 [2, 2, 512, 512], P(None, None, 'state')
- grad_glu_bias: float32 [2, 2, 512], P(None, None, 'state')
Inputs may be any that keep to these rules, and one draw needn't show every extreme that they name: A sequence's valid tokens are its first lengths[s] positions, and some sequence has all 1024.
All inputs are finite; a program needn't handle non-finite values. No bound on the sum of `lengths` on one device may be relied on, other than what follows from the above.
Results may differ from a plain program's by a relative error of at most 0.03.
Values may be sent and summed in bfloat16 or wider, within the bound.
No kernel may reach another device: no remote copies, remote signals or barrier semaphores. Data moves between devices by JAX's collectives and lax.ppermute only.
A program may use at most 64 MiB of HBM per device.

v0:
```python
import jax
import jax.numpy as jnp
from jax import lax
from jax.sharding import PartitionSpec as P

LAYERS = 2


epsilon = 1e-05


def sweep(real_part, imag_part, rate_re, rate_im, backward):
    if backward:
        real_part = jnp.flip(real_part, 2)
        imag_part = jnp.flip(imag_part, 2)
    power_re = jnp.broadcast_to(rate_re[:, None], real_part.shape)
    power_im = jnp.broadcast_to(rate_im[:, None], real_part.shape)

    def combine(early_pair, later_pair):
        early_are, early_aim, early_bre, early_bim = early_pair
        later_are, later_aim, later_bre, later_bim = later_pair
        return (
            early_are * later_are - early_aim * later_aim,
            early_are * later_aim + early_aim * later_are,
            later_are * early_bre - later_aim * early_bim + later_bre,
            later_are * early_bim + later_aim * early_bre + later_bim,
        )

    scanned = lax.associative_scan(combine, (power_re, power_im, real_part, imag_part), axis=2)
    out_re, out_im = (scanned[2], scanned[3])
    if backward:
        out_re = jnp.flip(out_re, 2)
        out_im = jnp.flip(out_im, 2)
    return (out_re, out_im)


def previous(states, backward):
    zeros_row = jnp.zeros_like(states[:, :, :1])
    if backward:
        return jnp.concatenate([states[:, :, 1:], zeros_row], 2)
    return jnp.concatenate([zeros_row, states[:, :, :-1]], 2)


def gelu_exact(values):
    return jax.nn.gelu(values, approximate=False)


def gelu_slope(values, upstream):
    return jax.vjp(gelu_exact, values)[1](upstream)[0]


def local(
    inputs,
    lengths,
    cotangent,
    bn_gain,
    bn_bias,
    b_weight,
    c_weight,
    nu_log,
    theta_log,
    gamma_log,
    skip_weight,
    glu_weight,
    glu_bias,
):
    seq_here, width_here, length = inputs.shape
    states_here = b_weight.shape[2]
    full_width = b_weight.shape[3]
    positions = lax.broadcasted_iota(jnp.int32, (seq_here, length), 1)
    valid_rows = (positions < lengths[:, None]).astype(jnp.float32)
    valid3 = valid_rows[:, None, :]
    local_count = jnp.sum(valid_rows)
    kept_layers = []
    hidden_state = inputs
    for layer_index in range(LAYERS):
        backward = layer_index % 2 == 1
        gain_here = bn_gain[layer_index][:, None]
        shift_here = bn_bias[layer_index][:, None]
        stat_sums = lax.psum(
            (
                jnp.sum(hidden_state * valid3, axis=(0, 2)),
                jnp.sum(hidden_state * hidden_state * valid3, axis=(0, 2)),
                local_count,
            ),
            "dp",
        )
        counted = stat_sums[2]
        centre = stat_sums[0] / counted
        inv_dev = lax.rsqrt(stat_sums[1] / counted - centre * centre + epsilon)[:, None]
        normal_z = (hidden_state - centre[:, None]) * inv_dev
        normalized_input = (valid3 * (normal_z * gain_here + shift_here)).astype(jnp.bfloat16)
        normed_full = lax.all_gather(normalized_input, "state", axis=1, tiled=True)
        b_matrix = b_weight[layer_index].reshape(2 * states_here, full_width)
        driven_input = jnp.einsum(
            "sdl,nd->snl", normed_full, b_matrix, preferred_element_type=jnp.float32
        )
        gamma_here = jnp.exp(gamma_log[layer_index])
        modulus = jnp.exp(-jnp.exp(nu_log[layer_index]))
        rotation = jnp.exp(theta_log[layer_index])
        rate_re = modulus * jnp.cos(rotation)
        rate_im = modulus * jnp.sin(rotation)
        gamma_col = gamma_here[:, None]
        open_re, open_im = sweep(
            gamma_col * driven_input[:, :states_here],
            gamma_col * driven_input[:, states_here:],
            rate_re,
            rate_im,
            backward,
        )
        state_cat = jnp.concatenate([valid3 * open_re, -(valid3 * open_im)], 1).astype(jnp.bfloat16)
        normed_own = normalized_input.astype(jnp.float32)
        skip_here = skip_weight[layer_index][:, None]
        b_columns = None
        c_matrix = c_weight[layer_index].reshape(2 * states_here, full_width)
        partial_value = jnp.einsum(
            "snl,nd->sdl", state_cat, c_matrix, preferred_element_type=jnp.float32
        )
        kept_pre = (
            lax.psum_scatter(
                partial_value.astype(jnp.bfloat16), "state", scatter_dimension=1, tiled=True
            ).astype(jnp.float32)
            + skip_here * normed_own
        )
        active_own = gelu_exact(kept_pre).astype(jnp.bfloat16)
        active_mask = lax.all_gather(active_own, "state", axis=1, tiled=True)
        glu_here = glu_weight[layer_index]
        gated_output = (
            jnp.einsum("sdl,ked->skel", active_mask, glu_here, preferred_element_type=jnp.float32)
            + glu_bias[layer_index][None, :, :, None]
        )
        linear_part = gated_output[:, 0]
        gate_part = jax.nn.sigmoid(gated_output[:, 1])
        kept_layers.append(
            (
                normal_z,
                inv_dev,
                counted,
                normed_own,
                normed_full,
                driven_input,
                open_re,
                open_im,
                state_cat,
                kept_pre,
                active_mask,
                linear_part,
                gate_part,
                rate_re,
                rate_im,
                gamma_here,
                b_columns,
            )
        )
        hidden_state = hidden_state + valid3 * (linear_part * gate_part)
    upstream = cotangent
    layer_grads = [None] * LAYERS
    gain_grads = [None] * LAYERS
    shift_grads = [None] * LAYERS
    for layer_index in reversed(range(LAYERS)):
        backward = layer_index % 2 == 1
        (
            normal_z,
            inv_dev,
            counted,
            normed_own,
            normed_full,
            driven_input,
            open_re,
            open_im,
            state_cat,
            kept_pre,
            active_mask,
            linear_part,
            gate_part,
            rate_re,
            rate_im,
            gamma_here,
            b_columns,
        ) = kept_layers[layer_index]
        gain_here = bn_gain[layer_index][:, None]
        skip_here = skip_weight[layer_index][:, None]
        masked_up = valid3 * upstream
        grad_linear = masked_up * gate_part
        grad_gate = masked_up * linear_part * gate_part * (1.0 - gate_part)
        grad_gated = jnp.stack([grad_linear, grad_gate], 1).astype(jnp.bfloat16)
        grad_glu_matrix = jnp.einsum(
            "sdl,skel->ked", active_mask, grad_gated, preferred_element_type=jnp.float32
        )
        grad_glu_bias = jnp.sum(grad_gated.astype(jnp.float32), axis=(0, 3))
        glu_here = glu_weight[layer_index]
        active_part = jnp.einsum(
            "skel,ked->sdl", grad_gated, glu_here, preferred_element_type=jnp.float32
        )
        grad_active = lax.psum_scatter(
            active_part.astype(jnp.bfloat16), "state", scatter_dimension=1, tiled=True
        ).astype(jnp.float32)
        grad_pre_own = gelu_slope(kept_pre, grad_active).astype(jnp.bfloat16)
        grad_pre_full = lax.all_gather(grad_pre_own, "state", axis=1, tiled=True)
        grad_pre_here = grad_pre_own.astype(jnp.float32)
        grad_skip = jnp.sum(grad_pre_here * normed_own, axis=(0, 2))
        c_matrix = c_weight[layer_index].reshape(2 * states_here, full_width)
        grad_c_matrix = jnp.einsum(
            "snl,sdl->nd", state_cat, grad_pre_full, preferred_element_type=jnp.float32
        )
        grad_state = jnp.einsum(
            "sdl,nd->snl", grad_pre_full, c_matrix, preferred_element_type=jnp.float32
        )
        grad_open_re = valid3 * grad_state[:, :states_here]
        grad_open_im = -(valid3 * grad_state[:, states_here:])
        adjoint_re, adjoint_im = sweep(grad_open_re, grad_open_im, rate_re, -rate_im, not backward)
        before_re = previous(open_re, backward)
        before_im = previous(open_im, backward)
        lam_grad_re = jnp.sum(adjoint_re * before_re + adjoint_im * before_im, axis=(0, 2))
        lam_grad_im = jnp.sum(adjoint_im * before_re - adjoint_re * before_im, axis=(0, 2))
        grad_nu = -jnp.exp(nu_log[layer_index]) * (rate_re * lam_grad_re + rate_im * lam_grad_im)
        grad_theta = jnp.exp(theta_log[layer_index]) * (
            rate_re * lam_grad_im - rate_im * lam_grad_re
        )
        grad_gamma = gamma_here * jnp.sum(
            adjoint_re * driven_input[:, :states_here] + adjoint_im * driven_input[:, states_here:],
            axis=(0, 2),
        )
        gamma_both = jnp.concatenate([gamma_here, gamma_here])[:, None]
        grad_driven = (gamma_both * valid3 * jnp.concatenate([adjoint_re, adjoint_im], 1)).astype(
            jnp.bfloat16
        )
        grad_b_matrix = jnp.einsum(
            "snl,sdl->nd", grad_driven, normed_full, preferred_element_type=jnp.float32
        )
        b_matrix = b_weight[layer_index].reshape(2 * states_here, full_width)
        normed_part = jnp.einsum(
            "snl,nd->sdl", grad_driven, b_matrix, preferred_element_type=jnp.float32
        )
        grad_normed = (
            lax.psum_scatter(
                normed_part.astype(jnp.bfloat16), "state", scatter_dimension=1, tiled=True
            ).astype(jnp.float32)
            + skip_here * grad_pre_here
        )
        grad_masked = valid3 * grad_normed
        grad_shift, grad_gain = lax.psum(
            (jnp.sum(grad_masked, axis=(0, 2)), jnp.sum(grad_masked * normal_z, axis=(0, 2))), "dp"
        )
        upstream = upstream + valid3 * inv_dev * gain_here * (
            grad_masked - grad_shift[:, None] / counted - normal_z * grad_gain[:, None] / counted
        )
        gain_grads[layer_index] = grad_gain
        shift_grads[layer_index] = grad_shift
        layer_grads[layer_index] = (
            lax.psum(
                grad_b_matrix.reshape(2, states_here, full_width).astype(jnp.bfloat16), "dp"
            ).astype(jnp.float32),
            lax.psum(
                grad_c_matrix.reshape(2, states_here, full_width).astype(jnp.bfloat16), "dp"
            ).astype(jnp.float32),
            lax.psum(grad_nu.astype(jnp.bfloat16), "dp").astype(jnp.float32),
            lax.psum(grad_theta.astype(jnp.bfloat16), "dp").astype(jnp.float32),
            lax.psum(grad_gamma.astype(jnp.bfloat16), "dp").astype(jnp.float32),
            lax.psum(grad_skip.astype(jnp.bfloat16), "dp").astype(jnp.float32),
            lax.psum(grad_glu_matrix.astype(jnp.bfloat16), "dp").astype(jnp.float32),
            lax.psum(grad_glu_bias.astype(jnp.bfloat16), "dp").astype(jnp.float32),
        )
    b_stack = jnp.stack([entry[0] for entry in layer_grads])
    c_stack = jnp.stack([entry[1] for entry in layer_grads])
    nu_stack = jnp.stack([entry[2] for entry in layer_grads])
    theta_stack = jnp.stack([entry[3] for entry in layer_grads])
    gamma_stack = jnp.stack([entry[4] for entry in layer_grads])
    skip_stack = jnp.stack([entry[5] for entry in layer_grads])
    glu_w_stack = jnp.stack([entry[6] for entry in layer_grads])
    glu_b_stack = jnp.stack([entry[7] for entry in layer_grads])
    return (
        hidden_state,
        upstream,
        jnp.stack(gain_grads),
        jnp.stack(shift_grads),
        b_stack,
        c_stack,
        nu_stack,
        theta_stack,
        gamma_stack,
        skip_stack,
        glu_w_stack,
        glu_b_stack,
    )


def solution(mesh):
    in_specs = (
        P("dp", "state", None),
        P("dp"),
        P("dp", "state", None),
        P(None, "state"),
        P(None, "state"),
        P(None, None, "state", None),
        P(None, None, "state", None),
        P(None, "state"),
        P(None, "state"),
        P(None, "state"),
        P(None, "state"),
        P(None, None, "state", None),
        P(None, None, "state"),
    )
    out_specs = (
        P("dp", "state", None),
        P("dp", "state", None),
        P(None, "state"),
        P(None, "state"),
        P(None, None, "state", None),
        P(None, None, "state", None),
        P(None, "state"),
        P(None, "state"),
        P(None, "state"),
        P(None, "state"),
        P(None, None, "state", None),
        P(None, None, "state"),
    )
    return jax.shard_map(local, mesh=mesh, in_specs=in_specs, out_specs=out_specs, check_vma=False)
```

profile of v0, /device:TPU:0, one launch (start us, length us, event | category | flops | bytes accessed | tf_op | source)
XLA Modules:
  0.0 889.7 jit_solution(9728251242882547287)
XLA Ops:
  10.8 23.8 %all-reduce.167 = (f32[128]{0:T(128)S(1)}, f32[]{:T(128)}, f32[128]{0:T(128)S(1)}) all-reduce(f32[128]{0:T(128)S(1)} %get-tuple-element.85, f32[]{:T(128)} %fusion.96, f32[128]{0:T(128)S(1)} %get-tuple-element.84), channel_id=1, replica_groups=mesh['dp'=8,'state'=4] {'dp'}, use_global_device_ids=true, to_apply=%region_1.0 | all-reduce | flops 257 | bytes 2056 | tf_op jit(solution)/shard_map/psum | solution.py:80
  40.5 10.0 %all-gather.7.cloned.1.call-done = bf16[1,512,1024]{1,2,0:T(8,128)(2,1)} async-done(((bf16[1,128,1024]{1,2,0:T(8,128)(2,1)}), bf16[1,512,1024]{1,2,0:T(8,128)(2,1)}) %all-gather.7.cloned.1.call-update) | async-done | bytes 1048592 | tf_op jit(solution)/shard_map/all_gather | solution.py:93
  66.2 4.7 copy.282
  73.0 24.4 %reduce-scatter.19.cloned.1.call-done = bf16[128,1024]{1,0:T(8,128)(2,1)} async-done(((bf16[512,1024]{1,0:T(8,128)(2,1)}), bf16[128,1024]{1,0:T(8,128)(2,1)}) %reduce-scatter.19.cloned.1.call-update) | async-done | bytes 262160
  102.0 16.4 %all-gather.9.cloned.1.call-done = bf16[1,512,1024]{1,2,0:T(8,128)(2,1)} async-done(((bf16[1,128,1024]{1,2,0:T(8,128)(2,1)}), bf16[1,512,1024]{1,2,0:T(8,128)(2,1)}) %all-gather.9.cloned.1.call-update) | async-done | bytes 1048592 | tf_op jit(solution)/shard_map/all_gather | solution.py:126
  120.3 21.4 %all-reduce.166 = (f32[128]{0:T(128)S(1)}, f32[128]{0:T(128)S(1)}) all-reduce(f32[128]{0:T(128)S(1)} %get-tuple-element.83, f32[128]{0:T(128)S(1)} %get-tuple-element.82), channel_id=1, replica_groups=mesh['dp'=8,'state'=4] {'dp'}, use_global_device_ids=true, to_apply=%region_8.0 | all-reduce | flops 256 | bytes 2048 | tf_op jit(solution)/shard_map/psum | solution.py:80
  144.8 11.9 %all-gather.11.cloned.1.call-done = bf16[1,512,1024]{1,2,0:T(8,128)(2,1)} async-done(((bf16[1,128,1024]{1,2,0:T(8,128)(2,1)}), bf16[1,512,1024]{1,2,0:T(8,128)(2,1)}) %all-gather.11.cloned.1.call-update) | async-done | bytes 1048592 | tf_op jit(solution)/shard_map/all_gather | solution.py:93
  165.1 2.5 slice.1980
  176.2 2.9 slice.1981
  180.5 3.0 slice.1985
  183.4 3.0 slice.1994
  262.2 3.0 slice.2111
  305.0 2.6 pad.570
  309.3 2.6 pad.568
  311.9 2.6 pad.569
  318.2 4.7 rev.18
  325.0 4.8 rev.17
  333.4 6.0 copy.284
  339.4 2.9 copy.310
  342.4 25.0 %reduce-scatter.21.cloned.1.call-done = bf16[128,1024]{1,0:T(8,128)(2,1)} async-done(((bf16[512,1024]{1,0:T(8,128)(2,1)}), bf16[128,1024]{1,0:T(8,128)(2,1)}) %reduce-scatter.21.cloned.1.call-update) | async-done | bytes 262160
  370.7 2.9 multiply_convert_fusion.4
  375.8 14.9 %all-gather.13.cloned.1.call-done = bf16[1,512,1024]{1,2,0:T(8,128)(2,1)} async-done(((bf16[1,128,1024]{1,2,0:T(8,128)(2,1)}), bf16[1,512,1024]{1,2,0:T(8,128)(2,1)}) %all-gather.13.cloned.1.call-update) | async-done | bytes 1048592 | tf_op jit(solution)/shard_map/all_gather | solution.py:126
  395.8 6.0 copy.286
  401.8 2.9 copy.309
  404.8 25.0 %reduce-scatter.23.cloned.1.call-done = bf16[128,1024]{1,0:T(8,128)(2,1)} async-done(((bf16[512,1024]{1,0:T(8,128)(2,1)}), bf16[128,1024]{1,0:T(8,128)(2,1)}) %reduce-scatter.23.cloned.1.call-update) | async-done | bytes 262160
  442.1 4.9 slice.2381
  449.0 4.9 slice.2379
  560.0 2.6 pad.608
  564.3 2.6 pad.610
  566.9 2.6 pad.609
  569.5 2.6 pad.611
  572.1 2.7 add_reduce_fusion.2
  577.3 6.0 copy.288
  583.3 2.9 copy.308
  586.3 25.0 %reduce-scatter.25.cloned.1.call-done = bf16[128,1024]{1,0:T(8,128)(2,1)} async-done(((bf16[512,1024]{1,0:T(8,128)(2,1)}), bf16[128,1024]{1,0:T(8,128)(2,1)}) %reduce-scatter.25.cloned.1.call-update) | async-done | bytes 262160
  617.1 21.3 %all-reduce.165 = (f32[128]{0:T(128)S(1)}, f32[128]{0:T(128)S(1)}) all-reduce(f32[128]{0:T(128)S(1)} %get-tuple-element.81, f32[128]{0:T(128)S(1)} %get-tuple-element.80), channel_id=1, replica_groups=mesh['dp'=8,'state'=4] {'dp'}, use_global_device_ids=true, to_apply=%region_17.18 | all-reduce | flops 256 | bytes 2048 | tf_op jit(solution)/shard_map/psum | solution.py:242
  643.7 4.7 copy.290
  649.9 21.3 %reduce-scatter.27.cloned.1.call-done = bf16[128,1024]{1,0:T(8,128)(2,1)} async-done(((bf16[512,1024]{1,0:T(8,128)(2,1)}), bf16[128,1024]{1,0:T(8,128)(2,1)}) %reduce-scatter.27.cloned.1.call-update) | async-done | bytes 262160
  682.5 8.7 all-gather.17.cloned.1.call-done
  706.8 3.5 rev.19
  710.3 2.6 pad.651
  714.8 3.4 rev.20
  729.1 3.9 copy.292
  733.0 3.2 copy.306
  745.1 63.4 %all-reduce.172.cloned.1.call-done = (bf16[1,2,64,512]{3,2,1,0:T(8,128)(2,1)}, bf16[1,2,64,512]{3,2,1,0:T(8,128)(2,1)}, bf16[1,2,64,512]{3,2,1,0:T(8,128)(2,1)},...) async-done(((bf16[1,2,64,512]{3,2,1,0:T(8,128)(2,1)}, bf16[1,2,64,512]{3,2,1,0:T(8,128)(2,1)}, ...) | async-done | bytes 1048592 | tf_op jit(solution)/shard_map/psum | solution.py:251
  814.3 21.0 %reduce-scatter.29.cloned.1.call-done = bf16[128,1024]{1,0:T(8,128)(2,1)} async-done(((bf16[512,1024]{1,0:T(8,128)(2,1)}), bf16[128,1024]{1,0:T(8,128)(2,1)}) %reduce-scatter.29.cloned.1.call-update) | async-done | bytes 262160
  837.4 21.4 %all-reduce.164 = (f32[128]{0:T(128)S(1)}, f32[128]{0:T(128)S(1)}) all-reduce(f32[128]{0:T(128)S(1)} %get-tuple-element.79, f32[128]{0:T(128)S(1)} %get-tuple-element.78), channel_id=1, replica_groups=mesh['dp'=8,'state'=4] {'dp'}, use_global_device_ids=true, to_apply=%region_23.24 | all-reduce | flops 256 | bytes 2048 | tf_op jit(solution)/shard_map/psum | solution.py:242
  862.5 17.4 %all-reduce.168 = (bf16[1,64]{1,0:T(2,128)(2,1)S(1)}, bf16[1,64]{1,0:T(2,128)(2,1)S(1)}, bf16[1,64]{1,0:T(2,128)(2,1)S(1)}, bf16[1,64]{1,0:T(2,128)(2,1)S(1)}, b...) all-reduce(bf16[1,64]{1,0:T(2,128)(2,1)S(1)} %get-tuple-element.392, ...), channel_id=1, replica_groups=mesh['dp'=8,'state'=4] {'dp'}, use_global_device_ids=true, to_apply=%region_33.34 | all-reduce | flops 1152 | bytes 4608 | tf_op jit(solution)/shard_map/psum | solution.py:257
  (1078 shorter events, 388.4 us)
Async XLA Ops:
  7.2 29.1 %copy-start.95 = (f32[2,64]{1,0:T(2,128)S(1)}, f32[2,64]{1,0:T(2,128)}, u32[]{:S(2)}) copy-start(f32[2,64]{1,0:T(2,128)} %param.21) | copy-start | bytes 1540
  7.2 29.1 %copy-start.97 = (f32[2,64]{1,0:T(2,128)S(1)}, f32[2,64]{1,0:T(2,128)}, u32[]{:S(2)}) copy-start(f32[2,64]{1,0:T(2,128)} %param.20) | copy-start | bytes 1540
  7.2 30.6 %copy-start.124 = (f32[2,64]{1,0:T(2,128)S(1)}, f32[2,64]{1,0:T(2,128)}, u32[]{:S(2)}) copy-start(f32[2,64]{1,0:T(2,128)} %param.22) | copy-start | bytes 1540
  7.2 32.5 %copy-start.53 = (bf16[2,2,64,512]{3,2,1,0:T(8,128)(2,1)S(1)}, bf16[2,2,64,512]{3,2,1,0:T(8,128)(2,1)}, u32[]{:S(2)}) copy-start(bf16[2,2,64,512]{3,2,1,0:T(8,128)(2,1)} %param.18) | copy-start | bytes 786436
  7.2 32.5 %copy-start.54 = (bf16[2,2,64,512]{3,2,1,0:T(8,128)(2,1)S(1)}, bf16[2,2,64,512]{3,2,1,0:T(8,128)(2,1)}, u32[]{:S(2)}) copy-start(bf16[2,2,64,512]{3,2,1,0:T(8,128)(2,1)} %param.19) | copy-start | bytes 786436
  7.2 43.2 %all-gather.7.cloned.1.call-start = ((), (), s32[]{:S(2)}) async-start(), calls=%async_computation.6 | async-start | bytes 1310720 | tf_op jit(solution)/shard_map/all_gather | solution.py:93
  10.6 88.5 %copy-start.76 = (f32[128]{0:T(128)}, f32[128]{0:T(128)S(1)}, u32[]{:S(2)}) copy-start(f32[128]{0:T(128)S(1)} %get-tuple-element.454) | copy-start | bytes 1540
  10.6 88.5 %copy-start.85 = (f32[128]{0:T(128)}, f32[128]{0:T(128)S(1)}, u32[]{:S(2)}) copy-start(f32[128]{0:T(128)S(1)} %get-tuple-element.448) | copy-start | bytes 1540
  10.6 131.8 %copy-start.79 = (f32[128]{0:T(128)}, f32[128]{0:T(128)S(1)}, u32[]{:S(2)}) copy-start(f32[128]{0:T(128)S(1)} %get-tuple-element.455) | copy-start | bytes 1540
  10.6 131.8 %copy-start.88 = (f32[128]{0:T(128)}, f32[128]{0:T(128)S(1)}, u32[]{:S(2)}) copy-start(f32[128]{0:T(128)S(1)} %get-tuple-element.447) | copy-start | bytes 1540
  35.3 63.9 %copy-start.66 = (f32[128]{0:T(128)}, f32[128]{0:T(128)S(1)}, u32[]{:S(2)}) copy-start(f32[128]{0:T(128)S(1)} %get-tuple-element.218) | copy-start | bytes 1540
  35.3 63.9 %copy-start.69 = (f32[128]{0:T(128)}, f32[128]{0:T(128)S(1)}, u32[]{:S(2)}) copy-start(f32[128]{0:T(128)S(1)} %get-tuple-element.219) | copy-start | bytes 1540
  36.2 61.2 %reduce-scatter.19.cloned.1.call-start = ((), (), s32[]{:S(2)}) async-start(), calls=%async_computation.12 | async-start | bytes 1310720
  37.1 149.3 %copy-start.90 = (f32[64]{0:T(128)}, f32[64]{0:T(128)S(1)}, u32[]{:S(2)}) copy-start(f32[64]{0:T(128)S(1)} %get-tuple-element.163) | copy-start | bytes 772
  37.1 159.4 %copy-start.64 = (f32[64]{0:T(128)}, f32[64]{0:T(128)S(1)}, u32[]{:S(2)}) copy-start(f32[64]{0:T(128)S(1)} %get-tuple-element.161) | copy-start | bytes 772
  37.8 105.7 %copy-start.117 = (f32[64]{0:T(128)}, f32[64]{0:T(128)S(1)}, u32[]{:S(2)}) copy-start(f32[64]{0:T(128)S(1)} %get-tuple-element.177) | copy-start | bytes 772
  37.8 105.8 %copy-start.118 = (f32[64]{0:T(128)}, f32[64]{0:T(128)S(1)}, u32[]{:S(2)}) copy-start(f32[64]{0:T(128)S(1)} %get-tuple-element.178) | copy-start | bytes 772
  38.4 119.9 %copy-start.111 = (f32[64]{0:T(128)}, f32[64]{0:T(128)S(1)}, u32[]{:S(2)}) copy-start(f32[64]{0:T(128)S(1)} %get-tuple-element.432) | copy-start | bytes 772
  39.8 116.9 %copy-start.43 = (bf16[1,2,64,512]{3,2,1,0:T(8,128)(2,1)}, bf16[1,2,64,512]{3,2,1,0:T(8,128)(2,1)S(1)}, u32[]{:S(2)}) copy-start(bf16[1,2,64,512]{3,2,1,0:T(8,128)(2,1)S(1)} %get-tuple-element.273) | copy-start | bytes 393220
  72.3 29.1 %copy-start.138 = (f32[2,2,128]{2,1,0:T(2,128)S(1)}, f32[2,2,128]{2,1,0:T(2,128)}, u32[]{:S(2)}) copy-start(f32[2,2,128]{2,1,0:T(2,128)} %param.25) | copy-start | bytes 6148
  72.3 46.0 %copy-start.34 = (bf16[2,2,128,512]{3,2,1,0:T(8,128)(2,1)S(1)}, bf16[2,2,128,512]{3,2,1,0:T(8,128)(2,1)}, u32[]{:S(2)}) copy-start(bf16[2,2,128,512]{3,2,1,0:T(8,128)(2,1)} %param.24) | copy-start | bytes 1572868
  72.4 46.0 %all-gather.9.cloned.1.call-start = ((), (), s32[]{:S(2)}) async-start(), calls=%async_computation.7 | async-start | bytes 1310720 | tf_op jit(solution)/shard_map/all_gather | solution.py:126
  73.0 47.1 %copy-start.81 = (f32[128]{0:T(128)}, f32[128]{0:T(128)S(1)}, u32[]{:S(2)}) copy-start(f32[128]{0:T(128)S(1)} %get-tuple-element.441) | copy-start | bytes 1540
  101.4 55.3 %all-gather.11.cloned.1.call-start = ((), (), s32[]{:S(2)}) async-start(), calls=%async_computation.8 | async-start | bytes 1310720 | tf_op jit(solution)/shard_map/all_gather | solution.py:93
  143.3 224.1 %reduce-scatter.21.cloned.1.call-start = ((), (), s32[]{:S(2)}) async-start(), calls=%async_computation.13 | async-start | bytes 1310720
  196.5 64.3 %copy-start.48 = (f32[1,64,511]{1,2,0:T(8,128)S(1)}, f32[1,64,511]{1,2,0:T(8,128)}, u32[]{:S(2)}) copy-start(f32[1,64,511]{1,2,0:T(8,128)} %slice.2107) | copy-start | bytes 392452
  211.7 69.4 %copy-start.55 = (f32[1,64,127]{1,2,0:T(8,128)S(1)}, f32[1,64,127]{1,2,0:T(8,128)}, u32[]{:S(2)}) copy-start(f32[1,64,127]{1,2,0:T(8,128)} %slice.2099) | copy-start | bytes 97540
  211.7 69.4 %copy-start.56 = (f32[1,64,127]{1,2,0:T(8,128)S(1)}, f32[1,64,127]{1,2,0:T(8,128)}, u32[]{:S(2)}) copy-start(f32[1,64,127]{1,2,0:T(8,128)} %slice.2095) | copy-start | bytes 97540
  342.3 28.4 %copy-start.73 = (f32[128]{0:T(128)S(1)}, f32[128]{0:T(128)}, u32[]{:S(2)}) copy-start(f32[128]{0:T(128)} %copy-done.72) | copy-start | bytes 1540
  342.4 48.3 %all-gather.13.cloned.1.call-start = ((), (), s32[]{:S(2)}) async-start(), calls=%async_computation.9 | async-start | bytes 1310720 | tf_op jit(solution)/shard_map/all_gather | solution.py:126
  373.7 56.2 %reduce-scatter.23.cloned.1.call-start = ((), (), s32[]{:S(2)}) async-start(), calls=%async_computation.14 | async-start | bytes 1310720
  404.8 49.2 %all-gather.15.cloned.1.call-start = ((), (), s32[]{:S(2)}) async-start(), calls=%async_computation.10 | async-start | bytes 1310720 | tf_op jit(solution)/shard_map/all_gather | solution.py:199
  436.1 175.3 %reduce-scatter.25.cloned.1.call-start = ((), (), s32[]{:S(2)}) async-start(), calls=%async_computation.15 | async-start | bytes 1310720
  586.2 29.0 %copy-start.75 = (f32[128]{0:T(128)S(1)}, f32[128]{0:T(128)}, u32[]{:S(2)}) copy-start(f32[128]{0:T(128)} %copy-done.74) | copy-start | bytes 1540
  586.2 29.0 %copy-start.80 = (f32[128]{0:T(128)S(1)}, f32[128]{0:T(128)}, u32[]{:S(2)}) copy-start(f32[128]{0:T(128)} %copy-done.79) | copy-start | bytes 1540
  586.2 29.0 %copy-start.84 = (f32[128]{0:T(128)S(1)}, f32[128]{0:T(128)}, u32[]{:S(2)}) copy-start(f32[128]{0:T(128)} %get-tuple-element.440) | copy-start | bytes 1540
  586.2 29.1 %copy-start.89 = (f32[128]{0:T(128)S(1)}, f32[128]{0:T(128)}, u32[]{:S(2)}) copy-start(f32[128]{0:T(128)} %copy-done.88) | copy-start | bytes 1540
  586.2 52.9 %copy-start.13 = (f32[1,128,1024]{1,2,0:T(8,128)S(1)}, f32[1,128,1024]{1,2,0:T(8,128)}, u32[]{:S(2)}) copy-start(f32[1,128,1024]{1,2,0:T(8,128)} %copy.248) | copy-start | bytes 1572868
  586.2 85.0 %reduce-scatter.27.cloned.1.call-start = ((), (), s32[]{:S(2)}) async-start(), calls=%async_computation.16 | async-start | bytes 1310720
  649.9 41.3 %all-gather.17.cloned.1.call-start = ((), (), s32[]{:S(2)}) async-start(), calls=%async_computation.11 | async-start | bytes 1310720 | tf_op jit(solution)/shard_map/all_gather | solution.py:199
  674.1 134.4 %all-reduce.172.cloned.1.call-start = ((), (), s32[]{:S(2)}) async-start(), calls=%async_computation.18 | async-start | bytes 2097152 | tf_op jit(solution)/shard_map/psum | solution.py:251
  728.5 106.8 %reduce-scatter.29.cloned.1.call-start = ((), (), s32[]{:S(2)}) async-start(), calls=%async_computation.17 | async-start | bytes 1310720
  810.3 26.7 %copy-start.68 = (f32[128]{0:T(128)S(1)}, f32[128]{0:T(128)}, u32[]{:S(2)}) copy-start(f32[128]{0:T(128)} %copy-done.66) | copy-start | bytes 1540
  810.3 26.7 %copy-start.71 = (f32[128]{0:T(128)S(1)}, f32[128]{0:T(128)}, u32[]{:S(2)}) copy-start(f32[128]{0:T(128)} %copy-done.69) | copy-start | bytes 1540
  810.3 26.7 %copy-start.78 = (f32[128]{0:T(128)S(1)}, f32[128]{0:T(128)}, u32[]{:S(2)}) copy-start(f32[128]{0:T(128)} %copy-done.76) | copy-start | bytes 1540
  810.3 26.7 %copy-start.83 = (f32[128]{0:T(128)S(1)}, f32[128]{0:T(128)}, u32[]{:S(2)}) copy-start(f32[128]{0:T(128)} %copy-done.81) | copy-start | bytes 1540
  810.3 26.7 %copy-start.87 = (f32[128]{0:T(128)S(1)}, f32[128]{0:T(128)}, u32[]{:S(2)}) copy-start(f32[128]{0:T(128)} %copy-done.85) | copy-start | bytes 1540
  812.2 47.2 %copy-start.1 = (f32[1,128,1024]{1,2,0:T(8,128)S(1)}, f32[1,128,1024]{1,2,0:T(8,128)}, u32[]{:S(2)}) copy-start(f32[1,128,1024]{1,2,0:T(8,128)} %copy-done) | copy-start | bytes 1572868
  (115 other events, 916.1 us)
Sparse Core Ops, SparseCore 0:
  36.3 14.0 all-gather.6
  72.5 24.8 reduce-scatter.18
  101.5 16.8 all-gather.8
  143.4 13.1 all-gather.10
  342.5 24.8 reduce-scatter.20
  373.8 16.8 all-gather.12
  404.9 24.8 reduce-scatter.22
  436.2 16.8 all-gather.14
  586.4 24.9 reduce-scatter.24
  650.0 21.2 reduce-scatter.26
  674.3 16.8 all-gather.16
  728.6 79.8 all-reduce.171
  811.0 24.2 reduce-scatter.28
where the time goes:
time: 906 us; the launch traced here: 890 us
  local copies, waits for them, and re-layouts  314 us (35%)
  waiting for transfers between devices  267 us (29%)
  other arithmetic  155 us (17%)
  blocking collectives  105 us (12%)
  matrix products  28.8 us (3%)
  between operations  18.9 us (2%)
    unnamed x19, waiting for transfers between devices  142 us
    slice x284, local copies, waits for them, and re-layouts, sweep(): lax.associative_scan(combine, (power_re, power_im, real_part, imag_part),...  140 us
    unnamed x328, local copies, waits for them, and re-layouts  79.5 us
    psum x1, waiting for transfers between devices, local(): lax.psum(grad_b_matrix.reshape(2, states_here, full_width).astype(jnp.bfl...  63.4 us
    pad x144, local copies, waits for them, and re-layouts, sweep(): lax.associative_scan(combine, (power_re, power_im, real_part, imag_part),...  59.1 us
    psum x2, blocking collectives, local(): lax.psum((jnp.sum(hidden_state * valid3, axis=(0, 2)), jnp.sum(hidden_sta...  45.1 us
    psum x2, blocking collectives, local(): lax.psum((jnp.sum(grad_masked, axis=(0, 2)), jnp.sum(grad_masked * normal...  42.7 us
    add x80, other arithmetic, sweep(): lax.associative_scan(combine, (power_re, power_im, real_part, imag_part),...  38.3 us
  transfers between devices with their start and end apart: 13, of which 12 were waited for; matrix products, arithmetic and copies ran while one was open for 6% of the time, Pallas kernels for 0%

commit v1 on v0

v1 whole, which is shorter than its diff:
```python
import functools

import jax
import jax.numpy as jnp
from jax import lax
from jax.experimental import pallas as pl
from jax.experimental.pallas import tpu as pltpu
from jax.sharding import PartitionSpec as P

LAYERS = 2
CHUNKS = 16
EPSILON = 1e-05
F32 = jnp.float32
LOW = jnp.bfloat16
PARAM_ROWS = 16
VMEM_BYTES = 56 * 1024 * 1024

GAIN, SHIFT, SKIP, BIAS_LINEAR, BIAS_GATE = range(5)
RATE_RE, RATE_IM, GAMMA = range(3)

NN = (((1,), (0,)), ((), ()))
NT = (((1,), (1,)), ((), ()))
TN = (((0,), (0,)), ((), ()))


def dot(left, right, dims):
    return lax.dot_general(left, right, dims, preferred_element_type=F32)


def rows_at(index, size):
    return pl.ds(pl.multiple_of(index * size, size), size)


def lanes_at(quarter, width):
    return pl.ds(pl.multiple_of(quarter * width, width), width)


def for_rows(total, size, body, init=None, unroll=1):
    def step(index, carry):
        return body(rows_at(index, size), index, carry)

    return lax.fori_loop(0, total // size, step, init, unroll=unroll)


def keep_rows(first_step, rows, steps, length):
    row = lax.broadcasted_iota(jnp.int32, (rows, 1), 0)
    position = (row % CHUNKS) * steps + row // CHUNKS + first_step
    return position < length


def gelu_parts(value):
    size = jnp.abs(value)
    below = 1.0 + size * (0.3275911 * 0.7071067811865476)
    guess = pl.reciprocal(below, approx=True)
    inverse = guess * (2.0 - below * guess)
    bell = jnp.exp(value * value * -0.5)
    tail = inverse * (
        0.5 * 0.254829592
        + inverse
        * (
            0.5 * -0.284496736
            + inverse * (0.5 * 1.421413741 + inverse * (0.5 * -1.453152027 + inverse * (0.5 * 1.061405429)))
        )
    )
    tail = tail * bell
    return jnp.where(value >= 0.0, 1.0 - tail, tail), bell * 0.3989422804014327


def sigmoid(value):
    return 0.5 * jnp.tanh(0.5 * value) + 0.5


def squared(re, im, times):
    for _ in range(times):
        re, im = re * re - im * im, 2.0 * re * im
    return re, im


def chunk_starts(re, im, rate_re, rate_im, reverse):
    row = lax.broadcasted_iota(jnp.int32, re.shape, 0)

    def moved(value, by):
        if reverse:
            return jnp.where(row < CHUNKS - by, pltpu.roll(value, CHUNKS - by, 0), 0.0)
        return jnp.where(row >= by, pltpu.roll(value, by, 0), 0.0)

    by = 1
    while by < CHUNKS:
        past_re, past_im = moved(re, by), moved(im, by)
        re, im = (
            re + rate_re * past_re - rate_im * past_im,
            im + rate_re * past_im + rate_im * past_re,
        )
        rate_re, rate_im = squared(rate_re, rate_im, 1)
        by *= 2
    return moved(re, 1), moved(im, 1)


def sweep(drive_ref, rate_re, rate_im, steps, reverse, emit, extra, unroll=4):
    states = rate_re.shape[1]
    shape = (CHUNKS, states)
    wide_re = jnp.broadcast_to(rate_re, shape)
    wide_im = jnp.broadcast_to(rate_im, shape)

    def advance(index, re, im):
        place = steps - 1 - index if reverse else index
        rows = rows_at(place, CHUNKS)
        drive_re = drive_ref[rows, :states]
        drive_im = drive_ref[rows, states:]
        new_re = (wide_re * re + drive_re) - wide_im * im
        new_im = (wide_re * im + drive_im) + wide_im * re
        return rows, place, new_re, new_im, drive_re, drive_im

    def first(index, carry):
        _, _, re, im, _, _ = advance(index, *carry)
        return re, im

    def second(index, carry):
        re, im, held = carry
        rows, place, re, im, drive_re, drive_im = advance(index, re, im)
        return re, im, emit(rows, place, re, im, drive_re, drive_im, held)

    zero = jnp.zeros(shape, F32)
    re, im = lax.fori_loop(0, steps, first, (zero, zero), unroll=unroll)
    far_re, far_im = rate_re, rate_im
    power = 1
    while power < steps:
        far_re, far_im = squared(far_re, far_im, 1)
        power *= 2
    re, im = chunk_starts(re, im, far_re, far_im, reverse)
    return lax.fori_loop(0, steps, second, (re, im, extra), unroll=unroll)[2]


def from_feature_rows(source_ref, held_ref, steps, emit):
    length = source_ref.shape[1]
    for block in range(length // 128):
        held_ref[block * 128 : (block + 1) * 128, :] = source_ref[:, block * 128 : (block + 1) * 128].T

    def step(index, carry):
        emit(rows_at(index, CHUNKS), index, held_ref[pl.ds(index, CHUNKS, stride=steps), :])
        return carry

    lax.fori_loop(0, steps, step, 0, unroll=4)


def to_feature_rows(load, held_ref, out_ref, steps):
    length = out_ref.shape[1]

    def step(index, carry):
        held_ref[pl.ds(index, CHUNKS, stride=steps), :] = load(rows_at(index, CHUNKS), index)
        return carry

    lax.fori_loop(0, steps, step, 0, unroll=4)
    for block in range(length // 128):
        out_ref[:, block * 128 : (block + 1) * 128] = held_ref[block * 128 : (block + 1) * 128, :].T


def enter_kernel(meta_ref, x_ref, params_ref, out_ref, sums_ref, held_ref):
    length = meta_ref[0]
    total = x_ref.shape[1]
    steps = total // CHUNKS
    out_ref[total:, :] = params_ref[...]
    sums_ref[...] = jnp.zeros_like(sums_ref)

    def emit(rows, index, value):
        out_ref[rows, :] = value
        kept = jnp.where(keep_rows(index, CHUNKS, steps, length), value, 0.0)
        sums_ref[0:16, :] += kept
        sums_ref[16:32, :] += kept * kept

    from_feature_rows(x_ref, held_ref, steps, emit)
    plain = jnp.sum(sums_ref[0:16, :], axis=0, keepdims=True)
    square = jnp.sum(sums_ref[16:32, :], axis=0, keepdims=True)
    sums_ref[0:1, :] = plain
    sums_ref[1:2, :] = square
    sums_ref[2:3, :] = jnp.full((1, 128), length, jnp.int32).astype(F32)


def cotangent_kernel(x_ref, out_ref, low_ref, held_ref):
    steps = x_ref.shape[1] // CHUNKS

    def emit(rows, index, value):
        out_ref[rows, :] = value
        low_ref[rows, :] = value.astype(LOW)

    from_feature_rows(x_ref, held_ref, steps, emit)


def assemble_states(parts, whole_ref):
    half = parts[0].shape[0] // 2
    states = half * len(parts)
    for place, part in enumerate(parts):
        whole_ref[place * half : (place + 1) * half, :] = part[:half, :]
        whole_ref[states + place * half : states + (place + 1) * half, :] = part[half:, :]


def assemble_output(parts, whole_ref):
    half = parts[0].shape[0] // 2
    states = half * len(parts)
    for place, part in enumerate(parts):
        whole_ref[place * half : (place + 1) * half, :] = part[:half, :]
        whole_ref[states + place * half : states + (place + 1) * half, :] = -part[half:, :]


def assemble_glu(parts, whole_ref, quarter):
    half = parts[0].shape[0] // 2
    width = half * len(parts)
    for place, part in enumerate(parts):
        whole_ref[lanes_at(quarter ^ place, half), :] = part[:half, :]
        whole_ref[pl.ds(pl.multiple_of(width + (quarter ^ place) * half, half), half), :] = part[half:, :]


def norm_rows(sums, counted):
    centre = sums[0:1, :] / counted
    meansq = sums[1:2, :] / counted
    return centre, lax.rsqrt(meansq - centre * centre + EPSILON)


def drive_phase(normed_ref, b_ref, drive_ref, gamma, part):
    total = normed_ref.shape[0]
    both = jnp.concatenate([gamma, gamma], axis=1)

    def body(rows, index, carry):
        drive_ref[rows, :] = dot(normed_ref[rows, :], b_ref[...], NT) * both
        return carry

    for_rows(total, part, body, 0)


def pre_phase(low_ref, c_ref, normed_ref, skip, active_ref, slope_ref, held_ref, part):
    total = normed_ref.shape[0]

    def body(rows, index, carry):
        held_ref[...] = dot(low_ref[rows, :], c_ref[...], NN)
        base = index * part

        def inner(local, place, carry):
            here = pl.ds(pl.multiple_of(base + place * 16, 16), 16)
            value = held_ref[local, :] + skip * normed_ref[here, :].astype(F32)
            cdf, density = gelu_parts(value)
            active_ref[here, :] = (value * cdf).astype(LOW)
            slope_ref[here, :] = (cdf + value * density).astype(slope_ref.dtype)
            return carry

        for_rows(part, 16, inner, 0, unroll=2)
        return carry

    for_rows(total, part, body, 0)


def start_kernel(
    meta_ref, x0, x1, x2, x3, sums_ref, b0, b1, b2, b3, c0, c1, c2, c3,
    normed_ref, drive_own_ref, low_ref, slope_ref, active_ref, b_ref, c_ref, feature_ref, state_ref, norm_ref,
    drive_ref, held_ref, stats_ref, part,
):
    length, quarter = meta_ref[0], meta_ref[1]
    parts = (x0, x1, x2, x3)
    total = normed_ref.shape[0]
    steps = total // CHUNKS
    width = x0.shape[1]
    assemble_states((b0, b1, b2, b3), b_ref)
    assemble_output((c0, c1, c2, c3), c_ref)
    lane = lax.broadcasted_iota(jnp.int32, (8, width), 1)
    for place, value in enumerate(parts):
        feature_ref[:, lanes_at(quarter ^ place, width)] = value[total:, :]
    for pair in range(2):
        early, late = parts[2 * pair][total + 8 :, :], parts[2 * pair + 1][total + 8 :, :]
        state_ref[:, pair * 128 : (pair + 1) * 128] = jnp.where(lane < 64, early, pltpu.roll(late, 64, 1))
    groups = sums_ref.shape[0] // 8
    for place in range(4):
        value = sums_ref[place * 8 : place * 8 + 8, :]
        for other in range(1, groups // 4):
            value += sums_ref[(other * 4 + place) * 8 : (other * 4 + place) * 8 + 8, :]
        stats_ref[:, place * width : (place + 1) * width] = value
    centre, inv_dev = norm_rows(stats_ref[0:2, :], stats_ref[2:3, :])
    norm_ref[...] = jnp.zeros_like(norm_ref)
    norm_ref[0:1, :] = centre
    norm_ref[1:2, :] = inv_dev
    norm_ref[2:3, :] = stats_ref[2:3, :]

    def normal(rows, index, carry):
        keep = keep_rows(index * 2, 32, steps, length)
        for place, value in enumerate(parts):
            lanes = lanes_at(quarter ^ place, width)
            z = (value[rows, :] - norm_ref[0:1, lanes]) * norm_ref[1:2, lanes]
            z = z * feature_ref[GAIN : GAIN + 1, lanes] + feature_ref[SHIFT : SHIFT + 1, lanes]
            normed_ref[rows, lanes] = jnp.where(keep, z, 0.0).astype(LOW)
        return carry

    for_rows(total, 32, normal, 0)
    state = state_ref[...]
    states = state.shape[1]
    drive_phase(normed_ref, b_ref, drive_ref, state[2 + GAMMA : 3 + GAMMA, :], part)

    def emit(rows, step, re, im, drive_re, drive_im, held):
        low_ref[rows, :states] = re.astype(LOW)
        low_ref[rows, states:] = im.astype(LOW)
        drive_own_ref[rows, :128] = drive_re[:, :128]
        drive_own_ref[rows, 128:] = drive_im[:, :128]
        return held

    sweep(drive_ref, state[2:3, :], state[3:4, :], steps, False, emit, 0)
    pre_phase(low_ref, c_ref, normed_ref, feature_ref[SKIP : SKIP + 1, :], active_ref, slope_ref, held_ref, part)


def glu_kernel(
    meta_ref, x0, x1, x2, x3, active_ref, w0, w1, w2, w3, feature_ref,
    stream_ref, linear_ref, gate_ref, w_ref, sums_ref,
    held_ref, part,
):
    length, quarter = meta_ref[0], meta_ref[1]
    parts = (x0, x1, x2, x3)
    total, full = active_ref.shape
    steps = total // CHUNKS
    width = x0.shape[1]
    assemble_glu((w0, w1, w2, w3), w_ref, quarter)
    sums_ref[...] = jnp.zeros_like(sums_ref)

    def body(rows, index, carry):
        held_ref[...] = dot(active_ref[rows, :], w_ref[...], NT)
        base = index * part

        def inner(local, place_index, carry):
            here = pl.ds(pl.multiple_of(base + place_index * 16, 16), 16)
            keep = keep_rows(index * (part // CHUNKS) + place_index, 16, steps, length)
            for place, value in enumerate(parts):
                lanes = lanes_at(quarter ^ place, width)
                far = pl.ds(pl.multiple_of(full + (quarter ^ place) * width, width), width)
                linear = held_ref[local, lanes] + feature_ref[BIAS_LINEAR : BIAS_LINEAR + 1, lanes]
                gate = sigmoid(held_ref[local, far] + feature_ref[BIAS_GATE : BIAS_GATE + 1, lanes])
                mixed = linear * gate
                gate_ref[here, lanes] = gate.astype(gate_ref.dtype)
                linear_ref[here, lanes] = (mixed * (1.0 - gate)).astype(linear_ref.dtype)
                moved = value[here, :] + jnp.where(keep, mixed, 0.0)
                stream_ref[here, lanes] = moved
                kept = jnp.where(keep, moved, 0.0)
                sums_ref[0:16, lanes] += kept
                sums_ref[16:32, lanes] += kept * kept
            return carry

        for_rows(part, 16, inner, 0, unroll=2)
        return carry

    for_rows(total, part, body, 0)
    plain = jnp.sum(sums_ref[0:16, :], axis=0, keepdims=True)
    square = jnp.sum(sums_ref[16:32, :], axis=0, keepdims=True)
    sums_ref[0:1, :] = plain
    sums_ref[1:2, :] = square


def total_rows(sums_ref, count):
    groups = sums_ref.shape[0] // 8
    value = sums_ref[0:8, :]
    for other in range(1, groups):
        value += sums_ref[other * 8 : other * 8 + 8, :]
    return value


def adjoint_phase(
    grad_gated_ref, w_ref, slope_ref, normed_ref, c_ref, low_ref, drive_own_ref, state, first_row, quarter, length,
    pre_grad_ref, held_ref, grad_state_ref, grad_driven_ref, small_ref, sum_ref, reverse, part,
):
    total, full = normed_ref.shape
    steps = total // CHUNKS
    width = 128
    states = state.shape[1]
    own = lanes_at(quarter, width)
    sum_ref[...] = jnp.zeros_like(sum_ref)

    def body(rows, index, carry):
        held_ref[:, :full] = dot(grad_gated_ref[rows, :], w_ref[...], NN)
        base = index * part

        def inner(local, place, carry):
            here = pl.ds(pl.multiple_of(base + place * 16, 16), 16)
            pre_grad_ref[here, :] = (held_ref[local, :full] * slope_ref[here, :].astype(F32)).astype(LOW)
            sum_ref[...] += pre_grad_ref[here, own].astype(F32) * normed_ref[here, own].astype(F32)
            return carry

        for_rows(part, 16, inner, 0, unroll=2)
        grad_state_ref[rows, :] = dot(pre_grad_ref[rows, :], c_ref[...], NT)
        return carry

    for_rows(total, part, body, 0)
    rate_re = state[first_row : first_row + 1, :]
    rate_im = state[first_row + 1 : first_row + 2, :]
    gamma = jnp.broadcast_to(state[first_row + 2 : first_row + 3, :], (CHUNKS, states))

    def emit(rows, step, re, im, drive_re, drive_im, held):
        out_re, out_im = gamma * re, gamma * im
        if not reverse:
            keep = keep_rows(step, CHUNKS, steps, length)
            out_re, out_im = jnp.where(keep, out_re, 0.0), jnp.where(keep, out_im, 0.0)
        grad_driven_ref[rows, :states] = out_re.astype(LOW)
        grad_driven_ref[rows, states:] = out_im.astype(LOW)
        one, two, three = held
        own_re, own_im = re[:, :128], im[:, :128]
        late_re, late_im = own_re - drive_re[:, :128], own_im - drive_im[:, :128]
        low_re = low_ref[rows, :128].astype(F32)
        low_im = low_ref[rows, states : states + 128].astype(F32)
        one = one + late_re * low_re + late_im * low_im
        two = two + late_im * low_re - late_re * low_im
        three = three + own_re * drive_own_ref[rows, :128] + own_im * drive_own_ref[rows, 128:]
        return one, two, three

    zero = jnp.zeros((CHUNKS, 128), F32)
    one, two, three = sweep(grad_state_ref, rate_re, -rate_im, steps, reverse, emit, (zero, zero, zero))
    small_ref[0:1, 0:128] = jnp.sum(one, axis=0, keepdims=True)
    small_ref[1:2, 0:128] = jnp.sum(two, axis=0, keepdims=True)
    small_ref[2:3, 0:128] = jnp.sum(three, axis=0, keepdims=True)
    small_ref[3:4, 0:128] = jnp.sum(sum_ref[...], axis=0, keepdims=True)


def weight_grads(grads_ref, grad_driven_ref, normed_ref, low_ref, pre_grad_ref, grad_gated_ref, active_ref, quarter, states):
    full = normed_ref.shape[1]
    half = states // 4
    for place in range(2):
        lanes = slice(place * states, place * states + 128)
        got = dot(grad_driven_ref[:, lanes], normed_ref[...], TN)[:half, :]
        grads_ref[place * half : (place + 1) * half, :] = got.astype(LOW)
        got = dot(low_ref[:, lanes], pre_grad_ref[...], TN)[:half, :]
        got = got if place == 0 else -got
        grads_ref[128 + place * half : 128 + (place + 1) * half, :] = got.astype(LOW)
        lanes = pl.ds(pl.multiple_of(place * full + quarter * 128, 128), 128)
        got = dot(grad_gated_ref[:, lanes], active_ref[...], TN)
        grads_ref[256 + place * 128 : 256 + (place + 1) * 128, :] = got.astype(LOW)


def middle_kernel(
    meta_ref, stream_ref, sums_ref, b0, b1, b2, b3, c0, c1, c2, c3, w0, w1, w2, w3, feature_ref, state_ref, norm0_ref,
    t0, t1, t2, t3,
    result_ref, base_ref, bn_ref, grads_ref, small_ref, norm_ref,
    b_ref, c_ref, w_ref, normed_ref, drive_ref, drive_own_ref, low_ref, slope_ref, active_ref, held_ref, own_ref,
    order_ref, grad_gated_ref, pre_grad_ref, grad_driven_ref, sum_ref, bias_ref, part,
):
    length, quarter = meta_ref[0], meta_ref[1]
    total, full = stream_ref.shape
    steps = total // CHUNKS
    width = 128
    own = lanes_at(quarter, width)
    assemble_states((b0, b1, b2, b3), b_ref)
    assemble_output((c0, c1, c2, c3), c_ref)
    assemble_glu((w0, w1, w2, w3), w_ref, quarter)
    counted = norm0_ref[2:3, :]
    centre, inv_dev = norm_rows(total_rows(sums_ref, 2), counted)
    norm_ref[...] = jnp.zeros_like(norm_ref)
    norm_ref[0:1, :] = centre
    norm_ref[1:2, :] = inv_dev
    norm_ref[2:3, :] = counted
    gain = feature_ref[5 + GAIN : 6 + GAIN, :]
    shift = feature_ref[5 + SHIFT : 6 + SHIFT, :]
    skip = feature_ref[5 + SKIP : 6 + SKIP, :]

    def normal(rows, index, carry):
        keep = keep_rows(index, 16, steps, length)
        z = (stream_ref[rows, :] - centre) * inv_dev
        normed_ref[rows, :] = jnp.where(keep, z * gain + shift, 0.0).astype(LOW)
        return carry

    for_rows(total, 16, normal, 0, unroll=2)
    state = state_ref[...]
    states = state.shape[1]
    drive_phase(normed_ref, b_ref, drive_ref, state[5 + GAMMA : 6 + GAMMA, :], part)

    def emit(rows, step, re, im, drive_re, drive_im, held):
        low_ref[rows, :states] = re.astype(LOW)
        low_ref[rows, states:] = im.astype(LOW)
        drive_own_ref[rows, :128] = drive_re[:, :128]
        drive_own_ref[rows, 128:] = drive_im[:, :128]
        return held

    sweep(drive_ref, state[5:6, :], state[6:7, :], steps, True, emit, 0)
    pre_phase(low_ref, c_ref, normed_ref, skip, active_ref, slope_ref, held_ref.at[:, :full], part)
    bias_ref[...] = jnp.zeros_like(bias_ref)

    def body(rows, index, carry):
        held_ref[...] = dot(active_ref[rows, :], w_ref[...], NT)
        base = index * part

        def inner(local, place_index, carry):
            here = pl.ds(pl.multiple_of(base + place_index * 16, 16), 16)
            keep = keep_rows(index * (part // CHUNKS) + place_index, 16, steps, length)
            for place, value in enumerate((t0, t1, t2, t3)):
                lanes = lanes_at(quarter ^ place, width)
                far = pl.ds(pl.multiple_of(full + (quarter ^ place) * width, width), width)
                linear = held_ref[local, lanes] + feature_ref[5 + BIAS_LINEAR : 6 + BIAS_LINEAR, lanes]
                gate = sigmoid(held_ref[local, far] + feature_ref[5 + BIAS_GATE : 6 + BIAS_GATE, lanes])
                mixed = linear * gate
                up = jnp.where(keep, value[here, :].astype(F32), 0.0)
                grad_linear = (up * gate).astype(LOW)
                grad_gate = (up * mixed * (1.0 - gate)).astype(LOW)
                grad_gated_ref[here, lanes] = grad_linear
                grad_gated_ref[here, far] = grad_gate
                if place == 0:
                    own_ref[here, :] = stream_ref[here, lanes] + jnp.where(keep, mixed, 0.0)
                    bias_ref[0:16, :] += grad_linear.astype(F32)
                    bias_ref[16:32, :] += grad_gate.astype(F32)
            return carry

        for_rows(part, 16, inner, 0, unroll=2)
        return carry

    for_rows(total, part, body, 0)
    to_feature_rows(lambda rows, index: own_ref[rows, :], order_ref, result_ref, steps)
    small_ref[...] = jnp.zeros_like(small_ref)
    adjoint_phase(
        grad_gated_ref, w_ref, slope_ref, normed_ref, c_ref, low_ref, drive_own_ref, state, 5, quarter, length,
        pre_grad_ref, held_ref, drive_ref, grad_driven_ref, small_ref, sum_ref, False, part,
    )
    small_ref[4:5, 0:128] = jnp.sum(bias_ref[0:16, :], axis=0, keepdims=True)
    small_ref[5:6, 0:128] = jnp.sum(bias_ref[16:32, :], axis=0, keepdims=True)
    weight_grads(
        grads_ref, grad_driven_ref, normed_ref, low_ref, pre_grad_ref, grad_gated_ref, active_ref, quarter, states
    )
    bn_ref[...] = jnp.zeros_like(bn_ref)
    scale = inv_dev * gain

    def back(rows, index, carry):
        held_ref[:, :full] = dot(grad_driven_ref[rows, :], b_ref[...], NN)
        base = index * part

        def inner(local, place_index, carry):
            here = pl.ds(pl.multiple_of(base + place_index * 16, 16), 16)
            grad = held_ref[local, :full] + skip * pre_grad_ref[here, :].astype(F32)
            z = (stream_ref[here, :] - centre) * inv_dev
            bn_ref[0:16, :] += grad
            bn_ref[16:32, :] += grad * z
            base_ref[here, :] = scale * grad
            return carry

        for_rows(part, 16, inner, 0, unroll=2)
        return carry

    for_rows(total, part, back, 0)

    def add(rows, index, carry):
        for place, value in enumerate((t0, t1, t2, t3)):
            lanes = lanes_at(quarter ^ place, width)
            base_ref[rows, lanes] += value[rows, :].astype(F32)
        return carry

    for_rows(total, 16, add, 0, unroll=2)
    plain = jnp.sum(bn_ref[0:16, :], axis=0, keepdims=True)
    scaled = jnp.sum(bn_ref[16:32, :], axis=0, keepdims=True)
    bn_ref[0:1, :] = plain
    bn_ref[1:2, :] = scaled


def last_kernel(
    meta_ref, stream_ref, base_ref, sums_ref, norm1_ref, gate_ref, linear_ref, slope_ref, active_ref, normed_ref, low_ref,
    drive_own_ref, b_ref, c_ref, w_ref, feature_ref, state_ref, x_ref, norm0_ref, grads1_ref, small1_ref,
    send_ref, up_ref, grad_ref,
    held_ref, grad_state_ref, grad_gated_ref, pre_grad_ref, grad_driven_ref, sum_ref, bias_ref, small_ref, bn_ref,
    grads_ref, row_ref, part,
):
    length, quarter = meta_ref[0], meta_ref[1]
    total, full = stream_ref.shape
    steps = total // CHUNKS
    width = 128
    own = lanes_at(quarter, width)
    counted = norm0_ref[2:3, :]
    whole = total_rows(sums_ref, 2)
    centre, inv_dev = norm1_ref[0:1, :], norm1_ref[1:2, :]
    gain = feature_ref[5 + GAIN : 6 + GAIN, :]
    scale = inv_dev * gain
    level = scale * whole[0:1, :] / counted
    tilt = scale * inv_dev * whole[1:2, :] / counted
    bias_ref[...] = jnp.zeros_like(bias_ref)

    def top(rows, index, carry):
        keep = keep_rows(index, 16, steps, length)
        up = base_ref[rows, :] - jnp.where(keep, level + (stream_ref[rows, :] - centre) * tilt, 0.0)
        row_ref[...] = up
        up_ref[rows, :] = row_ref[:, own]
        up = jnp.where(keep, up, 0.0)
        grad_gated_ref[rows, :full] = (up * gate_ref[rows, :].astype(F32)).astype(LOW)
        grad_gated_ref[rows, full:] = (up * linear_ref[rows, :].astype(F32)).astype(LOW)
        bias_ref[0:16, :] += grad_gated_ref[rows, own].astype(F32)
        bias_ref[16:32, :] += grad_gated_ref[rows, pl.ds(pl.multiple_of(full + quarter * width, width), width)].astype(F32)
        return carry

    for_rows(total, 16, top, 0, unroll=2)
    small_ref[...] = jnp.zeros_like(small_ref)
    state = state_ref[...]
    states = state.shape[1]
    adjoint_phase(
        grad_gated_ref, w_ref, slope_ref, normed_ref, c_ref, low_ref, drive_own_ref, state, 2, quarter, length,
        pre_grad_ref, held_ref, grad_state_ref, grad_driven_ref, small_ref, sum_ref, True, part,
    )
    small_ref[4:5, 0:128] = jnp.sum(bias_ref[0:16, :], axis=0, keepdims=True)
    small_ref[5:6, 0:128] = jnp.sum(bias_ref[16:32, :], axis=0, keepdims=True)
    weight_grads(
        grads_ref, grad_driven_ref, normed_ref, low_ref, pre_grad_ref, grad_gated_ref, active_ref, quarter, states
    )
    bn_ref[...] = jnp.zeros_like(bn_ref)
    centre0, inv_dev0 = norm0_ref[0:1, own], norm0_ref[1:2, own]
    skip = feature_ref[SKIP : SKIP + 1, own]

    def back(rows, index, carry):
        held_ref[:, :width] = dot(grad_driven_ref[rows, :], b_ref[:, own], NN)
        base = index * part

        def inner(local, place_index, carry):
            here = pl.ds(pl.multiple_of(base + place_index * 16, 16), 16)
            grad = held_ref[local, :width] + skip * pre_grad_ref[here, own].astype(F32)
            grad_ref[here, :] = grad
            z = (x_ref[here, :] - centre0) * inv_dev0
            bn_ref[0:16, :] += grad
            bn_ref[16:32, :] += grad * z
            return carry

        for_rows(part, 16, inner, 0, unroll=2)
        return carry

    for_rows(total, part, back, 0)
    groups = send_ref.shape[0]
    share = send_ref.shape[1] - 32
    row_ref[0:8, :] = small_ref[...]
    row_ref[8:16, :] = small1_ref[...]
    row_ref[6:7, 0:width] = jnp.sum(bn_ref[0:16, :], axis=0, keepdims=True)
    row_ref[7:8, 0:width] = jnp.sum(bn_ref[16:32, :], axis=0, keepdims=True)
    exact = row_ref[...]
    high = exact.astype(LOW)
    rest = (exact - high.astype(F32)).astype(LOW)
    sections = ((grads_ref, 0), (grads1_ref, 0), (grads_ref, 128), (grads1_ref, 128),
                (grads_ref, 256), (grads_ref, 384), (grads1_ref, 256), (grads1_ref, 384))
    for group in range(groups):
        source, start = sections[group * share // 128]
        start += group * share % 128
        send_ref[group, :share, :] = source[start : start + share, :]
    for group in range(groups):
        send_ref[group, share : share + 16, :] = high
        send_ref[group, share + 16 :, :] = rest


def finish_kernel(
    meta_ref, got_ref, up_ref, grad_ref, x_ref, norm0_ref, feature_ref, nu_ref, theta_ref, bn1_ref,
    send_ref, nu_out, theta_out, gamma_out, skip_out, bias_out, gain_out, shift_out, out_ref,
    held_ref, row_ref, order_ref,
):
    length, quarter = meta_ref[0], meta_ref[1]
    groups = got_ref.shape[0]
    share = got_ref.shape[1] - 32
    total, width = x_ref.shape[0] - PARAM_ROWS, x_ref.shape[1]
    steps = total // CHUNKS
    own = lanes_at(quarter, width)
    small = jnp.zeros((16, got_ref.shape[2]), F32)
    for group in range(groups):
        small += got_ref[group, share : share + 16, :].astype(F32) + got_ref[group, share + 16 :, :].astype(F32)
    row_ref[...] = small
    for piece in range(0, share, 16):
        value = got_ref[0, piece : piece + 16, :].astype(F32)
        for group in range(1, groups):
            value += got_ref[group, piece : piece + 16, :].astype(F32)
        value = value.astype(LOW)
        for group in range(groups):
            send_ref[group, piece : piece + 16, :] = value
    states = nu_out.shape[1]
    bn1 = total_rows(bn1_ref, 2)
    held_ref[0:8, :] = bn1
    for layer, first in ((0, 0), (1, 8)):
        nu_out[layer : layer + 1, :] = -jnp.exp(nu_ref[layer : layer + 1, :]) * row_ref[first : first + 1, :states]
        theta_out[layer : layer + 1, :] = jnp.exp(theta_ref[layer : layer + 1, :]) * row_ref[first + 1 : first + 2, :states]
        gamma_out[layer : layer + 1, :] = row_ref[first + 2 : first + 3, :states]
        skip_out[layer : layer + 1, :] = row_ref[first + 3 : first + 4, :width]
        bias_out[layer, 0:1, :] = row_ref[first + 4 : first + 5, :width]
        bias_out[layer, 1:2, :] = row_ref[first + 5 : first + 6, :width]
    shift_out[0:1, :] = row_ref[6:7, :width]
    gain_out[0:1, :] = row_ref[7:8, :width]
    shift_out[1:2, :] = held_ref[0:1, own]
    gain_out[1:2, :] = held_ref[1:2, own]
    counted = norm0_ref[2:3, own]
    centre, inv_dev = norm0_ref[0:1, own], norm0_ref[1:2, own]
    level = row_ref[6:7, :width] / counted
    tilt = row_ref[7:8, :width] * inv_dev / counted
    scale = inv_dev * feature_ref[GAIN : GAIN + 1, own]

    def load(rows, index):
        keep = keep_rows(index, CHUNKS, steps, length)
        inner = grad_ref[rows, :] - level - (x_ref[rows, :] - centre) * tilt
        return up_ref[rows, :] + jnp.where(keep, scale * inner, 0.0)

    to_feature_rows(load, order_ref, out_ref, steps)


def call(kernel, outs, scratch, args, smem=1, flops=0, name=None):
    specs = [
        pl.BlockSpec(memory_space=pltpu.SMEM if place < smem else pltpu.VMEM) for place in range(len(args))
    ]
    moved = sum(a.size * a.dtype.itemsize for a in args) + sum(o.size * o.dtype.itemsize for o in outs)
    return pl.pallas_call(
        kernel,
        out_shape=tuple(outs),
        in_specs=specs,
        out_specs=tuple(pl.BlockSpec(memory_space=pltpu.VMEM) for _ in outs),
        scratch_shapes=scratch,
        compiler_params=pltpu.CompilerParams(vmem_limit_bytes=VMEM_BYTES),
        cost_estimate=pl.CostEstimate(flops=int(flops), bytes_accessed=int(moved), transcendentals=0),
        name=name,
    )(*args)


def shape(*dims, dtype=F32):
    return jax.ShapeDtypeStruct(dims, dtype)


def swap(value, bit, sharers):
    pairs = [(q * sharers + r, (q ^ bit) * sharers + r) for q in range(4) for r in range(sharers)]
    return lax.ppermute(value, "state", pairs)


def gather(value, sharers):
    across = swap(value, 2, sharers)
    return value, swap(value, 1, sharers), across, swap(across, 1, sharers)


def spread(value, axes, count):
    whole = jnp.broadcast_to(value[None], (count,) + value.shape)
    return lax.all_to_all(whole, axes, 0, 0, tiled=True).reshape((-1,) + value.shape[1:])


def local(
    inputs, lengths, cotangent, bn_gain, bn_bias, b_weight, c_weight, nu_log, theta_log, gamma_log, skip_weight,
    glu_weight, glu_bias, dp_size, state_size,
):
    sharers = state_size // 4
    place = lax.axis_index("state").astype(jnp.int32)
    quarter = place // sharers

    def joined(value, axis):
        if sharers == 1:
            return value
        groups = [[q * sharers + r for r in range(sharers)] for q in range(4)]
        return lax.all_gather(value, "state", axis=axis, axis_index_groups=groups, tiled=True)

    def own(value, axis):
        if sharers == 1:
            return value
        size = value.shape[axis] // sharers
        return lax.dynamic_slice_in_dim(value, place % sharers * size, size, axis)

    inputs, cotangent = joined(inputs, 1), joined(cotangent, 1)
    bn_gain, bn_bias, skip_weight = joined(bn_gain, 1), joined(bn_bias, 1), joined(skip_weight, 1)
    nu_log, theta_log, gamma_log = joined(nu_log, 1), joined(theta_log, 1), joined(gamma_log, 1)
    b_weight, c_weight = joined(b_weight, 2), joined(c_weight, 2)
    glu_weight, glu_bias = joined(glu_weight, 2), joined(glu_bias, 2)
    width, total = inputs.shape[1:]
    full = b_weight.shape[3]
    states = b_weight.shape[2] * 4
    own_states = b_weight.shape[2]
    part = 256
    meta = jnp.stack([lengths[0], quarter])
    modulus = jnp.exp(-jnp.exp(nu_log))
    angle = jnp.exp(theta_log)
    rates = jnp.stack([modulus * jnp.cos(angle), modulus * jnp.sin(angle), jnp.exp(gamma_log)], 1)
    rates = jnp.pad(rates.reshape(6, own_states), ((0, 0), (0, width - own_states)))
    features = jnp.concatenate(
        [jnp.stack([bn_gain, bn_bias, skip_weight], 1), glu_bias], 1
    ).reshape(10, width)
    params = jnp.concatenate([features, rates], 0)

    b_parts = [gather(b_weight[layer].reshape(2 * own_states, full), sharers) for layer in range(LAYERS)]
    c_parts = [gather(c_weight[layer].reshape(2 * own_states, full), sharers) for layer in range(LAYERS)]
    w_parts = [gather(glu_weight[layer].reshape(2 * width, full), sharers) for layer in range(LAYERS)]

    packed, sums = call(
        enter_kernel,
        (shape(total + PARAM_ROWS, width), shape(32, width)),
        [pltpu.VMEM((total, width), F32)],
        (meta, inputs[0], params),
        name="enter",
    )
    x_parts = gather(packed, sharers)
    sums = spread(sums[:8], ("dp", "state"), dp_size * state_size)
    if sharers > 1:
        sums = sums.reshape(dp_size * 4, sharers, 8, width)[:, 0].reshape(-1, width)
    cotangent_own, cotangent_low = call(
        cotangent_kernel,
        (shape(total, width), shape(total, width, dtype=LOW)),
        [pltpu.VMEM((total, width), F32)],
        (cotangent[0],),
        smem=0,
        name="cotangent",
    )
    cotangent_parts = (cotangent_own,) + gather(cotangent_low, sharers)[1:]
    (normed0, drive0, low0, slope0, active0, b_all, c_all, feature, state, norm0) = call(
        functools.partial(start_kernel, part=part),
        (
            shape(total, full, dtype=LOW),
            shape(total, 256),
            shape(total, 2 * states, dtype=LOW),
            shape(total, full, dtype=LOW),
            shape(total, full, dtype=LOW),
            shape(2 * states, full, dtype=LOW),
            shape(2 * states, full, dtype=LOW),
            shape(PARAM_ROWS, full),
            shape(8, states),
            shape(8, full),
        ),
        [pltpu.VMEM((total, 2 * states), F32), pltpu.VMEM((part, full), F32), pltpu.VMEM((8, full), F32)],
        (meta, *x_parts, sums, *b_parts[0], *c_parts[0]),
        flops=4e9,
        name="start",
    )
    stream1, linear0, gate0, w_all, sums1 = call(
        functools.partial(glu_kernel, part=part),
        (
            shape(total, full),
            shape(total, full, dtype=LOW),
            shape(total, full, dtype=LOW),
            shape(2 * full, full, dtype=LOW),
            shape(32, full),
        ),
        [pltpu.VMEM((part, 2 * full), F32)],
        (meta, *x_parts, active0, *w_parts[0], feature),
        flops=3e9,
        name="glu",
    )
    sums1 = spread(sums1[:8], "dp", dp_size)
    result, base, bn1, grads1, small1, norm1 = call(
        functools.partial(middle_kernel, part=part),
        (
            shape(width, total),
            shape(total, full),
            shape(32, full),
            shape(4 * width, full, dtype=LOW),
            shape(8, full),
            shape(8, full),
        ),
        [
            pltpu.VMEM((2 * states, full), LOW),
            pltpu.VMEM((2 * states, full), LOW),
            pltpu.VMEM((2 * full, full), LOW),
            pltpu.VMEM((total, full), LOW),
            pltpu.VMEM((total, 2 * states), F32),
            pltpu.VMEM((total, 256), F32),
            pltpu.VMEM((total, 2 * states), LOW),
            pltpu.VMEM((total, full), F32),
            pltpu.VMEM((total, full), LOW),
            pltpu.VMEM((part, 2 * full), F32),
            pltpu.VMEM((total, width), F32),
            pltpu.VMEM((total, width), F32),
            pltpu.VMEM((total, 2 * full), LOW),
            pltpu.VMEM((total, full), LOW),
            pltpu.VMEM((total, 2 * states), LOW),
            pltpu.VMEM((16, width), F32),
            pltpu.VMEM((32, width), F32),
        ],
        (meta, stream1, sums1, *b_parts[1], *c_parts[1], *w_parts[1], feature, state, norm0, *cotangent_parts),
        flops=2e10,
        name="middle",
    )
    bn1 = spread(bn1[:8], "dp", dp_size)
    share = 8 * width // dp_size
    send, up0, grad0 = call(
        functools.partial(last_kernel, part=part),
        (shape(dp_size, share + 32, full, dtype=LOW), shape(total, width), shape(total, width)),
        [
            pltpu.VMEM((part, 2 * full), F32),
            pltpu.VMEM((total, 2 * states), F32),
            pltpu.VMEM((total, 2 * full), LOW),
            pltpu.VMEM((total, full), LOW),
            pltpu.VMEM((total, 2 * states), LOW),
            pltpu.VMEM((16, width), F32),
            pltpu.VMEM((32, width), F32),
            pltpu.VMEM((8, full), F32),
            pltpu.VMEM((32, width), F32),
            pltpu.VMEM((4 * width, full), LOW),
            pltpu.VMEM((16, full), F32),
        ],
        (meta, stream1, base, bn1, norm1, gate0, linear0, slope0, active0, normed0, low0, drive0, b_all, c_all, w_all,
         feature, state, packed, norm0, grads1, small1),
        flops=1e10,
        name="last",
    )
    got = lax.all_to_all(send, "dp", 0, 0, tiled=True)
    back, grad_nu, grad_theta, grad_gamma, grad_skip, grad_bias, grad_gain, grad_shift, grad_inputs = call(
        finish_kernel,
        (
            shape(dp_size, share, full, dtype=LOW),
            shape(LAYERS, own_states),
            shape(LAYERS, own_states),
            shape(LAYERS, own_states),
            shape(LAYERS, width),
            shape(LAYERS, 2, width),
            shape(LAYERS, width),
            shape(LAYERS, width),
            shape(width, total),
        ),
        [pltpu.VMEM((8, full), F32), pltpu.VMEM((16, full), F32), pltpu.VMEM((total, width), F32)],
        (meta, got, up0, grad0, packed, norm0, feature, nu_log, theta_log, bn1),
        name="finish",
    )
    whole = lax.all_to_all(back, "dp", 0, 0, tiled=True).reshape(8 * width, full).astype(F32)
    grad_b = whole[: 2 * width].reshape(LAYERS, 2, own_states, full)
    grad_c = whole[2 * width : 4 * width].reshape(LAYERS, 2, own_states, full)
    grad_glu = whole[4 * width :].reshape(LAYERS, 2, width, full)
    return (
        own(result[None], 1),
        own(grad_inputs[None], 1),
        own(grad_gain, 1),
        own(grad_shift, 1),
        own(grad_b, 2),
        own(grad_c, 2),
        own(grad_nu, 1),
        own(grad_theta, 1),
        own(grad_gamma, 1),
        own(grad_skip, 1),
        own(grad_glu, 2),
        own(grad_bias, 2),
    )


def solution(mesh):
    in_specs = (
        P("dp", "state", None),
        P("dp"),
        P("dp", "state", None),
        P(None, "state"),
        P(None, "state"),
        P(None, None, "state", None),
        P(None, None, "state", None),
        P(None, "state"),
        P(None, "state"),
        P(None, "state"),
        P(None, "state"),
        P(None, None, "state", None),
        P(None, None, "state"),
    )
    out_specs = (
        P("dp", "state", None),
        P("dp", "state", None),
        P(None, "state"),
        P(None, "state"),
        P(None, None, "state", None),
        P(None, None, "state", None),
        P(None, "state"),
        P(None, "state"),
        P(None, "state"),
        P(None, "state"),
        P(None, None, "state", None),
        P(None, None, "state"),
    )
    step = functools.partial(local, dp_size=mesh.shape["dp"], state_size=mesh.shape["state"])
    return jax.shard_map(step, mesh=mesh, in_specs=in_specs, out_specs=out_specs, check_vma=False)
```

time: 906 us -> 205 us (0.23); the launches traced: 890 us -> 204 us
  local copies, waits for them, and re-layouts: 314 us -> 10.9 us
  waiting for transfers between devices: 267 us -> 22.5 us
  other arithmetic: 155 us -> 2.69 us
  Pallas kernels: 0 us -> 68.5 us
  blocking collectives: 105 us -> 73.1 us
  matrix products: 28.8 us -> 0 us
  starting transfers between devices: 1.18 us -> 24.5 us
  between operations: 18.9 us -> 1.7 us
    slice x288 -> x8, local copies, waits for them, and re-layouts: 150 us -> 7.55 us  [the longest x1 1.18 us: local(): c_weight[layer].reshape(2 * own_states, full)]
    unnamed x19 -> x0, waiting for transfers between devices: 142 us -> none
    psum x5 -> x0, blocking collectives: 105 us -> none  [the longest x2 45.1 us: local(): lax.psum((jnp.sum(hidden_state * valid3, axis=(0, 2)), jnp.sum(hidden_sta...]
    add x161 -> x0, other arithmetic: 84.1 us -> none  [the longest x80 38.3 us: sweep(): lax.associative_scan(combine, (power_re, power_im, real_part, imag_part),...]
    unnamed x328 -> x56, local copies, waits for them, and re-layouts: 79.5 us -> 2.04 us
    all_to_all x0 -> x3, blocking collectives: none -> 73.1 us  [the longest x1 34 us: local(): got = lax.all_to_all(send, 'dp', 0, 0, tiled=True)]
    pallas_call x0 -> x7, Pallas kernels: none -> 68.5 us  [call(): pl.pallas_call(kernel, out_shape=tuple(outs), in_specs=specs, out_specs=t...]
    psum x1 -> x0, waiting for transfers between devices: 63.4 us -> none  [local(): lax.psum(grad_b_matrix.reshape(2, states_here, full_width).astype(jnp.bfl...]
  transfers between devices with their start and end apart: 13 -> 26, of which waited for: 12 -> 6; matrix products, arithmetic and copies ran while one was open for 6% -> 3% of each run, Pallas kernels for 0% -> 11%
where the time goes in v1:
time: 205 us; the launch traced here: 204 us
  blocking collectives  73.1 us (36%)
  Pallas kernels  68.5 us (33%)
  starting transfers between devices  24.5 us (12%)
  waiting for transfers between devices  22.5 us (11%)
  local copies, waits for them, and re-layouts  10.9 us (5%)
  other arithmetic  2.69 us (1%)
    pallas_call x7, Pallas kernels, call(): pl.pallas_call(kernel, out_shape=tuple(outs), in_specs=specs, out_specs=t...  68.5 us
    all_to_all x1, blocking collectives, local(): got = lax.all_to_all(send, 'dp', 0, 0, tiled=True)  34 us
    all_to_all x1, blocking collectives, local(): lax.all_to_all(back, 'dp', 0, 0, tiled=True).reshape(8 * width, full)  28.7 us
    ppermute x24, starting transfers between devices, swap(): return lax.ppermute(value, 'state', pairs)  15.2 us
    ppermute x24, waiting for transfers between devices, swap(): return lax.ppermute(value, 'state', pairs)  15 us
    all_to_all x1, blocking collectives, spread(): lax.all_to_all(whole, axes, 0, 0, tiled=True)  10.4 us
    all_to_all x2, starting transfers between devices, spread(): lax.all_to_all(whole, axes, 0, 0, tiled=True)  9.32 us
    all_to_all x2, waiting for transfers between devices, spread(): lax.all_to_all(whole, axes, 0, 0, tiled=True)  7.45 us
  transfers between devices with their start and end apart: 26, of which 6 were waited for; matrix products, arithmetic and copies ran while one was open for 3% of the time, Pallas kernels for 11%

profile of v1, /device:TPU:0, one launch (start us, length us, event | category | flops | bytes accessed | tf_op | source)
XLA Modules:
  0.0 203.9 jit_solution(12902829127298501319)
XLA Ops:
  1.3 0.8 multiply_bitcast_fusion.1
  2.1 0.7 pad_maximum_fusion
  2.8 0.6 pad_add_fusion.meta_ref
  3.4 0.6 select_maximum_fusion.params_ref
  4.0 2.5 %enter.1 = (f32[1040,128]{1,0:T(8,128)}, f32[32,128]{1,0:T(8,128)}) custom-call(s32[2]{0:T(128)} %pad_add_fusion.meta_ref, f32[128,1024]{1,0:T(8,128)} %bitcast.29, f32[16,128]{1,0:T(8,128)} %select_maximum_fusion.params_ref), custom_call_target="tpu_custom_call" | custom-call | bytes 1081352 | tf_op jit(solution)/shard_map/enter/pallas_call | solution.py:691
  6.6 2.9 %collective-permute-start.1 = (f32[1040,128]{1,0:T(8,128)}, f32[1040,128]{1,0:T(8,128)S(1)}, u32[]{:S(2)}, u32[]{:S(2)}) collective-permute-start(f32[1040,128]{1,0:T(8,128)} %get-tuple-element.49.x0.x_ref), channel_id=1, source_target_pairs={{0,2},{1,3},{2,0},{3,1},{4,6},{5,7},{6,4},{7,5},{8,10},{9,11},{10,... | collective-permute-start | bytes 1597448 | tf_op jit(solution)/shard_map/ppermute | solution.py:709
  9.5 1.0 fusion.3
  10.7 0.5 collective-permute-start
  11.2 1.9 collective-permute-start.13
  13.1 9.5 %collective-permute-done.1.x2 = f32[1040,128]{1,0:T(8,128)S(1)} collective-permute-done((f32[1040,128]{1,0:T(8,128)}, f32[1040,128]{1,0:T(8,128)S(1)}, u32[]{:S(2)}, u32[]{:S(2)}) %collective-permute-start.1) | collective-permute-done | bytes 532512 | tf_op jit(solution)/shard_map/ppermute | solution.py:709
  22.7 1.2 fusion.2
  23.9 1.6 collective-permute-done.4.b2
  25.5 2.1 %collective-permute-start.7 = (bf16[128,512]{1,0:T(8,128)(2,1)S(1)}, bf16[128,512]{1,0:T(8,128)(2,1)}, u32[]{:S(2)}, u32[]{:S(2)}) collective-permute-start(bf16[128,512]{1,0:T(8,128)(2,1)S(1)} %bitcast.50), channel_id=1, source_target_pairs={{0,2},{1,3},{2,0},{3,1},{4,6},{5,7},{6,4},{7,5},{8,10},{9,11},{10,... | collective-permute-start | bytes 393224 | tf_op jit(solution)/shard_map/ppermute | solution.py:709
  27.6 1.1 fusion.1
  29.0 0.3 collective-permute-start.16
  29.3 2.5 %collective-permute-done.7.c2 = bf16[128,512]{1,0:T(8,128)(2,1)} collective-permute-done((bf16[128,512]{1,0:T(8,128)(2,1)S(1)}, bf16[128,512]{1,0:T(8,128)(2,1)}, u32[]{:S(2)}, u32[]{:S(2)}) %collective-permute-start.7) | collective-permute-done | bytes 131104 | tf_op jit(solution)/shard_map/ppermute | solution.py:709
  31.8 2.2 %collective-permute-start.10 = (bf16[256,512]{1,0:T(8,128)(2,1)S(1)}, bf16[256,512]{1,0:T(8,128)(2,1)S(1)}, u32[]{:S(2)}, u32[]{:S(2)}) collective-permute-start(bf16[256,512]{1,0:T(8,128)(2,1)S(1)} %bitcast.36), channel_id=1, source_target_pairs={{0,2},{1,3},{2,0},{3,1},{4,6},{5,7},{6,4},{7,5},{8,10},{9,11},{10,... | collective-permute-start | bytes 786440 | tf_op jit(solution)/shard_map/ppermute | solution.py:709
  34.0 0.7 slice.39
  34.7 0.7 broadcast_in_dim.10
  35.4 4.9 %all-to-all-start = ((f32[32,8,128]{2,1,0:T(8,128)}), f32[32,8,128]{2,1,0:T(8,128)S(1)}, u32[]{:S(2)}, u32[]{:S(2)}) async-start(f32[32,8,128]{2,1,0:T(8,128)} %broadcast_in_dim.10), calls=%async_computation | async-start | bytes 262144 | tf_op jit(solution)/shard_map/all_to_all | solution.py:719
  40.3 0.3 collective-permute-start.5
  40.6 0.3 collective-permute-start.8
  40.9 2.6 %cotangent.1 = (f32[1024,128]{1,0:T(8,128)}, bf16[1024,128]{1,0:T(8,128)(2,1)}) custom-call(f32[128,1024]{1,0:T(8,128)} %bitcast.30), custom_call_target="tpu_custom_call" | custom-call | bytes 1310720 | tf_op jit(solution)/shard_map/cotangent/pallas_call | solution.py:691
  44.0 0.7 copy-done.13
  44.7 1.8 collective-permute-start.19
  46.5 0.3 collective-permute-start.22
  46.9 1.6 all-to-all-done
  48.6 0.6 copy-done.2
  49.2 11.1 %start.1 = (bf16[1024,512]{1,0:T(8,128)(2,1)}, f32[1024,256]{1,0:T(8,128)}, bf16[1024,512]{1,0:T(8,128)(2,1)}, bf16[1024,512]{1,0:T(8,128)(2,1)}, bf16[1024,512]...) custom-call(s32[2]{0:T(128)} %pad_add_fusion.meta_ref, ...), custom_call_target="tpu_custom_call" | custom-call | flops 4000000000 | bytes 9658376 | tf_op jit(solution)/shard_map/start/pallas_call | solution.py:691
  60.4 0.3 collective-permute-start.18
  61.0 0.3 collective-permute-start.14
  61.5 0.3 collective-permute-start.23
  61.8 8.7 %glu.1 = (f32[1024,512]{1,0:T(8,128)}, bf16[1024,512]{1,0:T(8,128)(2,1)}, bf16[1024,512]{1,0:T(8,128)(2,1)}, bf16[1024,512]{1,0:T(8,128)(2,1)}, f32[32,512]{1,0:T(8,128)}) custom-call(s32[2]{0:T(128)} %pad_add_fusion.meta_ref, f32[1040,128]{1,0:T(8,128)} %get-tuple-element.49.x0.x_ref, f32[1040,128]{1,0:T(8,128)} %copy-done.9, f32[1040,128]{1,0:T(8,128)} %copy-done.8, ...), custom_call_target="tpu_custom_call" | custom-call | flops 3000000000 | bytes 9568264 | tf_op jit(solution)/shard_map/glu/pallas_call | solution.py:691
  70.5 0.7 slice.43
  71.2 0.7 broadcast_in_dim.11
  71.9 4.4 %all-to-all-start.1 = ((f32[8,8,512]{2,1,0:T(8,128)}), f32[8,8,512]{2,1,0:T(8,128)S(1)}, u32[]{:S(2)}, u32[]{:S(2)}) async-start(f32[8,8,512]{2,1,0:T(8,128)} %broadcast_in_dim.11), calls=%async_computation.1 | async-start | bytes 262144 | tf_op jit(solution)/shard_map/all_to_all | solution.py:719
  76.4 1.3 collective-permute-done.17.c3
  77.8 5.8 %all-to-all-done.1 = f32[8,8,512]{2,1,0:T(8,128)S(1)} async-done(((f32[8,8,512]{2,1,0:T(8,128)}), f32[8,8,512]{2,1,0:T(8,128)S(1)}, u32[]{:S(2)}, u32[]{:S(2)}) %all-to-all-start.1) | async-done | bytes 131104 | tf_op jit(solution)/shard_map/all_to_all | solution.py:719
  83.7 0.6 copy-done.3
  84.3 24.6 %middle.1 = (f32[128,1024]{1,0:T(8,128)}, f32[1024,512]{1,0:T(8,128)}, f32[32,512]{1,0:T(8,128)}, bf16[512,512]{1,0:T(8,128)(2,1)}, f32[8,512]{1,0:T(8,128)}, /*index=5*/f32[8,512]{1,0:T(8,128)}) custom-call(s32[2]{0:T(128)} %pad_add_fusion.meta_ref, f32[1024,512]{1,0:T(8,128)} %get-tuple-element.53.stream_ref, f32[64,512]{1,0:T(8,128)} %bitcast.40, ...), custom_call_target="tpu_custom_call" | custom-call | flops 20000000000 | bytes 8937480 | tf_op jit(solution)/shard_map/middle/pallas_call | solution.py:691
  108.9 0.7 slice.47
  109.6 10.4 %all_to_all.25 = f32[8,8,512]{2,1,0:T(8,128)} all-to-all(f32[8,8,512]{2,1,0:T(8,128)S(1)} %broadcast_in_dim.13), channel_id=1, replica_groups=mesh['dp'=8,'state'=4] {'dp'}, dimensions={0} | all-to-all | bytes 262144 | tf_op jit(solution)/shard_map/all_to_all | solution.py:719
  120.0 15.3 %last.1 = (bf16[8,160,512]{2,1,0:T(8,128)(2,1)}, f32[1024,128]{1,0:T(8,128)}, f32[1024,128]{1,0:T(8,128)}) custom-call(s32[2]{0:T(128)} %pad_add_fusion.meta_ref, f32[1024,512]{1,0:T(8,128)} %get-tuple-element.53.stream_ref, f32[1024,512]{1,0:T(8,128)} %get-tuple-element.60.base_ref, f32[64,512]{1,0:T(8,128)} %bitcast.27, ...), custom_call_target="tpu_custom_call" | custom-call | flops 10000000000 | bytes 17268744 | tf_op jit(solution)/shard_map/last/pallas_call | solution.py:691
  135.3 34.0 %all_to_all.26.got_ref = bf16[8,160,512]{2,1,0:T(8,128)(2,1)} all-to-all(bf16[8,160,512]{2,1,0:T(8,128)(2,1)} %get-tuple-element.74), channel_id=1, replica_groups=mesh['dp'=8,'state'=4] {'dp'}, dimensions={0} | all-to-all | bytes 2621440 | tf_op jit(solution)/shard_map/all_to_all | solution.py:876
  169.3 3.7 %finish.1 = (bf16[8,128,512]{2,1,0:T(8,128)(2,1)}, f32[2,64]{1,0:T(2,128)}, f32[2,64]{1,0:T(2,128)}, f32[2,64]{1,0:T(2,128)}, f32[2,128]{1,0:T(2,128)}, /*index=...) custom-call(s32[2]{0:T(128)} %pad_add_fusion.meta_ref, ...), custom_call_target="tpu_custom_call" | custom-call | bytes 4652552 | tf_op jit(solution)/shard_map/finish/pallas_call | solution.py:691
  173.1 28.7 %all_to_all.27 = bf16[8,128,512]{2,1,0:T(8,128)(2,1)S(1)} all-to-all(bf16[8,128,512]{2,1,0:T(8,128)(2,1)} %get-tuple-element.80), channel_id=1, replica_groups=mesh['dp'=8,'state'=4] {'dp'}, dimensions={0} | all-to-all | bytes 2097152 | tf_op jit(solution)/shard_map/all_to_all | solution.py:894
  201.7 1.1 slice.53
  202.8 1.1 fusion
  (89 shorter events, 1.7 us)
Async XLA Ops:
  6.6 16.1 %collective-permute-start.1 = (f32[1040,128]{1,0:T(8,128)}, f32[1040,128]{1,0:T(8,128)S(1)}, u32[]{:S(2)}, u32[]{:S(2)}) collective-permute-start(f32[1040,128]{1,0:T(8,128)} %get-tuple-element.49.x0.x_ref), channel_id=1, source_target_pairs={{0,2},{1,3},{2,0},{3,1},{4,6},{5,7},{6,4},{7,5},{8,10},{9,11},{10,... | collective-permute-start | bytes 1597448 | tf_op jit(solution)/shard_map/ppermute | solution.py:709
  10.5 38.0 %copy-start.6 = (bf16[1,2,64,512]{3,2,1,0:T(8,128)(2,1)}, bf16[1,2,64,512]{3,2,1,0:T(8,128)(2,1)S(1)}, u32[]{:S(2)}) copy-start(bf16[1,2,64,512]{3,2,1,0:T(8,128)(2,1)S(1)} %get-tuple-element.93) | copy-start | bytes 393220
  10.5 49.8 %copy-start.4 = (bf16[1,2,64,512]{3,2,1,0:T(8,128)(2,1)}, bf16[1,2,64,512]{3,2,1,0:T(8,128)(2,1)S(1)}, u32[]{:S(2)}) copy-start(bf16[1,2,64,512]{3,2,1,0:T(8,128)(2,1)S(1)} %get-tuple-element.92) | copy-start | bytes 393220
  10.5 14.9 %collective-permute-start.4 = (bf16[128,512]{1,0:T(8,128)(2,1)S(1)}, bf16[128,512]{1,0:T(8,128)(2,1)S(1)}, u32[]{:S(2)}, u32[]{:S(2)}) collective-permute-start(bf16[128,512]{1,0:T(8,128)(2,1)S(1)} %bitcast.47), channel_id=1, source_target_pairs={{0,2},{1,3},{2,0},{3,1},{4,6},{5,7},{6,4},{7,5},{8,10},{9,11},{10,... | collective-permute-start | bytes 393224 | tf_op jit(solution)/shard_map/ppermute | solution.py:709
  10.6 14.9 %collective-permute-start.3 = (bf16[128,512]{1,0:T(8,128)(2,1)S(1)}, bf16[128,512]{1,0:T(8,128)(2,1)S(1)}, u32[]{:S(2)}, u32[]{:S(2)}) collective-permute-start(bf16[128,512]{1,0:T(8,128)(2,1)S(1)} %bitcast.48), channel_id=1, source_target_pairs={{0,1},{1,0},{2,3},{3,2},{4,5},{5,4},{6,7},{7,6},{8,9},{9,8},{10,11... | collective-permute-start | bytes 393224 | tf_op jit(solution)/shard_map/ppermute | solution.py:709
  10.7 35.8 %collective-permute-start = (f32[1040,128]{1,0:T(8,128)}, f32[1040,128]{1,0:T(8,128)S(1)}, u32[]{:S(2)}, u32[]{:S(2)}) collective-permute-start(f32[1040,128]{1,0:T(8,128)} %get-tuple-element.49.x0.x_ref), channel_id=1, source_target_pairs={{0,1},{1,0},{2,3},{3,2},{4,5},{5,4},{6,7},{7,6},{8,9},{9,8},{10,11... | collective-permute-start | bytes 1597448 | tf_op jit(solution)/shard_map/ppermute | solution.py:709
  11.2 17.5 %collective-permute-start.13 = (bf16[128,512]{1,0:T(8,128)(2,1)S(1)}, bf16[128,512]{1,0:T(8,128)(2,1)S(1)}, u32[]{:S(2)}, u32[]{:S(2)}) collective-permute-start(bf16[128,512]{1,0:T(8,128)(2,1)S(1)} %bitcast.41), channel_id=1, source_target_pairs={{0,2},{1,3},{2,0},{3,1},{4,6},{5,7},{6,4},{7,5},{8,10},{9,11},{10,... | collective-permute-start | bytes 393224 | tf_op jit(solution)/shard_map/ppermute | solution.py:709
  22.6 25.9 %copy-start.8 = (f32[1040,128]{1,0:T(8,128)}, f32[1040,128]{1,0:T(8,128)S(1)}, u32[]{:S(2)}) copy-start(f32[1040,128]{1,0:T(8,128)S(1)} %collective-permute-done.1.x2) | copy-start | bytes 1597444
  22.6 24.2 %collective-permute-start.2 = (f32[1040,128]{1,0:T(8,128)S(1)}, f32[1040,128]{1,0:T(8,128)S(1)}, u32[]{:S(2)}, u32[]{:S(2)}) collective-permute-start(f32[1040,128]{1,0:T(8,128)S(1)} %collective-permute-done.1.x2), channel_id=1, source_target_pairs={{0,1},{1,0},{2,3},{3,2},{4,5},{5,4},{6,7},{7,6},{8,9},{9,8},{10,11... | collective-permute-start | bytes 1597448 | tf_op jit(solution)/shard_map/ppermute | solution.py:709
  23.8 24.7 %copy-start.7 = (bf16[1,2,64,512]{3,2,1,0:T(8,128)(2,1)}, bf16[1,2,64,512]{3,2,1,0:T(8,128)(2,1)S(1)}, u32[]{:S(2)}) copy-start(bf16[1,2,64,512]{3,2,1,0:T(8,128)(2,1)S(1)} %get-tuple-element.91) | copy-start | bytes 393220
  23.8 36.5 %copy-start.5 = (bf16[1,2,64,512]{3,2,1,0:T(8,128)(2,1)}, bf16[1,2,64,512]{3,2,1,0:T(8,128)(2,1)S(1)}, u32[]{:S(2)}) copy-start(bf16[1,2,64,512]{3,2,1,0:T(8,128)(2,1)S(1)} %get-tuple-element.90) | copy-start | bytes 393220
  25.5 21.0 %copy-start.22 = (bf16[128,512]{1,0:T(8,128)(2,1)}, bf16[128,512]{1,0:T(8,128)(2,1)S(1)}, u32[]{:S(2)}) copy-start(bf16[128,512]{1,0:T(8,128)(2,1)S(1)} %collective-permute-done.4.b2) | copy-start | bytes 393220
  25.5 3.5 %collective-permute-start.12 = (bf16[128,512]{1,0:T(8,128)(2,1)S(1)}, bf16[128,512]{1,0:T(8,128)(2,1)S(1)}, u32[]{:S(2)}, u32[]{:S(2)}) collective-permute-start(bf16[128,512]{1,0:T(8,128)(2,1)S(1)} %bitcast.42), channel_id=1, source_target_pairs={{0,1},{1,0},{2,3},{3,2},{4,5},{5,4},{6,7},{7,6},{8,9},{9,8},{10,11... | collective-permute-start | bytes 393224 | tf_op jit(solution)/shard_map/ppermute | solution.py:709
  25.5 9.9 %copy-start.23 = (bf16[128,512]{1,0:T(8,128)(2,1)}, bf16[128,512]{1,0:T(8,128)(2,1)S(1)}, u32[]{:S(2)}) copy-start(bf16[128,512]{1,0:T(8,128)(2,1)S(1)} %collective-permute-done.3.b1) | copy-start | bytes 393220
  25.5 6.3 %collective-permute-start.7 = (bf16[128,512]{1,0:T(8,128)(2,1)S(1)}, bf16[128,512]{1,0:T(8,128)(2,1)}, u32[]{:S(2)}, u32[]{:S(2)}) collective-permute-start(bf16[128,512]{1,0:T(8,128)(2,1)S(1)} %bitcast.50), channel_id=1, source_target_pairs={{0,2},{1,3},{2,0},{3,1},{4,6},{5,7},{6,4},{7,5},{8,10},{9,11},{10,... | collective-permute-start | bytes 393224 | tf_op jit(solution)/shard_map/ppermute | solution.py:709
  28.7 31.7 %copy-start.1 = (bf16[1,2,128,512]{3,2,1,0:T(8,128)(2,1)}, bf16[1,2,128,512]{3,2,1,0:T(8,128)(2,1)S(1)}, u32[]{:S(2)}) copy-start(bf16[1,2,128,512]{3,2,1,0:T(8,128)(2,1)S(1)} %get-tuple-element.89) | copy-start | bytes 786436
  28.7 31.7 %copy-start = (bf16[1,2,128,512]{3,2,1,0:T(8,128)(2,1)}, bf16[1,2,128,512]{3,2,1,0:T(8,128)(2,1)S(1)}, u32[]{:S(2)}) copy-start(bf16[1,2,128,512]{3,2,1,0:T(8,128)(2,1)S(1)} %get-tuple-element.88) | copy-start | bytes 786436
  28.7 32.2 %copy-start.18 = (bf16[128,512]{1,0:T(8,128)(2,1)}, bf16[128,512]{1,0:T(8,128)(2,1)S(1)}, u32[]{:S(2)}) copy-start(bf16[128,512]{1,0:T(8,128)(2,1)S(1)} %collective-permute-done.13.b2) | copy-start | bytes 393220
  28.7 11.6 %collective-permute-start.6 = (bf16[128,512]{1,0:T(8,128)(2,1)S(1)}, bf16[128,512]{1,0:T(8,128)(2,1)}, u32[]{:S(2)}, u32[]{:S(2)}) collective-permute-start(bf16[128,512]{1,0:T(8,128)(2,1)S(1)} %bitcast.51), channel_id=1, source_target_pairs={{0,1},{1,0},{2,3},{3,2},{4,5},{5,4},{6,7},{7,6},{8,9},{9,8},{10,11... | collective-permute-start | bytes 393224 | tf_op jit(solution)/shard_map/ppermute | solution.py:709
  29.0 11.7 %collective-permute-start.16 = (bf16[128,512]{1,0:T(8,128)(2,1)S(1)}, bf16[128,512]{1,0:T(8,128)(2,1)S(1)}, u32[]{:S(2)}, u32[]{:S(2)}) collective-permute-start(bf16[128,512]{1,0:T(8,128)(2,1)S(1)} %bitcast.44), channel_id=1, source_target_pairs={{0,2},{1,3},{2,0},{3,1},{4,6},{5,7},{6,4},{7,5},{8,10},{9,11},{10,... | collective-permute-start | bytes 393224 | tf_op jit(solution)/shard_map/ppermute | solution.py:709
  31.8 12.2 %collective-permute-start.10 = (bf16[256,512]{1,0:T(8,128)(2,1)S(1)}, bf16[256,512]{1,0:T(8,128)(2,1)S(1)}, u32[]{:S(2)}, u32[]{:S(2)}) collective-permute-start(bf16[256,512]{1,0:T(8,128)(2,1)S(1)} %bitcast.36), channel_id=1, source_target_pairs={{0,2},{1,3},{2,0},{3,1},{4,6},{5,7},{6,4},{7,5},{8,10},{9,11},{10,... | collective-permute-start | bytes 786440 | tf_op jit(solution)/shard_map/ppermute | solution.py:709
  35.4 13.2 %all-to-all-start = ((f32[32,8,128]{2,1,0:T(8,128)}), f32[32,8,128]{2,1,0:T(8,128)S(1)}, u32[]{:S(2)}, u32[]{:S(2)}) async-start(f32[32,8,128]{2,1,0:T(8,128)} %broadcast_in_dim.10), calls=%async_computation | async-start | bytes 262144 | tf_op jit(solution)/shard_map/all_to_all | solution.py:719
  40.3 3.2 %collective-permute-start.5 = (bf16[128,512]{1,0:T(8,128)(2,1)S(1)}, bf16[128,512]{1,0:T(8,128)(2,1)S(1)}, u32[]{:S(2)}, u32[]{:S(2)}) collective-permute-start(bf16[128,512]{1,0:T(8,128)(2,1)S(1)} %collective-permute-done.4.b2), channel_id=1, source_target_pairs={{0,1},{1,0},{2,3},{3,2},{4,5},{5,4},{6,7},{7,6},{8,9},{9,8},{10,11... | collective-permute-start | bytes 393224 | tf_op jit(solution)/shard_map/ppermute | solution.py:709
  40.6 5.8 %copy-start.20 = (bf16[128,512]{1,0:T(8,128)(2,1)}, bf16[128,512]{1,0:T(8,128)(2,1)S(1)}, u32[]{:S(2)}) copy-start(bf16[128,512]{1,0:T(8,128)(2,1)S(1)} %collective-permute-done.16.c2) | copy-start | bytes 393220
  40.6 3.1 %collective-permute-start.8 = (bf16[128,512]{1,0:T(8,128)(2,1)}, bf16[128,512]{1,0:T(8,128)(2,1)S(1)}, u32[]{:S(2)}, u32[]{:S(2)}) collective-permute-start(bf16[128,512]{1,0:T(8,128)(2,1)} %collective-permute-done.7.c2), channel_id=1, source_target_pairs={{0,1},{1,0},{2,3},{3,2},{4,5},{5,4},{6,7},{7,6},{8,9},{9,8},{10,11... | collective-permute-start | bytes 393224 | tf_op jit(solution)/shard_map/ppermute | solution.py:709
  43.5 3.3 %copy-start.25 = (bf16[128,512]{1,0:T(8,128)(2,1)}, bf16[128,512]{1,0:T(8,128)(2,1)S(1)}, u32[]{:S(2)}) copy-start(bf16[128,512]{1,0:T(8,128)(2,1)S(1)} %collective-permute-done.5.b3) | copy-start | bytes 393220
  43.5 16.9 %collective-permute-start.15 = (bf16[128,512]{1,0:T(8,128)(2,1)S(1)}, bf16[128,512]{1,0:T(8,128)(2,1)}, u32[]{:S(2)}, u32[]{:S(2)}) collective-permute-start(bf16[128,512]{1,0:T(8,128)(2,1)S(1)} %bitcast.45), channel_id=1, source_target_pairs={{0,1},{1,0},{2,3},{3,2},{4,5},{5,4},{6,7},{7,6},{8,9},{9,8},{10,11... | collective-permute-start | bytes 393224 | tf_op jit(solution)/shard_map/ppermute | solution.py:709
  43.7 3.1 %copy-start.26 = (bf16[128,512]{1,0:T(8,128)(2,1)}, bf16[128,512]{1,0:T(8,128)(2,1)S(1)}, u32[]{:S(2)}) copy-start(bf16[128,512]{1,0:T(8,128)(2,1)S(1)} %collective-permute-done.8.c3) | copy-start | bytes 393220
  43.7 17.0 %collective-permute-start.9 = (bf16[256,512]{1,0:T(8,128)(2,1)S(1)}, bf16[256,512]{1,0:T(8,128)(2,1)}, u32[]{:S(2)}, u32[]{:S(2)}) collective-permute-start(bf16[256,512]{1,0:T(8,128)(2,1)S(1)} %bitcast.37), channel_id=1, source_target_pairs={{0,1},{1,0},{2,3},{3,2},{4,5},{5,4},{6,7},{7,6},{8,9},{9,8},{10,11... | collective-permute-start | bytes 786440 | tf_op jit(solution)/shard_map/ppermute | solution.py:709
  44.7 16.3 %collective-permute-start.19 = (bf16[256,512]{1,0:T(8,128)(2,1)S(1)}, bf16[256,512]{1,0:T(8,128)(2,1)S(1)}, u32[]{:S(2)}, u32[]{:S(2)}) collective-permute-start(bf16[256,512]{1,0:T(8,128)(2,1)S(1)} %bitcast.33), channel_id=1, source_target_pairs={{0,2},{1,3},{2,0},{3,1},{4,6},{5,7},{6,4},{7,5},{8,10},{9,11},{10,... | collective-permute-start | bytes 786440 | tf_op jit(solution)/shard_map/ppermute | solution.py:709
  46.5 14.8 %collective-permute-start.22 = (bf16[1024,128]{1,0:T(8,128)(2,1)}, bf16[1024,128]{1,0:T(8,128)(2,1)S(1)}, u32[]{:S(2)}, u32[]{:S(2)}) collective-permute-start(bf16[1024,128]{1,0:T(8,128)(2,1)} %get-tuple-element.58), channel_id=1, source_target_pairs={{0,2},{1,3},{2,0},{3,1},{4,6},{5,7},{6,4},{7,5},{8,10},{9,11},{10,... | collective-permute-start | bytes 786440 | tf_op jit(solution)/shard_map/ppermute | solution.py:709
  46.8 14.7 %collective-permute-start.11 = (bf16[256,512]{1,0:T(8,128)(2,1)}, bf16[256,512]{1,0:T(8,128)(2,1)}, u32[]{:S(2)}, u32[]{:S(2)}) collective-permute-start(bf16[256,512]{1,0:T(8,128)(2,1)} %copy-done.13), channel_id=1, source_target_pairs={{0,1},{1,0},{2,3},{3,2},{4,5},{5,4},{6,7},{7,6},{8,9},{9,8},{10,11... | collective-permute-start | bytes 786440 | tf_op jit(solution)/shard_map/ppermute | solution.py:709
  60.4 17.4 %collective-permute-start.18 = (bf16[256,512]{1,0:T(8,128)(2,1)S(1)}, bf16[256,512]{1,0:T(8,128)(2,1)S(1)}, u32[]{:S(2)}, u32[]{:S(2)}) collective-permute-start(bf16[256,512]{1,0:T(8,128)(2,1)S(1)} %bitcast.34), channel_id=1, source_target_pairs={{0,1},{1,0},{2,3},{3,2},{4,5},{5,4},{6,7},{7,6},{8,9},{9,8},{10,11... | collective-permute-start | bytes 786440 | tf_op jit(solution)/shard_map/ppermute | solution.py:709
  60.7 17.0 %collective-permute-start.21 = (bf16[1024,128]{1,0:T(8,128)(2,1)}, bf16[1024,128]{1,0:T(8,128)(2,1)S(1)}, u32[]{:S(2)}, u32[]{:S(2)}) collective-permute-start(bf16[1024,128]{1,0:T(8,128)(2,1)} %get-tuple-element.58), channel_id=1, source_target_pairs={{0,1},{1,0},{2,3},{3,2},{4,5},{5,4},{6,7},{7,6},{8,9},{9,8},{10,11... | collective-permute-start | bytes 786440 | tf_op jit(solution)/shard_map/ppermute | solution.py:709
  61.0 9.5 %copy-start.11 = (bf16[256,512]{1,0:T(8,128)(2,1)}, bf16[256,512]{1,0:T(8,128)(2,1)S(1)}, u32[]{:S(2)}) copy-start(bf16[256,512]{1,0:T(8,128)(2,1)S(1)} %collective-permute-done.19.w2) | copy-start | bytes 786436
  61.0 15.3 %collective-permute-start.14 = (bf16[128,512]{1,0:T(8,128)(2,1)S(1)}, bf16[128,512]{1,0:T(8,128)(2,1)S(1)}, u32[]{:S(2)}, u32[]{:S(2)}) collective-permute-start(bf16[128,512]{1,0:T(8,128)(2,1)S(1)} %collective-permute-done.13.b2), channel_id=1, source_target_pairs={{0,1},{1,0},{2,3},{3,2},{4,5},{5,4},{6,7},{7,6},{8,9},{9,8},{10,11... | collective-permute-start | bytes 393224 | tf_op jit(solution)/shard_map/ppermute | solution.py:709
  61.3 9.2 %copy-start.12 = (bf16[1024,128]{1,0:T(8,128)(2,1)}, bf16[1024,128]{1,0:T(8,128)(2,1)S(1)}, u32[]{:S(2)}) copy-start(bf16[1024,128]{1,0:T(8,128)(2,1)S(1)} %collective-permute-done.22.t2) | copy-start | bytes 786436
  61.3 16.4 %collective-permute-start.20 = (bf16[256,512]{1,0:T(8,128)(2,1)S(1)}, bf16[256,512]{1,0:T(8,128)(2,1)S(1)}, u32[]{:S(2)}, u32[]{:S(2)}) collective-permute-start(bf16[256,512]{1,0:T(8,128)(2,1)S(1)} %collective-permute-done.19.w2), channel_id=1, source_target_pairs={{0,1},{1,0},{2,3},{3,2},{4,5},{5,4},{6,7},{7,6},{8,9},{9,8},{10,11... | collective-permute-start | bytes 786440 | tf_op jit(solution)/shard_map/ppermute | solution.py:709
  61.5 16.2 %collective-permute-start.23 = (bf16[1024,128]{1,0:T(8,128)(2,1)S(1)}, bf16[1024,128]{1,0:T(8,128)(2,1)S(1)}, u32[]{:S(2)}, u32[]{:S(2)}) collective-permute-start(bf16[1024,128]{1,0:T(8,128)(2,1)S(1)} %collective-permute-done.22.t2), channel_id=1, source_target_pairs={{0,1},{1,0},{2,3},{3,2},{4,5},{5,4},{6,7},{7,6},{8,9},{9,8},{10,11... | collective-permute-start | bytes 786440 | tf_op jit(solution)/shard_map/ppermute | solution.py:709
  61.8 14.5 %copy-start.21 = (bf16[128,512]{1,0:T(8,128)(2,1)S(1)}, bf16[128,512]{1,0:T(8,128)(2,1)}, u32[]{:S(2)}) copy-start(bf16[128,512]{1,0:T(8,128)(2,1)} %copy-done.20) | copy-start | bytes 393220
  71.9 11.7 %all-to-all-start.1 = ((f32[8,8,512]{2,1,0:T(8,128)}), f32[8,8,512]{2,1,0:T(8,128)S(1)}, u32[]{:S(2)}, u32[]{:S(2)}) async-start(f32[8,8,512]{2,1,0:T(8,128)} %broadcast_in_dim.11), calls=%async_computation.1 | async-start | bytes 262144 | tf_op jit(solution)/shard_map/all_to_all | solution.py:719
  76.3 7.3 %copy-start.24 = (bf16[128,512]{1,0:T(8,128)(2,1)}, bf16[128,512]{1,0:T(8,128)(2,1)S(1)}, u32[]{:S(2)}) copy-start(bf16[128,512]{1,0:T(8,128)(2,1)S(1)} %collective-permute-done.14.b3) | copy-start | bytes 393220
  76.3 1.4 collective-permute-start.17
  77.7 5.9 %copy-start.27 = (bf16[128,512]{1,0:T(8,128)(2,1)}, bf16[128,512]{1,0:T(8,128)(2,1)S(1)}, u32[]{:S(2)}) copy-start(bf16[128,512]{1,0:T(8,128)(2,1)S(1)} %collective-permute-done.17.c3) | copy-start | bytes 393220
  77.7 5.9 %copy-start.14 = (bf16[256,512]{1,0:T(8,128)(2,1)}, bf16[256,512]{1,0:T(8,128)(2,1)S(1)}, u32[]{:S(2)}) copy-start(bf16[256,512]{1,0:T(8,128)(2,1)S(1)} %collective-permute-done.18.w1) | copy-start | bytes 786436
  77.7 5.9 %copy-start.15 = (bf16[1024,128]{1,0:T(8,128)(2,1)}, bf16[1024,128]{1,0:T(8,128)(2,1)S(1)}, u32[]{:S(2)}) copy-start(bf16[1024,128]{1,0:T(8,128)(2,1)S(1)} %collective-permute-done.21.t1) | copy-start | bytes 786436
  77.8 5.9 %copy-start.16 = (bf16[256,512]{1,0:T(8,128)(2,1)}, bf16[256,512]{1,0:T(8,128)(2,1)S(1)}, u32[]{:S(2)}) copy-start(bf16[256,512]{1,0:T(8,128)(2,1)S(1)} %collective-permute-done.20.w3) | copy-start | bytes 786436
  77.8 5.9 %copy-start.17 = (bf16[1024,128]{1,0:T(8,128)(2,1)}, bf16[1024,128]{1,0:T(8,128)(2,1)S(1)}, u32[]{:S(2)}) copy-start(bf16[1024,128]{1,0:T(8,128)(2,1)S(1)} %collective-permute-done.23.t3) | copy-start | bytes 786436
  (6 other events, 8.7 us)

commit v2 on v1

--- a/solution.py
+++ b/solution.py
@@ -40,6 +40,10 @@
         return body(rows_at(index, size), index, carry)
 
     return lax.fori_loop(0, total // size, step, init, unroll=unroll)
+
+
+def own_quarter():
+    return (lax.axis_index("state") // (lax.axis_size("state") // 4)).astype(jnp.int32)
 
 
 def keep_rows(first_step, rows, steps, length):
@@ -155,12 +159,56 @@
         out_ref[:, block * 128 : (block + 1) * 128] = held_ref[block * 128 : (block + 1) * 128, :].T
 
 
-def enter_kernel(meta_ref, x_ref, params_ref, out_ref, sums_ref, held_ref):
-    length = meta_ref[0]
+def spread_rows(sums_ref, spread_ref):
+    for group in range(spread_ref.shape[0]):
+        spread_ref[group, :, :] = sums_ref[0:8, :]
+
+
+def total_rows(sums_ref):
+    value = sums_ref[0, :, :]
+    for other in range(1, sums_ref.shape[0]):
+        value += sums_ref[other, :, :]
+    return value
+
+
+def enter_kernel(
+    length_ref, x_ref, gain_ref, shift_ref, skip_ref, bias_ref, nu_ref, theta_ref, gamma_ref, b_ref, c_ref, w_ref,
+    out_ref, spread_ref, b0_ref, cw0_ref, later_ref,
+    held_ref, sums_ref, stage_b, stage_c, stage_w, arrived, copied,
+):
+    length = length_ref[0]
     total = x_ref.shape[1]
     steps = total // CHUNKS
-    out_ref[total:, :] = params_ref[...]
+    own_states = nu_ref.shape[1]
+    half, full = b_ref.shape[1], w_ref.shape[1]
+    stages = ((b_ref, stage_b), (c_ref, stage_c), (w_ref, stage_w))
+    arrivals = [pltpu.make_async_copy(*move, arrived.at[place]) for place, move in enumerate(stages)]
+    for copy in arrivals:
+        copy.start()
+    moves = (
+        (stage_b.at[0], b0_ref),
+        (stage_c.at[0], cw0_ref.at[0:half]),
+        (stage_w.at[0], cw0_ref.at[half:]),
+        (stage_b.at[1], later_ref.at[0:half]),
+        (stage_c.at[1], later_ref.at[half : 2 * half]),
+        (stage_w.at[1], later_ref.at[2 * half :]),
+    )
+    copies = [pltpu.make_async_copy(*move, copied.at[place]) for place, move in enumerate(moves)]
+    out_ref[total:, :] = jnp.zeros((PARAM_ROWS, x_ref.shape[0]), F32)
+    for layer in range(LAYERS):
+        first = total + 5 * layer
+        out_ref[first + GAIN : first + GAIN + 1, :] = gain_ref[layer : layer + 1, :]
+        out_ref[first + SHIFT : first + SHIFT + 1, :] = shift_ref[layer : layer + 1, :]
+        out_ref[first + SKIP : first + SKIP + 1, :] = skip_ref[layer : layer + 1, :]
+        out_ref[first + BIAS_LINEAR : first + BIAS_GATE + 1, :] = bias_ref[layer, :, :]
+        first = total + 10 + 3 * layer
+        for row, source in enumerate((nu_ref, theta_ref, gamma_ref)):
+            out_ref[first + row : first + row + 1, :own_states] = source[layer : layer + 1, :]
     sums_ref[...] = jnp.zeros_like(sums_ref)
+    for copy in arrivals:
+        copy.wait()
+    for copy in copies:
+        copy.start()
 
     def emit(rows, index, value):
         out_ref[rows, :] = value
@@ -173,7 +221,10 @@
     square = jnp.sum(sums_ref[16:32, :], axis=0, keepdims=True)
     sums_ref[0:1, :] = plain
     sums_ref[1:2, :] = square
-    sums_ref[2:3, :] = jnp.full((1, 128), length, jnp.int32).astype(F32)
+    sums_ref[2:3, :] = jnp.full((1, x_ref.shape[0]), length, jnp.int32).astype(F32)
+    spread_rows(sums_ref, spread_ref)
+    for copy in copies:
+        copy.wait()
 
 
 def cotangent_kernel(x_ref, out_ref, low_ref, held_ref):
@@ -248,29 +299,35 @@
     for_rows(total, part, body, 0)
 
 
-def start_kernel(
-    meta_ref, x0, x1, x2, x3, sums_ref, b0, b1, b2, b3, c0, c1, c2, c3,
-    normed_ref, drive_own_ref, low_ref, slope_ref, active_ref, b_ref, c_ref, feature_ref, state_ref, norm_ref,
-    drive_ref, held_ref, stats_ref, part,
+def drive_kernel(
+    length_ref, x0, x1, x2, x3, sums_ref, b0, b1, b2, b3,
+    normed_ref, drive_own_ref, low_ref, b_ref, feature_ref, state_ref, norm_ref,
+    drive_ref, stats_ref, part,
 ):
-    length, quarter = meta_ref[0], meta_ref[1]
+    length, quarter = length_ref[0], own_quarter()
     parts = (x0, x1, x2, x3)
     total = normed_ref.shape[0]
     steps = total // CHUNKS
     width = x0.shape[1]
     assemble_states((b0, b1, b2, b3), b_ref)
-    assemble_output((c0, c1, c2, c3), c_ref)
     lane = lax.broadcasted_iota(jnp.int32, (8, width), 1)
     for place, value in enumerate(parts):
         feature_ref[:, lanes_at(quarter ^ place, width)] = value[total:, :]
     for pair in range(2):
         early, late = parts[2 * pair][total + 8 :, :], parts[2 * pair + 1][total + 8 :, :]
-        state_ref[:, pair * 128 : (pair + 1) * 128] = jnp.where(lane < 64, early, pltpu.roll(late, 64, 1))
-    groups = sums_ref.shape[0] // 8
+        logs = jnp.where(lane < 64, early, pltpu.roll(late, 64, 1))
+        lanes = slice(pair * width, (pair + 1) * width)
+        for layer in range(LAYERS):
+            first = 2 + 3 * layer
+            modulus = jnp.exp(-jnp.exp(logs[first : first + 1, :]))
+            angle = jnp.exp(logs[first + 1 : first + 2, :])
+            state_ref[first : first + 1, lanes] = modulus * jnp.cos(angle)
+            state_ref[first + 1 : first + 2, lanes] = modulus * jnp.sin(angle)
+            state_ref[first + 2 : first + 3, lanes] = jnp.exp(logs[first + 2 : first + 3, :])
     for place in range(4):
-        value = sums_ref[place * 8 : place * 8 + 8, :]
-        for other in range(1, groups // 4):
-            value += sums_ref[(other * 4 + place) * 8 : (other * 4 + place) * 8 + 8, :]
+        value = sums_ref[place, :, :]
+        for other in range(1, sums_ref.shape[0] // 4):
+            value += sums_ref[other * 4 + place, :, :]
         stats_ref[:, place * width : (place + 1) * width] = value
     centre, inv_dev = norm_rows(stats_ref[0:2, :], stats_ref[2:3, :])
     norm_ref[...] = jnp.zeros_like(norm_ref)
@@ -300,20 +357,24 @@
         return held
 
     sweep(drive_ref, state[2:3, :], state[3:4, :], steps, False, emit, 0)
-    pre_phase(low_ref, c_ref, normed_ref, feature_ref[SKIP : SKIP + 1, :], active_ref, slope_ref, held_ref, part)
 
 
 def glu_kernel(
-    meta_ref, x0, x1, x2, x3, active_ref, w0, w1, w2, w3, feature_ref,
-    stream_ref, linear_ref, gate_ref, w_ref, sums_ref,
-    held_ref, part,
+    length_ref, x0, x1, x2, x3, normed_ref, low_ref, cw0, cw1, cw2, cw3, feature_ref,
+    stream_ref, linear_ref, gate_ref, slope_ref, active_ref, c_ref, w_ref, spread_ref,
+    held_ref, sums_ref, part,
 ):
-    length, quarter = meta_ref[0], meta_ref[1]
+    length, quarter = length_ref[0], own_quarter()
     parts = (x0, x1, x2, x3)
     total, full = active_ref.shape
     steps = total // CHUNKS
     width = x0.shape[1]
-    assemble_glu((w0, w1, w2, w3), w_ref, quarter)
+    weights = (cw0, cw1, cw2, cw3)
+    assemble_output([part_ref.at[0:width] for part_ref in weights], c_ref)
+    assemble_glu([part_ref.at[width : 3 * width] for part_ref in weights], w_ref, quarter)
+    pre_phase(
+        low_ref, c_ref, normed_ref, feature_ref[SKIP : SKIP + 1, :], active_ref, slope_ref, held_ref.at[:, :full], part
+    )
     sums_ref[...] = jnp.zeros_like(sums_ref)
 
     def body(rows, index, carry):
@@ -346,24 +407,12 @@
     square = jnp.sum(sums_ref[16:32, :], axis=0, keepdims=True)
     sums_ref[0:1, :] = plain
     sums_ref[1:2, :] = square
-
-
-def total_rows(sums_ref, count):
-    groups = sums_ref.shape[0] // 8
-    value = sums_ref[0:8, :]
-    for other in range(1, groups):
-        value += sums_ref[other * 8 : other * 8 + 8, :]
-    return value
-
-
-def adjoint_phase(
-    grad_gated_ref, w_ref, slope_ref, normed_ref, c_ref, low_ref, drive_own_ref, state, first_row, quarter, length,
-    pre_grad_ref, held_ref, grad_state_ref, grad_driven_ref, small_ref, sum_ref, reverse, part,
-):
+    spread_rows(sums_ref, spread_ref)
+
+
+def pre_grad_phase(grad_gated_ref, w_ref, slope_ref, normed_ref, quarter, pre_grad_ref, held_ref, small_ref, sum_ref, part):
     total, full = normed_ref.shape
-    steps = total // CHUNKS
     width = 128
-    states = state.shape[1]
     own = lanes_at(quarter, width)
     sum_ref[...] = jnp.zeros_like(sum_ref)
 
@@ -378,6 +427,21 @@
             return carry
 
         for_rows(part, 16, inner, 0, unroll=2)
+        return carry
+
+    for_rows(total, part, body, 0)
+    small_ref[3:4, 0:128] = jnp.sum(sum_ref[...], axis=0, keepdims=True)
+
+
+def adjoint_phase(
+    pre_grad_ref, c_ref, low_ref, drive_own_ref, state, first_row, length,
+    grad_state_ref, grad_driven_ref, small_ref, reverse, part,
+):
+    total = pre_grad_ref.shape[0]
+    steps = total // CHUNKS
+    states = state.shape[1]
+
+    def body(rows, index, carry):
         grad_state_ref[rows, :] = dot(pre_grad_ref[rows, :], c_ref[...], NT)
         return carry
 
@@ -408,11 +472,17 @@
     small_ref[0:1, 0:128] = jnp.sum(one, axis=0, keepdims=True)
     small_ref[1:2, 0:128] = jnp.sum(two, axis=0, keepdims=True)
     small_ref[2:3, 0:128] = jnp.sum(three, axis=0, keepdims=True)
-    small_ref[3:4, 0:128] = jnp.sum(sum_ref[...], axis=0, keepdims=True)
-
-
-def weight_grads(grads_ref, grad_driven_ref, normed_ref, low_ref, pre_grad_ref, grad_gated_ref, active_ref, quarter, states):
-    full = normed_ref.shape[1]
+
+
+def glu_grads(grads_ref, first, grad_gated_ref, active_ref, quarter):
+    full = active_ref.shape[1]
+    for place in range(2):
+        lanes = pl.ds(pl.multiple_of(place * full + quarter * 128, 128), 128)
+        got = dot(grad_gated_ref[:, lanes], active_ref[...], TN)
+        grads_ref[first + place * 128 : first + (place + 1) * 128, :] = got.astype(LOW)
+
+
+def state_grads(grads_ref, grad_driven_ref, normed_ref, low_ref, pre_grad_ref, states):
     half = states // 4
     for place in range(2):
         lanes = slice(place * states, place * states + 128)
@@ -420,29 +490,26 @@
         grads_ref[place * half : (place + 1) * half, :] = got.astype(LOW)
         got = dot(low_ref[:, lanes], pre_grad_ref[...], TN)[:half, :]
         got = got if place == 0 else -got
-        grads_ref[128 + place * half : 128 + (place + 1) * half, :] = got.astype(LOW)
-        lanes = pl.ds(pl.multiple_of(place * full + quarter * 128, 128), 128)
-        got = dot(grad_gated_ref[:, lanes], active_ref[...], TN)
-        grads_ref[256 + place * 128 : 256 + (place + 1) * 128, :] = got.astype(LOW)
+        grads_ref[2 * half + place * half : 2 * half + (place + 1) * half, :] = got.astype(LOW)
 
 
 def middle_kernel(
-    meta_ref, stream_ref, sums_ref, b0, b1, b2, b3, c0, c1, c2, c3, w0, w1, w2, w3, feature_ref, state_ref, norm0_ref,
-    t0, t1, t2, t3,
-    result_ref, base_ref, bn_ref, grads_ref, small_ref, norm_ref,
+    length_ref, stream_ref, sums_ref, parts, ups, feature_ref, state_ref, norm0_ref,
+    result_ref, base_ref, spread_ref, norm_ref, grads_ref,
+    bn_ref, small_ref,
     b_ref, c_ref, w_ref, normed_ref, drive_ref, drive_own_ref, low_ref, slope_ref, active_ref, held_ref, own_ref,
     order_ref, grad_gated_ref, pre_grad_ref, grad_driven_ref, sum_ref, bias_ref, part,
 ):
-    length, quarter = meta_ref[0], meta_ref[1]
+    length, quarter = length_ref[0], own_quarter()
     total, full = stream_ref.shape
     steps = total // CHUNKS
     width = 128
     own = lanes_at(quarter, width)
-    assemble_states((b0, b1, b2, b3), b_ref)
-    assemble_output((c0, c1, c2, c3), c_ref)
-    assemble_glu((w0, w1, w2, w3), w_ref, quarter)
+    assemble_states([part_ref.at[0:128] for part_ref in parts], b_ref)
+    assemble_output([part_ref.at[128:256] for part_ref in parts], c_ref)
+    assemble_glu([part_ref.at[256:512] for part_ref in parts], w_ref, quarter)
     counted = norm0_ref[2:3, :]
-    centre, inv_dev = norm_rows(total_rows(sums_ref, 2), counted)
+    centre, inv_dev = norm_rows(total_rows(sums_ref), counted)
     norm_ref[...] = jnp.zeros_like(norm_ref)
     norm_ref[0:1, :] = centre
     norm_ref[1:2, :] = inv_dev
@@ -480,7 +547,7 @@
         def inner(local, place_index, carry):
             here = pl.ds(pl.multiple_of(base + place_index * 16, 16), 16)
             keep = keep_rows(index * (part // CHUNKS) + place_index, 16, steps, length)
-            for place, value in enumerate((t0, t1, t2, t3)):
+            for place, value in enumerate(ups):
                 lanes = lanes_at(quarter ^ place, width)
                 far = pl.ds(pl.multiple_of(full + (quarter ^ place) * width, width), width)
                 linear = held_ref[local, lanes] + feature_ref[5 + BIAS_LINEAR : 6 + BIAS_LINEAR, lanes]
@@ -503,15 +570,17 @@
     for_rows(total, part, body, 0)
     to_feature_rows(lambda rows, index: own_ref[rows, :], order_ref, result_ref, steps)
     small_ref[...] = jnp.zeros_like(small_ref)
+    pre_grad_phase(
+        grad_gated_ref, w_ref, slope_ref, normed_ref, quarter, pre_grad_ref, held_ref, small_ref, sum_ref, part
+    )
     adjoint_phase(
-        grad_gated_ref, w_ref, slope_ref, normed_ref, c_ref, low_ref, drive_own_ref, state, 5, quarter, length,
-        pre_grad_ref, held_ref, drive_ref, grad_driven_ref, small_ref, sum_ref, False, part,
+        pre_grad_ref, c_ref, low_ref, drive_own_ref, state, 5, length,
+        drive_ref, grad_driven_ref, small_ref, False, part,
     )
     small_ref[4:5, 0:128] = jnp.sum(bias_ref[0:16, :], axis=0, keepdims=True)
     small_ref[5:6, 0:128] = jnp.sum(bias_ref[16:32, :], axis=0, keepdims=True)
-    weight_grads(
-        grads_ref, grad_driven_ref, normed_ref, low_ref, pre_grad_ref, grad_gated_ref, active_ref, quarter, states
-    )
+    glu_grads(grads_ref, 2 * width, grad_gated_ref, active_ref, quarter)
+    state_grads(grads_ref, grad_driven_ref, normed_ref, low_ref, pre_grad_ref, states)
     bn_ref[...] = jnp.zeros_like(bn_ref)
     scale = inv_dev * gain
 
@@ -534,7 +603,7 @@
     for_rows(total, part, back, 0)
 
     def add(rows, index, carry):
-        for place, value in enumerate((t0, t1, t2, t3)):
+        for place, value in enumerate(ups):
             lanes = lanes_at(quarter ^ place, width)
             base_ref[rows, lanes] += value[rows, :].astype(F32)
         return carry
@@ -544,23 +613,24 @@
     scaled = jnp.sum(bn_ref[16:32, :], axis=0, keepdims=True)
     bn_ref[0:1, :] = plain
     bn_ref[1:2, :] = scaled
-
-
-def last_kernel(
-    meta_ref, stream_ref, base_ref, sums_ref, norm1_ref, gate_ref, linear_ref, slope_ref, active_ref, normed_ref, low_ref,
-    drive_own_ref, b_ref, c_ref, w_ref, feature_ref, state_ref, x_ref, norm0_ref, grads1_ref, small1_ref,
-    send_ref, up_ref, grad_ref,
-    held_ref, grad_state_ref, grad_gated_ref, pre_grad_ref, grad_driven_ref, sum_ref, bias_ref, small_ref, bn_ref,
-    grads_ref, row_ref, part,
+    bn_ref[2:8, :] = small_ref[0:6, :]
+    spread_rows(bn_ref, spread_ref)
+
+
+def last_glu_kernel(
+    length_ref, stream_ref, base_ref, sums_ref, norm_ref, gate_ref, linear_ref, slope_ref, active_ref, normed_ref, w_ref,
+    feature_ref,
+    up_ref, pre_grad_ref, grads_ref, small_ref,
+    held_ref, grad_gated_ref, sum_ref, bias_ref, row_ref, part,
 ):
-    length, quarter = meta_ref[0], meta_ref[1]
+    length, quarter = length_ref[0], own_quarter()
     total, full = stream_ref.shape
     steps = total // CHUNKS
     width = 128
     own = lanes_at(quarter, width)
-    counted = norm0_ref[2:3, :]
-    whole = total_rows(sums_ref, 2)
-    centre, inv_dev = norm1_ref[0:1, :], norm1_ref[1:2, :]
+    counted = norm_ref[2:3, :]
+    whole = total_rows(sums_ref)
+    centre, inv_dev = norm_ref[0:1, :], norm_ref[1:2, :]
     gain = feature_ref[5 + GAIN : 6 + GAIN, :]
     scale = inv_dev * gain
     level = scale * whole[0:1, :] / counted
@@ -581,17 +651,32 @@
 
     for_rows(total, 16, top, 0, unroll=2)
     small_ref[...] = jnp.zeros_like(small_ref)
-    state = state_ref[...]
-    states = state.shape[1]
-    adjoint_phase(
-        grad_gated_ref, w_ref, slope_ref, normed_ref, c_ref, low_ref, drive_own_ref, state, 2, quarter, length,
-        pre_grad_ref, held_ref, grad_state_ref, grad_driven_ref, small_ref, sum_ref, True, part,
+    pre_grad_phase(
+        grad_gated_ref, w_ref, slope_ref, normed_ref, quarter, pre_grad_ref, held_ref, small_ref, sum_ref, part
     )
     small_ref[4:5, 0:128] = jnp.sum(bias_ref[0:16, :], axis=0, keepdims=True)
     small_ref[5:6, 0:128] = jnp.sum(bias_ref[16:32, :], axis=0, keepdims=True)
-    weight_grads(
-        grads_ref, grad_driven_ref, normed_ref, low_ref, pre_grad_ref, grad_gated_ref, active_ref, quarter, states
-    )
+    glu_grads(grads_ref, 0, grad_gated_ref, active_ref, quarter)
+
+
+def last_state_kernel(
+    length_ref, pre_grad_ref, normed_ref, low_ref, drive_own_ref, b_ref, c_ref, glu_grads_ref, small_in_ref, feature_ref,
+    state_ref, x_ref, norm0_ref,
+    send_ref, grad_ref,
+    held_ref, grad_state_ref, grad_driven_ref, small_ref, bn_ref, grads_ref, row_ref, part,
+):
+    length, quarter = length_ref[0], own_quarter()
+    total, full = normed_ref.shape
+    width = 128
+    own = lanes_at(quarter, width)
+    small_ref[...] = small_in_ref[...]
+    state = state_ref[...]
+    adjoint_phase(
+        pre_grad_ref, c_ref, low_ref, drive_own_ref, state, 2, length,
+        grad_state_ref, grad_driven_ref, small_ref, True, part,
+    )
+    state_grads(grads_ref, grad_driven_ref, normed_ref, low_ref, pre_grad_ref, state.shape[1])
+    grads_ref[2 * width :, :] = glu_grads_ref[...]
     bn_ref[...] = jnp.zeros_like(bn_ref)
     centre0, inv_dev0 = norm0_ref[0:1, own], norm0_ref[1:2, own]
     skip = feature_ref[SKIP : SKIP + 1, own]
@@ -613,41 +698,22 @@
         return carry
 
     for_rows(total, part, back, 0)
+    small_ref[6:7, 0:width] = jnp.sum(bn_ref[0:16, :], axis=0, keepdims=True)
+    small_ref[7:8, 0:width] = jnp.sum(bn_ref[16:32, :], axis=0, keepdims=True)
+    row_ref[...] = jnp.zeros_like(row_ref)
+    for place in range(8):
+        row_ref[place // 4 : place // 4 + 1, place % 4 * width : (place % 4 + 1) * width] = small_ref[place : place + 1, 0:width]
+    exact = row_ref[0:8, :]
+    row_ref[8:16, :] = exact - exact.astype(LOW).astype(F32)
     groups = send_ref.shape[0]
-    share = send_ref.shape[1] - 32
-    row_ref[0:8, :] = small_ref[...]
-    row_ref[8:16, :] = small1_ref[...]
-    row_ref[6:7, 0:width] = jnp.sum(bn_ref[0:16, :], axis=0, keepdims=True)
-    row_ref[7:8, 0:width] = jnp.sum(bn_ref[16:32, :], axis=0, keepdims=True)
-    exact = row_ref[...]
-    high = exact.astype(LOW)
-    rest = (exact - high.astype(F32)).astype(LOW)
-    sections = ((grads_ref, 0), (grads1_ref, 0), (grads_ref, 128), (grads1_ref, 128),
-                (grads_ref, 256), (grads_ref, 384), (grads1_ref, 256), (grads1_ref, 384))
+    share = send_ref.shape[1] - 16
     for group in range(groups):
-        source, start = sections[group * share // 128]
-        start += group * share % 128
-        send_ref[group, :share, :] = source[start : start + share, :]
-    for group in range(groups):
-        send_ref[group, share : share + 16, :] = high
-        send_ref[group, share + 16 :, :] = rest
-
-
-def finish_kernel(
-    meta_ref, got_ref, up_ref, grad_ref, x_ref, norm0_ref, feature_ref, nu_ref, theta_ref, bn1_ref,
-    send_ref, nu_out, theta_out, gamma_out, skip_out, bias_out, gain_out, shift_out, out_ref,
-    held_ref, row_ref, order_ref,
-):
-    length, quarter = meta_ref[0], meta_ref[1]
-    groups = got_ref.shape[0]
-    share = got_ref.shape[1] - 32
-    total, width = x_ref.shape[0] - PARAM_ROWS, x_ref.shape[1]
-    steps = total // CHUNKS
-    own = lanes_at(quarter, width)
-    small = jnp.zeros((16, got_ref.shape[2]), F32)
-    for group in range(groups):
-        small += got_ref[group, share : share + 16, :].astype(F32) + got_ref[group, share + 16 :, :].astype(F32)
-    row_ref[...] = small
+        send_ref[group, :share, :] = grads_ref[group * share : (group + 1) * share, :]
+        send_ref[group, share:, :] = row_ref[...].astype(LOW)
+
+
+def add_kernel(got_ref, send_ref):
+    groups, share = got_ref.shape[:2]
     for piece in range(0, share, 16):
         value = got_ref[0, piece : piece + 16, :].astype(F32)
         for group in range(1, groups):
@@ -655,24 +721,52 @@
         value = value.astype(LOW)
         for group in range(groups):
             send_ref[group, piece : piece + 16, :] = value
+
+
+def share_kernel(got_ref, send_ref, small_ref):
+    groups = got_ref.shape[0]
+    share = got_ref.shape[1] - 16
+    for piece in range(0, share, 16):
+        value = got_ref[0, piece : piece + 16, :].astype(F32)
+        for group in range(1, groups):
+            value += got_ref[group, piece : piece + 16, :].astype(F32)
+        value = value.astype(LOW)
+        for group in range(groups):
+            send_ref[group, piece : piece + 16, :] = value
+    small = got_ref[0, share:, :].astype(F32)
+    for group in range(1, groups):
+        small += got_ref[group, share:, :].astype(F32)
+    small_ref[...] = small[0:8, :] + small[8:16, :]
+
+
+def finish_kernel(
+    length_ref, up_ref, grad_ref, x_ref, norm0_ref, feature_ref, nu_ref, theta_ref, bn1_ref, small0_ref,
+    nu_out, theta_out, gamma_out, skip_out, bias_out, gain_out, shift_out, out_ref,
+    held_ref, order_ref,
+):
+    length, quarter = length_ref[0], own_quarter()
+    total, width = up_ref.shape
+    steps = total // CHUNKS
+    own = lanes_at(quarter, width)
     states = nu_out.shape[1]
-    bn1 = total_rows(bn1_ref, 2)
-    held_ref[0:8, :] = bn1
-    for layer, first in ((0, 0), (1, 8)):
-        nu_out[layer : layer + 1, :] = -jnp.exp(nu_ref[layer : layer + 1, :]) * row_ref[first : first + 1, :states]
-        theta_out[layer : layer + 1, :] = jnp.exp(theta_ref[layer : layer + 1, :]) * row_ref[first + 1 : first + 2, :states]
-        gamma_out[layer : layer + 1, :] = row_ref[first + 2 : first + 3, :states]
-        skip_out[layer : layer + 1, :] = row_ref[first + 3 : first + 4, :width]
-        bias_out[layer, 0:1, :] = row_ref[first + 4 : first + 5, :width]
-        bias_out[layer, 1:2, :] = row_ref[first + 5 : first + 6, :width]
-    shift_out[0:1, :] = row_ref[6:7, :width]
-    gain_out[0:1, :] = row_ref[7:8, :width]
+    held_ref[0:8, :] = total_rows(bn1_ref)
+    for place in range(8):
+        held_ref[8 + place : 9 + place, :width] = small0_ref[place // 4 : place // 4 + 1, place % 4 * width : (place % 4 + 1) * width]
+    for layer, first in ((0, 8), (1, 2)):
+        nu_out[layer : layer + 1, :] = -jnp.exp(nu_ref[layer : layer + 1, :]) * held_ref[first : first + 1, :states]
+        theta_out[layer : layer + 1, :] = jnp.exp(theta_ref[layer : layer + 1, :]) * held_ref[first + 1 : first + 2, :states]
+        gamma_out[layer : layer + 1, :] = held_ref[first + 2 : first + 3, :states]
+        skip_out[layer : layer + 1, :] = held_ref[first + 3 : first + 4, :width]
+        bias_out[layer, 0:1, :] = held_ref[first + 4 : first + 5, :width]
+        bias_out[layer, 1:2, :] = held_ref[first + 5 : first + 6, :width]
+    shift_out[0:1, :] = held_ref[14:15, :width]
+    gain_out[0:1, :] = held_ref[15:16, :width]
     shift_out[1:2, :] = held_ref[0:1, own]
     gain_out[1:2, :] = held_ref[1:2, own]
     counted = norm0_ref[2:3, own]
     centre, inv_dev = norm0_ref[0:1, own], norm0_ref[1:2, own]
-    level = row_ref[6:7, :width] / counted
-    tilt = row_ref[7:8, :width] * inv_dev / counted
+    level = held_ref[14:15, :width] / counted
+    tilt = held_ref[15:16, :width] * inv_dev / counted
     scale = inv_dev * feature_ref[GAIN : GAIN + 1, own]
 
     def load(rows, index):
@@ -683,19 +777,28 @@
     to_feature_rows(load, order_ref, out_ref, steps)
 
 
-def call(kernel, outs, scratch, args, smem=1, flops=0, name=None):
-    specs = [
-        pl.BlockSpec(memory_space=pltpu.SMEM if place < smem else pltpu.VMEM) for place in range(len(args))
-    ]
-    moved = sum(a.size * a.dtype.itemsize for a in args) + sum(o.size * o.dtype.itemsize for o in outs)
+def widen_kernel(grads0_ref, grads1_ref, b_ref, c_ref, w_ref):
+    half = b_ref.shape[1]
+    for layer, source in enumerate((grads0_ref, grads1_ref)):
+        b_ref[layer, :, :] = source[0:half, :].astype(F32)
+        c_ref[layer, :, :] = source[half : 2 * half, :].astype(F32)
+        w_ref[layer, :, :] = source[2 * half :, :].astype(F32)
+
+
+def call(kernel, outs, scratch, args, smem=1, name=None, any_args=(), any_outs=()):
+    def space(place):
+        return pltpu.SMEM if place < smem else pl.ANY if place in any_args else pltpu.VMEM
+
     return pl.pallas_call(
         kernel,
         out_shape=tuple(outs),
-        in_specs=specs,
-        out_specs=tuple(pl.BlockSpec(memory_space=pltpu.VMEM) for _ in outs),
+        in_specs=[pl.BlockSpec(memory_space=space(place)) for place in range(len(args))],
+        out_specs=tuple(
+            pl.BlockSpec(memory_space=pl.ANY if place in any_outs else pltpu.VMEM) for place in range(len(outs))
+        ),
         scratch_shapes=scratch,
         compiler_params=pltpu.CompilerParams(vmem_limit_bytes=VMEM_BYTES),
-        cost_estimate=pl.CostEstimate(flops=int(flops), bytes_accessed=int(moved), transcendentals=0),
+        cost_estimate=pl.CostEstimate(flops=0, bytes_accessed=0, transcendentals=0),
         name=name,
     )(*args)
 
@@ -712,11 +815,6 @@
 def gather(value, sharers):
     across = swap(value, 2, sharers)
     return value, swap(value, 1, sharers), across, swap(across, 1, sharers)
-
-
-def spread(value, axes, count):
-    whole = jnp.broadcast_to(value[None], (count,) + value.shape)
-    return lax.all_to_all(whole, axes, 0, 0, tiled=True).reshape((-1,) + value.shape[1:])
 
 
 def local(
@@ -750,31 +848,42 @@
     own_states = b_weight.shape[2]
     part = 256
     meta = jnp.stack([lengths[0], quarter])
-    modulus = jnp.exp(-jnp.exp(nu_log))
-    angle = jnp.exp(theta_log)
-    rates = jnp.stack([modulus * jnp.cos(angle), modulus * jnp.sin(angle), jnp.exp(gamma_log)], 1)
-    rates = jnp.pad(rates.reshape(6, own_states), ((0, 0), (0, width - own_states)))
-    features = jnp.concatenate(
-        [jnp.stack([bn_gain, bn_bias, skip_weight], 1), glu_bias], 1
-    ).reshape(10, width)
-    params = jnp.concatenate([features, rates], 0)
-
-    b_parts = [gather(b_weight[layer].reshape(2 * own_states, full), sharers) for layer in range(LAYERS)]
-    c_parts = [gather(c_weight[layer].reshape(2 * own_states, full), sharers) for layer in range(LAYERS)]
-    w_parts = [gather(glu_weight[layer].reshape(2 * width, full), sharers) for layer in range(LAYERS)]
-
-    packed, sums = call(
+
+    def across(value, axes):
+        return lax.all_to_all(value, axes, 0, 0, tiled=True)
+
+    packed, sums, b0, cw0, later = call(
         enter_kernel,
-        (shape(total + PARAM_ROWS, width), shape(32, width)),
-        [pltpu.VMEM((total, width), F32)],
-        (meta, inputs[0], params),
+        (
+            shape(total + PARAM_ROWS, width),
+            shape(dp_size * state_size, 8, width),
+            shape(width, full, dtype=LOW),
+            shape(3 * width, full, dtype=LOW),
+            shape(4 * width, full, dtype=LOW),
+        ),
+        [
+            pltpu.VMEM((total, width), F32),
+            pltpu.VMEM((32, width), F32),
+            pltpu.VMEM((LAYERS, width, full), LOW),
+            pltpu.VMEM((LAYERS, width, full), LOW),
+            pltpu.VMEM((LAYERS, 2 * width, full), LOW),
+            pltpu.SemaphoreType.DMA((3,)),
+            pltpu.SemaphoreType.DMA((6,)),
+        ],
+        (lengths, inputs[0], bn_gain, bn_bias, skip_weight, glu_bias, nu_log, theta_log, gamma_log,
+         b_weight.reshape(LAYERS, width, full), c_weight.reshape(LAYERS, width, full),
+         glu_weight.reshape(LAYERS, 2 * width, full)),
+        any_args=(9, 10, 11),
+        any_outs=(2, 3, 4),
         name="enter",
     )
-    x_parts = gather(packed, sharers)
-    sums = spread(sums[:8], ("dp", "state"), dp_size * state_size)
+    near = [swap(value, 1, sharers) for value in (packed, b0, cw0)]
+    far = [swap(value, 2, sharers) for value in (packed, b0, cw0)]
+    sums = across(sums, ("dp", "state"))
     if sharers > 1:
-        sums = sums.reshape(dp_size * 4, sharers, 8, width)[:, 0].reshape(-1, width)
-    cotangent_own, cotangent_low = call(
+        sums = sums.reshape(dp_size * 4, sharers, 8, width)[:, 0]
+    cotangent, packed = lax.optimization_barrier((cotangent, packed))
+    up_own, up_low = call(
         cotangent_kernel,
         (shape(total, width), shape(total, width, dtype=LOW)),
         [pltpu.VMEM((total, width), F32)],
@@ -782,52 +891,69 @@
         smem=0,
         name="cotangent",
     )
-    cotangent_parts = (cotangent_own,) + gather(cotangent_low, sharers)[1:]
-    (normed0, drive0, low0, slope0, active0, b_all, c_all, feature, state, norm0) = call(
-        functools.partial(start_kernel, part=part),
+    far[0], far[1], sums, up_low = lax.optimization_barrier((far[0], far[1], sums, up_low))
+    x_parts = (packed, near[0], far[0], swap(far[0], 1, sharers))
+    b_parts = (b0, near[1], far[1], swap(far[1], 1, sharers))
+    normed0, drive0, low0, b_all, feature, state, norm0 = call(
+        functools.partial(drive_kernel, part=part),
         (
             shape(total, full, dtype=LOW),
             shape(total, 256),
             shape(total, 2 * states, dtype=LOW),
-            shape(total, full, dtype=LOW),
-            shape(total, full, dtype=LOW),
-            shape(2 * states, full, dtype=LOW),
             shape(2 * states, full, dtype=LOW),
             shape(PARAM_ROWS, full),
             shape(8, states),
             shape(8, full),
         ),
-        [pltpu.VMEM((total, 2 * states), F32), pltpu.VMEM((part, full), F32), pltpu.VMEM((8, full), F32)],
-        (meta, *x_parts, sums, *b_parts[0], *c_parts[0]),
-        flops=4e9,
-        name="start",
-    )
-    stream1, linear0, gate0, w_all, sums1 = call(
+        [pltpu.VMEM((total, 2 * states), F32), pltpu.VMEM((8, full), F32)],
+        (lengths, *x_parts, sums, *b_parts),
+        name="drive",
+    )
+    far[2], norm0 = lax.optimization_barrier((far[2], norm0))
+    cw_parts = (cw0, near[2], far[2], swap(far[2], 1, sharers))
+    later, up_low, *_ = lax.optimization_barrier((later, up_low, far[2]))
+    far += [swap(value, 2, sharers) for value in (later, up_low)]
+    stream1, linear0, gate0, slope0, active0, c_all, w_all, sums1 = call(
         functools.partial(glu_kernel, part=part),
         (
             shape(total, full),
             shape(total, full, dtype=LOW),
             shape(total, full, dtype=LOW),
+            shape(total, full, dtype=LOW),
+            shape(total, full, dtype=LOW),
+            shape(2 * states, full, dtype=LOW),
             shape(2 * full, full, dtype=LOW),
-            shape(32, full),
+            shape(dp_size, 8, full),
         ),
-        [pltpu.VMEM((part, 2 * full), F32)],
-        (meta, *x_parts, active0, *w_parts[0], feature),
-        flops=3e9,
+        [pltpu.VMEM((part, 2 * full), F32), pltpu.VMEM((32, full), F32)],
+        (lengths, *x_parts, normed0, low0, *cw_parts, feature),
         name="glu",
     )
-    sums1 = spread(sums1[:8], "dp", dp_size)
-    result, base, bn1, grads1, small1, norm1 = call(
-        functools.partial(middle_kernel, part=part),
+    sums1 = across(sums1, "dp")
+    far[3], far[4], *_ = lax.optimization_barrier((far[3], far[4], stream1))
+    later_parts, up_parts = (
+        (own_part, swap(value, 1, sharers), far_part, swap(far_part, 1, sharers))
+        for own_part, value, far_part in ((later, later, far[3]), (up_own, up_low, far[4]))
+    )
+    share = 4 * width // dp_size
+
+    def middle(*refs):
+        length_ref, stream_ref, sums_ref = refs[:3]
+        parts, ups, refs = refs[3:7], refs[7:11], refs[11:]
+        middle_kernel(length_ref, stream_ref, sums_ref, parts, ups, *refs, part=part)
+
+    result, base, bn1, norm1, grads1 = call(
+        middle,
         (
             shape(width, total),
             shape(total, full),
-            shape(32, full),
+            shape(dp_size, 8, full),
+            shape(8, full),
             shape(4 * width, full, dtype=LOW),
-            shape(8, full),
-            shape(8, full),
         ),
         [
+            pltpu.VMEM((32, full), F32),
+            pltpu.VMEM((8, full), F32),
             pltpu.VMEM((2 * states, full), LOW),
             pltpu.VMEM((2 * states, full), LOW),
             pltpu.VMEM((2 * full, full), LOW),
@@ -846,38 +972,60 @@
             pltpu.VMEM((16, width), F32),
             pltpu.VMEM((32, width), F32),
         ],
-        (meta, stream1, sums1, *b_parts[1], *c_parts[1], *w_parts[1], feature, state, norm0, *cotangent_parts),
-        flops=2e10,
+        (lengths, stream1, sums1, *later_parts, *up_parts, feature, state, norm0),
         name="middle",
     )
-    bn1 = spread(bn1[:8], "dp", dp_size)
-    share = 8 * width // dp_size
-    send, up0, grad0 = call(
-        functools.partial(last_kernel, part=part),
-        (shape(dp_size, share + 32, full, dtype=LOW), shape(total, width), shape(total, width)),
+    bn1 = across(bn1, "dp")
+    grads1 = across(grads1.reshape(dp_size, share, full), "dp")
+    up0, pre_grad0, glu_grads0, small0 = call(
+        functools.partial(last_glu_kernel, part=part),
+        (
+            shape(total, width),
+            shape(total, full, dtype=LOW),
+            shape(2 * width, full, dtype=LOW),
+            shape(8, full),
+        ),
+        [
+            pltpu.VMEM((part, 2 * full), F32),
+            pltpu.VMEM((total, 2 * full), LOW),
+            pltpu.VMEM((16, width), F32),
+            pltpu.VMEM((32, width), F32),
+            pltpu.VMEM((16, full), F32),
+        ],
+        (lengths, stream1, base, bn1, norm1, gate0, linear0, slope0, active0, normed0, w_all, feature),
+        name="last_glu",
+    )
+    grads1, pre_grad0 = lax.optimization_barrier((grads1, pre_grad0))
+    (grads1,) = call(add_kernel, (shape(dp_size, share, full, dtype=LOW),), [], (grads1,), smem=0, name="add")
+    pre_grad0, grads1 = lax.optimization_barrier((pre_grad0, grads1))
+    grads1 = across(grads1, "dp")
+    send, grad0 = call(
+        functools.partial(last_state_kernel, part=part),
+        (shape(dp_size, share + 16, full, dtype=LOW), shape(total, width)),
         [
             pltpu.VMEM((part, 2 * full), F32),
             pltpu.VMEM((total, 2 * states), F32),
-            pltpu.VMEM((total, 2 * full), LOW),
-            pltpu.VMEM((total, full), LOW),
             pltpu.VMEM((total, 2 * states), LOW),
-            pltpu.VMEM((16, width), F32),
-            pltpu.VMEM((32, width), F32),
             pltpu.VMEM((8, full), F32),
             pltpu.VMEM((32, width), F32),
             pltpu.VMEM((4 * width, full), LOW),
             pltpu.VMEM((16, full), F32),
         ],
-        (meta, stream1, base, bn1, norm1, gate0, linear0, slope0, active0, normed0, low0, drive0, b_all, c_all, w_all,
-         feature, state, packed, norm0, grads1, small1),
-        flops=1e10,
-        name="last",
-    )
-    got = lax.all_to_all(send, "dp", 0, 0, tiled=True)
-    back, grad_nu, grad_theta, grad_gamma, grad_skip, grad_bias, grad_gain, grad_shift, grad_inputs = call(
+        (lengths, pre_grad0, normed0, low0, drive0, b_all, c_all, glu_grads0, small0, feature, state, packed, norm0),
+        name="last_state",
+    )
+    send, grads1 = lax.optimization_barrier((send, grads1))
+    back, small0 = call(
+        share_kernel,
+        (shape(dp_size, share, full, dtype=LOW), shape(8, full)),
+        [],
+        (across(send, "dp"),),
+        smem=0,
+        name="share",
+    )
+    grad_nu, grad_theta, grad_gamma, grad_skip, grad_bias, grad_gain, grad_shift, grad_inputs = call(
         finish_kernel,
         (
-            shape(dp_size, share, full, dtype=LOW),
             shape(LAYERS, own_states),
             shape(LAYERS, own_states),
             shape(LAYERS, own_states),
@@ -887,14 +1035,23 @@
             shape(LAYERS, width),
             shape(width, total),
         ),
-        [pltpu.VMEM((8, full), F32), pltpu.VMEM((16, full), F32), pltpu.VMEM((total, width), F32)],
-        (meta, got, up0, grad0, packed, norm0, feature, nu_log, theta_log, bn1),
+        [pltpu.VMEM((16, full), F32), pltpu.VMEM((total, width), F32)],
+        (lengths, up0, grad0, packed, norm0, feature, nu_log, theta_log, bn1, small0),
         name="finish",
     )
-    whole = lax.all_to_all(back, "dp", 0, 0, tiled=True).reshape(8 * width, full).astype(F32)
-    grad_b = whole[: 2 * width].reshape(LAYERS, 2, own_states, full)
-    grad_c = whole[2 * width : 4 * width].reshape(LAYERS, 2, own_states, full)
-    grad_glu = whole[4 * width :].reshape(LAYERS, 2, width, full)
+    grads0 = across(back, "dp").reshape(4 * width, full)
+
+    grad_b, grad_c, grad_glu = call(
+        widen_kernel,
+        (shape(LAYERS, width, full), shape(LAYERS, width, full), shape(LAYERS, 2 * width, full)),
+        [],
+        (grads0, grads1.reshape(4 * width, full)),
+        smem=0,
+        name="widen",
+    )
+    grad_b = grad_b.reshape(LAYERS, 2, own_states, full)
+    grad_c = grad_c.reshape(LAYERS, 2, own_states, full)
+    grad_glu = grad_glu.reshape(LAYERS, 2, width, full)
     return (
         own(result[None], 1),
         own(grad_inputs[None], 1),

time: 205 us -> 188 us (0.917)
  blocking collectives: 73.1 us -> 32 us
  waiting for transfers between devices: 22.5 us -> 38.4 us
  Pallas kernels: 68.5 us -> 78.2 us
  starting transfers between devices: 24.5 us -> 31.8 us
  local copies, waits for them, and re-layouts: 10.9 us -> 4.91 us
  other arithmetic: 2.69 us -> 0 us
    all_to_all x3 -> x2, blocking collectives: 73.1 us -> 32 us  [across(): return lax.all_to_all(value, axes, 0, 0, tiled=True)]
    all_to_all x2 -> x5, waiting for transfers between devices: 7.45 us -> 27.2 us  [across(): return lax.all_to_all(value, axes, 0, 0, tiled=True)]
    all_to_all x2 -> x5, starting transfers between devices: 9.32 us -> 21.4 us  [across(): return lax.all_to_all(value, axes, 0, 0, tiled=True)]
    pallas_call x7 -> x11, Pallas kernels: 68.5 us -> 78.2 us  [call(): pl.pallas_call(kernel, out_shape=tuple(outs), in_specs=[pl.BlockSpec(memo...]
    slice x8 -> x0, local copies, waits for them, and re-layouts: 7.55 us -> none  [the longest x1 1.18 us: local(): c_weight[layer].reshape(2 * own_states, full)]
    ppermute x24 -> x15, starting transfers between devices: 15.2 us -> 10.4 us  [swap(): return lax.ppermute(value, 'state', pairs)]
    ppermute x24 -> x15, waiting for transfers between devices: 15 us -> 11.2 us  [swap(): return lax.ppermute(value, 'state', pairs)]
    unnamed x56 -> x46, local copies, waits for them, and re-layouts: 2.04 us -> 4.91 us
  transfers between devices with their start and end apart: 26 -> 20, of which waited for: 6 -> 10; matrix products, arithmetic and copies ran while one was open for 3% -> 0% of each run, Pallas kernels for 11% -> 23%
where the time goes in v2:
time: 188 us; the launch traced here: 187 us
  Pallas kernels  78.2 us (42%)
  waiting for transfers between devices  38.4 us (20%)
  blocking collectives  32 us (17%)
  starting transfers between devices  31.8 us (17%)
  local copies, waits for them, and re-layouts  4.91 us (3%)
    pallas_call x11, Pallas kernels, call(): pl.pallas_call(kernel, out_shape=tuple(outs), in_specs=[pl.BlockSpec(memo...  78.2 us
    all_to_all x2, blocking collectives, across(): return lax.all_to_all(value, axes, 0, 0, tiled=True)  32 us
    all_to_all x5, waiting for transfers between devices, across(): return lax.all_to_all(value, axes, 0, 0, tiled=True)  27.2 us
    all_to_all x5, starting transfers between devices, across(): return lax.all_to_all(value, axes, 0, 0, tiled=True)  21.4 us
    ppermute x15, waiting for transfers between devices, swap(): return lax.ppermute(value, 'state', pairs)  11.2 us
    ppermute x15, starting transfers between devices, swap(): return lax.ppermute(value, 'state', pairs)  10.4 us
    unnamed x46, local copies, waits for them, and re-layouts  4.91 us
  transfers between devices with their start and end apart: 20, of which 10 were waited for; matrix products, arithmetic and copies ran while one was open for 0% of the time, Pallas kernels for 23%

profile of v2, /device:TPU:0, one launch (start us, length us, event | category | flops | bytes accessed | tf_op | source)
XLA Modules:
  0.0 186.8 jit_solution(13086155260818041949)
XLA Ops:
  1.3 4.2 %enter.1 = (f32[1040,128]{1,0:T(8,128)}, f32[32,8,128]{2,1,0:T(8,128)}, bf16[128,512]{1,0:T(8,128)(2,1)}, bf16[384,512]{1,0:T(8,128)(2,1)}, bf16[512,512]{1,0:T(8,128)(2,1)}) custom-call(s32[1]{0:T(128)S(6)} %copy.25.length_ref.refs_0_, f32[128,1024]{1,0:T(8,128)} %bitcast.15, f32[2,128]{1,0:T(2,128)} %gain_ref.1, f32[2,128]{1,0:T(2,128)} %shift_ref.1, ...), custom_call_target="tpu_custom_call" | custom-call | tf_op jit(solution)/shard_map/enter/pallas_call | solution.py:792
  5.5 3.0 %collective-permute-start.1 = (f32[1040,128]{1,0:T(8,128)}, f32[1040,128]{1,0:T(8,128)S(1)}, u32[]{:S(2)}, u32[]{:S(2)}) collective-permute-start(f32[1040,128]{1,0:T(8,128)} %get-tuple-element.77.x0.x_ref), channel_id=1, source_target_pairs={{0,2},{1,3},{2,0},{3,1},{4,6},{5,7},{6,4},{7,5},{8,10},{9,11},{10,... | collective-permute-start | bytes 1597448 | tf_op jit(solution)/shard_map/ppermute | solution.py:812
  8.5 4.9 %all-to-all-start = ((f32[32,8,128]{2,1,0:T(8,128)}), f32[32,8,128]{2,1,0:T(8,128)S(1)}, u32[]{:S(2)}, u32[]{:S(2)}) async-start(f32[32,8,128]{2,1,0:T(8,128)} %get-tuple-element.79), calls=%async_computation | async-start | bytes 262144 | tf_op jit(solution)/shard_map/all_to_all | solution.py:853
  13.4 1.8 collective-permute-start.2
  15.3 2.5 %cotangent.1 = (f32[1024,128]{1,0:T(8,128)}, bf16[1024,128]{1,0:T(8,128)(2,1)}) custom-call(f32[128,1024]{1,0:T(8,128)} %bitcast.17), custom_call_target="tpu_custom_call" | custom-call | tf_op jit(solution)/shard_map/cotangent/pallas_call | solution.py:792
  17.8 7.2 %collective-permute-done.2.b2 = bf16[128,512]{1,0:T(8,128)(2,1)S(1)} collective-permute-done((bf16[128,512]{1,0:T(8,128)(2,1)}, bf16[128,512]{1,0:T(8,128)(2,1)S(1)}, u32[]{:S(2)}, u32[]{:S(2)}) %collective-permute-start.2) | collective-permute-done | bytes 131104 | tf_op jit(solution)/shard_map/ppermute | solution.py:812
  25.1 1.8 collective-permute-start.7
  26.9 0.2 collective-permute-start.4
  27.1 0.3 collective-permute-start.5
  27.4 1.0 collective-permute-done.4.b1
  28.6 0.6 copy-done.20
  29.1 0.2 copy-done.1
  29.4 0.8 copy-done.2
  30.2 6.6 %drive.1 = (bf16[1024,512]{1,0:T(8,128)(2,1)}, f32[1024,256]{1,0:T(8,128)}, bf16[1024,512]{1,0:T(8,128)(2,1)}, bf16[512,512]{1,0:T(8,128)(2,1)}, f32[16,512]{1,0...) custom-call(s32[1]{0:T(128)S(6)} %copy.25.length_ref.refs_0_, f32[1040,128]{1,0:T(8,128)} %get-tuple-element.77.x0.x_ref, ...), custom_call_target="tpu_custom_call" | custom-call | tf_op jit(solution)/shard_map/drive/pallas_call | solution.py:792
  36.8 0.1 collective-permute-done.7.cw2
  36.9 1.7 collective-permute-start.10
  38.6 0.5 collective-permute-start.8
  39.1 0.3 collective-permute-start.11
  39.4 0.9 collective-permute-done.6.cw1
  40.3 0.6 collective-permute-done.8.cw3
  40.9 0.2 copy-done.14
  41.1 0.5 copy-done.15
  41.7 13.5 %glu.1 = (f32[1024,512]{1,0:T(8,128)}, bf16[1024,512]{1,0:T(8,128)(2,1)}, bf16[1024,512]{1,0:T(8,128)(2,1)}, bf16[1024,512]{1,0:T(8,128)(2,1)}, bf16[1024,512]{1...) custom-call(s32[1]{0:T(128)S(6)} %copy.25.length_ref.refs_0_, ...), custom_call_target="tpu_custom_call" | custom-call | tf_op jit(solution)/shard_map/glu/pallas_call | solution.py:792
  55.1 1.4 collective-permute-done.11.refs_9_
  56.6 0.5 collective-permute-start.13
  57.1 0.1 collective-permute-start.14
  57.2 5.8 %all-to-all-start.1 = ((f32[8,8,512]{2,1,0:T(8,128)}), f32[8,8,512]{2,1,0:T(8,128)S(1)}, u32[]{:S(2)}, u32[]{:S(2)}) async-start(f32[8,8,512]{2,1,0:T(8,128)} %get-tuple-element.92), calls=%async_computation.1 | async-start | bytes 262144 | tf_op jit(solution)/shard_map/all_to_all | solution.py:853
  63.0 7.6 %all-to-all-done.1.refs_2_ = f32[8,8,512]{2,1,0:T(8,128)S(1)} async-done(((f32[8,8,512]{2,1,0:T(8,128)}), f32[8,8,512]{2,1,0:T(8,128)S(1)}, u32[]{:S(2)}, u32[]{:S(2)}) %all-to-all-start.1) | async-done | bytes 131104 | tf_op jit(solution)/shard_map/all_to_all | solution.py:853
  70.6 0.6 copy-done.11
  71.2 0.1 copy-done.18
  71.4 0.1 copy-done.9
  71.5 24.5 %middle.1 = (f32[128,1024]{1,0:T(8,128)}, f32[1024,512]{1,0:T(8,128)}, f32[8,8,512]{2,1,0:T(8,128)}, f32[8,512]{1,0:T(8,128)}, bf16[512,512]{1,0:T(8,128)(2,1)}) custom-call(s32[1]{0:T(128)S(6)} %copy.25.length_ref.refs_0_, f32[1024,512]{1,0:T(8,128)} %get-tuple-element.91.refs_1_.stream_ref, f32[8,8,512]{2,1,0:T(8,128)} %copy-done.11, ...), custom_call_target="tpu_custom_call" | custom-call | tf_op jit(solution)/shard_map/middle/pallas_call | solution.py:792
  96.0 11.3 %all_to_all.35.sums_ref.bn1_ref = f32[8,8,512]{2,1,0:T(8,128)} all-to-all(f32[8,8,512]{2,1,0:T(8,128)} %get-tuple-element.104), channel_id=1, replica_groups=mesh['dp'=8,'state'=4] {'dp'}, dimensions={0} | all-to-all | bytes 262144 | tf_op jit(solution)/shard_map/all_to_all | solution.py:853
  107.4 3.5 %all-to-all-start.3 = ((bf16[8,64,512]{2,1,0:T(8,128)(2,1)}), bf16[8,64,512]{2,1,0:T(8,128)(2,1)S(1)}, u32[]{:S(2)}, u32[]{:S(2)}) async-start(bf16[8,64,512]{2,1,0:T(8,128)(2,1)} %bitcast.18), calls=%async_computation.3 | async-start | bytes 1048576 | tf_op jit(solution)/shard_map/all_to_all | solution.py:853
  110.9 9.1 %last_glu.1 = (f32[1024,128]{1,0:T(8,128)}, bf16[1024,512]{1,0:T(8,128)(2,1)}, bf16[256,512]{1,0:T(8,128)(2,1)}, f32[8,512]{1,0:T(8,128)}) custom-call(s32[1]{0:T(128)S(6)} %copy.25.length_ref.refs_0_, f32[1024,512]{1,0:T(8,128)} %get-tuple-element.91.refs_1_.stream_ref, f32[1024,512]{1,0:T(8,128)} %get-tuple-element.103.base_ref, ...), custom_call_target="tpu_custom_call" | custom-call | tf_op jit(solution)/shard_map/last_glu/pallas_call | solution.py:792
  119.9 3.6 %all-to-all-done.3.got_ref = bf16[8,64,512]{2,1,0:T(8,128)(2,1)S(1)} async-done(((bf16[8,64,512]{2,1,0:T(8,128)(2,1)}), bf16[8,64,512]{2,1,0:T(8,128)(2,1)S(1)}, u32[]{:S(2)}, u32[]{:S(2)}) %all-to-all-start.3) | async-done | bytes 524320 | tf_op jit(solution)/shard_map/all_to_all | solution.py:853
  123.5 0.8 copy-done.5
  124.3 1.9 %add.1 = bf16[8,64,512]{2,1,0:T(8,128)(2,1)} custom-call(bf16[8,64,512]{2,1,0:T(8,128)(2,1)} %copy-done.5), custom_call_target="tpu_custom_call" | custom-call | tf_op jit(solution)/shard_map/add/pallas_call | solution.py:792
  126.2 3.6 %all-to-all-start.4 = ((bf16[8,64,512]{2,1,0:T(8,128)(2,1)}), bf16[8,64,512]{2,1,0:T(8,128)(2,1)S(1)}, u32[]{:S(2)}, u32[]{:S(2)}) async-start(bf16[8,64,512]{2,1,0:T(8,128)(2,1)} %add.1), calls=%async_computation.4 | async-start | bytes 1048576 | tf_op jit(solution)/shard_map/all_to_all | solution.py:853
  129.8 8.4 %last_state.1 = (bf16[8,80,512]{2,1,0:T(8,128)(2,1)}, f32[1024,128]{1,0:T(8,128)}) custom-call(s32[1]{0:T(128)S(6)} %copy.25.length_ref.refs_0_, bf16[1024,512]{1,0:T(8,128)(2,1)} %get-tuple-element.116.pre_grad_ref, bf16[1024,512]{1,0:T(8,128)(2,1)} %get-tuple-element.85.normed_ref, bf16[1024,512]{1,0:T(8,128)(2,1)} %get-tuple-element.86.low_ref, ...), custom_call_target="tpu_custom_call" | custom-call | tf_op jit(solution)/shard_map/last_state/pallas_call | solution.py:792
  138.2 5.3 %all-to-all-done.4 = bf16[8,64,512]{2,1,0:T(8,128)(2,1)S(1)} async-done(((bf16[8,64,512]{2,1,0:T(8,128)(2,1)}), bf16[8,64,512]{2,1,0:T(8,128)(2,1)S(1)}, u32[]{:S(2)}, u32[]{:S(2)}) %all-to-all-start.4) | async-done | bytes 524320 | tf_op jit(solution)/shard_map/all_to_all | solution.py:853
  143.5 20.7 %all_to_all.36.got_ref = bf16[8,80,512]{2,1,0:T(8,128)(2,1)} all-to-all(bf16[8,80,512]{2,1,0:T(8,128)(2,1)} %get-tuple-element.125), channel_id=1, replica_groups=mesh['dp'=8,'state'=4] {'dp'}, dimensions={0} | all-to-all | bytes 1310720 | tf_op jit(solution)/shard_map/all_to_all | solution.py:853
  164.2 2.0 %share.1 = (bf16[8,64,512]{2,1,0:T(8,128)(2,1)}, f32[8,512]{1,0:T(8,128)}) custom-call(bf16[8,80,512]{2,1,0:T(8,128)(2,1)} %all_to_all.36.got_ref), custom_call_target="tpu_custom_call" | custom-call | tf_op jit(solution)/shard_map/share/pallas_call | solution.py:792
  166.1 3.5 %all-to-all-start.6 = ((bf16[8,64,512]{2,1,0:T(8,128)(2,1)}), bf16[8,64,512]{2,1,0:T(8,128)(2,1)S(1)}, u32[]{:S(2)}, u32[]{:S(2)}) async-start(bf16[8,64,512]{2,1,0:T(8,128)(2,1)} %get-tuple-element.130), calls=%async_computation.6 | async-start | bytes 1048576 | tf_op jit(solution)/shard_map/all_to_all | solution.py:853
  169.6 3.1 %finish.1 = (f32[2,64]{1,0:T(2,128)}, f32[2,64]{1,0:T(2,128)}, f32[2,64]{1,0:T(2,128)}, f32[2,128]{1,0:T(2,128)}, f32[2,2,128]{2,1,0:T(2,128)}, /*index=5*/f32[2...) custom-call(s32[1]{0:T(128)S(6)} %copy.25.length_ref.refs_0_, f32[1024,128]{1,0:T(8,128)} %get-tuple-element.111.up_ref, ...), custom_call_target="tpu_custom_call" | custom-call | tf_op jit(solution)/shard_map/finish/pallas_call | solution.py:792
  172.7 10.7 %all-to-all-done.6 = bf16[8,64,512]{2,1,0:T(8,128)(2,1)S(1)} async-done(((bf16[8,64,512]{2,1,0:T(8,128)(2,1)}), bf16[8,64,512]{2,1,0:T(8,128)(2,1)S(1)}, u32[]{:S(2)}, u32[]{:S(2)}) %all-to-all-start.6) | async-done | bytes 524320 | tf_op jit(solution)/shard_map/all_to_all | solution.py:853
  183.4 0.8 copy-done.4
  184.2 2.5 %widen.1 = (f32[2,128,512]{2,1,0:T(8,128)}, f32[2,128,512]{2,1,0:T(8,128)}, f32[2,256,512]{2,1,0:T(8,128)}) custom-call(bf16[512,512]{1,0:T(8,128)(2,1)} %bitcast.14, bf16[512,512]{1,0:T(8,128)(2,1)} %bitcast.13), custom_call_target="tpu_custom_call" | custom-call | tf_op jit(solution)/shard_map/widen/pallas_call | solution.py:792
  (51 shorter events, 0.3 us)
Async XLA Ops:
  5.5 31.4 %copy-start.6 = (bf16[512,512]{1,0:T(8,128)(2,1)S(1)}, bf16[512,512]{1,0:T(8,128)(2,1)}, u32[]{:S(2)}) copy-start(bf16[512,512]{1,0:T(8,128)(2,1)} %get-tuple-element.95.refs_3_) | copy-start | bytes 1572868
  5.5 33.1 %copy-start.12 = (bf16[384,512]{1,0:T(8,128)(2,1)S(1)}, bf16[384,512]{1,0:T(8,128)(2,1)}, u32[]{:S(2)}) copy-start(bf16[384,512]{1,0:T(8,128)(2,1)} %get-tuple-element.87.cw0) | copy-start | bytes 1179652
  5.5 19.5 %collective-permute-start.1 = (f32[1040,128]{1,0:T(8,128)}, f32[1040,128]{1,0:T(8,128)S(1)}, u32[]{:S(2)}, u32[]{:S(2)}) collective-permute-start(f32[1040,128]{1,0:T(8,128)} %get-tuple-element.77.x0.x_ref), channel_id=1, source_target_pairs={{0,2},{1,3},{2,0},{3,1},{4,6},{5,7},{6,4},{7,5},{8,10},{9,11},{10,... | collective-permute-start | bytes 1597448 | tf_op jit(solution)/shard_map/ppermute | solution.py:812
  8.5 16.5 %all-to-all-start = ((f32[32,8,128]{2,1,0:T(8,128)}), f32[32,8,128]{2,1,0:T(8,128)S(1)}, u32[]{:S(2)}, u32[]{:S(2)}) async-start(f32[32,8,128]{2,1,0:T(8,128)} %get-tuple-element.79), calls=%async_computation | async-start | bytes 262144 | tf_op jit(solution)/shard_map/all_to_all | solution.py:853
  13.4 11.6 %collective-permute-start.2 = (bf16[128,512]{1,0:T(8,128)(2,1)}, bf16[128,512]{1,0:T(8,128)(2,1)S(1)}, u32[]{:S(2)}, u32[]{:S(2)}) collective-permute-start(bf16[128,512]{1,0:T(8,128)(2,1)} %get-tuple-element.78.b0), channel_id=1, source_target_pairs={{0,2},{1,3},{2,0},{3,1},{4,6},{5,7},{6,4},{7,5},{8,10},{9,11},{10,... | collective-permute-start | bytes 393224 | tf_op jit(solution)/shard_map/ppermute | solution.py:812
  15.3 13.2 %collective-permute-start = (f32[1040,128]{1,0:T(8,128)}, f32[1040,128]{1,0:T(8,128)S(1)}, u32[]{:S(2)}, u32[]{:S(2)}) collective-permute-start(f32[1040,128]{1,0:T(8,128)} %get-tuple-element.77.x0.x_ref), channel_id=1, source_target_pairs={{0,1},{1,0},{2,3},{3,2},{4,5},{5,4},{6,7},{7,6},{8,9},{9,8},{10,11... | collective-permute-start | bytes 1597448 | tf_op jit(solution)/shard_map/ppermute | solution.py:812
  17.8 21.3 %copy-start.22 = (bf16[1024,128]{1,0:T(8,128)(2,1)S(1)}, bf16[1024,128]{1,0:T(8,128)(2,1)}, u32[]{:S(2)}) copy-start(bf16[1024,128]{1,0:T(8,128)(2,1)} %get-tuple-element.96) | copy-start | bytes 786436
  25.0 3.5 %copy-start.19 = (bf16[128,512]{1,0:T(8,128)(2,1)}, bf16[128,512]{1,0:T(8,128)(2,1)S(1)}, u32[]{:S(2)}) copy-start(bf16[128,512]{1,0:T(8,128)(2,1)S(1)} %collective-permute-done.2.b2) | copy-start | bytes 393220
  25.0 3.5 %copy-start.10 = (f32[32,8,128]{2,1,0:T(8,128)}, f32[32,8,128]{2,1,0:T(8,128)S(1)}, u32[]{:S(2)}) copy-start(f32[32,8,128]{2,1,0:T(8,128)S(1)} %all-to-all-done.sums_ref) | copy-start | bytes 393220
  25.0 3.5 %copy-start = (f32[1040,128]{1,0:T(8,128)}, f32[1040,128]{1,0:T(8,128)S(1)}, u32[]{:S(2)}) copy-start(f32[1040,128]{1,0:T(8,128)S(1)} %collective-permute-done.1.x2) | copy-start | bytes 1597444
  25.0 3.5 %collective-permute-start.3 = (f32[1040,128]{1,0:T(8,128)S(1)}, f32[1040,128]{1,0:T(8,128)S(1)}, u32[]{:S(2)}, u32[]{:S(2)}) collective-permute-start(f32[1040,128]{1,0:T(8,128)S(1)} %collective-permute-done.1.x2), channel_id=1, source_target_pairs={{0,1},{1,0},{2,3},{3,2},{4,5},{5,4},{6,7},{7,6},{8,9},{9,8},{10,11... | collective-permute-start | bytes 1597448 | tf_op jit(solution)/shard_map/ppermute | solution.py:812
  25.1 11.7 %collective-permute-start.7 = (bf16[384,512]{1,0:T(8,128)(2,1)}, bf16[384,512]{1,0:T(8,128)(2,1)S(1)}, u32[]{:S(2)}, u32[]{:S(2)}) collective-permute-start(bf16[384,512]{1,0:T(8,128)(2,1)} %get-tuple-element.87.cw0), channel_id=1, source_target_pairs={{0,2},{1,3},{2,0},{3,1},{4,6},{5,7},{6,4},{7,5},{8,10},{9,11},{10,... | collective-permute-start | bytes 1179656 | tf_op jit(solution)/shard_map/ppermute | solution.py:812
  26.9 1.6 collective-permute-start.4
  27.1 1.4 collective-permute-start.5
  28.5 0.7 copy-start.20
  28.5 0.8 copy-start.1
  28.5 0.9 copy-start.21
  29.4 0.8 copy-start.2
  36.9 4.0 %copy-start.13 = (bf16[384,512]{1,0:T(8,128)(2,1)}, bf16[384,512]{1,0:T(8,128)(2,1)S(1)}, u32[]{:S(2)}) copy-start(bf16[384,512]{1,0:T(8,128)(2,1)S(1)} %collective-permute-done.7.cw2) | copy-start | bytes 1179652
  36.9 19.6 %collective-permute-start.10 = (bf16[512,512]{1,0:T(8,128)(2,1)S(1)}, bf16[512,512]{1,0:T(8,128)(2,1)S(1)}, u32[]{:S(2)}, u32[]{:S(2)}) collective-permute-start(bf16[512,512]{1,0:T(8,128)(2,1)S(1)} %copy-done.6), channel_id=1, source_target_pairs={{0,2},{1,3},{2,0},{3,1},{4,6},{5,7},{6,4},{7,5},{8,10},{9,11},{10,... | collective-permute-start | bytes 1572872 | tf_op jit(solution)/shard_map/ppermute | solution.py:812
  38.6 1.7 collective-permute-start.6
  38.6 2.3 %collective-permute-start.8 = (bf16[384,512]{1,0:T(8,128)(2,1)S(1)}, bf16[384,512]{1,0:T(8,128)(2,1)S(1)}, u32[]{:S(2)}, u32[]{:S(2)}) collective-permute-start(bf16[384,512]{1,0:T(8,128)(2,1)S(1)} %collective-permute-done.7.cw2), channel_id=1, source_target_pairs={{0,1},{1,0},{2,3},{3,2},{4,5},{5,4},{6,7},{7,6},{8,9},{9,8},{10,11... | collective-permute-start | bytes 1179656 | tf_op jit(solution)/shard_map/ppermute | solution.py:812
  39.1 17.4 %collective-permute-start.11 = (bf16[1024,128]{1,0:T(8,128)(2,1)S(1)}, bf16[1024,128]{1,0:T(8,128)(2,1)S(1)}, u32[]{:S(2)}, u32[]{:S(2)}) collective-permute-start(bf16[1024,128]{1,0:T(8,128)(2,1)S(1)} %copy-done.22), channel_id=1, source_target_pairs={{0,2},{1,3},{2,0},{3,1},{4,6},{5,7},{6,4},{7,5},{8,10},{9,11},{10,... | collective-permute-start | bytes 786440 | tf_op jit(solution)/shard_map/ppermute | solution.py:812
  39.4 23.6 %collective-permute-start.9 = (bf16[512,512]{1,0:T(8,128)(2,1)S(1)}, bf16[512,512]{1,0:T(8,128)(2,1)S(1)}, u32[]{:S(2)}, u32[]{:S(2)}) collective-permute-start(bf16[512,512]{1,0:T(8,128)(2,1)S(1)} %copy-done.6), channel_id=1, source_target_pairs={{0,1},{1,0},{2,3},{3,2},{4,5},{5,4},{6,7},{7,6},{8,9},{9,8},{10,11... | collective-permute-start | bytes 1572872 | tf_op jit(solution)/shard_map/ppermute | solution.py:812
  40.3 0.8 copy-start.14
  40.9 0.8 copy-start.15
  56.5 14.1 %copy-start.16 = (bf16[1024,128]{1,0:T(8,128)(2,1)}, bf16[1024,128]{1,0:T(8,128)(2,1)S(1)}, u32[]{:S(2)}) copy-start(bf16[1024,128]{1,0:T(8,128)(2,1)S(1)} %collective-permute-done.11.refs_9_) | copy-start | bytes 786436
  56.5 14.1 %copy-start.7 = (bf16[512,512]{1,0:T(8,128)(2,1)}, bf16[512,512]{1,0:T(8,128)(2,1)S(1)}, u32[]{:S(2)}) copy-start(bf16[512,512]{1,0:T(8,128)(2,1)S(1)} %collective-permute-done.10.refs_5_) | copy-start | bytes 1572868
  56.5 14.1 %collective-permute-start.12 = (bf16[512,512]{1,0:T(8,128)(2,1)S(1)}, bf16[512,512]{1,0:T(8,128)(2,1)S(1)}, u32[]{:S(2)}, u32[]{:S(2)}) collective-permute-start(bf16[512,512]{1,0:T(8,128)(2,1)S(1)} %collective-permute-done.10.refs_5_), channel_id=1, source_target_pairs={{0,1},{1,0},{2,3},{3,2},{4,5},{5,4},{6,7},{7,6},{8,9},{9,8},{10,11... | collective-permute-start | bytes 1572872 | tf_op jit(solution)/shard_map/ppermute | solution.py:812
  56.6 6.4 %collective-permute-start.13 = (bf16[1024,128]{1,0:T(8,128)(2,1)S(1)}, bf16[1024,128]{1,0:T(8,128)(2,1)S(1)}, u32[]{:S(2)}, u32[]{:S(2)}) collective-permute-start(bf16[1024,128]{1,0:T(8,128)(2,1)S(1)} %copy-done.22), channel_id=1, source_target_pairs={{0,1},{1,0},{2,3},{3,2},{4,5},{5,4},{6,7},{7,6},{8,9},{9,8},{10,11... | collective-permute-start | bytes 786440 | tf_op jit(solution)/shard_map/ppermute | solution.py:812
  57.1 13.5 %collective-permute-start.14 = (bf16[1024,128]{1,0:T(8,128)(2,1)S(1)}, bf16[1024,128]{1,0:T(8,128)(2,1)S(1)}, u32[]{:S(2)}, u32[]{:S(2)}) collective-permute-start(bf16[1024,128]{1,0:T(8,128)(2,1)S(1)} %collective-permute-done.11.refs_9_), channel_id=1, source_target_pairs={{0,1},{1,0},{2,3},{3,2},{4,5},{5,4},{6,7},{7,6},{8,9},{9,8},{10,11... | collective-permute-start | bytes 786440 | tf_op jit(solution)/shard_map/ppermute | solution.py:812
  57.2 13.4 %all-to-all-start.1 = ((f32[8,8,512]{2,1,0:T(8,128)}), f32[8,8,512]{2,1,0:T(8,128)S(1)}, u32[]{:S(2)}, u32[]{:S(2)}) async-start(f32[8,8,512]{2,1,0:T(8,128)} %get-tuple-element.92), calls=%async_computation.1 | async-start | bytes 262144 | tf_op jit(solution)/shard_map/all_to_all | solution.py:853
  63.0 7.6 %copy-start.17 = (bf16[1024,128]{1,0:T(8,128)(2,1)}, bf16[1024,128]{1,0:T(8,128)(2,1)S(1)}, u32[]{:S(2)}) copy-start(bf16[1024,128]{1,0:T(8,128)(2,1)S(1)} %collective-permute-done.13.refs_8_) | copy-start | bytes 786436
  63.0 7.6 %copy-start.8 = (bf16[512,512]{1,0:T(8,128)(2,1)}, bf16[512,512]{1,0:T(8,128)(2,1)S(1)}, u32[]{:S(2)}) copy-start(bf16[512,512]{1,0:T(8,128)(2,1)S(1)} %collective-permute-done.9.refs_4_) | copy-start | bytes 1572868
  70.6 0.7 copy-start.11
  70.6 0.8 copy-start.18
  70.6 0.9 copy-start.9
  107.4 16.2 %all-to-all-start.3 = ((bf16[8,64,512]{2,1,0:T(8,128)(2,1)}), bf16[8,64,512]{2,1,0:T(8,128)(2,1)S(1)}, u32[]{:S(2)}, u32[]{:S(2)}) async-start(bf16[8,64,512]{2,1,0:T(8,128)(2,1)} %bitcast.18), calls=%async_computation.3 | async-start | bytes 1048576 | tf_op jit(solution)/shard_map/all_to_all | solution.py:853
  123.5 0.8 copy-start.5
  126.2 17.3 %all-to-all-start.4 = ((bf16[8,64,512]{2,1,0:T(8,128)(2,1)}), bf16[8,64,512]{2,1,0:T(8,128)(2,1)S(1)}, u32[]{:S(2)}, u32[]{:S(2)}) async-start(bf16[8,64,512]{2,1,0:T(8,128)(2,1)} %add.1), calls=%async_computation.4 | async-start | bytes 1048576 | tf_op jit(solution)/shard_map/all_to_all | solution.py:853
  143.5 29.2 %copy-start.3 = (bf16[8,64,512]{2,1,0:T(8,128)(2,1)}, bf16[8,64,512]{2,1,0:T(8,128)(2,1)S(1)}, u32[]{:S(2)}) copy-start(bf16[8,64,512]{2,1,0:T(8,128)(2,1)S(1)} %all-to-all-done.4) | copy-start | bytes 1572868
  166.1 17.3 %all-to-all-start.6 = ((bf16[8,64,512]{2,1,0:T(8,128)(2,1)}), bf16[8,64,512]{2,1,0:T(8,128)(2,1)S(1)}, u32[]{:S(2)}, u32[]{:S(2)}) async-start(bf16[8,64,512]{2,1,0:T(8,128)(2,1)} %get-tuple-element.130), calls=%async_computation.6 | async-start | bytes 1048576 | tf_op jit(solution)/shard_map/all_to_all | solution.py:853
  183.4 0.8 copy-start.4

commit v3 on v0

v3 whole, which is shorter than its diff:
```python
import functools

import jax
import jax.numpy as jnp
from jax import lax
from jax.experimental import pallas as pl
from jax.experimental.pallas import tpu as pltpu
from jax.sharding import PartitionSpec as P

LAYERS = 2
CHUNKS = 16
PIECES = 4
EPSILON = 1e-05
F32 = jnp.float32
LOW = jnp.bfloat16
PARAM_ROWS = 16
VMEM_BYTES = 64 * 1024 * 1024
ENTER_FLOPS = 1e10

GAIN, SHIFT, SKIP, BIAS_LINEAR, BIAS_GATE = range(5)
RATE_RE, RATE_IM, GAMMA = range(3)

NN = (((1,), (0,)), ((), ()))
NT = (((1,), (1,)), ((), ()))
TN = (((0,), (0,)), ((), ()))


def dot(left, right, dims):
    return lax.dot_general(left, right, dims, preferred_element_type=F32)


def rows_at(index, size):
    return pl.ds(pl.multiple_of(index * size, size), size)


def lanes_at(quarter, width):
    return pl.ds(pl.multiple_of(quarter * width, width), width)


def for_rows(first, last, size, body, init=0, unroll=2):
    def step(index, carry):
        return body(rows_at(index, size), index, carry)

    return lax.fori_loop(first // size, last // size, step, init, unroll=unroll)


def own_quarter():
    return (lax.axis_index("state") // (lax.axis_size("state") // 4)).astype(jnp.int32)


def keep_rows(first_step, rows, steps, length):
    row = lax.broadcasted_iota(jnp.int32, (rows, 1), 0)
    position = (row % CHUNKS) * steps + row // CHUNKS + first_step
    return position < length


def gelu_parts(value):
    return 0.5 + 0.5 * lax.erf(value * 0.7071067811865476), jnp.exp(value * value * -0.5) * 0.3989422804014327


def squared(re, im, times):
    for _ in range(times):
        re, im = re * re - im * im, 2.0 * re * im
    return re, im


def folded(value):
    return value[0:8, :] + value[8:16, :]


def column_sum(value):
    return jnp.sum(value, axis=0, keepdims=True)


def chunk_starts(re, im, rate_re, rate_im, reverse):
    row = lax.broadcasted_iota(jnp.int32, re.shape, 0)

    def moved(value, by):
        if reverse:
            return jnp.where(row < CHUNKS - by, pltpu.roll(value, CHUNKS - by, 0), 0.0)
        return jnp.where(row >= by, pltpu.roll(value, by, 0), 0.0)

    by = 1
    while by < CHUNKS:
        past_re, past_im = moved(re, by), moved(im, by)
        re, im = (
            re + rate_re * past_re - rate_im * past_im,
            im + rate_re * past_im + rate_im * past_re,
        )
        rate_re, rate_im = squared(rate_re, rate_im, 1)
        by *= 2
    return moved(re, 1), moved(im, 1)


def sweep(drive_ref, rate_re, rate_im, steps, reverse, emit, extra, after=None, unroll=4):
    states = rate_re.shape[1]
    shape = (CHUNKS, states)
    wide_re = jnp.broadcast_to(rate_re, shape)
    wide_im = jnp.broadcast_to(rate_im, shape)

    def advance(index, re, im):
        place = steps - 1 - index if reverse else index
        rows = rows_at(place, CHUNKS)
        drive_re = drive_ref[rows, :states]
        drive_im = drive_ref[rows, states:]
        new_re = (wide_re * re + drive_re) - wide_im * im
        new_im = (wide_re * im + drive_im) + wide_im * re
        return rows, place, new_re, new_im, drive_re, drive_im

    def first(index, carry):
        _, _, re, im, _, _ = advance(index, *carry)
        return re, im

    def second(index, carry):
        re, im, held = carry
        rows, place, re, im, drive_re, drive_im = advance(index, re, im)
        return re, im, emit(rows, place, re, im, drive_re, drive_im, held)

    zero = jnp.zeros(shape, F32)
    re, im = lax.fori_loop(0, steps, first, (zero, zero), unroll=unroll)
    far_re, far_im = rate_re, rate_im
    power = 1
    while power < steps:
        far_re, far_im = squared(far_re, far_im, 1)
        power *= 2
    re, im = chunk_starts(re, im, far_re, far_im, reverse)
    carry = (re, im, extra)
    for piece in range(PIECES):
        size = steps // PIECES
        carry = lax.fori_loop(piece * size, (piece + 1) * size, second, carry, unroll=unroll)
        if after is not None:
            after(PIECES - 1 - piece if reverse else piece)
    return carry[2]


class Arrival:
    def __init__(self, source, ref, done, first, size, axis):
        self.ref = ref
        self.copies = []
        whole = ref.shape[axis]
        for piece, start in enumerate(range(0, whole, size)):
            where = (slice(None),) * axis + (pl.ds(start, min(size, whole - start)),)
            self.copies.append(
                pltpu.make_async_copy(source.at[where], ref.at[where], done.at[first + piece])
                if size < whole
                else pltpu.make_async_copy(source, ref, done.at[first])
            )
        self.short = whole % size > 0
        self.waited = set()

    def start(self, piece):
        last = len(self.copies) - self.short
        if piece < 0 and self.short:
            self.copies[-1].start()
        if 0 <= piece < last:
            self.copies[piece].start()

    def wait(self, piece=None):
        for place in range(len(self.copies)) if piece is None else (piece,):
            if place not in self.waited:
                self.copies[place].wait()
                self.waited.add(place)
        return self.ref


class Departure:
    def __init__(self, target, ref, done, first):
        self.target, self.ref, self.done, self.first = target, ref, done, first
        self.copies = []

    def send(self, start=None, size=None, source=None):
        place = self.done.at[self.first + len(self.copies)]
        where = self.target if start is None else self.target.at[pl.ds(start, size)]
        if source is None:
            source = self.ref if start is None else self.ref.at[pl.ds(start, size)]
        self.copies.append(pltpu.make_async_copy(source, where, place))
        self.copies[-1].start()

    def send_piece(self, piece):
        size = self.target.shape[0] // PIECES
        self.send(piece * size, size)

    def finish(self):
        if not self.copies:
            self.send()
        for copy in self.copies:
            copy.wait()


def call(kernel, outs, scratch, args, name, pieces=None, axes=None, bare=(), flops=0):
    pieces, axes = pieces or {}, axes or {}
    along = [axes.get(place, 0) for place in range(1, len(args))]
    sizes = [pieces.get(place, args[place].shape[axis]) for place, axis in enumerate(along, 1)]
    counts = [-(-args[place].shape[axis] // size) for place, (axis, size) in enumerate(zip(along, sizes), 1)]
    slots = 6
    copies_in = [pltpu.VMEM(a.shape, a.dtype) for a in args[1:]]
    copies_out = [pltpu.VMEM((8, 128) if place in bare else o.shape, o.dtype if place not in bare else F32) for place, o in enumerate(outs)]

    def body(*refs):
        refs = list(refs)

        def take(count):
            got = refs[:count]
            del refs[:count]
            return got

        (length_ref,) = take(1)
        sources = take(len(args) - 1)
        targets = take(len(outs))
        in_refs, out_refs = take(len(args) - 1), take(len(outs))
        arrived, sent = take(2)
        arrivals, first = [], 0
        for source, ref, size, count, axis in zip(sources, in_refs, sizes, counts, along):
            arrivals.append(Arrival(source, ref, arrived, first, size, axis))
            first += count
        for piece in range(-1, max(counts)):
            for arrival in arrivals:
                arrival.start(piece)
        departures = [
            Departure(target, ref, sent, place * slots) for place, (target, ref) in enumerate(zip(targets, out_refs))
        ]
        kernel(length_ref, arrivals, departures, *refs)
        for arrival in arrivals:
            arrival.wait()
        for departure in departures:
            departure.finish()

    return pl.pallas_call(
        body,
        out_shape=tuple(outs),
        in_specs=[pl.BlockSpec(memory_space=pltpu.SMEM if place == 0 else pl.ANY) for place in range(len(args))],
        out_specs=tuple(pl.BlockSpec(memory_space=pl.ANY) for _ in outs),
        scratch_shapes=[
            *copies_in,
            *copies_out,
            pltpu.SemaphoreType.DMA((sum(counts),)),
            pltpu.SemaphoreType.DMA((slots * len(outs),)),
            *scratch,
        ],
        compiler_params=pltpu.CompilerParams(vmem_limit_bytes=VMEM_BYTES),
        cost_estimate=pl.CostEstimate(flops=int(flops), bytes_accessed=0, transcendentals=0),
        name=name,
    )(*args)


def from_feature_rows(source, held_ref, steps, emit, init, after):
    length = source.ref.shape[1]
    blocks = length // 128
    for block in range(blocks):
        if block % (blocks // PIECES) == 0:
            source.wait(block // (blocks // PIECES))
        lanes = slice(block * 128, (block + 1) * 128)
        held_ref[lanes, :] = source.ref[:, lanes].T

    def step(index, carry):
        return emit(rows_at(index, CHUNKS), index, held_ref[pl.ds(index, CHUNKS, stride=steps), :], carry)

    carry = init
    for piece in range(PIECES):
        size = steps // PIECES
        carry = lax.fori_loop(piece * size, (piece + 1) * size, step, carry, unroll=4)
        after(piece)
    return carry


def to_feature_rows(load, held_ref, out, steps):
    length = out.ref.shape[1]

    def step(index, carry):
        held_ref[pl.ds(index, CHUNKS, stride=steps), :] = load(rows_at(index, CHUNKS), index)
        return carry

    lax.fori_loop(0, steps, step, 0, unroll=4)
    for block in range(length // 128):
        lanes = slice(block * 128, (block + 1) * 128)
        out.ref[:, lanes] = held_ref[lanes, :].T
    out.send()


def spread_rows(value, out):
    for group in range(out.ref.shape[0]):
        out.ref[group, :, :] = value
    out.send()


def narrowed(values, width):
    return jnp.concatenate([v[:, at : at + width] for v in values for at in range(0, v.shape[1], width)], axis=0)


def widened(rows, first, count):
    return jnp.concatenate([rows[first + place : first + place + 1, :] for place in range(count)], axis=1)


def total_rows(sums_ref):
    value = sums_ref[0, :, :]
    for other in range(1, sums_ref.shape[0]):
        value += sums_ref[other, :, :]
    return value


def assemble_states(parts, whole_ref):
    half = parts[0].shape[0] // 2
    states = half * len(parts)
    for place, part in enumerate(parts):
        whole_ref[place * half : (place + 1) * half, :] = part[:half, :]
        whole_ref[states + place * half : states + (place + 1) * half, :] = part[half:, :]


def assemble_output(parts, whole_ref):
    half = parts[0].shape[0] // 2
    states = half * len(parts)
    for place, part in enumerate(parts):
        whole_ref[place * half : (place + 1) * half, :] = part[:half, :]
        whole_ref[states + place * half : states + (place + 1) * half, :] = -part[half:, :]


def assemble_glu(parts, whole_ref, quarter):
    half = parts[0].shape[0] // 2
    width = half * len(parts)
    for place, part in enumerate(parts):
        whole_ref[lanes_at(quarter ^ place, half), :] = part[:half, :]
        whole_ref[pl.ds(pl.multiple_of(width + (quarter ^ place) * half, half), half), :] = part[half:, :]


def norm_rows(sums, counted):
    centre = sums[0:1, :] / counted
    meansq = sums[1:2, :] / counted
    return centre, lax.rsqrt(meansq - centre * centre + EPSILON)


def drive_phase(normed_ref, b_ref, drive_ref, gamma):
    drive_ref[...] = dot(normed_ref[...], b_ref[...], NT) * jnp.concatenate([gamma, gamma], axis=1)


def store_states(low_ref, drive_own_ref):
    def emit(rows, step, re, im, drive_re, drive_im, held):
        states = re.shape[1]
        low_ref[rows, :states] = re.astype(LOW)
        low_ref[rows, states:] = im.astype(LOW)
        drive_own_ref[rows, :128] = drive_re[:, :128].astype(drive_own_ref.dtype)
        drive_own_ref[rows, 128:] = drive_im[:, :128].astype(drive_own_ref.dtype)
        return held

    return emit


def pre_phase(low_ref, c_ref, normed_ref, skip, active_ref, slope_ref, held_ref, after=None):
    total, full = normed_ref.shape
    held_ref[:, :full] = dot(low_ref[...], c_ref[...], NN)

    def inner(rows, index, carry):
        value = held_ref[rows, :full] + skip * normed_ref[rows, :].astype(F32)
        cdf, density = gelu_parts(value)
        active_ref[rows, :] = (value * cdf).astype(LOW)
        slope_ref[rows, :] = (cdf + value * density).astype(slope_ref.dtype)
        return carry

    for piece in range(PIECES):
        for_rows(piece * total // PIECES, (piece + 1) * total // PIECES, 16, inner, unroll=4)
        if after is not None:
            after(piece)


def pre_grad_phase(grad_gated_ref, w_ref, slope_ref, normed_ref, quarter, pre_grad_ref, held_ref, small_ref):
    total, full = normed_ref.shape
    own = lanes_at(quarter, 128)
    held_ref[:, :full] = dot(grad_gated_ref[...], w_ref[...], NN)

    def inner(rows, index, carry):
        pre_grad_ref[rows, :] = (held_ref[rows, :full] * slope_ref[rows, :].astype(F32)).astype(LOW)
        return carry + folded(pre_grad_ref[rows, own].astype(F32) * normed_ref[rows, own].astype(F32))

    small_ref[3:4, 0:128] = column_sum(for_rows(0, total, 16, inner, jnp.zeros((8, 128), F32), unroll=4))


def adjoint_phase(pre_grad_ref, c_ref, low_ref, im_lane, drive_own_ref, state, first_row, length, grad_state_ref, grad_driven_ref, small_ref, reverse):
    total = pre_grad_ref.shape[0]
    steps = total // CHUNKS
    states = state.shape[1]
    grad_state_ref[...] = dot(pre_grad_ref[...], c_ref[...], NT)
    rate_re = state[first_row : first_row + 1, :]
    rate_im = state[first_row + 1 : first_row + 2, :]
    gamma = jnp.broadcast_to(state[first_row + 2 : first_row + 3, :], (CHUNKS, states))

    def emit(rows, step, re, im, drive_re, drive_im, held):
        out_re, out_im = gamma * re, gamma * im
        if not reverse:
            keep = keep_rows(step, CHUNKS, steps, length)
            out_re, out_im = jnp.where(keep, out_re, 0.0), jnp.where(keep, out_im, 0.0)
        grad_driven_ref[rows, :states] = out_re.astype(LOW)
        grad_driven_ref[rows, states:] = out_im.astype(LOW)
        one, two, three = held
        own_re, own_im = re[:, :128], im[:, :128]
        late_re, late_im = own_re - drive_re[:, :128], own_im - drive_im[:, :128]
        low_re = low_ref[rows, :128].astype(F32)
        low_im = low_ref[rows, im_lane : im_lane + 128].astype(F32)
        one = one + folded(late_re * low_re + late_im * low_im)
        two = two + folded(late_im * low_re - late_re * low_im)
        three = three + folded(
            own_re * drive_own_ref[rows, :128].astype(F32) + own_im * drive_own_ref[rows, 128:].astype(F32)
        )
        return one, two, three

    zero = jnp.zeros((8, 128), F32)
    one, two, three = sweep(grad_state_ref, rate_re, -rate_im, steps, reverse, emit, (zero, zero, zero))
    small_ref[0:1, 0:128] = column_sum(one)
    small_ref[1:2, 0:128] = column_sum(two)
    small_ref[2:3, 0:128] = column_sum(three)


def glu_grads(grads_ref, first, grad_gated_ref, active_ref, quarter):
    full = active_ref.shape[1]
    for place in range(2):
        lanes = pl.ds(pl.multiple_of(place * full + quarter * 128, 128), 128)
        got = dot(grad_gated_ref[:, lanes], active_ref[...], TN)
        grads_ref[first + place * 128 : first + (place + 1) * 128, :] = got.astype(LOW)


def state_grads(grads_ref, grad_driven_ref, normed_ref, low_re, low_im, pre_grad_ref, states):
    half = states // 4
    for place, low in enumerate((low_re, low_im)):
        lanes = slice(place * states, place * states + 128)
        got = dot(grad_driven_ref[:, lanes], normed_ref[...], TN)[:half, :]
        grads_ref[place * half : (place + 1) * half, :] = got.astype(LOW)
        got = dot(low, pre_grad_ref[...], TN)[:half, :]
        got = got if place == 0 else -got
        grads_ref[2 * half + place * half : 2 * half + (place + 1) * half, :] = got.astype(LOW)


def enter_kernel(length_ref, ins, outs, held_ref):
    x, b, c, w, gain, shift, skip, bias, nu, theta, gamma = ins
    tokens, spread, params, weights = outs
    length = length_ref[0]
    width, total = x.ref.shape
    steps = total // CHUNKS

    def emit(rows, index, value, carry):
        tokens.ref[rows, :] = value
        kept = jnp.where(keep_rows(index, CHUNKS, steps, length), value, 0.0)
        return carry[0] + folded(kept), carry[1] + folded(kept * kept)

    def after(piece):
        tokens.send_piece(piece)
        if piece == 1:
            b.wait()
            weights.send(0, width, source=b.ref.at[0])
            c.wait()
            weights.send(width, width, source=c.ref.at[0])
            w.wait()
            weights.send(2 * width, 2 * width, source=w.ref.at[0])

    zero = jnp.zeros((8, width), F32)
    plain, square = from_feature_rows(x, held_ref, steps, emit, (zero, zero), after)
    counted = jnp.full((1, width), length, jnp.int32).astype(F32)
    spread_rows(jnp.concatenate([column_sum(plain), column_sum(square), counted, jnp.zeros((5, width), F32)], axis=0), spread)
    for value in (gain, shift, skip, bias, nu, theta, gamma):
        value.wait()
    params.ref[...] = jnp.zeros((PARAM_ROWS, width), F32)
    for layer in range(LAYERS):
        first = 5 * layer
        params.ref[first + GAIN : first + GAIN + 1, :] = gain.ref[layer : layer + 1, :]
        params.ref[first + SHIFT : first + SHIFT + 1, :] = shift.ref[layer : layer + 1, :]
        params.ref[first + SKIP : first + SKIP + 1, :] = skip.ref[layer : layer + 1, :]
        params.ref[first + BIAS_LINEAR : first + BIAS_GATE + 1, :] = bias.ref[layer, :, :]
        first = 10 + 3 * layer
        for row, source in enumerate((nu, theta, gamma)):
            params.ref[first + row : first + row + 1, : source.ref.shape[1]] = source.ref[layer : layer + 1, :]


def cotangent_kernel(length_ref, ins, outs, held_ref):
    x, b, c, w = ins
    whole, later = outs
    width, total = x.ref.shape
    steps = total // CHUNKS
    each = steps // PIECES

    def emit(rows, index, value, carry):
        whole.ref[rows, :] = value
        place = pl.ds(pl.multiple_of(4 * width + index % each * CHUNKS, CHUNKS), CHUNKS)
        later.ref[place, lanes_at(index // each, width)] = value.astype(LOW)
        return carry

    def after(piece):
        whole.send_piece(piece)
        if piece == 1:
            b.wait()
            later.send(0, width, source=b.ref.at[1])
            c.wait()
            later.send(width, width, source=c.ref.at[1])
            w.wait()
            later.send(2 * width, 2 * width, source=w.ref.at[1])

    from_feature_rows(x, held_ref, steps, emit, 0, after)
    later.send(4 * width, total // PIECES)


def normal_kernel(length_ref, ins, outs, held_ref, stats_ref):
    sums, own_tokens = ins[:2]
    params, raws = ins[2:6], ins[6:]
    normed, stream, feature, state_out, norm = outs
    length, quarter = length_ref[0], own_quarter()
    total = normed.ref.shape[0]
    steps = total // CHUNKS
    width = own_tokens.ref.shape[1]
    lane = lax.broadcasted_iota(jnp.int32, (8, width), 1)
    tails = [part.wait() for part in params]
    for place, value in enumerate(tails):
        feature.ref[:, lanes_at(quarter ^ place, width)] = value[...]
    for pair in range(2):
        early, late = (value[8:16, :] for value in tails[2 * pair : 2 * pair + 2])
        logs = jnp.where(lane < 64, early, pltpu.roll(late, 64, 1))
        lanes = slice(pair * width, (pair + 1) * width)
        for layer in range(LAYERS):
            first = 2 + 3 * layer
            modulus = jnp.exp(-jnp.exp(logs[first : first + 1, :]))
            angle = jnp.exp(logs[first + 1 : first + 2, :])
            state_out.ref[first : first + 1, lanes] = modulus * jnp.cos(angle)
            state_out.ref[first + 1 : first + 2, lanes] = modulus * jnp.sin(angle)
            state_out.ref[first + 2 : first + 3, lanes] = jnp.exp(logs[first + 2 : first + 3, :])
    sums_ref = sums.wait()
    for place in range(4):
        value = sums_ref[place, :, :]
        for other in range(1, sums_ref.shape[0] // 4):
            value += sums_ref[other * 4 + place, :, :]
        stats_ref[:, place * width : (place + 1) * width] = value
    centre, inv_dev = norm_rows(stats_ref[0:2, :], stats_ref[2:3, :])
    norm.ref[...] = jnp.zeros_like(norm.ref)
    norm.ref[0:1, :] = centre
    norm.ref[1:2, :] = inv_dev
    norm.ref[2:3, :] = stats_ref[2:3, :]
    for out in (feature, state_out, norm):
        out.send()

    def normalized(place):
        lanes = lanes_at(quarter ^ place, width)

        def emit(rows, index, value, carry):
            stream.ref[rows, lanes] = value
            z = (value - norm.ref[0:1, lanes]) * norm.ref[1:2, lanes]
            z = z * feature.ref[GAIN : GAIN + 1, lanes] + feature.ref[SHIFT : SHIFT + 1, lanes]
            normed.ref[rows, lanes] = jnp.where(keep_rows(index, CHUNKS, steps, length), z, 0.0).astype(LOW)
            return carry

        return emit

    first = normalized(0)
    own_tokens.wait()
    for_rows(0, total, CHUNKS, lambda rows, index, carry: first(rows, index, own_tokens.ref[rows, :], carry), unroll=4)

    def after(piece):
        stream.send_piece(piece)
        normed.send_piece(piece)

    for place, raw in enumerate(raws, 1):
        from_feature_rows(raw, held_ref, steps, normalized(place), 0, after if place == 3 else lambda piece: None)


def start_kernel(length_ref, ins, outs, drive_ref, held_ref, b_ref, c_ref, w_ref, low_ref):
    feature_in, state_in, normed = ins[:3]
    weights, stream0 = ins[3:7], ins[7]
    drive_own, low_own, stream, linear_out, gate_out, slope, active, b_out, c_out, w_out, spread = outs
    length, quarter = length_ref[0], own_quarter()
    total, full = active.ref.shape
    steps = total // CHUNKS
    width = full // 4
    feature, state = feature_in.wait(), state_in.wait()[...]
    states = state.shape[1]
    normed.wait()
    for part in weights:
        part.wait()
    assemble_states([part.ref.at[0:width] for part in weights], b_ref)
    drive_phase(normed.ref, b_ref, drive_ref, state[2 + GAMMA : 3 + GAMMA, :])
    assemble_output([part.ref.at[width : 2 * width] for part in weights], c_ref)
    assemble_glu([part.ref.at[2 * width : 4 * width] for part in weights], w_ref, quarter)
    for out, source in ((b_out, b_ref), (c_out, c_ref), (w_out, w_ref)):
        out.send(source=source)
    store = store_states(low_ref, drive_own.ref)

    def emit(rows, step, re, im, drive_re, drive_im, held):
        low_own.ref[rows, :128] = re[:, :128].astype(LOW)
        low_own.ref[rows, 128:] = im[:, :128].astype(LOW)
        return store(rows, step, re, im, drive_re, drive_im, held)

    sweep(drive_ref, state[2:3, :], state[3:4, :], steps, False, emit, 0)
    drive_own.send()
    low_own.send()

    def after(piece):
        active.send_piece(piece)
        slope.send_piece(piece)

    pre_phase(low_ref, c_ref, normed.ref, feature[SKIP : SKIP + 1, :], active.ref, slope.ref, held_ref, after)
    held_ref[...] = dot(active.ref[...], w_ref[...], NT)

    def inner(rows, index, carry):
        keep = keep_rows(index, 16, steps, length)
        linear = held_ref[rows, :full] + feature[BIAS_LINEAR : BIAS_LINEAR + 1, :]
        gate = jax.nn.sigmoid(held_ref[rows, full:] + feature[BIAS_GATE : BIAS_GATE + 1, :])
        mixed = linear * gate
        gate_out.ref[rows, :] = gate.astype(LOW)
        linear_out.ref[rows, :] = (mixed * (1.0 - gate)).astype(LOW)
        moved = stream0.ref[rows, :] + jnp.where(keep, mixed, 0.0)
        stream.ref[rows, :] = moved
        kept = jnp.where(keep, moved, 0.0)
        return carry[0] + folded(kept), carry[1] + folded(kept * kept)

    zero = jnp.zeros((8, full), F32)
    carry = (zero, zero)
    for piece in range(PIECES):
        stream0.wait(piece)
        carry = for_rows(piece * total // PIECES, (piece + 1) * total // PIECES, 16, inner, carry)
        for out in (stream, linear_out, gate_out):
            out.send_piece(piece)
    spread_rows(narrowed([column_sum(carry[0]), column_sum(carry[1])], width), spread)


def middle_kernel(
    length_ref, ins, outs,
    small_ref, b_ref, c_ref, w_ref, normed_ref, drive_ref, drive_own_ref, low_ref, slope_ref, active_ref, held_ref,
    order_ref, up_ref, grad_gated_ref, pre_grad_ref, grad_driven_ref, grads_ref,
):
    sums, norm0, feature_in, state_in, stream, up_own = ins[:6]
    weights = ins[6:]
    result, base, spread, norm, *shares = outs
    length, quarter = length_ref[0], own_quarter()
    total, full = stream.ref.shape
    steps = total // CHUNKS
    width = 128
    counted = norm0.wait()[2:3, :]
    feature = feature_in.wait()
    state = state_in.wait()[...]
    states = state.shape[1]
    whole = total_rows(sums.wait())
    whole = jnp.concatenate([widened(whole, 0, 4), widened(whole, 4, 4)], axis=0)
    centre, inv_dev = norm_rows(whole, counted)
    norm.ref[...] = jnp.zeros_like(norm.ref)
    norm.ref[0:1, :] = centre
    norm.ref[1:2, :] = inv_dev
    norm.ref[2:3, :] = counted
    norm.send()
    gain = feature[5 + GAIN : 6 + GAIN, :]
    shift = feature[5 + SHIFT : 6 + SHIFT, :]
    skip = feature[5 + SKIP : 6 + SKIP, :]

    def normal(rows, index, carry):
        keep = keep_rows(index, 16, steps, length)
        z = (stream.ref[rows, :] - centre) * inv_dev
        normed_ref[rows, :] = jnp.where(keep, z * gain + shift, 0.0).astype(LOW)
        return carry

    for piece in range(PIECES):
        stream.wait(piece)
        for_rows(piece * total // PIECES, (piece + 1) * total // PIECES, 16, normal, unroll=4)
    for part in weights:
        part.wait()
    assemble_states([part.ref.at[0:width] for part in weights], b_ref)
    assemble_output([part.ref.at[width : 2 * width] for part in weights], c_ref)
    assemble_glu([part.ref.at[2 * width : 4 * width] for part in weights], w_ref, quarter)
    drive_phase(normed_ref, b_ref, drive_ref, state[5 + GAMMA : 6 + GAMMA, :])
    sweep(drive_ref, state[5:6, :], state[6:7, :], steps, True, store_states(low_ref, drive_own_ref), 0)
    pre_phase(low_ref, c_ref, normed_ref, skip, active_ref, slope_ref, held_ref)
    held_ref[...] = dot(active_ref[...], w_ref[...], NT)
    up_own.wait()
    own, own_far = lanes_at(quarter, width), lanes_at(quarter + 4, width)

    def spread_up(rows, index, carry):
        up_ref[rows, own] = up_own.ref[rows, :]
        return carry

    for_rows(0, total, 16, spread_up, unroll=4)
    for piece in range(PIECES):
        for place, part in enumerate(weights[1:], 1):
            lanes = lanes_at(quarter ^ place, width)
            size = total // PIECES
            up_ref[piece * size : (piece + 1) * size, lanes] = part.ref[4 * width :, piece * width : (piece + 1) * width].astype(F32)

    def inner(rows, index, carry):
        keep = keep_rows(index, 16, steps, length)
        linear = held_ref[rows, :full] + feature[5 + BIAS_LINEAR : 6 + BIAS_LINEAR, :]
        gate = jax.nn.sigmoid(held_ref[rows, full:] + feature[5 + BIAS_GATE : 6 + BIAS_GATE, :])
        mixed = linear * gate
        up = jnp.where(keep, up_ref[rows, :], 0.0)
        grad_gated_ref[rows, :full] = (up * gate).astype(LOW)
        grad_gated_ref[rows, full:] = (up * mixed * (1.0 - gate)).astype(LOW)
        held_ref[rows, :full] = jnp.where(keep, mixed, 0.0)
        return (
            carry[0] + folded(grad_gated_ref[rows, own].astype(F32)),
            carry[1] + folded(grad_gated_ref[rows, own_far].astype(F32)),
        )

    zero = jnp.zeros((8, width), F32)
    one, two = for_rows(0, total, 16, inner, (zero, zero))
    small_ref[...] = jnp.zeros_like(small_ref)
    small_ref[4:5, 0:128] = column_sum(one)
    small_ref[5:6, 0:128] = column_sum(two)
    to_feature_rows(lambda rows, index: stream.ref[rows, own] + held_ref[rows, own], order_ref, result, steps)
    pre_grad_phase(grad_gated_ref, w_ref, slope_ref, normed_ref, quarter, pre_grad_ref, held_ref, small_ref)
    adjoint_phase(
        pre_grad_ref, c_ref, low_ref, states, drive_own_ref, state, 5, length, drive_ref, grad_driven_ref, small_ref, False
    )
    held_ref[:, :full] = dot(grad_driven_ref[...], b_ref[...], NN)
    scale = inv_dev * gain

    def back(rows, index, carry):
        grad = held_ref[rows, :full] + skip * pre_grad_ref[rows, :].astype(F32)
        z = (stream.ref[rows, :] - centre) * inv_dev
        base.ref[rows, :] = scale * grad + up_ref[rows, :]
        return carry[0] + folded(grad), carry[1] + folded(grad * z)

    zero = jnp.zeros((8, full), F32)
    carry = (zero, zero)
    for piece in range(PIECES):
        carry = for_rows(piece * total // PIECES, (piece + 1) * total // PIECES, 16, back, carry)
        base.send_piece(piece)
    sent = narrowed([column_sum(carry[0]), column_sum(carry[1])], width)
    spread_rows(jnp.concatenate([sent, small_ref[:, 0:width]], axis=0), spread)
    glu_grads(grads_ref, 2 * width, grad_gated_ref, active_ref, quarter)
    state_grads(grads_ref, grad_driven_ref, normed_ref, low_ref[:, 0:128], low_ref[:, states : states + 128], pre_grad_ref, states)
    share = grads_ref.shape[0] // len(shares)
    for place, out in enumerate(shares):
        out.send(source=grads_ref.at[rows_at(lax.axis_index("dp") ^ place, share)])


def last_kernel(
    length_ref, ins, outs, held_ref, grad_state_ref, grad_gated_ref, pre_grad_ref, grad_driven_ref, small_ref, row_ref, grads_ref, pack_ref
):
    (sums, norm1, feature_in, state_in, norm0, stream, base, gate, linear, w, slope, normed, active, c, low, drive_own, b, x) = ins
    send, up_out, grad_out = outs
    length, quarter = length_ref[0], own_quarter()
    total, full = stream.ref.shape
    steps = total // CHUNKS
    width = 128
    own = lanes_at(quarter, width)
    feature, norm_ref = feature_in.wait(), norm1.wait()
    state = state_in.wait()[...]
    counted = norm_ref[2:3, :]
    whole = total_rows(sums.wait())
    whole = jnp.concatenate([widened(whole, 0, 4), widened(whole, 4, 4)], axis=0)
    centre, inv_dev = norm_ref[0:1, :], norm_ref[1:2, :]
    scale = inv_dev * feature[5 + GAIN : 6 + GAIN, :]
    level = scale * whole[0:1, :] / counted
    tilt = scale * inv_dev * whole[1:2, :] / counted

    def top(rows, index, carry):
        keep = keep_rows(index, 16, steps, length)
        up = base.ref[rows, :] - jnp.where(keep, level + (stream.ref[rows, :] - centre) * tilt, 0.0)
        row_ref[...] = up
        up_out.ref[rows, :] = row_ref[:, own]
        up = jnp.where(keep, up, 0.0)
        grad_gated_ref[rows, :full] = (up * gate.ref[rows, :].astype(F32)).astype(LOW)
        grad_gated_ref[rows, full:] = (up * linear.ref[rows, :].astype(F32)).astype(LOW)
        far = pl.ds(pl.multiple_of(full + quarter * width, width), width)
        return (
            carry[0] + folded(grad_gated_ref[rows, own].astype(F32)),
            carry[1] + folded(grad_gated_ref[rows, far].astype(F32)),
        )

    zero = jnp.zeros((8, width), F32)
    carry = (zero, zero)
    for piece in range(PIECES):
        for value in (stream, base, gate, linear):
            value.wait(piece)
        carry = for_rows(piece * total // PIECES, (piece + 1) * total // PIECES, 16, top, carry)
        up_out.send_piece(piece)
    small_ref[...] = jnp.zeros_like(small_ref)
    small_ref[4:5, 0:128] = column_sum(carry[0])
    small_ref[5:6, 0:128] = column_sum(carry[1])
    for value in (w, slope, normed):
        value.wait()
    pre_grad_phase(grad_gated_ref, w.ref, slope.ref, normed.ref, quarter, pre_grad_ref, held_ref, small_ref)
    for value in (active, c, low, drive_own):
        value.wait()
    glu_grads(grads_ref, 2 * width, grad_gated_ref, active.ref, quarter)
    adjoint_phase(
        pre_grad_ref, c.ref, low.ref, 128, drive_own.ref, state, 2, length, grad_state_ref, grad_driven_ref, small_ref, True
    )
    b.wait()
    x.wait()
    held_ref[:, :width] = dot(grad_driven_ref[...], b.ref[:, own], NN)
    centre0, inv_dev0 = norm0.wait()[0:1, own], norm0.ref[1:2, own]
    skip = feature[SKIP : SKIP + 1, own]

    def back(rows, index, carry):
        grad = held_ref[rows, :width] + skip * pre_grad_ref[rows, own].astype(F32)
        grad_out.ref[rows, :] = grad
        z = (x.ref[rows, :] - centre0) * inv_dev0
        return carry[0] + folded(grad), carry[1] + folded(grad * z)

    plain, scaled = for_rows(0, total, 16, back, (zero, zero), unroll=4)
    grad_out.send()
    small_ref[6:7, 0:width] = column_sum(plain)
    small_ref[7:8, 0:width] = column_sum(scaled)
    state_grads(grads_ref, grad_driven_ref, normed.ref, low.ref[:, :128], low.ref[:, 128:], pre_grad_ref, state.shape[1])
    pack_ref[...] = jnp.zeros_like(pack_ref)
    for place in range(8):
        pack_ref[place // 4 : place // 4 + 1, place % 4 * width : (place % 4 + 1) * width] = small_ref[place : place + 1, 0:width]
    exact = pack_ref[0:8, :]
    pack_ref[8:16, :] = exact - exact.astype(LOW).astype(F32)
    groups = send.ref.shape[0]
    share = send.ref.shape[1] - 16
    for group in range(groups):
        send.ref[group, :share, :] = grads_ref[group * share : (group + 1) * share, :]
        send.ref[group, share:, :] = pack_ref[...].astype(LOW)


def sum_shares(got, out, share):
    groups = got.ref.shape[0]
    for piece in range(0, share, 16):
        value = got.ref[0, piece : piece + 16, :].astype(F32)
        for group in range(1, groups):
            value += got.ref[group, piece : piece + 16, :].astype(F32)
        value = value.astype(LOW)
        for group in range(groups):
            out.ref[group, piece : piece + 16, :] = value


def add_kernel(length_ref, ins, outs):
    (out,) = outs
    for value in ins:
        value.wait()
    for piece in range(0, out.ref.shape[0], 16):
        at = slice(piece, piece + 16)
        total = ins[0].ref[at, :].astype(F32)
        for value in ins[1:]:
            total += value.ref[at, :].astype(F32)
        out.ref[at, :] = total.astype(LOW)


def share_kernel(length_ref, ins, outs):
    (got,) = ins
    out, small = outs
    got.wait()
    groups, share = got.ref.shape[0], got.ref.shape[1] - 16
    sum_shares(got, out, share)
    value = got.ref[0, share:, :].astype(F32)
    for group in range(1, groups):
        value += got.ref[group, share:, :].astype(F32)
    small.ref[...] = value[0:8, :] + value[8:16, :]


def finish_kernel(length_ref, ins, outs, held_ref, order_ref):
    small0, bn1, norm0, feature, nu, theta, up, grad, x = ins
    nu_out, theta_out, gamma_out, skip_out, bias_out, gain_out, shift_out, out = outs
    length, quarter = length_ref[0], own_quarter()
    total, width = up.ref.shape
    steps = total // CHUNKS
    own = lanes_at(quarter, width)
    states = nu_out.ref.shape[1]
    for value in ins:
        value.wait()
    whole = total_rows(bn1.ref)
    held_ref[0:1, :] = widened(whole, 0, 4)
    held_ref[1:2, :] = widened(whole, 4, 4)
    held_ref[16:32, :width] = whole
    for place in range(8):
        held_ref[8 + place : 9 + place, :width] = small0.ref[place // 4 : place // 4 + 1, place % 4 * width : (place % 4 + 1) * width]
    for layer, first in ((0, 8), (1, 24)):
        at = slice(layer, layer + 1)
        nu_out.ref[at, :] = -jnp.exp(nu.ref[at, :]) * held_ref[first : first + 1, :states]
        theta_out.ref[at, :] = jnp.exp(theta.ref[at, :]) * held_ref[first + 1 : first + 2, :states]
        gamma_out.ref[at, :] = held_ref[first + 2 : first + 3, :states]
        skip_out.ref[at, :] = held_ref[first + 3 : first + 4, :width]
        bias_out.ref[layer, 0:1, :] = held_ref[first + 4 : first + 5, :width]
        bias_out.ref[layer, 1:2, :] = held_ref[first + 5 : first + 6, :width]
    shift_out.ref[0:1, :] = held_ref[14:15, :width]
    gain_out.ref[0:1, :] = held_ref[15:16, :width]
    shift_out.ref[1:2, :] = held_ref[0:1, own]
    gain_out.ref[1:2, :] = held_ref[1:2, own]
    counted = norm0.ref[2:3, own]
    centre, inv_dev = norm0.ref[0:1, own], norm0.ref[1:2, own]
    level = held_ref[14:15, :width] / counted
    tilt = held_ref[15:16, :width] * inv_dev / counted
    scale = inv_dev * feature.ref[GAIN : GAIN + 1, own]

    def load(rows, index):
        keep = keep_rows(index, CHUNKS, steps, length)
        inner = grad.ref[rows, :] - level - (x.ref[rows, :] - centre) * tilt
        return up.ref[rows, :] + jnp.where(keep, scale * inner, 0.0)

    to_feature_rows(load, order_ref, out, steps)


def widen_kernel(length_ref, ins, outs, held_ref):
    b, c, w = outs
    half = b.ref.shape[1]
    grads0, *shares = ins
    share = shares[0].ref.shape[0]
    for place, value in enumerate(shares):
        held_ref[rows_at(lax.axis_index("dp") ^ place, share), :] = value.wait()[...]
    for layer, source_ref in ((1, held_ref), (0, grads0.ref)):
        if layer == 0:
            grads0.wait()
        for out, first, size in ((b, 0, half), (c, half, half), (w, 2 * half, 2 * half)):
            out.ref[layer, :, :] = source_ref[first : first + size, :].astype(F32)
            out.send(layer, 1)


def shape(*dims, dtype=F32):
    return jax.ShapeDtypeStruct(dims, dtype)


def swap(value, bit, sharers):
    pairs = [(q * sharers + r, (q ^ bit) * sharers + r) for q in range(4) for r in range(sharers)]
    return lax.ppermute(value, "state", pairs)


def across(value, axes):
    return lax.all_to_all(value, axes, 0, 0, tiled=True)


def local(
    inputs, lengths, cotangent, bn_gain, bn_bias, b_weight, c_weight, nu_log, theta_log, gamma_log, skip_weight,
    glu_weight, glu_bias, dp_size, state_size,
):
    sharers = state_size // 4
    place = lax.axis_index("state").astype(jnp.int32)

    def joined(value, axis):
        if sharers == 1:
            return value
        groups = [[q * sharers + r for r in range(sharers)] for q in range(4)]
        return lax.all_gather(value, "state", axis=axis, axis_index_groups=groups, tiled=True)

    def own(value, axis):
        if sharers == 1:
            return value
        size = value.shape[axis] // sharers
        return lax.dynamic_slice_in_dim(value, place % sharers * size, size, axis)

    inputs, cotangent = joined(inputs, 1), joined(cotangent, 1)
    bn_gain, bn_bias, skip_weight = joined(bn_gain, 1), joined(bn_bias, 1), joined(skip_weight, 1)
    nu_log, theta_log, gamma_log = joined(nu_log, 1), joined(theta_log, 1), joined(gamma_log, 1)
    b_weight, c_weight = joined(b_weight, 2), joined(c_weight, 2)
    glu_weight, glu_bias = joined(glu_weight, 2), joined(glu_bias, 2)
    width, total = inputs.shape[1:]
    full = b_weight.shape[3]
    states = b_weight.shape[2] * 4
    own_states = b_weight.shape[2]
    share = 4 * width // dp_size
    piece = total // PIECES

    def exchange(value, bit):
        return lax.ppermute(value, "dp", [(i, i ^ bit) for i in range(dp_size)])


    b_weight, c_weight = b_weight.reshape(LAYERS, width, full), c_weight.reshape(LAYERS, width, full)
    glu_weight = glu_weight.reshape(LAYERS, 2 * width, full)
    raw = inputs[0]
    raw_near, raw_far = swap(raw, 1, sharers), swap(raw, 2, sharers)
    tokens, sums, params, weights0 = call(
        enter_kernel,
        (
            shape(total, width),
            shape(dp_size * state_size, 8, width),
            shape(PARAM_ROWS, width),
            shape(4 * width, full, dtype=LOW),
        ),
        [pltpu.VMEM((total, width), F32)],
        (lengths, raw, b_weight, c_weight, glu_weight, bn_gain, bn_bias, skip_weight, glu_bias, nu_log, theta_log, gamma_log),
        "enter",
        pieces={1: piece},
        axes={1: 1},
        bare=(3,),
        flops=ENTER_FLOPS,
    )
    params_near, params_far = swap(params, 1, sharers), swap(params, 2, sharers)
    near0, far0 = swap(weights0, 1, sharers), swap(weights0, 2, sharers)
    sums = across(sums, ("dp", "state"))
    if sharers > 1:
        sums = sums.reshape(dp_size * 4, sharers, 8, width)[:, 0]
    cotangent, tokens = lax.optimization_barrier((cotangent, tokens))
    up_own, later = call(
        cotangent_kernel,
        (shape(total, width), shape(6 * width, full, dtype=LOW)),
        [pltpu.VMEM((total, width), F32)],
        (lengths, cotangent[0], b_weight, c_weight, glu_weight),
        "cotangent",
        pieces={1: piece},
        axes={1: 1},
    )
    raw_far, params_far, sums = lax.optimization_barrier((raw_far, params_far, sums))
    normed0, stream0, feature, state, norm0 = call(
        normal_kernel,
        (shape(total, full, dtype=LOW), shape(total, full), shape(PARAM_ROWS, full), shape(8, states), shape(8, full)),
        [pltpu.VMEM((total, width), F32), pltpu.VMEM((8, full), F32)],
        (lengths, sums, tokens, params, params_near, params_far, swap(params_far, 1, sharers),
         raw_near, raw_far, swap(raw_far, 1, sharers)),
        "normal",
        pieces={7: piece, 8: piece, 9: piece},
        axes={7: 1, 8: 1, 9: 1},
    )
    far0, normed0, later = lax.optimization_barrier((far0, normed0, later))
    later_far = swap(later, 2, sharers)
    drive0, low0, stream1, linear0, gate0, slope0, active0, b_all, c_all, w_all, sums1 = call(
        start_kernel,
        (
            shape(total, 256),
            shape(total, 256, dtype=LOW),
            shape(total, full),
            shape(total, full, dtype=LOW),
            shape(total, full, dtype=LOW),
            shape(total, full, dtype=LOW),
            shape(total, full, dtype=LOW),
            shape(2 * states, full, dtype=LOW),
            shape(2 * states, full, dtype=LOW),
            shape(2 * full, full, dtype=LOW),
            shape(dp_size, 8, width),
        ),
        [
            pltpu.VMEM((total, 2 * states), F32),
            pltpu.VMEM((total, 2 * full), F32),
            pltpu.VMEM((2 * states, full), LOW),
            pltpu.VMEM((2 * states, full), LOW),
            pltpu.VMEM((2 * full, full), LOW),
            pltpu.VMEM((total, 2 * states), LOW),
        ],
        (lengths, feature, state, normed0, weights0, near0, far0, swap(far0, 1, sharers), stream0),
        "start",
        pieces={8: piece},
        bare=(7, 8, 9),
    )
    sums1 = across(sums1, "dp")
    later_far, sums1 = lax.optimization_barrier((later_far, sums1))
    result, base, bn1, norm1, *shares1 = call(
        middle_kernel,
        (
            shape(width, total),
            shape(total, full),
            shape(dp_size, 16, width),
            shape(8, full),
            *(shape(share, full, dtype=LOW) for _ in range(dp_size)),
        ),
        [
            pltpu.VMEM((8, full), F32),
            pltpu.VMEM((2 * states, full), LOW),
            pltpu.VMEM((2 * states, full), LOW),
            pltpu.VMEM((2 * full, full), LOW),
            pltpu.VMEM((total, full), LOW),
            pltpu.VMEM((total, 2 * states), F32),
            pltpu.VMEM((total, 256), F32),
            pltpu.VMEM((total, 2 * states), LOW),
            pltpu.VMEM((total, full), F32),
            pltpu.VMEM((total, full), LOW),
            pltpu.VMEM((total, 2 * full), F32),
            pltpu.VMEM((total, width), F32),
            pltpu.VMEM((total, full), F32),
            pltpu.VMEM((total, 2 * full), LOW),
            pltpu.VMEM((total, full), LOW),
            pltpu.VMEM((total, 2 * states), LOW),
            pltpu.VMEM((4 * width, full), LOW),
        ],
        (lengths, sums1, norm0, feature, state, stream1, up_own, later, swap(later, 1, sharers), later_far,
         swap(later_far, 1, sharers)),
        "middle",
        pieces={5: piece},
        bare=tuple(range(4, 4 + dp_size)),
    )
    bn1 = across(bn1, "dp")
    shares1 = [shares1[0]] + [exchange(shares1[bit], bit) for bit in range(1, dp_size)]
    send, up0, grad0 = call(
        last_kernel,
        (shape(dp_size, share + 16, full, dtype=LOW), shape(total, width), shape(total, width)),
        [
            pltpu.VMEM((total, full), F32),
            pltpu.VMEM((total, 2 * states), F32),
            pltpu.VMEM((total, 2 * full), LOW),
            pltpu.VMEM((total, full), LOW),
            pltpu.VMEM((total, 2 * states), LOW),
            pltpu.VMEM((8, full), F32),
            pltpu.VMEM((16, full), F32),
            pltpu.VMEM((4 * width, full), LOW),
            pltpu.VMEM((16, full), F32),
        ],
        (lengths, bn1, norm1, feature, state, norm0, stream1, base, gate0, linear0, w_all, slope0, normed0, active0, c_all, low0,
         drive0, b_all, tokens),
        "last",
        pieces={6: piece, 7: piece, 8: piece, 9: piece},
    )
    *shares1, send = lax.optimization_barrier((*shares1, send))
    (share1,) = call(add_kernel, (shape(share, full, dtype=LOW),), [], (lengths, *shares1), "add")
    shares1 = [share1] + [exchange(share1, bit) for bit in range(1, dp_size)]
    got = across(send, "dp")
    *shares1, got = lax.optimization_barrier((*shares1, got))
    back, small0 = call(
        share_kernel,
        (shape(dp_size, share, full, dtype=LOW), shape(8, full)),
        [],
        (lengths, got),
        "share",
    )
    grad_nu, grad_theta, grad_gamma, grad_skip, grad_bias, grad_gain, grad_shift, grad_inputs = call(
        finish_kernel,
        (
            shape(LAYERS, own_states),
            shape(LAYERS, own_states),
            shape(LAYERS, own_states),
            shape(LAYERS, width),
            shape(LAYERS, 2, width),
            shape(LAYERS, width),
            shape(LAYERS, width),
            shape(width, total),
        ),
        [pltpu.VMEM((32, full), F32), pltpu.VMEM((total, width), F32)],
        (lengths, small0, bn1, norm0, feature, nu_log, theta_log, up0, grad0, tokens),
        "finish",
    )
    grads0 = across(back, "dp").reshape(4 * width, full)
    grad_b, grad_c, grad_glu = call(
        widen_kernel,
        (shape(LAYERS, width, full), shape(LAYERS, width, full), shape(LAYERS, 2 * width, full)),
        [pltpu.VMEM((4 * width, full), LOW)],
        (lengths, grads0, *shares1),
        "widen",
    )
    grad_b = grad_b.reshape(LAYERS, 2, own_states, full)
    grad_c = grad_c.reshape(LAYERS, 2, own_states, full)
    grad_glu = grad_glu.reshape(LAYERS, 2, width, full)
    return (
        own(result[None], 1),
        own(grad_inputs[None], 1),
        own(grad_gain, 1),
        own(grad_shift, 1),
        own(grad_b, 2),
        own(grad_c, 2),
        own(grad_nu, 1),
        own(grad_theta, 1),
        own(grad_gamma, 1),
        own(grad_skip, 1),
        own(grad_glu, 2),
        own(grad_bias, 2),
    )


def solution(mesh):
    in_specs = (
        P("dp", "state", None),
        P("dp"),
        P("dp", "state", None),
        P(None, "state"),
        P(None, "state"),
        P(None, None, "state", None),
        P(None, None, "state", None),
        P(None, "state"),
        P(None, "state"),
        P(None, "state"),
        P(None, "state"),
        P(None, None, "state", None),
        P(None, None, "state"),
    )
    out_specs = (
        P("dp", "state", None),
        P("dp", "state", None),
        P(None, "state"),
        P(None, "state"),
        P(None, None, "state", None),
        P(None, None, "state", None),
        P(None, "state"),
        P(None, "state"),
        P(None, "state"),
        P(None, "state"),
        P(None, None, "state", None),
        P(None, None, "state"),
    )
    step = functools.partial(local, dp_size=mesh.shape["dp"], state_size=mesh.shape["state"])
    return jax.shard_map(step, mesh=mesh, in_specs=in_specs, out_specs=out_specs, check_vma=False)
```

time: 906 us -> 163 us (0.18); the launches traced: 890 us -> 162 us
  local copies, waits for them, and re-layouts: 314 us -> 0 us
  waiting for transfers between devices: 267 us -> 37.3 us
  other arithmetic: 155 us -> 0 us
  blocking collectives: 105 us -> 0 us
  Pallas kernels: 0 us -> 67.3 us
  starting transfers between devices: 1.18 us -> 56.1 us
  matrix products: 28.8 us -> 0 us
  between operations: 18.9 us -> 1.67 us
    slice x288 -> x0, local copies, waits for them, and re-layouts: 150 us -> none  [the longest x284 140 us: sweep(): lax.associative_scan(combine, (power_re, power_im, real_part, imag_part),...]
    unnamed x19 -> x0, waiting for transfers between devices: 142 us -> none
    psum x5 -> x0, blocking collectives: 105 us -> none  [the longest x2 45.1 us: local(): lax.psum((jnp.sum(hidden_state * valid3, axis=(0, 2)), jnp.sum(hidden_sta...]
    add x161 -> x0, other arithmetic: 84.1 us -> none  [the longest x80 38.3 us: sweep(): lax.associative_scan(combine, (power_re, power_im, real_part, imag_part),...]
    unnamed x328 -> x0, local copies, waits for them, and re-layouts: 79.5 us -> none
    pallas_call x0 -> x10, Pallas kernels: none -> 67.3 us  [call(): pl.pallas_call(body, out_shape=tuple(outs), in_specs=[pl.BlockSpec(memory...]
    psum x1 -> x0, waiting for transfers between devices: 63.4 us -> none  [local(): lax.psum(grad_b_matrix.reshape(2, states_here, full_width).astype(jnp.bfl...]
    all_gather x6 -> x0, waiting for transfers between devices: 61.8 us -> none  [the longest x2 31.3 us: local(): active_mask = lax.all_gather(active_own, 'state', axis=1, tiled=True)]
  transfers between devices with their start and end apart: 13 -> 31, of which waited for: 12 -> 11; matrix products, arithmetic and copies ran while one was open for 6% -> 0% of each run, Pallas kernels for 0% -> 27%
where the time goes in v3:
time: 163 us; the launch traced here: 162 us
  Pallas kernels  67.3 us (41%)
  starting transfers between devices  56.1 us (34%)
  waiting for transfers between devices  37.3 us (23%)
  between operations  1.67 us (1%)
    pallas_call x10, Pallas kernels, call(): pl.pallas_call(body, out_shape=tuple(outs), in_specs=[pl.BlockSpec(memory...  67.3 us
    ppermute x14, starting transfers between devices, exchange(): return lax.ppermute(value, 'dp', [(i, i ^ bit) for i in range(dp_size)])  27.5 us
    all_to_all x5, starting transfers between devices, across(): return lax.all_to_all(value, axes, 0, 0, tiled=True)  21.6 us
    all_to_all x5, waiting for transfers between devices, across(): return lax.all_to_all(value, axes, 0, 0, tiled=True)  16.6 us
    ppermute x12, waiting for transfers between devices, swap(): return lax.ppermute(value, 'state', pairs)  11.9 us
    ppermute x14, waiting for transfers between devices, exchange(): return lax.ppermute(value, 'dp', [(i, i ^ bit) for i in range(dp_size)])  8.75 us
    ppermute x12, starting transfers between devices, swap(): return lax.ppermute(value, 'state', pairs)  7.01 us
  transfers between devices with their start and end apart: 31, of which 11 were waited for; matrix products, arithmetic and copies ran while one was open for 0% of the time, Pallas kernels for 27%

profile of v3, /device:TPU:0, one launch (start us, length us, event | category | flops | bytes accessed | tf_op | source)
XLA Modules:
  0.0 162.3 jit_solution(6323895402478583401)
XLA Ops:
  0.6 3.0 %collective-permute-start.1 = (f32[128,1024]{1,0:T(8,128)}, f32[128,1024]{1,0:T(8,128)}, u32[]{:S(2)}, u32[]{:S(2)}) collective-permute-start(f32[128,1024]{1,0:T(8,128)} %bitcast.19), channel_id=1, source_target_pairs={{0,2},{1,3},{2,0},{3,1},{4,6},{5,7},{6,4},{7,5},{8,10},{9,11},{10,... | collective-permute-start | bytes 1572872 | tf_op jit(solution)/shard_map/ppermute | solution.py:904
  4.3 3.8 %enter.1 = (f32[1024,128]{1,0:T(8,128)}, f32[32,8,128]{2,1,0:T(8,128)}, f32[16,128]{1,0:T(8,128)}, bf16[512,512]{1,0:T(8,128)(2,1)}) custom-call(s32[1]{0:T(128)S(6)} %copy.25.refs_0_, f32[128,1024]{1,0:T(8,128)} %bitcast.20, bf16[2,128,512]{2,1,0:T(8,128)(2,1)} %bitcast.14, bf16[2,128,512]{2,1,0:T(8,128)(2,1)} %bitcast.16, bf16[2,256,512]{2,1,0:T(8,128)(2,1)} %bitcast.11, ...), custom_call_target="tpu_custom_call" | custom-call | flops 10000000000 | tf_op jit(solution)/shard_map/enter/pallas_call | solution.py:228
  8.1 5.1 %all-to-all-start = ((f32[32,8,128]{2,1,0:T(8,128)}), f32[32,8,128]{2,1,0:T(8,128)}, u32[]{:S(2)}, u32[]{:S(2)}) async-start(f32[32,8,128]{2,1,0:T(8,128)} %get-tuple-element.92), calls=%async_computation | async-start | bytes 262144 | tf_op jit(solution)/shard_map/all_to_all | solution.py:908
  13.2 1.8 %collective-permute-start.2 = (f32[16,128]{1,0:T(8,128)}, f32[16,128]{1,0:T(8,128)}, u32[]{:S(2)}, u32[]{:S(2)}) collective-permute-start(f32[16,128]{1,0:T(8,128)} %get-tuple-element.91.refs_3_), channel_id=1, source_target_pairs={{0,2},{1,3},{2,0},{3,1},{4,6},{5,7},{6,4},{7,5},{8,10},{9,11},{10,... | collective-permute-start | bytes 24584 | tf_op jit(solution)/shard_map/ppermute | solution.py:904
  14.9 2.3 %collective-permute-done.2.refs_5_ = f32[16,128]{1,0:T(8,128)} collective-permute-done((f32[16,128]{1,0:T(8,128)}, f32[16,128]{1,0:T(8,128)}, u32[]{:S(2)}, u32[]{:S(2)}) %collective-permute-start.2) | collective-permute-done | bytes 8224 | tf_op jit(solution)/shard_map/ppermute | solution.py:904
  17.2 4.2 %all-to-all-done.refs_1_ = f32[32,8,128]{2,1,0:T(8,128)} async-done(((f32[32,8,128]{2,1,0:T(8,128)}), f32[32,8,128]{2,1,0:T(8,128)}, u32[]{:S(2)}, u32[]{:S(2)}) %all-to-all-start) | async-done | bytes 131104 | tf_op jit(solution)/shard_map/all_to_all | solution.py:908
  21.4 0.2 collective-permute-start.6
  21.6 0.4 collective-permute-start
  22.1 0.4 collective-permute-start.4
  22.5 3.1 %cotangent.1 = (f32[1024,128]{1,0:T(8,128)}, bf16[768,512]{1,0:T(8,128)(2,1)}) custom-call(s32[1]{0:T(128)S(6)} %copy.25.refs_0_, f32[128,1024]{1,0:T(8,128)} %bitcast.13, bf16[2,128,512]{2,1,0:T(8,128)(2,1)} %bitcast.15, bf16[2,128,512]{2,1,0:T(8,128)(2,1)} %bitcast.17, bf16[2,256,512]{2,1,0:T(8,128)(2,1)} %bitcast.12), custom_call_target="tpu_custom_call" | custom-call | tf_op jit(solution)/shard_map/cotangent/pallas_call | solution.py:228
  25.7 5.9 %normal.1 = (bf16[1024,512]{1,0:T(8,128)(2,1)}, f32[1024,512]{1,0:T(8,128)}, f32[16,512]{1,0:T(8,128)}, f32[8,256]{1,0:T(8,128)}, f32[8,512]{1,0:T(8,128)}) custom-call(s32[1]{0:T(128)S(6)} %copy.25.refs_0_, f32[32,8,128]{2,1,0:T(8,128)} %all-to-all-done.refs_1_, f32[1024,128]{1,0:T(8,128)} %get-tuple-element.95.refs_2_.refs_18_.refs_9_, ...), custom_call_target="tpu_custom_call" | custom-call | tf_op jit(solution)/shard_map/normal/pallas_call | solution.py:228
  31.6 4.5 %collective-permute-done.refs_6_ = bf16[512,512]{1,0:T(8,128)(2,1)} collective-permute-done((bf16[512,512]{1,0:T(8,128)(2,1)}, bf16[512,512]{1,0:T(8,128)(2,1)}, u32[]{:S(2)}, u32[]{:S(2)}) %collective-permute-start) | collective-permute-done | bytes 524320 | tf_op jit(solution)/shard_map/ppermute | solution.py:904
  36.0 0.4 collective-permute-start.7
  36.5 0.5 collective-permute-start.9
  37.0 1.7 %collective-permute-done.8.refs_5_ = bf16[512,512]{1,0:T(8,128)(2,1)} collective-permute-done((bf16[512,512]{1,0:T(8,128)(2,1)}, bf16[512,512]{1,0:T(8,128)(2,1)}, u32[]{:S(2)}, u32[]{:S(2)}) %collective-permute-start.8) | collective-permute-done | bytes 524320 | tf_op jit(solution)/shard_map/ppermute | solution.py:904
  38.7 0.7 collective-permute-done.9.refs_7_
  39.5 9.7 %start.1 = (f32[1024,256]{1,0:T(8,128)}, bf16[1024,256]{1,0:T(8,128)(2,1)}, f32[1024,512]{1,0:T(8,128)}, bf16[1024,512]{1,0:T(8,128)(2,1)}, bf16[1024,512]{1,0:T...) custom-call(s32[1]{0:T(128)S(6)} %copy.25.refs_0_, ...), custom_call_target="tpu_custom_call" | custom-call | tf_op jit(solution)/shard_map/start/pallas_call | solution.py:228
  49.2 4.2 %all-to-all-start.1 = ((f32[8,8,128]{2,1,0:T(8,128)}), f32[8,8,128]{2,1,0:T(8,128)}, u32[]{:S(2)}, u32[]{:S(2)}) async-start(f32[8,8,128]{2,1,0:T(8,128)} %get-tuple-element.107), calls=%async_computation.1 | async-start | bytes 65536 | tf_op jit(solution)/shard_map/all_to_all | solution.py:908
  53.4 0.2 collective-permute-start.10
  53.6 6.3 %all-to-all-done.1.refs_1_ = f32[8,8,128]{2,1,0:T(8,128)} async-done(((f32[8,8,128]{2,1,0:T(8,128)}), f32[8,8,128]{2,1,0:T(8,128)}, u32[]{:S(2)}, u32[]{:S(2)}) %all-to-all-start.1) | async-done | bytes 32800 | tf_op jit(solution)/shard_map/all_to_all | solution.py:908
  59.9 2.6 %collective-permute-done.11.refs_10_ = bf16[768,512]{1,0:T(8,128)(2,1)} collective-permute-done((bf16[768,512]{1,0:T(8,128)(2,1)}, bf16[768,512]{1,0:T(8,128)(2,1)}, u32[]{:S(2)}, u32[]{:S(2)}) %collective-permute-start.11) | collective-permute-done | bytes 786464 | tf_op jit(solution)/shard_map/ppermute | solution.py:904
  62.5 18.1 %middle.1 = (f32[128,1024]{1,0:T(8,128)}, f32[1024,512]{1,0:T(8,128)}, f32[8,16,128]{2,1,0:T(8,128)}, f32[8,512]{1,0:T(8,128)}, bf16[64,512]{1,0:T(8,128)(2,1)},...) custom-call(s32[1]{0:T(128)S(6)} %copy.25.refs_0_, ...), custom_call_target="tpu_custom_call" | custom-call | tf_op jit(solution)/shard_map/middle/pallas_call | solution.py:228
  80.6 0.5 collective-permute-start.12
  81.2 0.7 collective-permute-start.13
  81.9 4.0 %all-to-all-start.2 = ((f32[8,16,128]{2,1,0:T(8,128)}), f32[8,16,128]{2,1,0:T(8,128)}, u32[]{:S(2)}, u32[]{:S(2)}) async-start(f32[8,16,128]{2,1,0:T(8,128)} %get-tuple-element.122), calls=%async_computation.2 | async-start | bytes 131072 | tf_op jit(solution)/shard_map/all_to_all | solution.py:908
  85.8 2.8 %collective-permute-start.14 = (bf16[64,512]{1,0:T(8,128)(2,1)}, bf16[64,512]{1,0:T(8,128)(2,1)}, u32[]{:S(2)}, u32[]{:S(2)}) collective-permute-start(bf16[64,512]{1,0:T(8,128)(2,1)} %get-tuple-element.117), channel_id=1, source_target_pairs={{0,12},{4,8},{8,4},{12,0},{16,28},{20,24},{24,20},{28,16},{1,13},{... | collective-permute-start | bytes 196616 | tf_op jit(solution)/shard_map/ppermute | solution.py:943
  88.7 2.4 %collective-permute-start.15 = (bf16[64,512]{1,0:T(8,128)(2,1)}, bf16[64,512]{1,0:T(8,128)(2,1)}, u32[]{:S(2)}, u32[]{:S(2)}) collective-permute-start(bf16[64,512]{1,0:T(8,128)(2,1)} %get-tuple-element.118), channel_id=1, source_target_pairs={{0,16},{4,20},{8,24},{12,28},{16,0},{20,4},{24,8},{28,12},{1,17},{... | collective-permute-start | bytes 196616 | tf_op jit(solution)/shard_map/ppermute | solution.py:943
  91.0 0.5 collective-permute-start.16
  91.6 2.4 %collective-permute-start.17 = (bf16[64,512]{1,0:T(8,128)(2,1)}, bf16[64,512]{1,0:T(8,128)(2,1)}, u32[]{:S(2)}, u32[]{:S(2)}) collective-permute-start(bf16[64,512]{1,0:T(8,128)(2,1)} %get-tuple-element.120), channel_id=1, source_target_pairs={{0,24},{4,28},{8,16},{12,20},{16,8},{20,12},{24,0},{28,4},{1,25},{... | collective-permute-start | bytes 196616 | tf_op jit(solution)/shard_map/ppermute | solution.py:943
  94.0 2.4 %collective-permute-start.18 = (bf16[64,512]{1,0:T(8,128)(2,1)}, bf16[64,512]{1,0:T(8,128)(2,1)}, u32[]{:S(2)}, u32[]{:S(2)}) collective-permute-start(bf16[64,512]{1,0:T(8,128)(2,1)} %get-tuple-element.121), channel_id=1, source_target_pairs={{0,28},{4,24},{8,20},{12,16},{16,12},{20,8},{24,4},{28,0},{1,29},{... | collective-permute-start | bytes 196616 | tf_op jit(solution)/shard_map/ppermute | solution.py:943
  96.3 12.5 %last.1 = (bf16[8,80,512]{2,1,0:T(8,128)(2,1)}, f32[1024,128]{1,0:T(8,128)}, f32[1024,128]{1,0:T(8,128)}) custom-call(s32[1]{0:T(128)S(6)} %copy.25.refs_0_, f32[8,16,128]{2,1,0:T(8,128)} %all-to-all-done.2.refs_1_.refs_2_, f32[8,512]{1,0:T(8,128)} %get-tuple-element.123.refs_2_, f32[16,512]{1,0:T(8,128)} %get-tuple-element.102.refs_1_.refs_3_.refs_4_, ...), custom_call_target="tpu_custom_call" | custom-call | tf_op jit(solution)/shard_map/last/pallas_call | solution.py:228
  108.9 4.2 %all-to-all-start.3 = ((bf16[8,80,512]{2,1,0:T(8,128)(2,1)}), bf16[8,80,512]{2,1,0:T(8,128)(2,1)}, u32[]{:S(2)}, u32[]{:S(2)}) async-start(bf16[8,80,512]{2,1,0:T(8,128)(2,1)} %get-tuple-element.143), calls=%async_computation.3 | async-start | bytes 1310720 | tf_op jit(solution)/shard_map/all_to_all | solution.py:908
  113.1 1.9 %add.1.refs_2_ = bf16[64,512]{1,0:T(8,128)(2,1)} custom-call(s32[1]{0:T(128)S(6)} %copy.25.refs_0_, bf16[64,512]{1,0:T(8,128)(2,1)} %get-tuple-element.135.refs_1_, bf16[64,512]{1,0:T(8,128)(2,1)} %collective-permute-done.12.refs_2_, bf16[64,512]{1,0:T(8,128)(2,1)} %collective-permute-done.13.refs_3_, bf16[64,512]{1,0:T(8,128)(2,1)} %collective-permute-done.14.refs_4_, ...), custom_call_target="tpu_custom_call" | custom-call | tf_op jit(solution)/shard_map/add/pallas_call | solution.py:228
  115.0 2.0 %collective-permute-start.19 = (bf16[64,512]{1,0:T(8,128)(2,1)}, bf16[64,512]{1,0:T(8,128)(2,1)}, u32[]{:S(2)}, u32[]{:S(2)}) collective-permute-start(bf16[64,512]{1,0:T(8,128)(2,1)} %add.1.refs_2_), channel_id=1, source_target_pairs={{0,4},{4,0},{8,12},{12,8},{16,20},{20,16},{24,28},{28,24},{1,5},{5... | collective-permute-start | bytes 196616 | tf_op jit(solution)/shard_map/ppermute | solution.py:943
  116.9 1.5 collective-permute-start.20
  118.4 0.1 collective-permute-start.21
  118.5 2.8 %collective-permute-start.22 = (bf16[64,512]{1,0:T(8,128)(2,1)}, bf16[64,512]{1,0:T(8,128)(2,1)}, u32[]{:S(2)}, u32[]{:S(2)}) collective-permute-start(bf16[64,512]{1,0:T(8,128)(2,1)} %add.1.refs_2_), channel_id=1, source_target_pairs={{0,16},{4,20},{8,24},{12,28},{16,0},{20,4},{24,8},{28,12},{1,17},{... | collective-permute-start | bytes 196616 | tf_op jit(solution)/shard_map/ppermute | solution.py:943
  121.4 1.4 collective-permute-start.23
  122.8 3.3 %collective-permute-start.24 = (bf16[64,512]{1,0:T(8,128)(2,1)}, bf16[64,512]{1,0:T(8,128)(2,1)}, u32[]{:S(2)}, u32[]{:S(2)}) collective-permute-start(bf16[64,512]{1,0:T(8,128)(2,1)} %add.1.refs_2_), channel_id=1, source_target_pairs={{0,24},{4,28},{8,16},{12,20},{16,8},{20,12},{24,0},{28,4},{1,25},{... | collective-permute-start | bytes 196616 | tf_op jit(solution)/shard_map/ppermute | solution.py:943
  126.1 0.4 collective-permute-done.20.refs_4_
  126.5 4.7 %collective-permute-start.25 = (bf16[64,512]{1,0:T(8,128)(2,1)}, bf16[64,512]{1,0:T(8,128)(2,1)}, u32[]{:S(2)}, u32[]{:S(2)}) collective-permute-start(bf16[64,512]{1,0:T(8,128)(2,1)} %add.1.refs_2_), channel_id=1, source_target_pairs={{0,28},{4,24},{8,20},{12,16},{16,12},{20,8},{24,4},{28,0},{1,29},{... | collective-permute-start | bytes 196616 | tf_op jit(solution)/shard_map/ppermute | solution.py:943
  131.2 6.7 %collective-permute-done.22.refs_6_ = bf16[64,512]{1,0:T(8,128)(2,1)} collective-permute-done((bf16[64,512]{1,0:T(8,128)(2,1)}, bf16[64,512]{1,0:T(8,128)(2,1)}, u32[]{:S(2)}, u32[]{:S(2)}) %collective-permute-start.22) | collective-permute-done | bytes 65568 | tf_op jit(solution)/shard_map/ppermute | solution.py:943
  137.9 1.6 collective-permute-done.23.refs_7_
  139.6 2.7 %share.1 = (bf16[8,64,512]{2,1,0:T(8,128)(2,1)}, f32[8,512]{1,0:T(8,128)}) custom-call(s32[1]{0:T(128)S(6)} %copy.25.refs_0_, bf16[8,80,512]{2,1,0:T(8,128)(2,1)} %all-to-all-done.3.refs_1_), custom_call_target="tpu_custom_call" | custom-call | tf_op jit(solution)/shard_map/share/pallas_call | solution.py:228
  142.2 4.2 %all-to-all-start.4 = ((bf16[8,64,512]{2,1,0:T(8,128)(2,1)}), bf16[8,64,512]{2,1,0:T(8,128)(2,1)}, u32[]{:S(2)}, u32[]{:S(2)}) async-start(bf16[8,64,512]{2,1,0:T(8,128)(2,1)} %get-tuple-element.151), calls=%async_computation.4 | async-start | bytes 1048576 | tf_op jit(solution)/shard_map/all_to_all | solution.py:908
  146.4 6.9 %finish.1 = (f32[2,64]{1,0:T(2,128)}, f32[2,64]{1,0:T(2,128)}, f32[2,64]{1,0:T(2,128)}, f32[2,128]{1,0:T(2,128)}, f32[2,2,128]{2,1,0:T(2,128)}, /*index=5*/f32[2...) custom-call(s32[1]{0:T(128)S(6)} %copy.25.refs_0_, f32[8,512]{1,0:T(8,128)} %get-tuple-element.145.refs_1_, ...), custom_call_target="tpu_custom_call" | custom-call | tf_op jit(solution)/shard_map/finish/pallas_call | solution.py:228
  153.3 6.1 %all-to-all-done.4 = bf16[8,64,512]{2,1,0:T(8,128)(2,1)} async-done(((bf16[8,64,512]{2,1,0:T(8,128)(2,1)}), bf16[8,64,512]{2,1,0:T(8,128)(2,1)}, u32[]{:S(2)}, u32[]{:S(2)}) %all-to-all-start.4) | async-done | bytes 524320 | tf_op jit(solution)/shard_map/all_to_all | solution.py:908
  159.4 2.7 %widen.1 = (f32[2,128,512]{2,1,0:T(8,128)}, f32[2,128,512]{2,1,0:T(8,128)}, f32[2,256,512]{2,1,0:T(8,128)}) custom-call(s32[1]{0:T(128)S(6)} %copy.25.refs_0_, bf16[512,512]{1,0:T(8,128)(2,1)} %bitcast.7.refs_1_, bf16[64,512]{1,0:T(8,128)(2,1)} %add.1.refs_2_, bf16[64,512]{1,0:T(8,128)(2,1)} %collective-permute-done.19.refs_3_, ...), custom_call_target="tpu_custom_call" | custom-call | tf_op jit(solution)/shard_map/widen/pallas_call | solution.py:228
  (24 shorter events, 0.1 us)
Async XLA Ops:
  0.6 20.7 %collective-permute-start.1 = (f32[128,1024]{1,0:T(8,128)}, f32[128,1024]{1,0:T(8,128)}, u32[]{:S(2)}, u32[]{:S(2)}) collective-permute-start(f32[128,1024]{1,0:T(8,128)} %bitcast.19), channel_id=1, source_target_pairs={{0,2},{1,3},{2,0},{3,1},{4,6},{5,7},{6,4},{7,5},{8,10},{9,11},{10,... | collective-permute-start | bytes 1572872 | tf_op jit(solution)/shard_map/ppermute | solution.py:904
  8.1 13.3 %all-to-all-start = ((f32[32,8,128]{2,1,0:T(8,128)}), f32[32,8,128]{2,1,0:T(8,128)}, u32[]{:S(2)}, u32[]{:S(2)}) async-start(f32[32,8,128]{2,1,0:T(8,128)} %get-tuple-element.92), calls=%async_computation | async-start | bytes 262144 | tf_op jit(solution)/shard_map/all_to_all | solution.py:908
  13.2 4.0 %collective-permute-start.2 = (f32[16,128]{1,0:T(8,128)}, f32[16,128]{1,0:T(8,128)}, u32[]{:S(2)}, u32[]{:S(2)}) collective-permute-start(f32[16,128]{1,0:T(8,128)} %get-tuple-element.91.refs_3_), channel_id=1, source_target_pairs={{0,2},{1,3},{2,0},{3,1},{4,6},{5,7},{6,4},{7,5},{8,10},{9,11},{10,... | collective-permute-start | bytes 24584 | tf_op jit(solution)/shard_map/ppermute | solution.py:904
  14.9 10.7 %collective-permute-start.5 = (f32[128,1024]{1,0:T(8,128)}, f32[128,1024]{1,0:T(8,128)}, u32[]{:S(2)}, u32[]{:S(2)}) collective-permute-start(f32[128,1024]{1,0:T(8,128)} %bitcast.21), channel_id=1, source_target_pairs={{0,1},{1,0},{2,3},{3,2},{4,5},{5,4},{6,7},{7,6},{8,9},{9,8},{10,11... | collective-permute-start | bytes 1572872 | tf_op jit(solution)/shard_map/ppermute | solution.py:904
  21.4 4.3 %collective-permute-start.6 = (f32[128,1024]{1,0:T(8,128)}, f32[128,1024]{1,0:T(8,128)}, u32[]{:S(2)}, u32[]{:S(2)}) collective-permute-start(f32[128,1024]{1,0:T(8,128)} %collective-permute-done.1.refs_8_), channel_id=1, source_target_pairs={{0,1},{1,0},{2,3},{3,2},{4,5},{5,4},{6,7},{7,6},{8,9},{9,8},{10,11... | collective-permute-start | bytes 1572872 | tf_op jit(solution)/shard_map/ppermute | solution.py:904
  21.6 14.4 %collective-permute-start = (bf16[512,512]{1,0:T(8,128)(2,1)}, bf16[512,512]{1,0:T(8,128)(2,1)}, u32[]{:S(2)}, u32[]{:S(2)}) collective-permute-start(bf16[512,512]{1,0:T(8,128)(2,1)} %get-tuple-element.90.refs_4_), channel_id=1, source_target_pairs={{0,2},{1,3},{2,0},{3,1},{4,6},{5,7},{6,4},{7,5},{8,10},{9,11},{10,... | collective-permute-start | bytes 1572872 | tf_op jit(solution)/shard_map/ppermute | solution.py:904
  22.0 3.7 %collective-permute-start.3 = (f32[16,128]{1,0:T(8,128)}, f32[16,128]{1,0:T(8,128)}, u32[]{:S(2)}, u32[]{:S(2)}) collective-permute-start(f32[16,128]{1,0:T(8,128)} %get-tuple-element.91.refs_3_), channel_id=1, source_target_pairs={{0,1},{1,0},{2,3},{3,2},{4,5},{5,4},{6,7},{7,6},{8,9},{9,8},{10,11... | collective-permute-start | bytes 24584 | tf_op jit(solution)/shard_map/ppermute | solution.py:904
  22.1 3.6 %collective-permute-start.4 = (f32[16,128]{1,0:T(8,128)}, f32[16,128]{1,0:T(8,128)}, u32[]{:S(2)}, u32[]{:S(2)}) collective-permute-start(f32[16,128]{1,0:T(8,128)} %collective-permute-done.2.refs_5_), channel_id=1, source_target_pairs={{0,1},{1,0},{2,3},{3,2},{4,5},{5,4},{6,7},{7,6},{8,9},{9,8},{10,11... | collective-permute-start | bytes 24584 | tf_op jit(solution)/shard_map/ppermute | solution.py:904
  36.0 23.8 %collective-permute-start.7 = (bf16[768,512]{1,0:T(8,128)(2,1)}, bf16[768,512]{1,0:T(8,128)(2,1)}, u32[]{:S(2)}, u32[]{:S(2)}) collective-permute-start(bf16[768,512]{1,0:T(8,128)(2,1)} %get-tuple-element.101.refs_7_), channel_id=1, source_target_pairs={{0,2},{1,3},{2,0},{3,1},{4,6},{5,7},{6,4},{7,5},{8,10},{9,11},{10,... | collective-permute-start | bytes 2359304 | tf_op jit(solution)/shard_map/ppermute | solution.py:904
  36.5 2.3 %collective-permute-start.8 = (bf16[512,512]{1,0:T(8,128)(2,1)}, bf16[512,512]{1,0:T(8,128)(2,1)}, u32[]{:S(2)}, u32[]{:S(2)}) collective-permute-start(bf16[512,512]{1,0:T(8,128)(2,1)} %get-tuple-element.90.refs_4_), channel_id=1, source_target_pairs={{0,1},{1,0},{2,3},{3,2},{4,5},{5,4},{6,7},{7,6},{8,9},{9,8},{10,11... | collective-permute-start | bytes 1572872 | tf_op jit(solution)/shard_map/ppermute | solution.py:904
  36.5 3.0 %collective-permute-start.9 = (bf16[512,512]{1,0:T(8,128)(2,1)}, bf16[512,512]{1,0:T(8,128)(2,1)}, u32[]{:S(2)}, u32[]{:S(2)}) collective-permute-start(bf16[512,512]{1,0:T(8,128)(2,1)} %collective-permute-done.refs_6_), channel_id=1, source_target_pairs={{0,1},{1,0},{2,3},{3,2},{4,5},{5,4},{6,7},{7,6},{8,9},{9,8},{10,11... | collective-permute-start | bytes 1572872 | tf_op jit(solution)/shard_map/ppermute | solution.py:904
  49.2 10.7 %all-to-all-start.1 = ((f32[8,8,128]{2,1,0:T(8,128)}), f32[8,8,128]{2,1,0:T(8,128)}, u32[]{:S(2)}, u32[]{:S(2)}) async-start(f32[8,8,128]{2,1,0:T(8,128)} %get-tuple-element.107), calls=%async_computation.1 | async-start | bytes 65536 | tf_op jit(solution)/shard_map/all_to_all | solution.py:908
  53.4 6.5 %collective-permute-start.10 = (bf16[768,512]{1,0:T(8,128)(2,1)}, bf16[768,512]{1,0:T(8,128)(2,1)}, u32[]{:S(2)}, u32[]{:S(2)}) collective-permute-start(bf16[768,512]{1,0:T(8,128)(2,1)} %get-tuple-element.101.refs_7_), channel_id=1, source_target_pairs={{0,1},{1,0},{2,3},{3,2},{4,5},{5,4},{6,7},{7,6},{8,9},{9,8},{10,11... | collective-permute-start | bytes 2359304 | tf_op jit(solution)/shard_map/ppermute | solution.py:904
  59.9 2.6 %collective-permute-start.11 = (bf16[768,512]{1,0:T(8,128)(2,1)}, bf16[768,512]{1,0:T(8,128)(2,1)}, u32[]{:S(2)}, u32[]{:S(2)}) collective-permute-start(bf16[768,512]{1,0:T(8,128)(2,1)} %collective-permute-done.7.refs_9_), channel_id=1, source_target_pairs={{0,1},{1,0},{2,3},{3,2},{4,5},{5,4},{6,7},{7,6},{8,9},{9,8},{10,11... | collective-permute-start | bytes 2359304 | tf_op jit(solution)/shard_map/ppermute | solution.py:904
  80.6 10.9 %collective-permute-start.12 = (bf16[64,512]{1,0:T(8,128)(2,1)}, bf16[64,512]{1,0:T(8,128)(2,1)}, u32[]{:S(2)}, u32[]{:S(2)}) collective-permute-start(bf16[64,512]{1,0:T(8,128)(2,1)} %get-tuple-element.115), channel_id=1, source_target_pairs={{0,4},{4,0},{8,12},{12,8},{16,20},{20,16},{24,28},{28,24},{1,5},{5... | collective-permute-start | bytes 196616 | tf_op jit(solution)/shard_map/ppermute | solution.py:943
  81.2 12.8 %collective-permute-start.13 = (bf16[64,512]{1,0:T(8,128)(2,1)}, bf16[64,512]{1,0:T(8,128)(2,1)}, u32[]{:S(2)}, u32[]{:S(2)}) collective-permute-start(bf16[64,512]{1,0:T(8,128)(2,1)} %get-tuple-element.116), channel_id=1, source_target_pairs={{0,8},{4,12},{8,0},{12,4},{16,24},{20,28},{24,16},{28,20},{1,9},{5... | collective-permute-start | bytes 196616 | tf_op jit(solution)/shard_map/ppermute | solution.py:943
  81.9 14.4 %all-to-all-start.2 = ((f32[8,16,128]{2,1,0:T(8,128)}), f32[8,16,128]{2,1,0:T(8,128)}, u32[]{:S(2)}, u32[]{:S(2)}) async-start(f32[8,16,128]{2,1,0:T(8,128)} %get-tuple-element.122), calls=%async_computation.2 | async-start | bytes 131072 | tf_op jit(solution)/shard_map/all_to_all | solution.py:908
  85.8 23.0 %collective-permute-start.14 = (bf16[64,512]{1,0:T(8,128)(2,1)}, bf16[64,512]{1,0:T(8,128)(2,1)}, u32[]{:S(2)}, u32[]{:S(2)}) collective-permute-start(bf16[64,512]{1,0:T(8,128)(2,1)} %get-tuple-element.117), channel_id=1, source_target_pairs={{0,12},{4,8},{8,4},{12,0},{16,28},{20,24},{24,20},{28,16},{1,13},{... | collective-permute-start | bytes 196616 | tf_op jit(solution)/shard_map/ppermute | solution.py:943
  88.7 20.2 %collective-permute-start.15 = (bf16[64,512]{1,0:T(8,128)(2,1)}, bf16[64,512]{1,0:T(8,128)(2,1)}, u32[]{:S(2)}, u32[]{:S(2)}) collective-permute-start(bf16[64,512]{1,0:T(8,128)(2,1)} %get-tuple-element.118), channel_id=1, source_target_pairs={{0,16},{4,20},{8,24},{12,28},{16,0},{20,4},{24,8},{28,12},{1,17},{... | collective-permute-start | bytes 196616 | tf_op jit(solution)/shard_map/ppermute | solution.py:943
  91.0 17.8 %collective-permute-start.16 = (bf16[64,512]{1,0:T(8,128)(2,1)}, bf16[64,512]{1,0:T(8,128)(2,1)}, u32[]{:S(2)}, u32[]{:S(2)}) collective-permute-start(bf16[64,512]{1,0:T(8,128)(2,1)} %get-tuple-element.119), channel_id=1, source_target_pairs={{0,20},{4,16},{8,28},{12,24},{16,4},{20,0},{24,12},{28,8},{1,21},{... | collective-permute-start | bytes 196616 | tf_op jit(solution)/shard_map/ppermute | solution.py:943
  91.6 17.3 %collective-permute-start.17 = (bf16[64,512]{1,0:T(8,128)(2,1)}, bf16[64,512]{1,0:T(8,128)(2,1)}, u32[]{:S(2)}, u32[]{:S(2)}) collective-permute-start(bf16[64,512]{1,0:T(8,128)(2,1)} %get-tuple-element.120), channel_id=1, source_target_pairs={{0,24},{4,28},{8,16},{12,20},{16,8},{20,12},{24,0},{28,4},{1,25},{... | collective-permute-start | bytes 196616 | tf_op jit(solution)/shard_map/ppermute | solution.py:943
  94.0 14.9 %collective-permute-start.18 = (bf16[64,512]{1,0:T(8,128)(2,1)}, bf16[64,512]{1,0:T(8,128)(2,1)}, u32[]{:S(2)}, u32[]{:S(2)}) collective-permute-start(bf16[64,512]{1,0:T(8,128)(2,1)} %get-tuple-element.121), channel_id=1, source_target_pairs={{0,28},{4,24},{8,20},{12,16},{16,12},{20,8},{24,4},{28,0},{1,29},{... | collective-permute-start | bytes 196616 | tf_op jit(solution)/shard_map/ppermute | solution.py:943
  108.9 30.7 %all-to-all-start.3 = ((bf16[8,80,512]{2,1,0:T(8,128)(2,1)}), bf16[8,80,512]{2,1,0:T(8,128)(2,1)}, u32[]{:S(2)}, u32[]{:S(2)}) async-start(bf16[8,80,512]{2,1,0:T(8,128)(2,1)} %get-tuple-element.143), calls=%async_computation.3 | async-start | bytes 1310720 | tf_op jit(solution)/shard_map/all_to_all | solution.py:908
  115.0 7.8 %collective-permute-start.19 = (bf16[64,512]{1,0:T(8,128)(2,1)}, bf16[64,512]{1,0:T(8,128)(2,1)}, u32[]{:S(2)}, u32[]{:S(2)}) collective-permute-start(bf16[64,512]{1,0:T(8,128)(2,1)} %add.1.refs_2_), channel_id=1, source_target_pairs={{0,4},{4,0},{8,12},{12,8},{16,20},{20,16},{24,28},{28,24},{1,5},{5... | collective-permute-start | bytes 196616 | tf_op jit(solution)/shard_map/ppermute | solution.py:943
  116.9 9.5 %collective-permute-start.20 = (bf16[64,512]{1,0:T(8,128)(2,1)}, bf16[64,512]{1,0:T(8,128)(2,1)}, u32[]{:S(2)}, u32[]{:S(2)}) collective-permute-start(bf16[64,512]{1,0:T(8,128)(2,1)} %add.1.refs_2_), channel_id=1, source_target_pairs={{0,8},{4,12},{8,0},{12,4},{16,24},{20,28},{24,16},{28,20},{1,9},{5... | collective-permute-start | bytes 196616 | tf_op jit(solution)/shard_map/ppermute | solution.py:943
  118.4 12.8 %collective-permute-start.21 = (bf16[64,512]{1,0:T(8,128)(2,1)}, bf16[64,512]{1,0:T(8,128)(2,1)}, u32[]{:S(2)}, u32[]{:S(2)}) collective-permute-start(bf16[64,512]{1,0:T(8,128)(2,1)} %add.1.refs_2_), channel_id=1, source_target_pairs={{0,12},{4,8},{8,4},{12,0},{16,28},{20,24},{24,20},{28,16},{1,13},{... | collective-permute-start | bytes 196616 | tf_op jit(solution)/shard_map/ppermute | solution.py:943
  118.5 19.4 %collective-permute-start.22 = (bf16[64,512]{1,0:T(8,128)(2,1)}, bf16[64,512]{1,0:T(8,128)(2,1)}, u32[]{:S(2)}, u32[]{:S(2)}) collective-permute-start(bf16[64,512]{1,0:T(8,128)(2,1)} %add.1.refs_2_), channel_id=1, source_target_pairs={{0,16},{4,20},{8,24},{12,28},{16,0},{20,4},{24,8},{28,12},{1,17},{... | collective-permute-start | bytes 196616 | tf_op jit(solution)/shard_map/ppermute | solution.py:943
  121.4 18.2 %collective-permute-start.23 = (bf16[64,512]{1,0:T(8,128)(2,1)}, bf16[64,512]{1,0:T(8,128)(2,1)}, u32[]{:S(2)}, u32[]{:S(2)}) collective-permute-start(bf16[64,512]{1,0:T(8,128)(2,1)} %add.1.refs_2_), channel_id=1, source_target_pairs={{0,20},{4,16},{8,28},{12,24},{16,4},{20,0},{24,12},{28,8},{1,21},{... | collective-permute-start | bytes 196616 | tf_op jit(solution)/shard_map/ppermute | solution.py:943
  122.8 16.8 %collective-permute-start.24 = (bf16[64,512]{1,0:T(8,128)(2,1)}, bf16[64,512]{1,0:T(8,128)(2,1)}, u32[]{:S(2)}, u32[]{:S(2)}) collective-permute-start(bf16[64,512]{1,0:T(8,128)(2,1)} %add.1.refs_2_), channel_id=1, source_target_pairs={{0,24},{4,28},{8,16},{12,20},{16,8},{20,12},{24,0},{28,4},{1,25},{... | collective-permute-start | bytes 196616 | tf_op jit(solution)/shard_map/ppermute | solution.py:943
  126.5 13.1 %collective-permute-start.25 = (bf16[64,512]{1,0:T(8,128)(2,1)}, bf16[64,512]{1,0:T(8,128)(2,1)}, u32[]{:S(2)}, u32[]{:S(2)}) collective-permute-start(bf16[64,512]{1,0:T(8,128)(2,1)} %add.1.refs_2_), channel_id=1, source_target_pairs={{0,28},{4,24},{8,20},{12,16},{16,12},{20,8},{24,4},{28,0},{1,29},{... | collective-permute-start | bytes 196616 | tf_op jit(solution)/shard_map/ppermute | solution.py:943
  142.2 17.2 %all-to-all-start.4 = ((bf16[8,64,512]{2,1,0:T(8,128)(2,1)}), bf16[8,64,512]{2,1,0:T(8,128)(2,1)}, u32[]{:S(2)}, u32[]{:S(2)}) async-start(bf16[8,64,512]{2,1,0:T(8,128)(2,1)} %get-tuple-element.151), calls=%async_computation.4 | async-start | bytes 1048576 | tf_op jit(solution)/shard_map/all_to_all | solution.py:908

commit v4 on v3

--- a/solution.py
+++ b/solution.py
@@ -13,9 +13,9 @@
 EPSILON = 1e-05
 F32 = jnp.float32
 LOW = jnp.bfloat16
-PARAM_ROWS = 16
+PARAM_ROWS = 24
+OWN_MEAN = 16
 VMEM_BYTES = 64 * 1024 * 1024
-ENTER_FLOPS = 1e10
 
 GAIN, SHIFT, SKIP, BIAS_LINEAR, BIAS_GATE = range(5)
 RATE_RE, RATE_IM, GAMMA = range(3)
@@ -180,14 +180,16 @@
         size = self.target.shape[0] // PIECES
         self.send(piece * size, size)
 
-    def finish(self):
+    def send_unsent(self):
         if not self.copies:
             self.send()
+
+    def finish(self):
         for copy in self.copies:
             copy.wait()
 
 
-def call(kernel, outs, scratch, args, name, pieces=None, axes=None, bare=(), flops=0):
+def call(kernel, outs, scratch, args, name, pieces=None, axes=None, bare=(), late=(), order=None, flops=0):
     pieces, axes = pieces or {}, axes or {}
     along = [axes.get(place, 0) for place in range(1, len(args))]
     sizes = [pieces.get(place, args[place].shape[axis]) for place, axis in enumerate(along, 1)]
@@ -213,15 +215,19 @@
         for source, ref, size, count, axis in zip(sources, in_refs, sizes, counts, along):
             arrivals.append(Arrival(source, ref, arrived, first, size, axis))
             first += count
-        for piece in range(-1, max(counts)):
-            for arrival in arrivals:
-                arrival.start(piece)
+        for group in (False, True):
+            for piece in (-1, *(order or ()), *(piece for piece in range(max(counts)) if piece not in (order or ()))):
+                for place, arrival in enumerate(arrivals, 1):
+                    if (place in late) is group:
+                        arrival.start(piece)
         departures = [
             Departure(target, ref, sent, place * slots) for place, (target, ref) in enumerate(zip(targets, out_refs))
         ]
         kernel(length_ref, arrivals, departures, *refs)
         for arrival in arrivals:
             arrival.wait()
+        for departure in departures:
+            departure.send_unsent()
         for departure in departures:
             departure.finish()
 
@@ -428,8 +434,8 @@
 
 
 def enter_kernel(length_ref, ins, outs, held_ref):
-    x, b, c, w, gain, shift, skip, bias, nu, theta, gamma = ins
-    tokens, spread, params, weights = outs
+    x, gain, shift, skip, bias, nu, theta, gamma, b, c, w = ins
+    tokens, spread, params, first_out = outs
     length = length_ref[0]
     width, total = x.ref.shape
     steps = total // CHUNKS
@@ -439,20 +445,22 @@
         kept = jnp.where(keep_rows(index, CHUNKS, steps, length), value, 0.0)
         return carry[0] + folded(kept), carry[1] + folded(kept * kept)
 
-    def after(piece):
-        tokens.send_piece(piece)
-        if piece == 1:
-            b.wait()
-            weights.send(0, width, source=b.ref.at[0])
-            c.wait()
-            weights.send(width, width, source=c.ref.at[0])
-            w.wait()
-            weights.send(2 * width, 2 * width, source=w.ref.at[0])
-
     zero = jnp.zeros((8, width), F32)
-    plain, square = from_feature_rows(x, held_ref, steps, emit, (zero, zero), after)
+    plain, square = from_feature_rows(x, held_ref, steps, emit, (zero, zero), tokens.send_piece)
+    plain = column_sum(plain)
     counted = jnp.full((1, width), length, jnp.int32).astype(F32)
-    spread_rows(jnp.concatenate([column_sum(plain), column_sum(square), counted, jnp.zeros((5, width), F32)], axis=0), spread)
+    spread_rows(jnp.concatenate([plain, column_sum(square), counted, jnp.zeros((5, width), F32)], axis=0), spread)
+    mean = plain / counted
+
+    each = total // PIECES
+
+    def centred(rows, index, carry):
+        place = pl.ds(pl.multiple_of(4 * width + index * 32 % each, 32), 32)
+        first_out.ref[place, lanes_at(index * 32 // each, width)] = (tokens.ref[rows, :] - mean).astype(LOW)
+        return carry
+
+    for_rows(0, total, 32, centred, unroll=4)
+    first_out.send(4 * width, each)
     for value in (gain, shift, skip, bias, nu, theta, gamma):
         value.wait()
     params.ref[...] = jnp.zeros((PARAM_ROWS, width), F32)
@@ -465,6 +473,14 @@
         first = 10 + 3 * layer
         for row, source in enumerate((nu, theta, gamma)):
             params.ref[first + row : first + row + 1, : source.ref.shape[1]] = source.ref[layer : layer + 1, :]
+    params.ref[OWN_MEAN : OWN_MEAN + 1, :] = mean
+    params.send()
+    b.wait()
+    first_out.send(0, width, source=b.ref.at[0])
+    c.wait()
+    first_out.send(width, width, source=c.ref.at[0])
+    w.wait()
+    first_out.send(2 * width, 2 * width, source=w.ref.at[0])
 
 
 def cotangent_kernel(length_ref, ins, outs, held_ref):
@@ -494,14 +510,14 @@
     later.send(4 * width, total // PIECES)
 
 
-def normal_kernel(length_ref, ins, outs, held_ref, stats_ref):
-    sums, own_tokens = ins[:2]
-    params, raws = ins[2:6], ins[6:]
-    normed, stream, feature, state_out, norm = outs
+def start_kernel(length_ref, ins, outs, stats_ref, stream_ref, drive_ref, held_ref, b_ref, c_ref, w_ref, low_ref):
+    sums, params, tokens = ins[0], ins[1:5], ins[5]
+    weights = ins[6:10]
+    feature, state_out, norm, normed, drive_own, low_own, stream, linear_out, gate_out, slope, active, b_out, c_out, w_out, spread = outs
     length, quarter = length_ref[0], own_quarter()
-    total = normed.ref.shape[0]
+    total, full = active.ref.shape
     steps = total // CHUNKS
-    width = own_tokens.ref.shape[1]
+    width = full // 4
     lane = lax.broadcasted_iota(jnp.int32, (8, width), 1)
     tails = [part.wait() for part in params]
     for place, value in enumerate(tails):
@@ -531,49 +547,42 @@
     for out in (feature, state_out, norm):
         out.send()
 
-    def normalized(place):
-        lanes = lanes_at(quarter ^ place, width)
-
-        def emit(rows, index, value, carry):
-            stream.ref[rows, lanes] = value
+    each = total // PIECES
+
+    def normal(rows, index, carry):
+        keep = keep_rows(index, 16, steps, length)
+        there = pl.ds(pl.multiple_of(4 * width + index * 16 % each, 16), 16)
+        for place, part in enumerate(weights):
+            lanes = lanes_at(quarter ^ place, width)
+            if place == 0:
+                value = tokens.ref[rows, :]
+            else:
+                value = part.ref[there, lanes_at(index * 16 // each, width)].astype(F32)
+                value = value + feature.ref[OWN_MEAN : OWN_MEAN + 1, lanes]
+            stream_ref[rows, lanes] = value
             z = (value - norm.ref[0:1, lanes]) * norm.ref[1:2, lanes]
             z = z * feature.ref[GAIN : GAIN + 1, lanes] + feature.ref[SHIFT : SHIFT + 1, lanes]
-            normed.ref[rows, lanes] = jnp.where(keep_rows(index, CHUNKS, steps, length), z, 0.0).astype(LOW)
-            return carry
-
-        return emit
-
-    first = normalized(0)
-    own_tokens.wait()
-    for_rows(0, total, CHUNKS, lambda rows, index, carry: first(rows, index, own_tokens.ref[rows, :], carry), unroll=4)
-
-    def after(piece):
-        stream.send_piece(piece)
+            normed.ref[rows, lanes] = jnp.where(keep, z, 0.0).astype(LOW)
+        return carry
+
+    for part in weights[1:]:
+        part.wait(4)
+        part.wait(5)
+    for piece in range(PIECES):
+        tokens.wait(piece)
+        for_rows(piece * total // PIECES, (piece + 1) * total // PIECES, 16, normal)
         normed.send_piece(piece)
-
-    for place, raw in enumerate(raws, 1):
-        from_feature_rows(raw, held_ref, steps, normalized(place), 0, after if place == 3 else lambda piece: None)
-
-
-def start_kernel(length_ref, ins, outs, drive_ref, held_ref, b_ref, c_ref, w_ref, low_ref):
-    feature_in, state_in, normed = ins[:3]
-    weights, stream0 = ins[3:7], ins[7]
-    drive_own, low_own, stream, linear_out, gate_out, slope, active, b_out, c_out, w_out, spread = outs
-    length, quarter = length_ref[0], own_quarter()
-    total, full = active.ref.shape
-    steps = total // CHUNKS
-    width = full // 4
-    feature, state = feature_in.wait(), state_in.wait()[...]
+    for part in weights:
+        part.wait(0)
+    assemble_states([part.ref.at[0:width] for part in weights], b_ref)
+    b_out.send(source=b_ref)
+    state = state_out.ref[...]
     states = state.shape[1]
-    normed.wait()
+    drive_phase(normed.ref, b_ref, drive_ref, state[2 + GAMMA : 3 + GAMMA, :])
     for part in weights:
-        part.wait()
-    assemble_states([part.ref.at[0:width] for part in weights], b_ref)
-    drive_phase(normed.ref, b_ref, drive_ref, state[2 + GAMMA : 3 + GAMMA, :])
+        part.wait(1)
     assemble_output([part.ref.at[width : 2 * width] for part in weights], c_ref)
-    assemble_glu([part.ref.at[2 * width : 4 * width] for part in weights], w_ref, quarter)
-    for out, source in ((b_out, b_ref), (c_out, c_ref), (w_out, w_ref)):
-        out.send(source=source)
+    c_out.send(source=c_ref)
     store = store_states(low_ref, drive_own.ref)
 
     def emit(rows, step, re, im, drive_re, drive_im, held):
@@ -589,17 +598,19 @@
         active.send_piece(piece)
         slope.send_piece(piece)
 
-    pre_phase(low_ref, c_ref, normed.ref, feature[SKIP : SKIP + 1, :], active.ref, slope.ref, held_ref, after)
+    pre_phase(low_ref, c_ref, normed.ref, feature.ref[SKIP : SKIP + 1, :], active.ref, slope.ref, held_ref, after)
+    assemble_glu([part.wait().at[2 * width : 4 * width] for part in weights], w_ref, quarter)
+    w_out.send(source=w_ref)
     held_ref[...] = dot(active.ref[...], w_ref[...], NT)
 
     def inner(rows, index, carry):
         keep = keep_rows(index, 16, steps, length)
-        linear = held_ref[rows, :full] + feature[BIAS_LINEAR : BIAS_LINEAR + 1, :]
-        gate = jax.nn.sigmoid(held_ref[rows, full:] + feature[BIAS_GATE : BIAS_GATE + 1, :])
+        linear = held_ref[rows, :full] + feature.ref[BIAS_LINEAR : BIAS_LINEAR + 1, :]
+        gate = jax.nn.sigmoid(held_ref[rows, full:] + feature.ref[BIAS_GATE : BIAS_GATE + 1, :])
         mixed = linear * gate
         gate_out.ref[rows, :] = gate.astype(LOW)
         linear_out.ref[rows, :] = (mixed * (1.0 - gate)).astype(LOW)
-        moved = stream0.ref[rows, :] + jnp.where(keep, mixed, 0.0)
+        moved = stream_ref[rows, :] + jnp.where(keep, mixed, 0.0)
         stream.ref[rows, :] = moved
         kept = jnp.where(keep, moved, 0.0)
         return carry[0] + folded(kept), carry[1] + folded(kept * kept)
@@ -607,7 +618,6 @@
     zero = jnp.zeros((8, full), F32)
     carry = (zero, zero)
     for piece in range(PIECES):
-        stream0.wait(piece)
         carry = for_rows(piece * total // PIECES, (piece + 1) * total // PIECES, 16, inner, carry)
         for out in (stream, linear_out, gate_out):
             out.send_piece(piece)
@@ -716,16 +726,14 @@
     spread_rows(jnp.concatenate([sent, small_ref[:, 0:width]], axis=0), spread)
     glu_grads(grads_ref, 2 * width, grad_gated_ref, active_ref, quarter)
     state_grads(grads_ref, grad_driven_ref, normed_ref, low_ref[:, 0:128], low_ref[:, states : states + 128], pre_grad_ref, states)
-    share = grads_ref.shape[0] // len(shares)
-    for place, out in enumerate(shares):
-        out.send(source=grads_ref.at[rows_at(lax.axis_index("dp") ^ place, share)])
+    send_halves(grads_ref, shares, 0)
 
 
 def last_kernel(
-    length_ref, ins, outs, held_ref, grad_state_ref, grad_gated_ref, pre_grad_ref, grad_driven_ref, small_ref, row_ref, grads_ref, pack_ref
+    length_ref, ins, outs, held_ref, grad_state_ref, grad_gated_ref, pre_grad_ref, grad_driven_ref, small_ref, row_ref, grads_ref, pack_ref, low_ref
 ):
     (sums, norm1, feature_in, state_in, norm0, stream, base, gate, linear, w, slope, normed, active, c, low, drive_own, b, x) = ins
-    send, up_out, grad_out = outs
+    kept, sent, up_out, grad_out = outs
     length, quarter = length_ref[0], own_quarter()
     total, full = stream.ref.shape
     steps = total // CHUNKS
@@ -796,45 +804,66 @@
         pack_ref[place // 4 : place // 4 + 1, place % 4 * width : (place % 4 + 1) * width] = small_ref[place : place + 1, 0:width]
     exact = pack_ref[0:8, :]
     pack_ref[8:16, :] = exact - exact.astype(LOW).astype(F32)
-    groups = send.ref.shape[0]
-    share = send.ref.shape[1] - 16
-    for group in range(groups):
-        send.ref[group, :share, :] = grads_ref[group * share : (group + 1) * share, :]
-        send.ref[group, share:, :] = pack_ref[...].astype(LOW)
-
-
-def sum_shares(got, out, share):
-    groups = got.ref.shape[0]
-    for piece in range(0, share, 16):
-        value = got.ref[0, piece : piece + 16, :].astype(F32)
-        for group in range(1, groups):
-            value += got.ref[group, piece : piece + 16, :].astype(F32)
-        value = value.astype(LOW)
-        for group in range(groups):
-            out.ref[group, piece : piece + 16, :] = value
-
-
-def add_kernel(length_ref, ins, outs):
-    (out,) = outs
+    half = grads_ref.shape[0] // 2
+    low_ref[...] = pack_ref[...].astype(LOW)
+    mine = lax.axis_index("dp") & 1
+    for out, which in ((kept, mine), (sent, 1 - mine)):
+        out.send(0, half, source=grads_ref.at[rows_at(which, half)])
+        out.send(half, 16, source=low_ref)
+
+
+def send_halves(source_ref, outs, stage):
+    kept = lax.axis_index("dp") >> stage & 1
+    half = source_ref.shape[0] // 2
+    for out, which in zip(outs, (kept, 1 - kept)):
+        out.send(source=source_ref.at[rows_at(which, half)])
+
+
+def add_kernel(length_ref, ins, outs, sum_ref, stage):
+    kept, other = ins
+    kept.wait()
+    other.wait()
+    for piece in range(0, kept.ref.shape[0], 16):
+        at = slice(piece, piece + 16)
+        sum_ref[at, :] = (kept.ref[at, :].astype(F32) + other.ref[at, :].astype(F32)).astype(LOW)
+    send_halves(sum_ref, outs, stage)
+
+
+def pair_kernel(length_ref, ins, outs, sum_ref, pack_ref):
+    kept, other = ins
+    kept.wait()
+    other.wait()
+    half = kept.ref.shape[0] - 16
+    share = half // len(outs)
+    small = kept.ref[half:, :].astype(F32) + other.ref[half:, :].astype(F32)
+    small = small[0:8, :] + small[8:16, :]
+    pack_ref[...] = jnp.concatenate([small, small - small.astype(LOW).astype(F32)], axis=0).astype(LOW)
+    for piece in range(0, half, 16):
+        at = slice(piece, piece + 16)
+        sum_ref[at, :] = (kept.ref[at, :].astype(F32) + other.ref[at, :].astype(F32)).astype(LOW)
+    for place, out in enumerate(outs):
+        out.send(0, share, source=sum_ref.at[rows_at((lax.axis_index("dp") >> 1) ^ place, share)])
+        out.send(share, 16, source=pack_ref)
+
+
+def share_kernel(length_ref, ins, outs):
+    *blocks, kept, other = ins
+    out, small = outs
+    share = kept.ref.shape[0]
     for value in ins:
         value.wait()
-    for piece in range(0, out.ref.shape[0], 16):
+    for piece in range(0, share, 16):
         at = slice(piece, piece + 16)
-        total = ins[0].ref[at, :].astype(F32)
-        for value in ins[1:]:
-            total += value.ref[at, :].astype(F32)
-        out.ref[at, :] = total.astype(LOW)
-
-
-def share_kernel(length_ref, ins, outs):
-    (got,) = ins
-    out, small = outs
-    got.wait()
-    groups, share = got.ref.shape[0], got.ref.shape[1] - 16
-    sum_shares(got, out, share)
-    value = got.ref[0, share:, :].astype(F32)
-    for group in range(1, groups):
-        value += got.ref[group, share:, :].astype(F32)
+        value = blocks[0].ref[at, :].astype(F32)
+        for block in blocks[1:]:
+            value += block.ref[at, :].astype(F32)
+        out.ref[at, :] = value.astype(LOW)
+        value = kept.ref[at, :].astype(F32) + other.ref[at, :].astype(F32)
+        out.ref[share + piece : share + piece + 16, :] = value.astype(LOW)
+    out.send()
+    value = blocks[0].ref[share:, :].astype(F32)
+    for block in blocks[1:]:
+        value += block.ref[share:, :].astype(F32)
     small.ref[...] = value[0:8, :] + value[8:16, :]
 
 
@@ -881,18 +910,19 @@
 
 
 def widen_kernel(length_ref, ins, outs, held_ref):
-    b, c, w = outs
-    half = b.ref.shape[1]
-    grads0, *shares = ins
-    share = shares[0].ref.shape[0]
-    for place, value in enumerate(shares):
-        held_ref[rows_at(lax.axis_index("dp") ^ place, share), :] = value.wait()[...]
-    for layer, source_ref in ((1, held_ref), (0, grads0.ref)):
-        if layer == 0:
-            grads0.wait()
-        for out, first, size in ((b, 0, half), (c, half, half), (w, 2 * half, 2 * half)):
-            out.ref[layer, :, :] = source_ref[first : first + size, :].astype(F32)
-            out.send(layer, 1)
+    half = outs[0].ref.shape[1]
+    groups = len(ins)
+    share = ins[0].ref.shape[0] // 2
+    stages = groups.bit_length() - 1
+    for place, value in enumerate(ins):
+        value.wait()
+        owner = lax.axis_index("dp") ^ place
+        index = sum((owner >> stage & 1) << (stages - 1 - stage) for stage in range(stages))
+        for layer, at in ((0, (owner & 1) * (groups // 2) + (owner >> 1)), (1, index)):
+            held_ref[layer, rows_at(at, share), :] = value.ref[layer * share : (layer + 1) * share, :].astype(F32)
+    for layer in range(LAYERS):
+        for out, first, size in zip(outs, (0, half, 2 * half), (half, half, 2 * half)):
+            out.send(layer, 1, source=held_ref.at[pl.ds(layer, 1), pl.ds(first, size)])
 
 
 def shape(*dims, dtype=F32):
@@ -939,32 +969,43 @@
     share = 4 * width // dp_size
     piece = total // PIECES
 
+    stages = dp_size.bit_length() - 1
+
     def exchange(value, bit):
         return lax.ppermute(value, "dp", [(i, i ^ bit) for i in range(dp_size)])
 
+    def add(halves, stage):
+        kept, other = halves
+        rows = kept.shape[0]
+        return call(
+            functools.partial(add_kernel, stage=stage + 1),
+            (shape(rows // 2, full, dtype=LOW),) * 2,
+            [pltpu.VMEM((rows, full), LOW)],
+            (lengths, kept, other),
+            "add",
+            bare=(0, 1),
+        )
+
 
     b_weight, c_weight = b_weight.reshape(LAYERS, width, full), c_weight.reshape(LAYERS, width, full)
     glu_weight = glu_weight.reshape(LAYERS, 2 * width, full)
-    raw = inputs[0]
-    raw_near, raw_far = swap(raw, 1, sharers), swap(raw, 2, sharers)
-    tokens, sums, params, weights0 = call(
+    tokens, sums, params, first = call(
         enter_kernel,
         (
             shape(total, width),
             shape(dp_size * state_size, 8, width),
             shape(PARAM_ROWS, width),
-            shape(4 * width, full, dtype=LOW),
+            shape(6 * width, full, dtype=LOW),
         ),
         [pltpu.VMEM((total, width), F32)],
-        (lengths, raw, b_weight, c_weight, glu_weight, bn_gain, bn_bias, skip_weight, glu_bias, nu_log, theta_log, gamma_log),
+        (lengths, inputs[0], bn_gain, bn_bias, skip_weight, glu_bias, nu_log, theta_log, gamma_log, b_weight, c_weight, glu_weight),
         "enter",
         pieces={1: piece},
         axes={1: 1},
-        bare=(3,),
-        flops=ENTER_FLOPS,
-    )
-    params_near, params_far = swap(params, 1, sharers), swap(params, 2, sharers)
-    near0, far0 = swap(weights0, 1, sharers), swap(weights0, 2, sharers)
+        late=(9, 10, 11),
+    )
+    near = [swap(value, 1, sharers) for value in (params, first)]
+    far = [swap(value, 2, sharers) for value in (params, first)]
     sums = across(sums, ("dp", "state"))
     if sharers > 1:
         sums = sums.reshape(dp_size * 4, sharers, 8, width)[:, 0]
@@ -977,23 +1018,19 @@
         "cotangent",
         pieces={1: piece},
         axes={1: 1},
-    )
-    raw_far, params_far, sums = lax.optimization_barrier((raw_far, params_far, sums))
-    normed0, stream0, feature, state, norm0 = call(
-        normal_kernel,
-        (shape(total, full, dtype=LOW), shape(total, full), shape(PARAM_ROWS, full), shape(8, states), shape(8, full)),
-        [pltpu.VMEM((total, width), F32), pltpu.VMEM((8, full), F32)],
-        (lengths, sums, tokens, params, params_near, params_far, swap(params_far, 1, sharers),
-         raw_near, raw_far, swap(raw_far, 1, sharers)),
-        "normal",
-        pieces={7: piece, 8: piece, 9: piece},
-        axes={7: 1, 8: 1, 9: 1},
-    )
-    far0, normed0, later = lax.optimization_barrier((far0, normed0, later))
+        late=(2, 3, 4),
+    )
+    *far, near[0], near[1], sums, later = lax.optimization_barrier((*far, *near, sums, later))
+    diagonal = [swap(value, 1, sharers) for value in far]
     later_far = swap(later, 2, sharers)
-    drive0, low0, stream1, linear0, gate0, slope0, active0, b_all, c_all, w_all, sums1 = call(
+    parts = list(zip((params, first), near, far, diagonal))
+    feature, state, norm0, normed0, drive0, low0, stream1, linear0, gate0, slope0, active0, b_all, c_all, w_all, sums1 = call(
         start_kernel,
         (
+            shape(PARAM_ROWS, full),
+            shape(8, states),
+            shape(8, full),
+            shape(total, full, dtype=LOW),
             shape(total, 256),
             shape(total, 256, dtype=LOW),
             shape(total, full),
@@ -1007,6 +1044,8 @@
             shape(dp_size, 8, width),
         ),
         [
+            pltpu.VMEM((8, full), F32),
+            pltpu.VMEM((total, full), F32),
             pltpu.VMEM((total, 2 * states), F32),
             pltpu.VMEM((total, 2 * full), F32),
             pltpu.VMEM((2 * states, full), LOW),
@@ -1014,21 +1053,24 @@
             pltpu.VMEM((2 * full, full), LOW),
             pltpu.VMEM((total, 2 * states), LOW),
         ],
-        (lengths, feature, state, normed0, weights0, near0, far0, swap(far0, 1, sharers), stream0),
+        (lengths, sums, *parts[0], tokens, *parts[1]),
         "start",
-        pieces={8: piece},
-        bare=(7, 8, 9),
+        pieces={6: piece} | {place: width for place in (7, 8, 9, 10)},
+        order=(4, 5),
+        bare=(11, 12, 13),
+        flops=1e9,
     )
     sums1 = across(sums1, "dp")
     later_far, sums1 = lax.optimization_barrier((later_far, sums1))
-    result, base, bn1, norm1, *shares1 = call(
+    result, base, bn1, norm1, *halves1 = call(
         middle_kernel,
         (
             shape(width, total),
             shape(total, full),
             shape(dp_size, 16, width),
             shape(8, full),
-            *(shape(share, full, dtype=LOW) for _ in range(dp_size)),
+            shape(2 * width, full, dtype=LOW),
+            shape(2 * width, full, dtype=LOW),
         ),
         [
             pltpu.VMEM((8, full), F32),
@@ -1053,13 +1095,23 @@
          swap(later_far, 1, sharers)),
         "middle",
         pieces={5: piece},
-        bare=tuple(range(4, 4 + dp_size)),
+        late=(6, 7, 8, 9, 10),
+        bare=(4, 5),
+        flops=1e9,
     )
     bn1 = across(bn1, "dp")
-    shares1 = [shares1[0]] + [exchange(shares1[bit], bit) for bit in range(1, dp_size)]
-    send, up0, grad0 = call(
+    halves1[1] = exchange(halves1[1], 1)
+    halves1 = list(add(halves1, 0))
+    bn1, *halves1 = lax.optimization_barrier((bn1, *halves1))
+    halves1[1] = exchange(halves1[1], 2)
+    kept0, sent0, up0, grad0 = call(
         last_kernel,
-        (shape(dp_size, share + 16, full, dtype=LOW), shape(total, width), shape(total, width)),
+        (
+            shape(2 * width + 16, full, dtype=LOW),
+            shape(2 * width + 16, full, dtype=LOW),
+            shape(total, width),
+            shape(total, width),
+        ),
         [
             pltpu.VMEM((total, full), F32),
             pltpu.VMEM((total, 2 * states), F32),
@@ -1070,24 +1122,44 @@
             pltpu.VMEM((16, full), F32),
             pltpu.VMEM((4 * width, full), LOW),
             pltpu.VMEM((16, full), F32),
+            pltpu.VMEM((16, full), LOW),
         ],
         (lengths, bn1, norm1, feature, state, norm0, stream1, base, gate0, linear0, w_all, slope0, normed0, active0, c_all, low0,
          drive0, b_all, tokens),
         "last",
+        bare=(0, 1),
         pieces={6: piece, 7: piece, 8: piece, 9: piece},
-    )
-    *shares1, send = lax.optimization_barrier((*shares1, send))
-    (share1,) = call(add_kernel, (shape(share, full, dtype=LOW),), [], (lengths, *shares1), "add")
-    shares1 = [share1] + [exchange(share1, bit) for bit in range(1, dp_size)]
-    got = across(send, "dp")
-    *shares1, got = lax.optimization_barrier((*shares1, got))
+        late=tuple(range(10, 19)),
+        flops=1e11,
+    )
+    sent0 = exchange(sent0, 1)
+    *halves1, kept0 = lax.optimization_barrier((*halves1, kept0))
+    for stage in range(1, stages):
+        if stage > 1:
+            halves1[1] = exchange(halves1[1], 1 << stage)
+        if stage < stages - 1:
+            halves1 = list(add(halves1, stage))
+    blocks = call(
+        pair_kernel,
+        (shape(share + 16, full, dtype=LOW),) * (dp_size // 2),
+        [pltpu.VMEM((2 * width, full), LOW), pltpu.VMEM((16, full), LOW)],
+        (lengths, kept0, sent0),
+        "pair",
+        bare=tuple(range(dp_size // 2)),
+    )
+    blocks = [blocks[0]] + [exchange(blocks[place], 2 * place) for place in range(1, dp_size // 2)]
+    halves1[1], *blocks = lax.optimization_barrier((halves1[1], *blocks))
     back, small0 = call(
         share_kernel,
-        (shape(dp_size, share, full, dtype=LOW), shape(8, full)),
+        (shape(2 * share, full, dtype=LOW), shape(8, full)),
         [],
-        (lengths, got),
+        (lengths, *blocks, *halves1),
         "share",
     )
+    backs = {0: back, 1: exchange(back, 1)}
+    for place in range(2, dp_size, 2):
+        backs[place] = exchange(back, place)
+        backs[place + 1] = exchange(backs[place], 1)
     grad_nu, grad_theta, grad_gamma, grad_skip, grad_bias, grad_gain, grad_shift, grad_inputs = call(
         finish_kernel,
         (
@@ -1104,13 +1176,13 @@
         (lengths, small0, bn1, norm0, feature, nu_log, theta_log, up0, grad0, tokens),
         "finish",
     )
-    grads0 = across(back, "dp").reshape(4 * width, full)
     grad_b, grad_c, grad_glu = call(
         widen_kernel,
         (shape(LAYERS, width, full), shape(LAYERS, width, full), shape(LAYERS, 2 * width, full)),
-        [pltpu.VMEM((4 * width, full), LOW)],
-        (lengths, grads0, *shares1),
+        [pltpu.VMEM((LAYERS, 4 * width, full), F32)],
+        (lengths, *(backs[place] for place in range(dp_size))),
         "widen",
+        bare=(0, 1, 2),
     )
     grad_b = grad_b.reshape(LAYERS, 2, own_states, full)
     grad_c = grad_c.reshape(LAYERS, 2, own_states, full)

time: 163 us -> 145 us (0.89)
  starting transfers between devices: 56.1 us -> 35.2 us
  waiting for transfers between devices: 37.3 us -> 48 us
  Pallas kernels: 67.3 us -> 59.9 us
    ppermute x14, waiting for transfers between devices: 8.75 us -> 25.2 us  [exchange(): return lax.ppermute(value, 'dp', [(i, i ^ bit) for i in range(dp_size)])]
    ppermute x14, starting transfers between devices: 27.5 us -> 14.3 us  [exchange(): return lax.ppermute(value, 'dp', [(i, i ^ bit) for i in range(dp_size)])]
    all_to_all x5 -> x3, waiting for transfers between devices: 16.6 us -> 7.22 us  [across(): return lax.all_to_all(value, axes, 0, 0, tiled=True)]
    pallas_call x10 -> x11, Pallas kernels: 67.3 us -> 59.9 us  [call(): pl.pallas_call(body, out_shape=tuple(outs), in_specs=[pl.BlockSpec(memory...]
    all_to_all x5 -> x3, starting transfers between devices: 21.6 us -> 14.4 us  [across(): return lax.all_to_all(value, axes, 0, 0, tiled=True)]
    ppermute x12 -> x9, waiting for transfers between devices: 11.9 us -> 15.6 us  [swap(): return lax.ppermute(value, 'state', pairs)]
    ppermute x12 -> x9, starting transfers between devices: 7.01 us -> 6.6 us  [swap(): return lax.ppermute(value, 'state', pairs)]
  transfers between devices with their start and end apart: 31 -> 26, of which waited for: 11 -> 15; matrix products, arithmetic and copies ran while one was open for 0% -> 0% of each run, Pallas kernels for 27% -> 14%
where the time goes in v4:
time: 145 us
  Pallas kernels  59.9 us (41%)
  waiting for transfers between devices  48 us (33%)
  starting transfers between devices  35.2 us (24%)
  between operations  1.62 us (1%)
    pallas_call x11, Pallas kernels, call(): pl.pallas_call(body, out_shape=tuple(outs), in_specs=[pl.BlockSpec(memory...  59.9 us
    ppermute x14, waiting for transfers between devices, exchange(): return lax.ppermute(value, 'dp', [(i, i ^ bit) for i in range(dp_size)])  25.2 us
    ppermute x9, waiting for transfers between devices, swap(): return lax.ppermute(value, 'state', pairs)  15.6 us
    all_to_all x3, starting transfers between devices, across(): return lax.all_to_all(value, axes, 0, 0, tiled=True)  14.4 us
    ppermute x14, starting transfers between devices, exchange(): return lax.ppermute(value, 'dp', [(i, i ^ bit) for i in range(dp_size)])  14.3 us
    all_to_all x3, waiting for transfers between devices, across(): return lax.all_to_all(value, axes, 0, 0, tiled=True)  7.22 us
    ppermute x9, starting transfers between devices, swap(): return lax.ppermute(value, 'state', pairs)  6.6 us
  transfers between devices with their start and end apart: 26, of which 15 were waited for; matrix products, arithmetic and copies ran while one was open for 0% of the time, Pallas kernels for 14%

profile of v4, /device:TPU:0, one launch (start us, length us, event | category | flops | bytes accessed | tf_op | source)
XLA Modules:
  0.0 144.7 jit_solution(13442958408362942091)
XLA Ops:
  1.3 3.3 %enter.1 = (f32[1024,128]{1,0:T(8,128)}, f32[32,8,128]{2,1,0:T(8,128)}, f32[24,128]{1,0:T(8,128)}, bf16[768,512]{1,0:T(8,128)(2,1)}) custom-call(s32[1]{0:T(128)S(6)} %copy.25.refs_0_, f32[128,1024]{1,0:T(8,128)} %bitcast.16, f32[2,128]{1,0:T(2,128)} %refs_2_.1, f32[2,128]{1,0:T(2,128)} %refs_3_.1, f32[2,128]{1,0:T(2,128)} %refs_4_.1, f32[2,2,128]{2,1,0:T(2,128)} %refs_5_.2, ...), custom_call_target="tpu_custom_call" | custom-call | tf_op jit(solution)/shard_map/enter/pallas_call | solution.py:234
  4.6 0.5 collective-permute-start.3
  5.2 2.6 %collective-permute-start.1 = (bf16[768,512]{1,0:T(8,128)(2,1)}, bf16[768,512]{1,0:T(8,128)(2,1)}, u32[]{:S(2)}, u32[]{:S(2)}) collective-permute-start(bf16[768,512]{1,0:T(8,128)(2,1)} %get-tuple-element.86.refs_7_), channel_id=1, source_target_pairs={{0,2},{1,3},{2,0},{3,1},{4,6},{5,7},{6,4},{7,5},{8,10},{9,11},{10,... | collective-permute-start | bytes 2359304 | tf_op jit(solution)/shard_map/ppermute | solution.py:934
  7.7 5.1 %all-to-all-start = ((f32[32,8,128]{2,1,0:T(8,128)}), f32[32,8,128]{2,1,0:T(8,128)}, u32[]{:S(2)}, u32[]{:S(2)}) async-start(f32[32,8,128]{2,1,0:T(8,128)} %get-tuple-element.87), calls=%async_computation | async-start | bytes 262144 | tf_op jit(solution)/shard_map/all_to_all | solution.py:938
  12.8 0.2 collective-permute-start.2
  13.0 1.7 %collective-permute-start = (f32[24,128]{1,0:T(8,128)}, f32[24,128]{1,0:T(8,128)}, u32[]{:S(2)}, u32[]{:S(2)}) collective-permute-start(f32[24,128]{1,0:T(8,128)} %get-tuple-element.85.refs_2_), channel_id=1, source_target_pairs={{0,2},{1,3},{2,0},{3,1},{4,6},{5,7},{6,4},{7,5},{8,10},{9,11},{10,... | collective-permute-start | bytes 36872 | tf_op jit(solution)/shard_map/ppermute | solution.py:934
  14.7 2.9 %cotangent.1 = (f32[1024,128]{1,0:T(8,128)}, bf16[768,512]{1,0:T(8,128)(2,1)}) custom-call(s32[1]{0:T(128)S(6)} %copy.25.refs_0_, f32[128,1024]{1,0:T(8,128)} %bitcast.17, bf16[2,128,512]{2,1,0:T(8,128)(2,1)} %bitcast.13, bf16[2,128,512]{2,1,0:T(8,128)(2,1)} %bitcast.15, bf16[2,256,512]{2,1,0:T(8,128)(2,1)} %bitcast.11), custom_call_target="tpu_custom_call" | custom-call | tf_op jit(solution)/shard_map/cotangent/pallas_call | solution.py:234
  17.6 10.3 %collective-permute-done.refs_4_ = f32[24,128]{1,0:T(8,128)} collective-permute-done((f32[24,128]{1,0:T(8,128)}, f32[24,128]{1,0:T(8,128)}, u32[]{:S(2)}, u32[]{:S(2)}) %collective-permute-start) | collective-permute-done | bytes 12320 | tf_op jit(solution)/shard_map/ppermute | solution.py:934
  27.8 1.1 all-to-all-done.refs_1_
  29.0 1.5 %collective-permute-start.4 = (bf16[768,512]{1,0:T(8,128)(2,1)}, bf16[768,512]{1,0:T(8,128)(2,1)}, u32[]{:S(2)}, u32[]{:S(2)}) collective-permute-start(bf16[768,512]{1,0:T(8,128)(2,1)} %get-tuple-element.91.refs_7_), channel_id=1, source_target_pairs={{0,2},{1,3},{2,0},{3,1},{4,6},{5,7},{6,4},{7,5},{8,10},{9,11},{10,... | collective-permute-start | bytes 2359304 | tf_op jit(solution)/shard_map/ppermute | solution.py:934
  30.5 0.1 collective-permute-start.5
  30.5 1.4 collective-permute-done.5.refs_5_
  32.0 10.8 %start.1 = (f32[24,512]{1,0:T(8,128)}, f32[8,256]{1,0:T(8,128)}, f32[8,512]{1,0:T(8,128)}, bf16[1024,512]{1,0:T(8,128)(2,1)}, f32[1024,256]{1,0:T(8,128)}, /*ind...) custom-call(s32[1]{0:T(128)S(6)} %copy.25.refs_0_, ...), custom_call_target="tpu_custom_call" | custom-call | flops 1000000000 | tf_op jit(solution)/shard_map/start/pallas_call | solution.py:234
  42.8 5.2 %all-to-all-start.1 = ((f32[8,8,128]{2,1,0:T(8,128)}), f32[8,8,128]{2,1,0:T(8,128)}, u32[]{:S(2)}, u32[]{:S(2)}) async-start(f32[8,8,128]{2,1,0:T(8,128)} %get-tuple-element.98), calls=%async_computation.1 | async-start | bytes 65536 | tf_op jit(solution)/shard_map/all_to_all | solution.py:938
  48.0 1.3 collective-permute-done.4.refs_9_
  49.2 5.5 %all-to-all-done.1.refs_1_ = f32[8,8,128]{2,1,0:T(8,128)} async-done(((f32[8,8,128]{2,1,0:T(8,128)}), f32[8,8,128]{2,1,0:T(8,128)}, u32[]{:S(2)}, u32[]{:S(2)}) %all-to-all-start.1) | async-done | bytes 32800 | tf_op jit(solution)/shard_map/all_to_all | solution.py:938
  54.7 2.6 %collective-permute-done.8.refs_10_ = bf16[768,512]{1,0:T(8,128)(2,1)} collective-permute-done((bf16[768,512]{1,0:T(8,128)(2,1)}, bf16[768,512]{1,0:T(8,128)(2,1)}, u32[]{:S(2)}, u32[]{:S(2)}) %collective-permute-start.8) | collective-permute-done | bytes 786464 | tf_op jit(solution)/shard_map/ppermute | solution.py:934
  57.4 17.7 %middle.1 = (f32[128,1024]{1,0:T(8,128)}, f32[1024,512]{1,0:T(8,128)}, f32[8,16,128]{2,1,0:T(8,128)}, f32[8,512]{1,0:T(8,128)}, bf16[256,512]{1,0:T(8,128)(2,1)}, /*index=5*/bf16[256,512]{1,0:T(8,128)(2,1)}) custom-call(s32[1]{0:T(128)S(6)} %copy.25.refs_0_, f32[8,8,128]{2,1,0:T(8,128)} %all-to-all-done.1.refs_1_, ...), custom_call_target="tpu_custom_call" | custom-call | flops 1000000000 | tf_op jit(solution)/shard_map/middle/pallas_call | solution.py:234
  75.1 0.5 collective-permute-start.9
  75.6 4.1 %all-to-all-start.2 = ((f32[8,16,128]{2,1,0:T(8,128)}), f32[8,16,128]{2,1,0:T(8,128)}, u32[]{:S(2)}, u32[]{:S(2)}) async-start(f32[8,16,128]{2,1,0:T(8,128)} %get-tuple-element.107), calls=%async_computation.2 | async-start | bytes 131072 | tf_op jit(solution)/shard_map/all_to_all | solution.py:938
  79.8 4.2 %collective-permute-done.9.refs_2_ = bf16[256,512]{1,0:T(8,128)(2,1)} collective-permute-done((bf16[256,512]{1,0:T(8,128)(2,1)}, bf16[256,512]{1,0:T(8,128)(2,1)}, u32[]{:S(2)}, u32[]{:S(2)}) %collective-permute-start.9) | collective-permute-done | bytes 262176 | tf_op jit(solution)/shard_map/ppermute | solution.py:975
  84.0 1.9 %add.2 = (bf16[128,512]{1,0:T(8,128)(2,1)}, bf16[128,512]{1,0:T(8,128)(2,1)}) custom-call(s32[1]{0:T(128)S(6)} %copy.25.refs_0_, bf16[256,512]{1,0:T(8,128)(2,1)} %get-tuple-element.108.refs_1_, bf16[256,512]{1,0:T(8,128)(2,1)} %collective-permute-done.9.refs_2_), custom_call_target="tpu_custom_call" | custom-call | tf_op jit(solution)/shard_map/add/pallas_call | solution.py:234
  85.9 0.6 all-to-all-done.2.refs_1_.refs_2_
  86.5 11.2 %last.1 = (bf16[272,512]{1,0:T(8,128)(2,1)}, bf16[272,512]{1,0:T(8,128)(2,1)}, f32[1024,128]{1,0:T(8,128)}, f32[1024,128]{1,0:T(8,128)}) custom-call(s32[1]{0:T(128)S(6)} %copy.25.refs_0_, f32[8,16,128]{2,1,0:T(8,128)} %all-to-all-done.2.refs_1_.refs_2_, f32[8,512]{1,0:T(8,128)} %get-tuple-element.115.refs_2_, f32[24,512]{1,0:T(8,128)} %get-tuple-element.101.refs_3_.refs_4_, ...), custom_call_target="tpu_custom_call" | custom-call | flops 99999997952 | tf_op jit(solution)/shard_map/last/pallas_call | solution.py:234
  97.7 0.5 collective-permute-start.12
  98.2 0.8 collective-permute-start.10
  99.0 4.5 %collective-permute-done.10.refs_2_ = bf16[128,512]{1,0:T(8,128)(2,1)} collective-permute-done((bf16[128,512]{1,0:T(8,128)(2,1)}, bf16[128,512]{1,0:T(8,128)(2,1)}, u32[]{:S(2)}, u32[]{:S(2)}) %collective-permute-start.10) | collective-permute-done | bytes 131104 | tf_op jit(solution)/shard_map/ppermute | solution.py:975
  103.5 2.0 %collective-permute-done.12.refs_2_ = bf16[272,512]{1,0:T(8,128)(2,1)} collective-permute-done((bf16[272,512]{1,0:T(8,128)(2,1)}, bf16[272,512]{1,0:T(8,128)(2,1)}, u32[]{:S(2)}, u32[]{:S(2)}) %collective-permute-start.12) | collective-permute-done | bytes 278560 | tf_op jit(solution)/shard_map/ppermute | solution.py:975
  105.5 2.0 %pair.1 = (bf16[80,512]{1,0:T(8,128)(2,1)}, bf16[80,512]{1,0:T(8,128)(2,1)}, bf16[80,512]{1,0:T(8,128)(2,1)}, bf16[80,512]{1,0:T(8,128)(2,1)}) custom-call(s32[1]{0:T(128)S(6)} %copy.25.refs_0_, bf16[272,512]{1,0:T(8,128)(2,1)} %get-tuple-element.131.refs_1_, bf16[272,512]{1,0:T(8,128)(2,1)} %collective-permute-done.12.refs_2_), custom_call_target="tpu_custom_call" | custom-call | tf_op jit(solution)/shard_map/pair/pallas_call | solution.py:234
  107.5 0.3 collective-permute-start.13
  107.8 0.9 collective-permute-start.14
  108.7 3.3 %collective-permute-start.15 = (bf16[80,512]{1,0:T(8,128)(2,1)}, bf16[80,512]{1,0:T(8,128)(2,1)}, u32[]{:S(2)}, u32[]{:S(2)}) collective-permute-start(bf16[80,512]{1,0:T(8,128)(2,1)} %get-tuple-element.136), channel_id=1, source_target_pairs={{0,24},{4,28},{8,16},{12,20},{16,8},{20,12},{24,0},{28,4},{1,25},{... | collective-permute-start | bytes 245768 | tf_op jit(solution)/shard_map/ppermute | solution.py:975
  112.0 1.8 %add.3 = (bf16[64,512]{1,0:T(8,128)(2,1)}, bf16[64,512]{1,0:T(8,128)(2,1)}) custom-call(s32[1]{0:T(128)S(6)} %copy.25.refs_0_, bf16[128,512]{1,0:T(8,128)(2,1)} %get-tuple-element.128.refs_1_, bf16[128,512]{1,0:T(8,128)(2,1)} %collective-permute-done.10.refs_2_), custom_call_target="tpu_custom_call" | custom-call | tf_op jit(solution)/shard_map/add/pallas_call | solution.py:234
  113.8 0.1 collective-permute-start.11
  113.9 5.5 %collective-permute-done.11.refs_6_ = bf16[64,512]{1,0:T(8,128)(2,1)} collective-permute-done((bf16[64,512]{1,0:T(8,128)(2,1)}, bf16[64,512]{1,0:T(8,128)(2,1)}, u32[]{:S(2)}, u32[]{:S(2)}) %collective-permute-start.11) | collective-permute-done | bytes 65568 | tf_op jit(solution)/shard_map/ppermute | solution.py:975
  119.3 1.9 %share.1 = (bf16[128,512]{1,0:T(8,128)(2,1)}, f32[8,512]{1,0:T(8,128)}) custom-call(s32[1]{0:T(128)S(6)} %copy.25.refs_0_, bf16[80,512]{1,0:T(8,128)(2,1)} %get-tuple-element.137.refs_1_, bf16[80,512]{1,0:T(8,128)(2,1)} %collective-permute-done.13.refs_2_, bf16[80,512]{1,0:T(8,128)(2,1)} %collective-permute-done.14.refs_3_, ...), custom_call_target="tpu_custom_call" | custom-call | tf_op jit(solution)/shard_map/share/pallas_call | solution.py:234
  121.2 2.2 %collective-permute-start.21 = (bf16[128,512]{1,0:T(8,128)(2,1)}, bf16[128,512]{1,0:T(8,128)(2,1)}, u32[]{:S(2)}, u32[]{:S(2)}) collective-permute-start(bf16[128,512]{1,0:T(8,128)(2,1)} %get-tuple-element.149.refs_1_), channel_id=1, source_target_pairs={{0,24},{4,28},{8,16},{12,20},{16,8},{20,12},{24,0},{28,4},{1,25},{... | collective-permute-start | bytes 393224 | tf_op jit(solution)/shard_map/ppermute | solution.py:975
  123.4 2.3 %collective-permute-start.17 = (bf16[128,512]{1,0:T(8,128)(2,1)}, bf16[128,512]{1,0:T(8,128)(2,1)}, u32[]{:S(2)}, u32[]{:S(2)}) collective-permute-start(bf16[128,512]{1,0:T(8,128)(2,1)} %get-tuple-element.149.refs_1_), channel_id=1, source_target_pairs={{0,8},{4,12},{8,0},{12,4},{16,24},{20,28},{24,16},{28,20},{1,9},{5... | collective-permute-start | bytes 393224 | tf_op jit(solution)/shard_map/ppermute | solution.py:975
  125.7 0.8 collective-permute-start.16
  126.4 3.4 %collective-permute-done.21.refs_7_ = bf16[128,512]{1,0:T(8,128)(2,1)} collective-permute-done((bf16[128,512]{1,0:T(8,128)(2,1)}, bf16[128,512]{1,0:T(8,128)(2,1)}, u32[]{:S(2)}, u32[]{:S(2)}) %collective-permute-start.21) | collective-permute-done | bytes 131104 | tf_op jit(solution)/shard_map/ppermute | solution.py:975
  129.8 0.7 collective-permute-start.22
  130.5 3.7 %collective-permute-done.19.refs_5_ = bf16[128,512]{1,0:T(8,128)(2,1)} collective-permute-done((bf16[128,512]{1,0:T(8,128)(2,1)}, bf16[128,512]{1,0:T(8,128)(2,1)}, u32[]{:S(2)}, u32[]{:S(2)}) %collective-permute-start.19) | collective-permute-done | bytes 131104 | tf_op jit(solution)/shard_map/ppermute | solution.py:975
  134.2 0.5 collective-permute-start.20
  134.7 1.5 %collective-permute-start.18 = (bf16[128,512]{1,0:T(8,128)(2,1)}, bf16[128,512]{1,0:T(8,128)(2,1)}, u32[]{:S(2)}, u32[]{:S(2)}) collective-permute-start(bf16[128,512]{1,0:T(8,128)(2,1)} %collective-permute-done.17.refs_3_), channel_id=1, source_target_pairs={{0,4},{4,0},{8,12},{12,8},{16,20},{20,16},{24,28},{28,24},{1,5},{5... | collective-permute-start | bytes 393224 | tf_op jit(solution)/shard_map/ppermute | solution.py:975
  136.2 3.6 %finish.1 = (f32[2,64]{1,0:T(2,128)}, f32[2,64]{1,0:T(2,128)}, f32[2,64]{1,0:T(2,128)}, f32[2,128]{1,0:T(2,128)}, f32[2,2,128]{2,1,0:T(2,128)}, /*index=5*/f32[2...) custom-call(s32[1]{0:T(128)S(6)} %copy.25.refs_0_, f32[8,512]{1,0:T(8,128)} %get-tuple-element.143.refs_1_, ...), custom_call_target="tpu_custom_call" | custom-call | tf_op jit(solution)/shard_map/finish/pallas_call | solution.py:234
  139.8 0.5 collective-permute-done.20.refs_6_
  140.3 1.4 collective-permute-done.18.refs_4_
  141.7 2.8 %widen.1 = (f32[2,128,512]{2,1,0:T(8,128)}, f32[2,128,512]{2,1,0:T(8,128)}, f32[2,256,512]{2,1,0:T(8,128)}) custom-call(s32[1]{0:T(128)S(6)} %copy.25.refs_0_, bf16[128,512]{1,0:T(8,128)(2,1)} %get-tuple-element.149.refs_1_, bf16[128,512]{1,0:T(8,128)(2,1)} %collective-permute-done.16.refs_2_, bf16[128,512]{1,0:T(8,128)(2,1)} %collective-permute-done.17.refs_3_, ...), custom_call_target="tpu_custom_call" | custom-call | tf_op jit(solution)/shard_map/widen/pallas_call | solution.py:234
  (15 shorter events, 0.0 us)
Async XLA Ops:
  4.6 24.3 %collective-permute-start.3 = (bf16[768,512]{1,0:T(8,128)(2,1)}, bf16[768,512]{1,0:T(8,128)(2,1)}, u32[]{:S(2)}, u32[]{:S(2)}) collective-permute-start(bf16[768,512]{1,0:T(8,128)(2,1)} %get-tuple-element.86.refs_7_), channel_id=1, source_target_pairs={{0,1},{1,0},{2,3},{3,2},{4,5},{5,4},{6,7},{7,6},{8,9},{9,8},{10,11... | collective-permute-start | bytes 2359304 | tf_op jit(solution)/shard_map/ppermute | solution.py:934
  5.2 23.8 %collective-permute-start.1 = (bf16[768,512]{1,0:T(8,128)(2,1)}, bf16[768,512]{1,0:T(8,128)(2,1)}, u32[]{:S(2)}, u32[]{:S(2)}) collective-permute-start(bf16[768,512]{1,0:T(8,128)(2,1)} %get-tuple-element.86.refs_7_), channel_id=1, source_target_pairs={{0,2},{1,3},{2,0},{3,1},{4,6},{5,7},{6,4},{7,5},{8,10},{9,11},{10,... | collective-permute-start | bytes 2359304 | tf_op jit(solution)/shard_map/ppermute | solution.py:934
  7.7 21.2 %all-to-all-start = ((f32[32,8,128]{2,1,0:T(8,128)}), f32[32,8,128]{2,1,0:T(8,128)}, u32[]{:S(2)}, u32[]{:S(2)}) async-start(f32[32,8,128]{2,1,0:T(8,128)} %get-tuple-element.87), calls=%async_computation | async-start | bytes 262144 | tf_op jit(solution)/shard_map/all_to_all | solution.py:938
  12.8 4.8 %collective-permute-start.2 = (f32[24,128]{1,0:T(8,128)}, f32[24,128]{1,0:T(8,128)}, u32[]{:S(2)}, u32[]{:S(2)}) collective-permute-start(f32[24,128]{1,0:T(8,128)} %get-tuple-element.85.refs_2_), channel_id=1, source_target_pairs={{0,1},{1,0},{2,3},{3,2},{4,5},{5,4},{6,7},{7,6},{8,9},{9,8},{10,11... | collective-permute-start | bytes 36872 | tf_op jit(solution)/shard_map/ppermute | solution.py:934
  13.0 14.8 %collective-permute-start = (f32[24,128]{1,0:T(8,128)}, f32[24,128]{1,0:T(8,128)}, u32[]{:S(2)}, u32[]{:S(2)}) collective-permute-start(f32[24,128]{1,0:T(8,128)} %get-tuple-element.85.refs_2_), channel_id=1, source_target_pairs={{0,2},{1,3},{2,0},{3,1},{4,6},{5,7},{6,4},{7,5},{8,10},{9,11},{10,... | collective-permute-start | bytes 36872 | tf_op jit(solution)/shard_map/ppermute | solution.py:934
  28.9 3.0 %collective-permute-start.6 = (bf16[768,512]{1,0:T(8,128)(2,1)}, bf16[768,512]{1,0:T(8,128)(2,1)}, u32[]{:S(2)}, u32[]{:S(2)}) collective-permute-start(bf16[768,512]{1,0:T(8,128)(2,1)} %collective-permute-done.1.refs_9_), channel_id=1, source_target_pairs={{0,1},{1,0},{2,3},{3,2},{4,5},{5,4},{6,7},{7,6},{8,9},{9,8},{10,11... | collective-permute-start | bytes 2359304 | tf_op jit(solution)/shard_map/ppermute | solution.py:934
  29.0 20.3 %collective-permute-start.4 = (bf16[768,512]{1,0:T(8,128)(2,1)}, bf16[768,512]{1,0:T(8,128)(2,1)}, u32[]{:S(2)}, u32[]{:S(2)}) collective-permute-start(bf16[768,512]{1,0:T(8,128)(2,1)} %get-tuple-element.91.refs_7_), channel_id=1, source_target_pairs={{0,2},{1,3},{2,0},{3,1},{4,6},{5,7},{6,4},{7,5},{8,10},{9,11},{10,... | collective-permute-start | bytes 2359304 | tf_op jit(solution)/shard_map/ppermute | solution.py:934
  30.5 1.5 %collective-permute-start.5 = (f32[24,128]{1,0:T(8,128)}, f32[24,128]{1,0:T(8,128)}, u32[]{:S(2)}, u32[]{:S(2)}) collective-permute-start(f32[24,128]{1,0:T(8,128)} %collective-permute-done.refs_4_), channel_id=1, source_target_pairs={{0,1},{1,0},{2,3},{3,2},{4,5},{5,4},{6,7},{7,6},{8,9},{9,8},{10,11... | collective-permute-start | bytes 36872 | tf_op jit(solution)/shard_map/ppermute | solution.py:934
  42.8 11.9 %all-to-all-start.1 = ((f32[8,8,128]{2,1,0:T(8,128)}), f32[8,8,128]{2,1,0:T(8,128)}, u32[]{:S(2)}, u32[]{:S(2)}) async-start(f32[8,8,128]{2,1,0:T(8,128)} %get-tuple-element.98), calls=%async_computation.1 | async-start | bytes 65536 | tf_op jit(solution)/shard_map/all_to_all | solution.py:938
  47.9 6.8 %collective-permute-start.7 = (bf16[768,512]{1,0:T(8,128)(2,1)}, bf16[768,512]{1,0:T(8,128)(2,1)}, u32[]{:S(2)}, u32[]{:S(2)}) collective-permute-start(bf16[768,512]{1,0:T(8,128)(2,1)} %get-tuple-element.91.refs_7_), channel_id=1, source_target_pairs={{0,1},{1,0},{2,3},{3,2},{4,5},{5,4},{6,7},{7,6},{8,9},{9,8},{10,11... | collective-permute-start | bytes 2359304 | tf_op jit(solution)/shard_map/ppermute | solution.py:934
  54.7 2.6 %collective-permute-start.8 = (bf16[768,512]{1,0:T(8,128)(2,1)}, bf16[768,512]{1,0:T(8,128)(2,1)}, u32[]{:S(2)}, u32[]{:S(2)}) collective-permute-start(bf16[768,512]{1,0:T(8,128)(2,1)} %collective-permute-done.4.refs_9_), channel_id=1, source_target_pairs={{0,1},{1,0},{2,3},{3,2},{4,5},{5,4},{6,7},{7,6},{8,9},{9,8},{10,11... | collective-permute-start | bytes 2359304 | tf_op jit(solution)/shard_map/ppermute | solution.py:934
  75.1 8.9 %collective-permute-start.9 = (bf16[256,512]{1,0:T(8,128)(2,1)}, bf16[256,512]{1,0:T(8,128)(2,1)}, u32[]{:S(2)}, u32[]{:S(2)}) collective-permute-start(bf16[256,512]{1,0:T(8,128)(2,1)} %get-tuple-element.109), channel_id=1, source_target_pairs={{0,4},{4,0},{8,12},{12,8},{16,20},{20,16},{24,28},{28,24},{1,5},{5... | collective-permute-start | bytes 786440 | tf_op jit(solution)/shard_map/ppermute | solution.py:975
  75.6 10.9 %all-to-all-start.2 = ((f32[8,16,128]{2,1,0:T(8,128)}), f32[8,16,128]{2,1,0:T(8,128)}, u32[]{:S(2)}, u32[]{:S(2)}) async-start(f32[8,16,128]{2,1,0:T(8,128)} %get-tuple-element.107), calls=%async_computation.2 | async-start | bytes 131072 | tf_op jit(solution)/shard_map/all_to_all | solution.py:938
  97.7 7.8 %collective-permute-start.12 = (bf16[272,512]{1,0:T(8,128)(2,1)}, bf16[272,512]{1,0:T(8,128)(2,1)}, u32[]{:S(2)}, u32[]{:S(2)}) collective-permute-start(bf16[272,512]{1,0:T(8,128)(2,1)} %get-tuple-element.132), channel_id=1, source_target_pairs={{0,4},{4,0},{8,12},{12,8},{16,20},{20,16},{24,28},{28,24},{1,5},{5... | collective-permute-start | bytes 835592 | tf_op jit(solution)/shard_map/ppermute | solution.py:975
  98.2 5.3 %collective-permute-start.10 = (bf16[128,512]{1,0:T(8,128)(2,1)}, bf16[128,512]{1,0:T(8,128)(2,1)}, u32[]{:S(2)}, u32[]{:S(2)}) collective-permute-start(bf16[128,512]{1,0:T(8,128)(2,1)} %get-tuple-element.113), channel_id=1, source_target_pairs={{0,8},{4,12},{8,0},{12,4},{16,24},{20,28},{24,16},{28,20},{1,9},{5... | collective-permute-start | bytes 393224 | tf_op jit(solution)/shard_map/ppermute | solution.py:975
  107.5 11.8 %collective-permute-start.13 = (bf16[80,512]{1,0:T(8,128)(2,1)}, bf16[80,512]{1,0:T(8,128)(2,1)}, u32[]{:S(2)}, u32[]{:S(2)}) collective-permute-start(bf16[80,512]{1,0:T(8,128)(2,1)} %get-tuple-element.134), channel_id=1, source_target_pairs={{0,8},{4,12},{8,0},{12,4},{16,24},{20,28},{24,16},{28,20},{1,9},{5... | collective-permute-start | bytes 245768 | tf_op jit(solution)/shard_map/ppermute | solution.py:975
  107.8 11.5 %collective-permute-start.14 = (bf16[80,512]{1,0:T(8,128)(2,1)}, bf16[80,512]{1,0:T(8,128)(2,1)}, u32[]{:S(2)}, u32[]{:S(2)}) collective-permute-start(bf16[80,512]{1,0:T(8,128)(2,1)} %get-tuple-element.135), channel_id=1, source_target_pairs={{0,16},{4,20},{8,24},{12,28},{16,0},{20,4},{24,8},{28,12},{1,17},{... | collective-permute-start | bytes 245768 | tf_op jit(solution)/shard_map/ppermute | solution.py:975
  108.7 10.6 %collective-permute-start.15 = (bf16[80,512]{1,0:T(8,128)(2,1)}, bf16[80,512]{1,0:T(8,128)(2,1)}, u32[]{:S(2)}, u32[]{:S(2)}) collective-permute-start(bf16[80,512]{1,0:T(8,128)(2,1)} %get-tuple-element.136), channel_id=1, source_target_pairs={{0,24},{4,28},{8,16},{12,20},{16,8},{20,12},{24,0},{28,4},{1,25},{... | collective-permute-start | bytes 245768 | tf_op jit(solution)/shard_map/ppermute | solution.py:975
  113.8 5.5 %collective-permute-start.11 = (bf16[64,512]{1,0:T(8,128)(2,1)}, bf16[64,512]{1,0:T(8,128)(2,1)}, u32[]{:S(2)}, u32[]{:S(2)}) collective-permute-start(bf16[64,512]{1,0:T(8,128)(2,1)} %get-tuple-element.130), channel_id=1, source_target_pairs={{0,16},{4,20},{8,24},{12,28},{16,0},{20,4},{24,8},{28,12},{1,17},{... | collective-permute-start | bytes 196616 | tf_op jit(solution)/shard_map/ppermute | solution.py:975
  121.2 8.6 %collective-permute-start.21 = (bf16[128,512]{1,0:T(8,128)(2,1)}, bf16[128,512]{1,0:T(8,128)(2,1)}, u32[]{:S(2)}, u32[]{:S(2)}) collective-permute-start(bf16[128,512]{1,0:T(8,128)(2,1)} %get-tuple-element.149.refs_1_), channel_id=1, source_target_pairs={{0,24},{4,28},{8,16},{12,20},{16,8},{20,12},{24,0},{28,4},{1,25},{... | collective-permute-start | bytes 393224 | tf_op jit(solution)/shard_map/ppermute | solution.py:975
  123.4 10.8 %collective-permute-start.19 = (bf16[128,512]{1,0:T(8,128)(2,1)}, bf16[128,512]{1,0:T(8,128)(2,1)}, u32[]{:S(2)}, u32[]{:S(2)}) collective-permute-start(bf16[128,512]{1,0:T(8,128)(2,1)} %get-tuple-element.149.refs_1_), channel_id=1, source_target_pairs={{0,16},{4,20},{8,24},{12,28},{16,0},{20,4},{24,8},{28,12},{1,17},{... | collective-permute-start | bytes 393224 | tf_op jit(solution)/shard_map/ppermute | solution.py:975
  123.4 11.3 %collective-permute-start.17 = (bf16[128,512]{1,0:T(8,128)(2,1)}, bf16[128,512]{1,0:T(8,128)(2,1)}, u32[]{:S(2)}, u32[]{:S(2)}) collective-permute-start(bf16[128,512]{1,0:T(8,128)(2,1)} %get-tuple-element.149.refs_1_), channel_id=1, source_target_pairs={{0,8},{4,12},{8,0},{12,4},{16,24},{20,28},{24,16},{28,20},{1,9},{5... | collective-permute-start | bytes 393224 | tf_op jit(solution)/shard_map/ppermute | solution.py:975
  125.7 14.1 %collective-permute-start.16 = (bf16[128,512]{1,0:T(8,128)(2,1)}, bf16[128,512]{1,0:T(8,128)(2,1)}, u32[]{:S(2)}, u32[]{:S(2)}) collective-permute-start(bf16[128,512]{1,0:T(8,128)(2,1)} %get-tuple-element.149.refs_1_), channel_id=1, source_target_pairs={{0,4},{4,0},{8,12},{12,8},{16,20},{20,16},{24,28},{28,24},{1,5},{5... | collective-permute-start | bytes 393224 | tf_op jit(solution)/shard_map/ppermute | solution.py:975
  129.8 10.0 %collective-permute-start.22 = (bf16[128,512]{1,0:T(8,128)(2,1)}, bf16[128,512]{1,0:T(8,128)(2,1)}, u32[]{:S(2)}, u32[]{:S(2)}) collective-permute-start(bf16[128,512]{1,0:T(8,128)(2,1)} %collective-permute-done.21.refs_7_), channel_id=1, source_target_pairs={{0,4},{4,0},{8,12},{12,8},{16,20},{20,16},{24,28},{28,24},{1,5},{5... | collective-permute-start | bytes 393224 | tf_op jit(solution)/shard_map/ppermute | solution.py:975
  134.2 6.2 %collective-permute-start.20 = (bf16[128,512]{1,0:T(8,128)(2,1)}, bf16[128,512]{1,0:T(8,128)(2,1)}, u32[]{:S(2)}, u32[]{:S(2)}) collective-permute-start(bf16[128,512]{1,0:T(8,128)(2,1)} %collective-permute-done.19.refs_5_), channel_id=1, source_target_pairs={{0,4},{4,0},{8,12},{12,8},{16,20},{20,16},{24,28},{28,24},{1,5},{5... | collective-permute-start | bytes 393224 | tf_op jit(solution)/shard_map/ppermute | solution.py:975
  134.7 7.1 %collective-permute-start.18 = (bf16[128,512]{1,0:T(8,128)(2,1)}, bf16[128,512]{1,0:T(8,128)(2,1)}, u32[]{:S(2)}, u32[]{:S(2)}) collective-permute-start(bf16[128,512]{1,0:T(8,128)(2,1)} %collective-permute-done.17.refs_3_), channel_id=1, source_target_pairs={{0,4},{4,0},{8,12},{12,8},{16,20},{20,16},{24,28},{28,24},{1,5},{5... | collective-permute-start | bytes 393224 | tf_op jit(solution)/shard_map/ppermute | solution.py:975

commit v5 on v4

--- a/solution.py
+++ b/solution.py
@@ -13,7 +13,7 @@
 EPSILON = 1e-05
 F32 = jnp.float32
 LOW = jnp.bfloat16
-PARAM_ROWS = 24
+PARAM_ROWS = 32
 OWN_MEAN = 16
 VMEM_BYTES = 64 * 1024 * 1024
 
@@ -42,6 +42,15 @@
         return body(rows_at(index, size), index, carry)
 
     return lax.fori_loop(first // size, last // size, step, init, unroll=unroll)
+
+
+def blocks_of(first, last, size=16):
+    return [(slice(at, at + size), at // size) for at in range(first, last, size)]
+
+
+def pieces_of(total):
+    size = total // PIECES
+    return [slice(at, at + size) for at in range(0, total, size)]
 
 
 def own_quarter():
@@ -92,7 +101,7 @@
     return moved(re, 1), moved(im, 1)
 
 
-def sweep(drive_ref, rate_re, rate_im, steps, reverse, emit, extra, after=None, unroll=4):
+def sweep(drive_ref, rate_re, rate_im, steps, reverse, emit, extra, after=None, beside=None, unroll=4):
     states = rate_re.shape[1]
     shape = (CHUNKS, states)
     wide_re = jnp.broadcast_to(rate_re, shape)
@@ -100,7 +109,7 @@
 
     def advance(index, re, im):
         place = steps - 1 - index if reverse else index
-        rows = rows_at(place, CHUNKS)
+        rows = slice(place * CHUNKS, (place + 1) * CHUNKS) if isinstance(place, int) else rows_at(place, CHUNKS)
         drive_re = drive_ref[rows, :states]
         drive_im = drive_ref[rows, states:]
         new_re = (wide_re * re + drive_re) - wide_im * im
@@ -127,7 +136,12 @@
     carry = (re, im, extra)
     for piece in range(PIECES):
         size = steps // PIECES
-        carry = lax.fori_loop(piece * size, (piece + 1) * size, second, carry, unroll=unroll)
+        if beside is not None:
+            beside[piece]()
+            for index in range(piece * size, (piece + 1) * size):
+                carry = second(index, carry)
+        else:
+            carry = lax.fori_loop(piece * size, (piece + 1) * size, second, carry, unroll=unroll)
         if after is not None:
             after(PIECES - 1 - piece if reverse else piece)
     return carry[2]
@@ -350,40 +364,55 @@
     return emit
 
 
-def pre_phase(low_ref, c_ref, normed_ref, skip, active_ref, slope_ref, held_ref, after=None):
-    total, full = normed_ref.shape
-    held_ref[:, :full] = dot(low_ref[...], c_ref[...], NN)
-
-    def inner(rows, index, carry):
+def pre_products(low_ref, c_ref, held_ref):
+    total, full = low_ref.shape[0], c_ref.shape[1]
+    for piece in pieces_of(total):
+        held_ref[piece, :full] = dot(low_ref[piece, :], c_ref[...], NN)
+
+
+def pre_piece(piece, held_ref, normed_ref, skip, active_ref, slope_ref):
+    full = normed_ref.shape[1]
+    for rows, _ in blocks_of(piece.start, piece.stop):
         value = held_ref[rows, :full] + skip * normed_ref[rows, :].astype(F32)
         cdf, density = gelu_parts(value)
         active_ref[rows, :] = (value * cdf).astype(LOW)
         slope_ref[rows, :] = (cdf + value * density).astype(slope_ref.dtype)
-        return carry
-
-    for piece in range(PIECES):
-        for_rows(piece * total // PIECES, (piece + 1) * total // PIECES, 16, inner, unroll=4)
-        if after is not None:
-            after(piece)
-
-
-def pre_grad_phase(grad_gated_ref, w_ref, slope_ref, normed_ref, quarter, pre_grad_ref, held_ref, small_ref):
-    total, full = normed_ref.shape
+
+
+def pre_grad_piece(piece, held_ref, slope_ref, pre_grad_ref):
+    full = slope_ref.shape[1]
+    for rows, _ in blocks_of(piece.start, piece.stop):
+        pre_grad_ref[rows, :] = (held_ref[rows, :full] * slope_ref[rows, :].astype(F32)).astype(LOW)
+
+
+def skip_sums(pre_grad_ref, normed_ref, quarter, small_ref):
     own = lanes_at(quarter, 128)
-    held_ref[:, :full] = dot(grad_gated_ref[...], w_ref[...], NN)
 
     def inner(rows, index, carry):
-        pre_grad_ref[rows, :] = (held_ref[rows, :full] * slope_ref[rows, :].astype(F32)).astype(LOW)
         return carry + folded(pre_grad_ref[rows, own].astype(F32) * normed_ref[rows, own].astype(F32))
 
-    small_ref[3:4, 0:128] = column_sum(for_rows(0, total, 16, inner, jnp.zeros((8, 128), F32), unroll=4))
-
-
-def adjoint_phase(pre_grad_ref, c_ref, low_ref, im_lane, drive_own_ref, state, first_row, length, grad_state_ref, grad_driven_ref, small_ref, reverse):
-    total = pre_grad_ref.shape[0]
+    small_ref[3:4, 0:128] = column_sum(for_rows(0, pre_grad_ref.shape[0], 16, inner, jnp.zeros((8, 128), F32), unroll=4))
+
+
+def bias_sums(grad_gated_ref, quarter, small_ref):
+    own, far = lanes_at(quarter, 128), lanes_at(quarter + 4, 128)
+
+    def inner(rows, index, carry):
+        return (
+            carry[0] + folded(grad_gated_ref[rows, own].astype(F32)),
+            carry[1] + folded(grad_gated_ref[rows, far].astype(F32)),
+        )
+
+    zero = jnp.zeros((8, 128), F32)
+    one, two = for_rows(0, grad_gated_ref.shape[0], 16, inner, (zero, zero), unroll=4)
+    small_ref[4:5, 0:128] = column_sum(one)
+    small_ref[5:6, 0:128] = column_sum(two)
+
+
+def adjoint_phase(low_ref, im_lane, drive_own_ref, state, first_row, length, grad_state_ref, grad_driven_ref, small_ref, reverse, beside):
+    total = grad_state_ref.shape[0]
     steps = total // CHUNKS
     states = state.shape[1]
-    grad_state_ref[...] = dot(pre_grad_ref[...], c_ref[...], NT)
     rate_re = state[first_row : first_row + 1, :]
     rate_im = state[first_row + 1 : first_row + 2, :]
     gamma = jnp.broadcast_to(state[first_row + 2 : first_row + 3, :], (CHUNKS, states))
@@ -408,34 +437,44 @@
         return one, two, three
 
     zero = jnp.zeros((8, 128), F32)
-    one, two, three = sweep(grad_state_ref, rate_re, -rate_im, steps, reverse, emit, (zero, zero, zero))
+    one, two, three = sweep(grad_state_ref, rate_re, -rate_im, steps, reverse, emit, (zero, zero, zero), beside=beside)
     small_ref[0:1, 0:128] = column_sum(one)
     small_ref[1:2, 0:128] = column_sum(two)
     small_ref[2:3, 0:128] = column_sum(three)
 
 
-def glu_grads(grads_ref, first, grad_gated_ref, active_ref, quarter):
+def glu_products(grads_ref, first, grad_gated_ref, active_ref, quarter):
     full = active_ref.shape[1]
-    for place in range(2):
+
+    def product(place):
         lanes = pl.ds(pl.multiple_of(place * full + quarter * 128, 128), 128)
         got = dot(grad_gated_ref[:, lanes], active_ref[...], TN)
         grads_ref[first + place * 128 : first + (place + 1) * 128, :] = got.astype(LOW)
 
-
-def state_grads(grads_ref, grad_driven_ref, normed_ref, low_re, low_im, pre_grad_ref, states):
+    return [functools.partial(product, place) for place in range(2)]
+
+
+def output_products(grads_ref, low_re, low_im, pre_grad_ref, states):
     half = states // 4
-    for place, low in enumerate((low_re, low_im)):
+
+    def product(place, low, sign):
+        got = sign * dot(low(), pre_grad_ref[...], TN)[:half, :]
+        grads_ref[2 * half + place * half : 2 * half + (place + 1) * half, :] = got.astype(LOW)
+
+    return [functools.partial(product, 0, low_re, 1.0), functools.partial(product, 1, low_im, -1.0)]
+
+
+def input_products(grads_ref, grad_driven_ref, normed_ref, states):
+    half = states // 4
+    for place in range(2):
         lanes = slice(place * states, place * states + 128)
         got = dot(grad_driven_ref[:, lanes], normed_ref[...], TN)[:half, :]
         grads_ref[place * half : (place + 1) * half, :] = got.astype(LOW)
-        got = dot(low, pre_grad_ref[...], TN)[:half, :]
-        got = got if place == 0 else -got
-        grads_ref[2 * half + place * half : 2 * half + (place + 1) * half, :] = got.astype(LOW)
-
-
-def enter_kernel(length_ref, ins, outs, held_ref):
+
+
+def enter_kernel(length_ref, ins, outs, held_ref, params_ref):
     x, gain, shift, skip, bias, nu, theta, gamma, b, c, w = ins
-    tokens, spread, params, first_out = outs
+    tokens, spread, first_out = outs
     length = length_ref[0]
     width, total = x.ref.shape
     steps = total // CHUNKS
@@ -460,27 +499,34 @@
         return carry
 
     for_rows(0, total, 32, centred, unroll=4)
-    first_out.send(4 * width, each)
     for value in (gain, shift, skip, bias, nu, theta, gamma):
         value.wait()
-    params.ref[...] = jnp.zeros((PARAM_ROWS, width), F32)
+    params_ref[...] = jnp.zeros(params_ref.shape, F32)
     for layer in range(LAYERS):
         first = 5 * layer
-        params.ref[first + GAIN : first + GAIN + 1, :] = gain.ref[layer : layer + 1, :]
-        params.ref[first + SHIFT : first + SHIFT + 1, :] = shift.ref[layer : layer + 1, :]
-        params.ref[first + SKIP : first + SKIP + 1, :] = skip.ref[layer : layer + 1, :]
-        params.ref[first + BIAS_LINEAR : first + BIAS_GATE + 1, :] = bias.ref[layer, :, :]
+        params_ref[first + GAIN : first + GAIN + 1, :] = gain.ref[layer : layer + 1, :]
+        params_ref[first + SHIFT : first + SHIFT + 1, :] = shift.ref[layer : layer + 1, :]
+        params_ref[first + SKIP : first + SKIP + 1, :] = skip.ref[layer : layer + 1, :]
+        params_ref[first + BIAS_LINEAR : first + BIAS_GATE + 1, :] = bias.ref[layer, :, :]
         first = 10 + 3 * layer
         for row, source in enumerate((nu, theta, gamma)):
-            params.ref[first + row : first + row + 1, : source.ref.shape[1]] = source.ref[layer : layer + 1, :]
-    params.ref[OWN_MEAN : OWN_MEAN + 1, :] = mean
-    params.send()
-    b.wait()
-    first_out.send(0, width, source=b.ref.at[0])
-    c.wait()
-    first_out.send(width, width, source=c.ref.at[0])
-    w.wait()
-    first_out.send(2 * width, 2 * width, source=w.ref.at[0])
+            params_ref[first + row : first + row + 1, : source.ref.shape[1]] = source.ref[layer : layer + 1, :]
+    params_ref[OWN_MEAN : OWN_MEAN + 1, :] = mean
+    rest = params_ref[...]
+    first_out.ref[6 * width :, :] = jnp.zeros((32, 4 * width), LOW)
+    for place in range(3):
+        high = rest.astype(LOW)
+        first_out.ref[6 * width : 6 * width + PARAM_ROWS, place * width : (place + 1) * width] = high
+        rest = rest - high.astype(F32)
+    first_out.send(4 * width, 2 * width + 32)
+    send_weights(0, b, c, w, first_out)
+
+
+def send_weights(layer, b, c, w, whole):
+    width = b.ref.shape[1]
+    for value, first, size in ((b, 0, width), (c, width, width), (w, 2 * width, 2 * width)):
+        value.wait()
+        whole.send(first, size, source=value.ref.at[layer])
 
 
 def cotangent_kernel(length_ref, ins, outs, held_ref):
@@ -499,31 +545,32 @@
     def after(piece):
         whole.send_piece(piece)
         if piece == 1:
-            b.wait()
-            later.send(0, width, source=b.ref.at[1])
-            c.wait()
-            later.send(width, width, source=c.ref.at[1])
-            w.wait()
-            later.send(2 * width, 2 * width, source=w.ref.at[1])
+            send_weights(1, b, c, w, later)
 
     from_feature_rows(x, held_ref, steps, emit, 0, after)
     later.send(4 * width, total // PIECES)
 
 
-def start_kernel(length_ref, ins, outs, stats_ref, stream_ref, drive_ref, held_ref, b_ref, c_ref, w_ref, low_ref):
-    sums, params, tokens = ins[0], ins[1:5], ins[5]
-    weights = ins[6:10]
+def start_kernel(length_ref, ins, outs, stats_ref, stream_ref, drive_ref, pre_ref, held_ref, b_ref, c_ref, w_ref, low_ref):
+    sums, tokens, *parts = ins
     feature, state_out, norm, normed, drive_own, low_own, stream, linear_out, gate_out, slope, active, b_out, c_out, w_out, spread = outs
     length, quarter = length_ref[0], own_quarter()
     total, full = active.ref.shape
     steps = total // CHUNKS
     width = full // 4
     lane = lax.broadcasted_iota(jnp.int32, (8, width), 1)
-    tails = [part.wait() for part in params]
-    for place, value in enumerate(tails):
-        feature.ref[:, lanes_at(quarter ^ place, width)] = value[...]
+    tails = []
+    rows_refs = []
+    for part in parts:
+        for piece in (6, 4, 5):
+            part.wait(piece)
+        rows_refs.append(part.ref.at[pl.ds(4 * width, 2 * width + PARAM_ROWS)])
+    for place, part_ref in enumerate(rows_refs):
+        value = sum(part_ref[2 * width :, at * width : (at + 1) * width].astype(F32) for at in range(3))
+        feature.ref[:, lanes_at(quarter ^ place, width)] = value
+        tails.append(value[8:16, :])
     for pair in range(2):
-        early, late = (value[8:16, :] for value in tails[2 * pair : 2 * pair + 2])
+        early, late = tails[2 * pair : 2 * pair + 2]
         logs = jnp.where(lane < 64, early, pltpu.roll(late, 64, 1))
         lanes = slice(pair * width, (pair + 1) * width)
         for layer in range(LAYERS):
@@ -551,13 +598,13 @@
 
     def normal(rows, index, carry):
         keep = keep_rows(index, 16, steps, length)
-        there = pl.ds(pl.multiple_of(4 * width + index * 16 % each, 16), 16)
-        for place, part in enumerate(weights):
+        there = pl.ds(pl.multiple_of(index * 16 % each, 16), 16)
+        for place, part_ref in enumerate(rows_refs):
             lanes = lanes_at(quarter ^ place, width)
             if place == 0:
                 value = tokens.ref[rows, :]
             else:
-                value = part.ref[there, lanes_at(index * 16 // each, width)].astype(F32)
+                value = part_ref[there, lanes_at(index * 16 // each, width)].astype(F32)
                 value = value + feature.ref[OWN_MEAN : OWN_MEAN + 1, lanes]
             stream_ref[rows, lanes] = value
             z = (value - norm.ref[0:1, lanes]) * norm.ref[1:2, lanes]
@@ -565,23 +612,16 @@
             normed.ref[rows, lanes] = jnp.where(keep, z, 0.0).astype(LOW)
         return carry
 
-    for part in weights[1:]:
-        part.wait(4)
-        part.wait(5)
     for piece in range(PIECES):
         tokens.wait(piece)
         for_rows(piece * total // PIECES, (piece + 1) * total // PIECES, 16, normal)
         normed.send_piece(piece)
-    for part in weights:
-        part.wait(0)
-    assemble_states([part.ref.at[0:width] for part in weights], b_ref)
+    assemble_states([part.wait(0).at[0:width] for part in parts], b_ref)
     b_out.send(source=b_ref)
     state = state_out.ref[...]
     states = state.shape[1]
     drive_phase(normed.ref, b_ref, drive_ref, state[2 + GAMMA : 3 + GAMMA, :])
-    for part in weights:
-        part.wait(1)
-    assemble_output([part.ref.at[width : 2 * width] for part in weights], c_ref)
+    assemble_output([part.wait(1).at[width : 2 * width] for part in parts], c_ref)
     c_out.send(source=c_ref)
     store = store_states(low_ref, drive_own.ref)
 
@@ -594,43 +634,44 @@
     drive_own.send()
     low_own.send()
 
-    def after(piece):
-        active.send_piece(piece)
-        slope.send_piece(piece)
-
-    pre_phase(low_ref, c_ref, normed.ref, feature.ref[SKIP : SKIP + 1, :], active.ref, slope.ref, held_ref, after)
-    assemble_glu([part.wait().at[2 * width : 4 * width] for part in weights], w_ref, quarter)
+    assemble_glu([part.wait().at[2 * width : 4 * width] for part in parts], w_ref, quarter)
     w_out.send(source=w_ref)
-    held_ref[...] = dot(active.ref[...], w_ref[...], NT)
-
-    def inner(rows, index, carry):
-        keep = keep_rows(index, 16, steps, length)
-        linear = held_ref[rows, :full] + feature.ref[BIAS_LINEAR : BIAS_LINEAR + 1, :]
-        gate = jax.nn.sigmoid(held_ref[rows, full:] + feature.ref[BIAS_GATE : BIAS_GATE + 1, :])
-        mixed = linear * gate
-        gate_out.ref[rows, :] = gate.astype(LOW)
-        linear_out.ref[rows, :] = (mixed * (1.0 - gate)).astype(LOW)
-        moved = stream_ref[rows, :] + jnp.where(keep, mixed, 0.0)
-        stream.ref[rows, :] = moved
-        kept = jnp.where(keep, moved, 0.0)
-        return carry[0] + folded(kept), carry[1] + folded(kept * kept)
-
-    zero = jnp.zeros((8, full), F32)
-    carry = (zero, zero)
-    for piece in range(PIECES):
-        carry = for_rows(piece * total // PIECES, (piece + 1) * total // PIECES, 16, inner, carry)
+    skip = feature.ref[SKIP : SKIP + 1, :]
+    bias_linear = feature.ref[BIAS_LINEAR : BIAS_LINEAR + 1, :]
+    bias_gate = feature.ref[BIAS_GATE : BIAS_GATE + 1, :]
+    pre_products(low_ref, c_ref, pre_ref)
+    for piece in pieces_of(total):
+        pre_piece(piece, pre_ref, normed.ref, skip, active.ref, slope.ref)
+        held_ref[piece, :] = dot(active.ref[piece, :], w_ref[...], NT)
+    active.send()
+    slope.send()
+    plain, square = jnp.zeros((8, full), F32), jnp.zeros((8, full), F32)
+    for place, piece in enumerate(pieces_of(total)):
+        for rows, index in blocks_of(piece.start, piece.stop):
+            keep = keep_rows(index, 16, steps, length)
+            linear = held_ref[rows, :full] + bias_linear
+            gate = jax.nn.sigmoid(held_ref[rows, full:] + bias_gate)
+            mixed = linear * gate
+            gate_out.ref[rows, :] = gate.astype(LOW)
+            linear_out.ref[rows, :] = (mixed * (1.0 - gate)).astype(LOW)
+            moved = stream_ref[rows, :] + jnp.where(keep, mixed, 0.0)
+            stream.ref[rows, :] = moved
+            kept = jnp.where(keep, moved, 0.0)
+            plain += folded(kept)
+            square += folded(kept * kept)
         for out in (stream, linear_out, gate_out):
-            out.send_piece(piece)
+            out.send_piece(place)
+    carry = plain, square
     spread_rows(narrowed([column_sum(carry[0]), column_sum(carry[1])], width), spread)
 
 
 def middle_kernel(
     length_ref, ins, outs,
-    small_ref, b_ref, c_ref, w_ref, normed_ref, drive_ref, drive_own_ref, low_ref, slope_ref, active_ref, held_ref,
+    small_ref, b_ref, c_ref, w_ref, normed_ref, drive_ref, drive_own_ref, low_ref, slope_ref, active_ref, held_ref, pre_ref, mixed_ref,
     order_ref, up_ref, grad_gated_ref, pre_grad_ref, grad_driven_ref, grads_ref,
 ):
     sums, norm0, feature_in, state_in, stream, up_own = ins[:6]
-    weights = ins[6:]
+    parts = ins[6:]
     result, base, spread, norm, *shares = outs
     length, quarter = length_ref[0], own_quarter()
     total, full = stream.ref.shape
@@ -652,87 +693,85 @@
     shift = feature[5 + SHIFT : 6 + SHIFT, :]
     skip = feature[5 + SKIP : 6 + SKIP, :]
 
-    def normal(rows, index, carry):
-        keep = keep_rows(index, 16, steps, length)
-        z = (stream.ref[rows, :] - centre) * inv_dev
-        normed_ref[rows, :] = jnp.where(keep, z * gain + shift, 0.0).astype(LOW)
-        return carry
-
-    for piece in range(PIECES):
-        stream.wait(piece)
-        for_rows(piece * total // PIECES, (piece + 1) * total // PIECES, 16, normal, unroll=4)
-    for part in weights:
+    for part in parts:
+        part.wait(0)
+    assemble_states([part.ref.at[0:width] for part in parts], b_ref)
+    gamma = state[5 + GAMMA : 6 + GAMMA, :]
+    gammas = jnp.concatenate([gamma, gamma], axis=1)
+    for place, piece in enumerate(pieces_of(total)):
+        stream.wait(place)
+        for rows, index in blocks_of(piece.start, piece.stop):
+            z = (stream.ref[rows, :] - centre) * inv_dev
+            normed_ref[rows, :] = jnp.where(keep_rows(index, 16, steps, length), z * gain + shift, 0.0).astype(LOW)
+        drive_ref[piece, :] = dot(normed_ref[piece, :], b_ref[...], NT) * gammas
+    sweep(drive_ref, state[5:6, :], state[6:7, :], steps, True, store_states(low_ref, drive_own_ref), 0)
+    for part in parts:
         part.wait()
-    assemble_states([part.ref.at[0:width] for part in weights], b_ref)
-    assemble_output([part.ref.at[width : 2 * width] for part in weights], c_ref)
-    assemble_glu([part.ref.at[2 * width : 4 * width] for part in weights], w_ref, quarter)
-    drive_phase(normed_ref, b_ref, drive_ref, state[5 + GAMMA : 6 + GAMMA, :])
-    sweep(drive_ref, state[5:6, :], state[6:7, :], steps, True, store_states(low_ref, drive_own_ref), 0)
-    pre_phase(low_ref, c_ref, normed_ref, skip, active_ref, slope_ref, held_ref)
-    held_ref[...] = dot(active_ref[...], w_ref[...], NT)
+    assemble_output([part.ref.at[width : 2 * width] for part in parts], c_ref)
+    assemble_glu([part.ref.at[2 * width : 4 * width] for part in parts], w_ref, quarter)
     up_own.wait()
-    own, own_far = lanes_at(quarter, width), lanes_at(quarter + 4, width)
+    own = lanes_at(quarter, width)
 
     def spread_up(rows, index, carry):
         up_ref[rows, own] = up_own.ref[rows, :]
         return carry
 
     for_rows(0, total, 16, spread_up, unroll=4)
-    for piece in range(PIECES):
-        for place, part in enumerate(weights[1:], 1):
-            lanes = lanes_at(quarter ^ place, width)
-            size = total // PIECES
-            up_ref[piece * size : (piece + 1) * size, lanes] = part.ref[4 * width :, piece * width : (piece + 1) * width].astype(F32)
-
-    def inner(rows, index, carry):
-        keep = keep_rows(index, 16, steps, length)
-        linear = held_ref[rows, :full] + feature[5 + BIAS_LINEAR : 6 + BIAS_LINEAR, :]
-        gate = jax.nn.sigmoid(held_ref[rows, full:] + feature[5 + BIAS_GATE : 6 + BIAS_GATE, :])
-        mixed = linear * gate
-        up = jnp.where(keep, up_ref[rows, :], 0.0)
-        grad_gated_ref[rows, :full] = (up * gate).astype(LOW)
-        grad_gated_ref[rows, full:] = (up * mixed * (1.0 - gate)).astype(LOW)
-        held_ref[rows, :full] = jnp.where(keep, mixed, 0.0)
-        return (
-            carry[0] + folded(grad_gated_ref[rows, own].astype(F32)),
-            carry[1] + folded(grad_gated_ref[rows, own_far].astype(F32)),
-        )
-
-    zero = jnp.zeros((8, width), F32)
-    one, two = for_rows(0, total, 16, inner, (zero, zero))
+    for place, piece in enumerate(pieces_of(total)):
+        for other in range(1, 4):
+            lanes = lanes_at(quarter ^ other, width)
+            up_ref[piece, lanes] = parts[other].ref[4 * width :, place * width : (place + 1) * width].astype(F32)
+    bias_linear = feature[5 + BIAS_LINEAR : 6 + BIAS_LINEAR, :]
+    bias_gate = feature[5 + BIAS_GATE : 6 + BIAS_GATE, :]
+    pre_products(low_ref, c_ref, pre_ref)
+    for piece in pieces_of(total):
+        pre_piece(piece, pre_ref, normed_ref, skip, active_ref, slope_ref)
+        held_ref[piece, :] = dot(active_ref[piece, :], w_ref[...], NT)
+    for piece in pieces_of(total):
+        for rows, index in blocks_of(piece.start, piece.stop):
+            keep = keep_rows(index, 16, steps, length)
+            linear = held_ref[rows, :full] + bias_linear
+            gate = jax.nn.sigmoid(held_ref[rows, full:] + bias_gate)
+            mixed = linear * gate
+            up = jnp.where(keep, up_ref[rows, :], 0.0)
+            grad_gated_ref[rows, :full] = (up * gate).astype(LOW)
+            grad_gated_ref[rows, full:] = (up * mixed * (1.0 - gate)).astype(LOW)
+            mixed_ref[rows, :] = jnp.where(keep, mixed, 0.0)
+        pre_ref[piece, :] = dot(grad_gated_ref[piece, :], w_ref[...], NN)
+    for piece in pieces_of(total):
+        pre_grad_piece(piece, pre_ref, slope_ref, pre_grad_ref)
+        drive_ref[piece, :] = dot(pre_grad_ref[piece, :], c_ref[...], NT)
     small_ref[...] = jnp.zeros_like(small_ref)
-    small_ref[4:5, 0:128] = column_sum(one)
-    small_ref[5:6, 0:128] = column_sum(two)
-    to_feature_rows(lambda rows, index: stream.ref[rows, own] + held_ref[rows, own], order_ref, result, steps)
-    pre_grad_phase(grad_gated_ref, w_ref, slope_ref, normed_ref, quarter, pre_grad_ref, held_ref, small_ref)
+    bias_sums(grad_gated_ref, quarter, small_ref)
+    skip_sums(pre_grad_ref, normed_ref, quarter, small_ref)
+    to_feature_rows(lambda rows, index: stream.ref[rows, own] + mixed_ref[rows, own], order_ref, result, steps)
     adjoint_phase(
-        pre_grad_ref, c_ref, low_ref, states, drive_own_ref, state, 5, length, drive_ref, grad_driven_ref, small_ref, False
-    )
-    held_ref[:, :full] = dot(grad_driven_ref[...], b_ref[...], NN)
+        low_ref, states, drive_own_ref, state, 5, length, drive_ref, grad_driven_ref, small_ref, False,
+        glu_products(grads_ref, 2 * width, grad_gated_ref, active_ref, quarter)
+        + output_products(grads_ref, lambda: low_ref[:, 0:128], lambda: low_ref[:, states : states + 128], pre_grad_ref, states),
+    )
     scale = inv_dev * gain
-
-    def back(rows, index, carry):
-        grad = held_ref[rows, :full] + skip * pre_grad_ref[rows, :].astype(F32)
-        z = (stream.ref[rows, :] - centre) * inv_dev
-        base.ref[rows, :] = scale * grad + up_ref[rows, :]
-        return carry[0] + folded(grad), carry[1] + folded(grad * z)
-
-    zero = jnp.zeros((8, full), F32)
-    carry = (zero, zero)
-    for piece in range(PIECES):
-        carry = for_rows(piece * total // PIECES, (piece + 1) * total // PIECES, 16, back, carry)
-        base.send_piece(piece)
-    sent = narrowed([column_sum(carry[0]), column_sum(carry[1])], width)
+    for piece in pieces_of(total):
+        pre_ref[piece, :] = dot(grad_driven_ref[piece, :], b_ref[...], NN)
+    plain, scaled = jnp.zeros((8, full), F32), jnp.zeros((8, full), F32)
+    for place, piece in enumerate(pieces_of(total)):
+        for rows, _ in blocks_of(piece.start, piece.stop):
+            grad = pre_ref[rows, :] + skip * pre_grad_ref[rows, :].astype(F32)
+            z = (stream.ref[rows, :] - centre) * inv_dev
+            base.ref[rows, :] = scale * grad + up_ref[rows, :]
+            plain += folded(grad)
+            scaled += folded(grad * z)
+        base.send_piece(place)
+    input_products(grads_ref, grad_driven_ref, normed_ref, states)
+    sent = narrowed([column_sum(plain), column_sum(scaled)], width)
     spread_rows(jnp.concatenate([sent, small_ref[:, 0:width]], axis=0), spread)
-    glu_grads(grads_ref, 2 * width, grad_gated_ref, active_ref, quarter)
-    state_grads(grads_ref, grad_driven_ref, normed_ref, low_ref[:, 0:128], low_ref[:, states : states + 128], pre_grad_ref, states)
     send_halves(grads_ref, shares, 0)
 
 
 def last_kernel(
-    length_ref, ins, outs, held_ref, grad_state_ref, grad_gated_ref, pre_grad_ref, grad_driven_ref, small_ref, row_ref, grads_ref, pack_ref, low_ref
+    length_ref, ins, outs, held_ref, grad_state_ref, grad_gated_ref, pre_grad_ref, grad_driven_ref, small_ref, up_ref, grads_ref, pack_ref, low_ref
 ):
-    (sums, norm1, feature_in, state_in, norm0, stream, base, gate, linear, w, slope, normed, active, c, low, drive_own, b, x) = ins
+    (sums, norm1, feature_in, state_in, norm0, stream, base, gate, linear, w, slope, c, normed, active, low, drive_own, b, x) = ins
     kept, sent, up_out, grad_out = outs
     length, quarter = length_ref[0], own_quarter()
     total, full = stream.ref.shape
@@ -749,42 +788,46 @@
     level = scale * whole[0:1, :] / counted
     tilt = scale * inv_dev * whole[1:2, :] / counted
 
-    def top(rows, index, carry):
-        keep = keep_rows(index, 16, steps, length)
-        up = base.ref[rows, :] - jnp.where(keep, level + (stream.ref[rows, :] - centre) * tilt, 0.0)
-        row_ref[...] = up
-        up_out.ref[rows, :] = row_ref[:, own]
-        up = jnp.where(keep, up, 0.0)
-        grad_gated_ref[rows, :full] = (up * gate.ref[rows, :].astype(F32)).astype(LOW)
-        grad_gated_ref[rows, full:] = (up * linear.ref[rows, :].astype(F32)).astype(LOW)
-        far = pl.ds(pl.multiple_of(full + quarter * width, width), width)
-        return (
-            carry[0] + folded(grad_gated_ref[rows, own].astype(F32)),
-            carry[1] + folded(grad_gated_ref[rows, far].astype(F32)),
-        )
-
-    zero = jnp.zeros((8, width), F32)
-    carry = (zero, zero)
-    for piece in range(PIECES):
+    for place, piece in enumerate(pieces_of(total)):
         for value in (stream, base, gate, linear):
-            value.wait(piece)
-        carry = for_rows(piece * total // PIECES, (piece + 1) * total // PIECES, 16, top, carry)
-        up_out.send_piece(piece)
+            value.wait(place)
+        if place == 0:
+            w.wait()
+        for rows, index in blocks_of(piece.start, piece.stop):
+            keep = keep_rows(index, 16, steps, length)
+            up = base.ref[rows, :] - jnp.where(keep, level + (stream.ref[rows, :] - centre) * tilt, 0.0)
+            up_ref[rows, :] = up
+            up = jnp.where(keep, up, 0.0)
+            grad_gated_ref[rows, :full] = (up * gate.ref[rows, :].astype(F32)).astype(LOW)
+            grad_gated_ref[rows, full:] = (up * linear.ref[rows, :].astype(F32)).astype(LOW)
+        held_ref[piece, :] = dot(grad_gated_ref[piece, :], w.ref[...], NN)
+    for value in (slope, c):
+        value.wait()
+    for piece in pieces_of(total):
+        pre_grad_piece(piece, held_ref, slope.ref, pre_grad_ref)
+        grad_state_ref[piece, :] = dot(pre_grad_ref[piece, :], c.ref[...], NT)
     small_ref[...] = jnp.zeros_like(small_ref)
-    small_ref[4:5, 0:128] = column_sum(carry[0])
-    small_ref[5:6, 0:128] = column_sum(carry[1])
-    for value in (w, slope, normed):
+
+    def own_up(rows, index, carry):
+        up_out.ref[rows, :] = up_ref[rows, own]
+        return carry
+
+    for_rows(0, total, 16, own_up, unroll=4)
+    up_out.send()
+    for value in (normed, active, low, drive_own):
         value.wait()
-    pre_grad_phase(grad_gated_ref, w.ref, slope.ref, normed.ref, quarter, pre_grad_ref, held_ref, small_ref)
-    for value in (active, c, low, drive_own):
-        value.wait()
-    glu_grads(grads_ref, 2 * width, grad_gated_ref, active.ref, quarter)
+    bias_sums(grad_gated_ref, quarter, small_ref)
+    skip_sums(pre_grad_ref, normed.ref, quarter, small_ref)
     adjoint_phase(
-        pre_grad_ref, c.ref, low.ref, 128, drive_own.ref, state, 2, length, grad_state_ref, grad_driven_ref, small_ref, True
+        low.ref, 128, drive_own.ref, state, 2, length, grad_state_ref, grad_driven_ref, small_ref, True,
+        glu_products(grads_ref, 2 * width, grad_gated_ref, active.ref, quarter)
+        + output_products(grads_ref, lambda: low.ref[:, :128], lambda: low.ref[:, 128:], pre_grad_ref, state.shape[1]),
     )
     b.wait()
     x.wait()
     held_ref[:, :width] = dot(grad_driven_ref[...], b.ref[:, own], NN)
+    input_products(grads_ref, grad_driven_ref, normed.ref, state.shape[1])
+    zero = jnp.zeros((8, width), F32)
     centre0, inv_dev0 = norm0.wait()[0:1, own], norm0.ref[1:2, own]
     skip = feature[SKIP : SKIP + 1, own]
 
@@ -798,7 +841,6 @@
     grad_out.send()
     small_ref[6:7, 0:width] = column_sum(plain)
     small_ref[7:8, 0:width] = column_sum(scaled)
-    state_grads(grads_ref, grad_driven_ref, normed.ref, low.ref[:, :128], low.ref[:, 128:], pre_grad_ref, state.shape[1])
     pack_ref[...] = jnp.zeros_like(pack_ref)
     for place in range(8):
         pack_ref[place // 4 : place // 4 + 1, place % 4 * width : (place % 4 + 1) * width] = small_ref[place : place + 1, 0:width]
@@ -830,9 +872,10 @@
 
 
 def pair_kernel(length_ref, ins, outs, sum_ref, pack_ref):
-    kept, other = ins
-    kept.wait()
-    other.wait()
+    kept, other, *last = ins
+    back, *outs = outs
+    for value in ins:
+        value.wait()
     half = kept.ref.shape[0] - 16
     share = half // len(outs)
     small = kept.ref[half:, :].astype(F32) + other.ref[half:, :].astype(F32)
@@ -844,25 +887,25 @@
     for place, out in enumerate(outs):
         out.send(0, share, source=sum_ref.at[rows_at((lax.axis_index("dp") >> 1) ^ place, share)])
         out.send(share, 16, source=pack_ref)
+    for piece in range(0, share, 16):
+        at = slice(piece, piece + 16)
+        back.ref[at, :] = (last[0].ref[at, :].astype(F32) + last[1].ref[at, :].astype(F32)).astype(LOW)
 
 
 def share_kernel(length_ref, ins, outs):
-    *blocks, kept, other = ins
     out, small = outs
-    share = kept.ref.shape[0]
+    share = out.ref.shape[0]
     for value in ins:
         value.wait()
     for piece in range(0, share, 16):
         at = slice(piece, piece + 16)
-        value = blocks[0].ref[at, :].astype(F32)
-        for block in blocks[1:]:
+        value = ins[0].ref[at, :].astype(F32)
+        for block in ins[1:]:
             value += block.ref[at, :].astype(F32)
         out.ref[at, :] = value.astype(LOW)
-        value = kept.ref[at, :].astype(F32) + other.ref[at, :].astype(F32)
-        out.ref[share + piece : share + piece + 16, :] = value.astype(LOW)
     out.send()
-    value = blocks[0].ref[share:, :].astype(F32)
-    for block in blocks[1:]:
+    value = ins[0].ref[share:, :].astype(F32)
+    for block in ins[1:]:
         value += block.ref[share:, :].astype(F32)
     small.ref[...] = value[0:8, :] + value[8:16, :]
 
@@ -911,16 +954,17 @@
 
 def widen_kernel(length_ref, ins, outs, held_ref):
     half = outs[0].ref.shape[1]
-    groups = len(ins)
-    share = ins[0].ref.shape[0] // 2
+    groups = len(ins) // 2
+    share = ins[0].ref.shape[0]
     stages = groups.bit_length() - 1
-    for place, value in enumerate(ins):
-        value.wait()
-        owner = lax.axis_index("dp") ^ place
-        index = sum((owner >> stage & 1) << (stages - 1 - stage) for stage in range(stages))
-        for layer, at in ((0, (owner & 1) * (groups // 2) + (owner >> 1)), (1, index)):
-            held_ref[layer, rows_at(at, share), :] = value.ref[layer * share : (layer + 1) * share, :].astype(F32)
-    for layer in range(LAYERS):
+    for layer, values in ((1, ins[:groups]), (0, ins[groups:])):
+        for place, value in enumerate(values):
+            value.wait()
+            owner = lax.axis_index("dp") ^ place
+            at = (owner & 1) * (groups // 2) + (owner >> 1)
+            if layer == 1:
+                at = sum((owner >> stage & 1) << (stages - 1 - stage) for stage in range(stages))
+            held_ref[layer, rows_at(at, share), :] = value.ref[...].astype(F32)
         for out, first, size in zip(outs, (0, half, 2 * half), (half, half, 2 * half)):
             out.send(layer, 1, source=held_ref.at[pl.ds(layer, 1), pl.ds(first, size)])
 
@@ -989,30 +1033,31 @@
 
     b_weight, c_weight = b_weight.reshape(LAYERS, width, full), c_weight.reshape(LAYERS, width, full)
     glu_weight = glu_weight.reshape(LAYERS, 2 * width, full)
-    tokens, sums, params, first = call(
+    tokens, sums, first = call(
         enter_kernel,
         (
             shape(total, width),
             shape(dp_size * state_size, 8, width),
-            shape(PARAM_ROWS, width),
-            shape(6 * width, full, dtype=LOW),
+            shape(6 * width + PARAM_ROWS, full, dtype=LOW),
         ),
-        [pltpu.VMEM((total, width), F32)],
+        [pltpu.VMEM((total, width), F32), pltpu.VMEM((PARAM_ROWS, width), F32)],
         (lengths, inputs[0], bn_gain, bn_bias, skip_weight, glu_bias, nu_log, theta_log, gamma_log, b_weight, c_weight, glu_weight),
         "enter",
         pieces={1: piece},
         axes={1: 1},
         late=(9, 10, 11),
     )
-    near = [swap(value, 1, sharers) for value in (params, first)]
-    far = [swap(value, 2, sharers) for value in (params, first)]
+    near, far = swap(first, 1, sharers), swap(first, 2, sharers)
     sums = across(sums, ("dp", "state"))
     if sharers > 1:
         sums = sums.reshape(dp_size * 4, sharers, 8, width)[:, 0]
     cotangent, tokens = lax.optimization_barrier((cotangent, tokens))
     up_own, later = call(
         cotangent_kernel,
-        (shape(total, width), shape(6 * width, full, dtype=LOW)),
+        (
+            shape(total, width),
+            shape(6 * width, full, dtype=LOW),
+        ),
         [pltpu.VMEM((total, width), F32)],
         (lengths, cotangent[0], b_weight, c_weight, glu_weight),
         "cotangent",
@@ -1020,10 +1065,9 @@
         axes={1: 1},
         late=(2, 3, 4),
     )
-    *far, near[0], near[1], sums, later = lax.optimization_barrier((*far, *near, sums, later))
-    diagonal = [swap(value, 1, sharers) for value in far]
+    near, far, sums, later = lax.optimization_barrier((near, far, sums, later))
+    parts = (first, near, far, swap(far, 1, sharers))
     later_far = swap(later, 2, sharers)
-    parts = list(zip((params, first), near, far, diagonal))
     feature, state, norm0, normed0, drive0, low0, stream1, linear0, gate0, slope0, active0, b_all, c_all, w_all, sums1 = call(
         start_kernel,
         (
@@ -1047,21 +1091,23 @@
             pltpu.VMEM((8, full), F32),
             pltpu.VMEM((total, full), F32),
             pltpu.VMEM((total, 2 * states), F32),
+            pltpu.VMEM((total, full), F32),
             pltpu.VMEM((total, 2 * full), F32),
             pltpu.VMEM((2 * states, full), LOW),
             pltpu.VMEM((2 * states, full), LOW),
             pltpu.VMEM((2 * full, full), LOW),
             pltpu.VMEM((total, 2 * states), LOW),
         ],
-        (lengths, sums, *parts[0], tokens, *parts[1]),
+        (lengths, sums, tokens, *parts),
         "start",
-        pieces={6: piece} | {place: width for place in (7, 8, 9, 10)},
+        pieces={2: piece} | {place: width for place in (3, 4, 5, 6)},
         order=(4, 5),
         bare=(11, 12, 13),
         flops=1e9,
     )
     sums1 = across(sums1, "dp")
     later_far, sums1 = lax.optimization_barrier((later_far, sums1))
+    later_parts = (later, swap(later, 1, sharers), later_far, swap(later_far, 1, sharers))
     result, base, bn1, norm1, *halves1 = call(
         middle_kernel,
         (
@@ -1084,6 +1130,8 @@
             pltpu.VMEM((total, full), F32),
             pltpu.VMEM((total, full), LOW),
             pltpu.VMEM((total, 2 * full), F32),
+            pltpu.VMEM((total, full), F32),
+            pltpu.VMEM((total, full), F32),
             pltpu.VMEM((total, width), F32),
             pltpu.VMEM((total, full), F32),
             pltpu.VMEM((total, 2 * full), LOW),
@@ -1091,10 +1139,9 @@
             pltpu.VMEM((total, 2 * states), LOW),
             pltpu.VMEM((4 * width, full), LOW),
         ],
-        (lengths, sums1, norm0, feature, state, stream1, up_own, later, swap(later, 1, sharers), later_far,
-         swap(later_far, 1, sharers)),
+        (lengths, sums1, norm0, feature, state, stream1, up_own, *later_parts),
         "middle",
-        pieces={5: piece},
+        pieces={5: piece} | {place: width for place in (7, 8, 9, 10)},
         late=(6, 7, 8, 9, 10),
         bare=(4, 5),
         flops=1e9,
@@ -1119,47 +1166,48 @@
             pltpu.VMEM((total, full), LOW),
             pltpu.VMEM((total, 2 * states), LOW),
             pltpu.VMEM((8, full), F32),
-            pltpu.VMEM((16, full), F32),
+            pltpu.VMEM((total, full), F32),
             pltpu.VMEM((4 * width, full), LOW),
             pltpu.VMEM((16, full), F32),
             pltpu.VMEM((16, full), LOW),
         ],
-        (lengths, bn1, norm1, feature, state, norm0, stream1, base, gate0, linear0, w_all, slope0, normed0, active0, c_all, low0,
+        (lengths, bn1, norm1, feature, state, norm0, stream1, base, gate0, linear0, w_all, slope0, c_all, normed0, active0, low0,
          drive0, b_all, tokens),
         "last",
         bare=(0, 1),
         pieces={6: piece, 7: piece, 8: piece, 9: piece},
-        late=tuple(range(10, 19)),
+        late=tuple(range(11, 19)),
         flops=1e11,
     )
+    *halves1, kept0, sent0 = lax.optimization_barrier((*halves1, kept0, sent0))
     sent0 = exchange(sent0, 1)
-    *halves1, kept0 = lax.optimization_barrier((*halves1, kept0))
     for stage in range(1, stages):
         if stage > 1:
             halves1[1] = exchange(halves1[1], 1 << stage)
         if stage < stages - 1:
             halves1 = list(add(halves1, stage))
-    blocks = call(
+    back1, *blocks = call(
         pair_kernel,
-        (shape(share + 16, full, dtype=LOW),) * (dp_size // 2),
+        (shape(share, full, dtype=LOW),) + (shape(share + 16, full, dtype=LOW),) * (dp_size // 2),
         [pltpu.VMEM((2 * width, full), LOW), pltpu.VMEM((16, full), LOW)],
-        (lengths, kept0, sent0),
+        (lengths, kept0, sent0, *halves1),
         "pair",
-        bare=tuple(range(dp_size // 2)),
+        bare=tuple(range(1, 1 + dp_size // 2)),
     )
     blocks = [blocks[0]] + [exchange(blocks[place], 2 * place) for place in range(1, dp_size // 2)]
-    halves1[1], *blocks = lax.optimization_barrier((halves1[1], *blocks))
-    back, small0 = call(
+    back0, small0 = call(
         share_kernel,
-        (shape(2 * share, full, dtype=LOW), shape(8, full)),
+        (shape(share, full, dtype=LOW), shape(8, full)),
         [],
-        (lengths, *blocks, *halves1),
+        (lengths, *blocks),
         "share",
     )
-    backs = {0: back, 1: exchange(back, 1)}
-    for place in range(2, dp_size, 2):
-        backs[place] = exchange(back, place)
-        backs[place + 1] = exchange(backs[place], 1)
+
+    def to_all(value):
+        got = [value] + [exchange(value, place) for place in range(2, dp_size, 2)]
+        return [each for first in got for each in (first, exchange(first, 1))]
+
+    backs = to_all(back1) + to_all(back0)
     grad_nu, grad_theta, grad_gamma, grad_skip, grad_bias, grad_gain, grad_shift, grad_inputs = call(
         finish_kernel,
         (
@@ -1180,7 +1228,7 @@
         widen_kernel,
         (shape(LAYERS, width, full), shape(LAYERS, width, full), shape(LAYERS, 2 * width, full)),
         [pltpu.VMEM((LAYERS, 4 * width, full), F32)],
-        (lengths, *(backs[place] for place in range(dp_size))),
+        (lengths, *backs),
         "widen",
         bare=(0, 1, 2),
     )

time: 145 us -> 135 us (0.931)
  waiting for transfers between devices: 48 us -> 36.6 us
  starting transfers between devices: 35.2 us -> 43.4 us
  Pallas kernels: 59.9 us -> 53.2 us
    ppermute x14 -> x21, waiting for transfers between devices: 25.2 us -> 12.4 us  [exchange(): return lax.ppermute(value, 'dp', [(i, i ^ bit) for i in range(dp_size)])]
    ppermute x14 -> x21, starting transfers between devices: 14.3 us -> 24.6 us  [exchange(): return lax.ppermute(value, 'dp', [(i, i ^ bit) for i in range(dp_size)])]
    all_to_all x3, waiting for transfers between devices: 7.22 us -> 17.1 us  [across(): return lax.all_to_all(value, axes, 0, 0, tiled=True)]
    ppermute x9 -> x6, waiting for transfers between devices: 15.6 us -> 7.1 us  [swap(): return lax.ppermute(value, 'state', pairs)]
    pallas_call x11, Pallas kernels: 59.9 us -> 53.2 us  [call(): pl.pallas_call(body, out_shape=tuple(outs), in_specs=[pl.BlockSpec(memory...]
    ppermute x9 -> x6, starting transfers between devices: 6.6 us -> 4.51 us  [swap(): return lax.ppermute(value, 'state', pairs)]
  transfers between devices with their start and end apart: 26 -> 30, of which waited for: 15 -> 11; matrix products, arithmetic and copies ran while one was open for 0% -> 0% of each run, Pallas kernels for 14% -> 23%
where the time goes in v5:
time: 135 us
  Pallas kernels  53.2 us (39%)
  starting transfers between devices  43.4 us (32%)
  waiting for transfers between devices  36.6 us (27%)
  between operations  1.66 us (1%)
    pallas_call x11, Pallas kernels, call(): pl.pallas_call(body, out_shape=tuple(outs), in_specs=[pl.BlockSpec(memory...  53.2 us
    ppermute x21, starting transfers between devices, exchange(): return lax.ppermute(value, 'dp', [(i, i ^ bit) for i in range(dp_size)])  24.6 us
    all_to_all x3, waiting for transfers between devices, across(): return lax.all_to_all(value, axes, 0, 0, tiled=True)  17.1 us
    all_to_all x3, starting transfers between devices, across(): return lax.all_to_all(value, axes, 0, 0, tiled=True)  14.2 us
    ppermute x21, waiting for transfers between devices, exchange(): return lax.ppermute(value, 'dp', [(i, i ^ bit) for i in range(dp_size)])  12.4 us
    ppermute x6, waiting for transfers between devices, swap(): return lax.ppermute(value, 'state', pairs)  7.1 us
    ppermute x6, starting transfers between devices, swap(): return lax.ppermute(value, 'state', pairs)  4.51 us
  transfers between devices with their start and end apart: 30, of which 11 were waited for; matrix products, arithmetic and copies ran while one was open for 0% of the time, Pallas kernels for 23%

profile of v5, /device:TPU:0, one launch (start us, length us, event | category | flops | bytes accessed | tf_op | source)
XLA Modules:
  0.0 134.9 jit_solution(11951168945972355922)
XLA Ops:
  1.3 3.3 %enter.1 = (f32[1024,128]{1,0:T(8,128)}, f32[32,8,128]{2,1,0:T(8,128)}, bf16[800,512]{1,0:T(8,128)(2,1)}) custom-call(s32[1]{0:T(128)S(6)} %copy.25.refs_0_, f32[128,1024]{1,0:T(8,128)} %bitcast.16, f32[2,128]{1,0:T(2,128)} %refs_2_.1, f32[2,128]{1,0:T(2,128)} %refs_3_.1, f32[2,128]{1,0:T(2,128)} %refs_4_.1, f32[2,2,128]{2,1,0:T(2,128)} %refs_5_.2, ...), custom_call_target="tpu_custom_call" | custom-call | tf_op jit(solution)/shard_map/enter/pallas_call | solution.py:248
  4.6 3.0 %collective-permute-start.1 = (bf16[800,512]{1,0:T(8,128)(2,1)}, bf16[800,512]{1,0:T(8,128)(2,1)}, u32[]{:S(2)}, u32[]{:S(2)}) collective-permute-start(bf16[800,512]{1,0:T(8,128)(2,1)} %get-tuple-element.79.refs_3_), channel_id=1, source_target_pairs={{0,2},{1,3},{2,0},{3,1},{4,6},{5,7},{6,4},{7,5},{8,10},{9,11},{10,... | collective-permute-start | bytes 2457608 | tf_op jit(solution)/shard_map/ppermute | solution.py:978
  7.6 5.2 %all-to-all-start = ((f32[32,8,128]{2,1,0:T(8,128)}), f32[32,8,128]{2,1,0:T(8,128)}, u32[]{:S(2)}, u32[]{:S(2)}) async-start(f32[32,8,128]{2,1,0:T(8,128)} %get-tuple-element.80), calls=%async_computation | async-start | bytes 262144 | tf_op jit(solution)/shard_map/all_to_all | solution.py:982
  12.8 2.9 %cotangent.1 = (f32[1024,128]{1,0:T(8,128)}, bf16[768,512]{1,0:T(8,128)(2,1)}) custom-call(s32[1]{0:T(128)S(6)} %copy.25.refs_0_, f32[128,1024]{1,0:T(8,128)} %bitcast.17, bf16[2,128,512]{2,1,0:T(8,128)(2,1)} %bitcast.13, bf16[2,128,512]{2,1,0:T(8,128)(2,1)} %bitcast.15, bf16[2,256,512]{2,1,0:T(8,128)(2,1)} %bitcast.11), custom_call_target="tpu_custom_call" | custom-call | tf_op jit(solution)/shard_map/cotangent/pallas_call | solution.py:248
  15.7 13.1 %all-to-all-done.refs_1_ = f32[32,8,128]{2,1,0:T(8,128)} async-done(((f32[32,8,128]{2,1,0:T(8,128)}), f32[32,8,128]{2,1,0:T(8,128)}, u32[]{:S(2)}, u32[]{:S(2)}) %all-to-all-start) | async-done | bytes 131104 | tf_op jit(solution)/shard_map/all_to_all | solution.py:982
  28.8 1.5 %collective-permute-start.2 = (bf16[768,512]{1,0:T(8,128)(2,1)}, bf16[768,512]{1,0:T(8,128)(2,1)}, u32[]{:S(2)}, u32[]{:S(2)}) collective-permute-start(bf16[768,512]{1,0:T(8,128)(2,1)} %get-tuple-element.84.refs_7_), channel_id=1, source_target_pairs={{0,2},{1,3},{2,0},{3,1},{4,6},{5,7},{6,4},{7,5},{8,10},{9,11},{10,... | collective-permute-start | bytes 2359304 | tf_op jit(solution)/shard_map/ppermute | solution.py:978
  30.3 1.2 collective-permute-done.3.refs_6_
  31.5 9.4 %start.1 = (f32[32,512]{1,0:T(8,128)}, f32[8,256]{1,0:T(8,128)}, f32[8,512]{1,0:T(8,128)}, bf16[1024,512]{1,0:T(8,128)(2,1)}, f32[1024,256]{1,0:T(8,128)}, /*ind...) custom-call(s32[1]{0:T(128)S(6)} %copy.25.refs_0_, ...), custom_call_target="tpu_custom_call" | custom-call | flops 1000000000 | tf_op jit(solution)/shard_map/start/pallas_call | solution.py:248
  40.9 4.9 %all-to-all-start.1 = ((f32[8,8,128]{2,1,0:T(8,128)}), f32[8,8,128]{2,1,0:T(8,128)}, u32[]{:S(2)}, u32[]{:S(2)}) async-start(f32[8,8,128]{2,1,0:T(8,128)} %get-tuple-element.89), calls=%async_computation.1 | async-start | bytes 65536 | tf_op jit(solution)/shard_map/all_to_all | solution.py:982
  45.8 3.3 %collective-permute-done.2.refs_9_ = bf16[768,512]{1,0:T(8,128)(2,1)} collective-permute-done((bf16[768,512]{1,0:T(8,128)(2,1)}, bf16[768,512]{1,0:T(8,128)(2,1)}, u32[]{:S(2)}, u32[]{:S(2)}) %collective-permute-start.2) | collective-permute-done | bytes 786464 | tf_op jit(solution)/shard_map/ppermute | solution.py:978
  49.1 3.5 %all-to-all-done.1.refs_1_ = f32[8,8,128]{2,1,0:T(8,128)} async-done(((f32[8,8,128]{2,1,0:T(8,128)}), f32[8,8,128]{2,1,0:T(8,128)}, u32[]{:S(2)}, u32[]{:S(2)}) %all-to-all-start.1) | async-done | bytes 32800 | tf_op jit(solution)/shard_map/all_to_all | solution.py:982
  52.6 2.6 %collective-permute-done.5.refs_10_ = bf16[768,512]{1,0:T(8,128)(2,1)} collective-permute-done((bf16[768,512]{1,0:T(8,128)(2,1)}, bf16[768,512]{1,0:T(8,128)(2,1)}, u32[]{:S(2)}, u32[]{:S(2)}) %collective-permute-start.5) | collective-permute-done | bytes 786464 | tf_op jit(solution)/shard_map/ppermute | solution.py:978
  55.2 14.3 %middle.1 = (f32[128,1024]{1,0:T(8,128)}, f32[1024,512]{1,0:T(8,128)}, f32[8,16,128]{2,1,0:T(8,128)}, f32[8,512]{1,0:T(8,128)}, bf16[256,512]{1,0:T(8,128)(2,1)}, /*index=5*/bf16[256,512]{1,0:T(8,128)(2,1)}) custom-call(s32[1]{0:T(128)S(6)} %copy.25.refs_0_, f32[8,8,128]{2,1,0:T(8,128)} %all-to-all-done.1.refs_1_, ...), custom_call_target="tpu_custom_call" | custom-call | flops 1000000000 | tf_op jit(solution)/shard_map/middle/pallas_call | solution.py:248
  69.5 0.5 collective-permute-start.6
  70.0 4.2 %all-to-all-start.2 = ((f32[8,16,128]{2,1,0:T(8,128)}), f32[8,16,128]{2,1,0:T(8,128)}, u32[]{:S(2)}, u32[]{:S(2)}) async-start(f32[8,16,128]{2,1,0:T(8,128)} %get-tuple-element.98), calls=%async_computation.2 | async-start | bytes 131072 | tf_op jit(solution)/shard_map/all_to_all | solution.py:982
  74.2 4.2 %collective-permute-done.6.refs_2_ = bf16[256,512]{1,0:T(8,128)(2,1)} collective-permute-done((bf16[256,512]{1,0:T(8,128)(2,1)}, bf16[256,512]{1,0:T(8,128)(2,1)}, u32[]{:S(2)}, u32[]{:S(2)}) %collective-permute-start.6) | collective-permute-done | bytes 262176 | tf_op jit(solution)/shard_map/ppermute | solution.py:1019
  78.4 1.9 %add.2 = (bf16[128,512]{1,0:T(8,128)(2,1)}, bf16[128,512]{1,0:T(8,128)(2,1)}) custom-call(s32[1]{0:T(128)S(6)} %copy.25.refs_0_, bf16[256,512]{1,0:T(8,128)(2,1)} %get-tuple-element.99.refs_1_, bf16[256,512]{1,0:T(8,128)(2,1)} %collective-permute-done.6.refs_2_), custom_call_target="tpu_custom_call" | custom-call | tf_op jit(solution)/shard_map/add/pallas_call | solution.py:248
  80.3 0.6 all-to-all-done.2.refs_1_.refs_2_
  80.9 0.2 collective-permute-start.7
  81.1 9.4 %last.1 = (bf16[272,512]{1,0:T(8,128)(2,1)}, bf16[272,512]{1,0:T(8,128)(2,1)}, f32[1024,128]{1,0:T(8,128)}, f32[1024,128]{1,0:T(8,128)}) custom-call(s32[1]{0:T(128)S(6)} %copy.25.refs_0_, f32[8,16,128]{2,1,0:T(8,128)} %all-to-all-done.2.refs_1_.refs_2_, f32[8,512]{1,0:T(8,128)} %get-tuple-element.106.refs_2_, f32[32,512]{1,0:T(8,128)} %get-tuple-element.92.refs_3_.refs_4_, ...), custom_call_target="tpu_custom_call" | custom-call | flops 99999997952 | tf_op jit(solution)/shard_map/last/pallas_call | solution.py:248
  90.6 1.1 collective-permute-start.8
  91.6 1.8 %add.3 = (bf16[64,512]{1,0:T(8,128)(2,1)}, bf16[64,512]{1,0:T(8,128)(2,1)}) custom-call(s32[1]{0:T(128)S(6)} %copy.25.refs_0_, bf16[128,512]{1,0:T(8,128)(2,1)} %get-tuple-element.122.refs_1_, bf16[128,512]{1,0:T(8,128)(2,1)} %collective-permute-done.7.refs_2_), custom_call_target="tpu_custom_call" | custom-call | tf_op jit(solution)/shard_map/add/pallas_call | solution.py:248
  93.4 0.8 collective-permute-start.9
  94.2 4.8 %collective-permute-done.9.refs_4_ = bf16[64,512]{1,0:T(8,128)(2,1)} collective-permute-done((bf16[64,512]{1,0:T(8,128)(2,1)}, bf16[64,512]{1,0:T(8,128)(2,1)}, u32[]{:S(2)}, u32[]{:S(2)}) %collective-permute-start.9) | collective-permute-done | bytes 65568 | tf_op jit(solution)/shard_map/ppermute | solution.py:1019
  99.0 2.2 %pair.1 = (bf16[64,512]{1,0:T(8,128)(2,1)}, bf16[80,512]{1,0:T(8,128)(2,1)}, bf16[80,512]{1,0:T(8,128)(2,1)}, bf16[80,512]{1,0:T(8,128)(2,1)}, bf16[80,512]{1,0:T(8,128)(2,1)}) custom-call(s32[1]{0:T(128)S(6)} %copy.25.refs_0_, bf16[272,512]{1,0:T(8,128)(2,1)} %get-tuple-element.120.refs_1_, bf16[272,512]{1,0:T(8,128)(2,1)} %collective-permute-done.8.refs_2_, ...), custom_call_target="tpu_custom_call" | custom-call | tf_op jit(solution)/shard_map/pair/pallas_call | solution.py:248
  101.1 1.9 %collective-permute-start.18 = (bf16[64,512]{1,0:T(8,128)(2,1)}, bf16[64,512]{1,0:T(8,128)(2,1)}, u32[]{:S(2)}, u32[]{:S(2)}) collective-permute-start(bf16[64,512]{1,0:T(8,128)(2,1)} %get-tuple-element.136.refs_1_), channel_id=1, source_target_pairs={{0,24},{4,28},{8,16},{12,20},{16,8},{20,12},{24,0},{28,4},{1,25},{... | collective-permute-start | bytes 196616 | tf_op jit(solution)/shard_map/ppermute | solution.py:1019
  103.0 0.9 collective-permute-start.16
  103.9 1.7 %collective-permute-start.10 = (bf16[80,512]{1,0:T(8,128)(2,1)}, bf16[80,512]{1,0:T(8,128)(2,1)}, u32[]{:S(2)}, u32[]{:S(2)}) collective-permute-start(bf16[80,512]{1,0:T(8,128)(2,1)} %get-tuple-element.127), channel_id=1, source_target_pairs={{0,8},{4,12},{8,0},{12,4},{16,24},{20,28},{24,16},{28,20},{1,9},{5... | collective-permute-start | bytes 245768 | tf_op jit(solution)/shard_map/ppermute | solution.py:1019
  105.6 0.3 collective-permute-start.11
  105.9 2.4 %collective-permute-start.12 = (bf16[80,512]{1,0:T(8,128)(2,1)}, bf16[80,512]{1,0:T(8,128)(2,1)}, u32[]{:S(2)}, u32[]{:S(2)}) collective-permute-start(bf16[80,512]{1,0:T(8,128)(2,1)} %get-tuple-element.129), channel_id=1, source_target_pairs={{0,24},{4,28},{8,16},{12,20},{16,8},{20,12},{24,0},{28,4},{1,25},{... | collective-permute-start | bytes 245768 | tf_op jit(solution)/shard_map/ppermute | solution.py:1019
  108.3 2.3 %collective-permute-start.14 = (bf16[64,512]{1,0:T(8,128)(2,1)}, bf16[64,512]{1,0:T(8,128)(2,1)}, u32[]{:S(2)}, u32[]{:S(2)}) collective-permute-start(bf16[64,512]{1,0:T(8,128)(2,1)} %get-tuple-element.136.refs_1_), channel_id=1, source_target_pairs={{0,8},{4,12},{8,0},{12,4},{16,24},{20,28},{24,16},{28,20},{1,9},{5... | collective-permute-start | bytes 196616 | tf_op jit(solution)/shard_map/ppermute | solution.py:1019
  110.6 2.6 %collective-permute-done.16.refs_5_ = bf16[64,512]{1,0:T(8,128)(2,1)} collective-permute-done((bf16[64,512]{1,0:T(8,128)(2,1)}, bf16[64,512]{1,0:T(8,128)(2,1)}, u32[]{:S(2)}, u32[]{:S(2)}) %collective-permute-start.16) | collective-permute-done | bytes 65568 | tf_op jit(solution)/shard_map/ppermute | solution.py:1019
  113.2 1.7 %collective-permute-start.13 = (bf16[64,512]{1,0:T(8,128)(2,1)}, bf16[64,512]{1,0:T(8,128)(2,1)}, u32[]{:S(2)}, u32[]{:S(2)}) collective-permute-start(bf16[64,512]{1,0:T(8,128)(2,1)} %get-tuple-element.136.refs_1_), channel_id=1, source_target_pairs={{0,4},{4,0},{8,12},{12,8},{16,20},{20,16},{24,28},{28,24},{1,5},{5... | collective-permute-start | bytes 196616 | tf_op jit(solution)/shard_map/ppermute | solution.py:1019
  114.9 0.4 collective-permute-start.19
  115.3 1.7 %collective-permute-start.17 = (bf16[64,512]{1,0:T(8,128)(2,1)}, bf16[64,512]{1,0:T(8,128)(2,1)}, u32[]{:S(2)}, u32[]{:S(2)}) collective-permute-start(bf16[64,512]{1,0:T(8,128)(2,1)} %collective-permute-done.16.refs_5_), channel_id=1, source_target_pairs={{0,4},{4,0},{8,12},{12,8},{16,20},{20,16},{24,28},{28,24},{1,5},{5... | collective-permute-start | bytes 196616 | tf_op jit(solution)/shard_map/ppermute | solution.py:1019
  116.9 1.8 %share.1 = (bf16[64,512]{1,0:T(8,128)(2,1)}, f32[8,512]{1,0:T(8,128)}) custom-call(s32[1]{0:T(128)S(6)} %copy.25.refs_0_, bf16[80,512]{1,0:T(8,128)(2,1)} %get-tuple-element.126.refs_1_, bf16[80,512]{1,0:T(8,128)(2,1)} %collective-permute-done.10.refs_2_, bf16[80,512]{1,0:T(8,128)(2,1)} %collective-permute-done.11.refs_3_, ...), custom_call_target="tpu_custom_call" | custom-call | tf_op jit(solution)/shard_map/share/pallas_call | solution.py:248
  118.7 0.7 collective-permute-start.25
  119.4 0.1 collective-permute-start.23
  119.5 3.7 %collective-permute-start.21 = (bf16[64,512]{1,0:T(8,128)(2,1)}, bf16[64,512]{1,0:T(8,128)(2,1)}, u32[]{:S(2)}, u32[]{:S(2)}) collective-permute-start(bf16[64,512]{1,0:T(8,128)(2,1)} %get-tuple-element.137.refs_9_), channel_id=1, source_target_pairs={{0,8},{4,12},{8,0},{12,4},{16,24},{20,28},{24,16},{28,20},{1,9},{5... | collective-permute-start | bytes 196616 | tf_op jit(solution)/shard_map/ppermute | solution.py:1019
  123.2 0.4 collective-permute-start.15
  123.6 1.7 %collective-permute-start.20 = (bf16[64,512]{1,0:T(8,128)(2,1)}, bf16[64,512]{1,0:T(8,128)(2,1)}, u32[]{:S(2)}, u32[]{:S(2)}) collective-permute-start(bf16[64,512]{1,0:T(8,128)(2,1)} %get-tuple-element.137.refs_9_), channel_id=1, source_target_pairs={{0,4},{4,0},{8,12},{12,8},{16,20},{20,16},{24,28},{28,24},{1,5},{5... | collective-permute-start | bytes 196616 | tf_op jit(solution)/shard_map/ppermute | solution.py:1019
  125.2 0.1 collective-permute-done.25.refs_15_
  125.3 0.3 collective-permute-start.26
  125.6 0.7 collective-permute-done.23.refs_13_
  126.3 1.0 collective-permute-start.24
  127.3 1.0 collective-permute-start.22
  128.3 3.6 %finish.1 = (f32[2,64]{1,0:T(2,128)}, f32[2,64]{1,0:T(2,128)}, f32[2,64]{1,0:T(2,128)}, f32[2,128]{1,0:T(2,128)}, f32[2,2,128]{2,1,0:T(2,128)}, /*index=5*/f32[2...) custom-call(s32[1]{0:T(128)S(6)} %copy.25.refs_0_, f32[8,512]{1,0:T(8,128)} %get-tuple-element.130.refs_1_, ...), custom_call_target="tpu_custom_call" | custom-call | tf_op jit(solution)/shard_map/finish/pallas_call | solution.py:248
  132.0 2.7 %widen.1 = (f32[2,128,512]{2,1,0:T(8,128)}, f32[2,128,512]{2,1,0:T(8,128)}, f32[2,256,512]{2,1,0:T(8,128)}) custom-call(s32[1]{0:T(128)S(6)} %copy.25.refs_0_, bf16[64,512]{1,0:T(8,128)(2,1)} %get-tuple-element.136.refs_1_, bf16[64,512]{1,0:T(8,128)(2,1)} %collective-permute-done.13.refs_2_, bf16[64,512]{1,0:T(8,128)(2,1)} %collective-permute-done.14.refs_3_, ...), custom_call_target="tpu_custom_call" | custom-call | tf_op jit(solution)/shard_map/widen/pallas_call | solution.py:248
  (23 shorter events, 0.1 us)
Async XLA Ops:
  4.6 24.2 %collective-permute-start.1 = (bf16[800,512]{1,0:T(8,128)(2,1)}, bf16[800,512]{1,0:T(8,128)(2,1)}, u32[]{:S(2)}, u32[]{:S(2)}) collective-permute-start(bf16[800,512]{1,0:T(8,128)(2,1)} %get-tuple-element.79.refs_3_), channel_id=1, source_target_pairs={{0,2},{1,3},{2,0},{3,1},{4,6},{5,7},{6,4},{7,5},{8,10},{9,11},{10,... | collective-permute-start | bytes 2457608 | tf_op jit(solution)/shard_map/ppermute | solution.py:978
  7.6 21.2 %collective-permute-start = (bf16[800,512]{1,0:T(8,128)(2,1)}, bf16[800,512]{1,0:T(8,128)(2,1)}, u32[]{:S(2)}, u32[]{:S(2)}) collective-permute-start(bf16[800,512]{1,0:T(8,128)(2,1)} %get-tuple-element.79.refs_3_), channel_id=1, source_target_pairs={{0,1},{1,0},{2,3},{3,2},{4,5},{5,4},{6,7},{7,6},{8,9},{9,8},{10,11... | collective-permute-start | bytes 2457608 | tf_op jit(solution)/shard_map/ppermute | solution.py:978
  7.6 21.2 %all-to-all-start = ((f32[32,8,128]{2,1,0:T(8,128)}), f32[32,8,128]{2,1,0:T(8,128)}, u32[]{:S(2)}, u32[]{:S(2)}) async-start(f32[32,8,128]{2,1,0:T(8,128)} %get-tuple-element.80), calls=%async_computation | async-start | bytes 262144 | tf_op jit(solution)/shard_map/all_to_all | solution.py:982
  28.8 2.7 %collective-permute-start.3 = (bf16[800,512]{1,0:T(8,128)(2,1)}, bf16[800,512]{1,0:T(8,128)(2,1)}, u32[]{:S(2)}, u32[]{:S(2)}) collective-permute-start(bf16[800,512]{1,0:T(8,128)(2,1)} %collective-permute-done.1.refs_5_), channel_id=1, source_target_pairs={{0,1},{1,0},{2,3},{3,2},{4,5},{5,4},{6,7},{7,6},{8,9},{9,8},{10,11... | collective-permute-start | bytes 2457608 | tf_op jit(solution)/shard_map/ppermute | solution.py:978
  28.8 20.3 %collective-permute-start.2 = (bf16[768,512]{1,0:T(8,128)(2,1)}, bf16[768,512]{1,0:T(8,128)(2,1)}, u32[]{:S(2)}, u32[]{:S(2)}) collective-permute-start(bf16[768,512]{1,0:T(8,128)(2,1)} %get-tuple-element.84.refs_7_), channel_id=1, source_target_pairs={{0,2},{1,3},{2,0},{3,1},{4,6},{5,7},{6,4},{7,5},{8,10},{9,11},{10,... | collective-permute-start | bytes 2359304 | tf_op jit(solution)/shard_map/ppermute | solution.py:978
  40.9 11.7 %all-to-all-start.1 = ((f32[8,8,128]{2,1,0:T(8,128)}), f32[8,8,128]{2,1,0:T(8,128)}, u32[]{:S(2)}, u32[]{:S(2)}) async-start(f32[8,8,128]{2,1,0:T(8,128)} %get-tuple-element.89), calls=%async_computation.1 | async-start | bytes 65536 | tf_op jit(solution)/shard_map/all_to_all | solution.py:982
  45.8 6.8 %collective-permute-start.4 = (bf16[768,512]{1,0:T(8,128)(2,1)}, bf16[768,512]{1,0:T(8,128)(2,1)}, u32[]{:S(2)}, u32[]{:S(2)}) collective-permute-start(bf16[768,512]{1,0:T(8,128)(2,1)} %get-tuple-element.84.refs_7_), channel_id=1, source_target_pairs={{0,1},{1,0},{2,3},{3,2},{4,5},{5,4},{6,7},{7,6},{8,9},{9,8},{10,11... | collective-permute-start | bytes 2359304 | tf_op jit(solution)/shard_map/ppermute | solution.py:978
  52.5 2.6 %collective-permute-start.5 = (bf16[768,512]{1,0:T(8,128)(2,1)}, bf16[768,512]{1,0:T(8,128)(2,1)}, u32[]{:S(2)}, u32[]{:S(2)}) collective-permute-start(bf16[768,512]{1,0:T(8,128)(2,1)} %collective-permute-done.2.refs_9_), channel_id=1, source_target_pairs={{0,1},{1,0},{2,3},{3,2},{4,5},{5,4},{6,7},{7,6},{8,9},{9,8},{10,11... | collective-permute-start | bytes 2359304 | tf_op jit(solution)/shard_map/ppermute | solution.py:978
  69.5 8.9 %collective-permute-start.6 = (bf16[256,512]{1,0:T(8,128)(2,1)}, bf16[256,512]{1,0:T(8,128)(2,1)}, u32[]{:S(2)}, u32[]{:S(2)}) collective-permute-start(bf16[256,512]{1,0:T(8,128)(2,1)} %get-tuple-element.100), channel_id=1, source_target_pairs={{0,4},{4,0},{8,12},{12,8},{16,20},{20,16},{24,28},{28,24},{1,5},{5... | collective-permute-start | bytes 786440 | tf_op jit(solution)/shard_map/ppermute | solution.py:1019
  70.0 10.9 %all-to-all-start.2 = ((f32[8,16,128]{2,1,0:T(8,128)}), f32[8,16,128]{2,1,0:T(8,128)}, u32[]{:S(2)}, u32[]{:S(2)}) async-start(f32[8,16,128]{2,1,0:T(8,128)} %get-tuple-element.98), calls=%async_computation.2 | async-start | bytes 131072 | tf_op jit(solution)/shard_map/all_to_all | solution.py:982
  80.9 9.6 %collective-permute-start.7 = (bf16[128,512]{1,0:T(8,128)(2,1)}, bf16[128,512]{1,0:T(8,128)(2,1)}, u32[]{:S(2)}, u32[]{:S(2)}) collective-permute-start(bf16[128,512]{1,0:T(8,128)(2,1)} %get-tuple-element.104), channel_id=1, source_target_pairs={{0,8},{4,12},{8,0},{12,4},{16,24},{20,28},{24,16},{28,20},{1,9},{5... | collective-permute-start | bytes 393224 | tf_op jit(solution)/shard_map/ppermute | solution.py:1019
  90.6 8.4 %collective-permute-start.8 = (bf16[272,512]{1,0:T(8,128)(2,1)}, bf16[272,512]{1,0:T(8,128)(2,1)}, u32[]{:S(2)}, u32[]{:S(2)}) collective-permute-start(bf16[272,512]{1,0:T(8,128)(2,1)} %get-tuple-element.121), channel_id=1, source_target_pairs={{0,4},{4,0},{8,12},{12,8},{16,20},{20,16},{24,28},{28,24},{1,5},{5... | collective-permute-start | bytes 835592 | tf_op jit(solution)/shard_map/ppermute | solution.py:1019
  93.4 5.6 %collective-permute-start.9 = (bf16[64,512]{1,0:T(8,128)(2,1)}, bf16[64,512]{1,0:T(8,128)(2,1)}, u32[]{:S(2)}, u32[]{:S(2)}) collective-permute-start(bf16[64,512]{1,0:T(8,128)(2,1)} %get-tuple-element.125), channel_id=1, source_target_pairs={{0,16},{4,20},{8,24},{12,28},{16,0},{20,4},{24,8},{28,12},{1,17},{... | collective-permute-start | bytes 196616 | tf_op jit(solution)/shard_map/ppermute | solution.py:1019
  101.1 7.2 %collective-permute-start.18 = (bf16[64,512]{1,0:T(8,128)(2,1)}, bf16[64,512]{1,0:T(8,128)(2,1)}, u32[]{:S(2)}, u32[]{:S(2)}) collective-permute-start(bf16[64,512]{1,0:T(8,128)(2,1)} %get-tuple-element.136.refs_1_), channel_id=1, source_target_pairs={{0,24},{4,28},{8,16},{12,20},{16,8},{20,12},{24,0},{28,4},{1,25},{... | collective-permute-start | bytes 196616 | tf_op jit(solution)/shard_map/ppermute | solution.py:1019
  103.0 10.2 %collective-permute-start.16 = (bf16[64,512]{1,0:T(8,128)(2,1)}, bf16[64,512]{1,0:T(8,128)(2,1)}, u32[]{:S(2)}, u32[]{:S(2)}) collective-permute-start(bf16[64,512]{1,0:T(8,128)(2,1)} %get-tuple-element.136.refs_1_), channel_id=1, source_target_pairs={{0,16},{4,20},{8,24},{12,28},{16,0},{20,4},{24,8},{28,12},{1,17},{... | collective-permute-start | bytes 196616 | tf_op jit(solution)/shard_map/ppermute | solution.py:1019
  103.9 11.0 %collective-permute-start.10 = (bf16[80,512]{1,0:T(8,128)(2,1)}, bf16[80,512]{1,0:T(8,128)(2,1)}, u32[]{:S(2)}, u32[]{:S(2)}) collective-permute-start(bf16[80,512]{1,0:T(8,128)(2,1)} %get-tuple-element.127), channel_id=1, source_target_pairs={{0,8},{4,12},{8,0},{12,4},{16,24},{20,28},{24,16},{28,20},{1,9},{5... | collective-permute-start | bytes 245768 | tf_op jit(solution)/shard_map/ppermute | solution.py:1019
  105.6 9.7 %collective-permute-start.11 = (bf16[80,512]{1,0:T(8,128)(2,1)}, bf16[80,512]{1,0:T(8,128)(2,1)}, u32[]{:S(2)}, u32[]{:S(2)}) collective-permute-start(bf16[80,512]{1,0:T(8,128)(2,1)} %get-tuple-element.128), channel_id=1, source_target_pairs={{0,16},{4,20},{8,24},{12,28},{16,0},{20,4},{24,8},{28,12},{1,17},{... | collective-permute-start | bytes 245768 | tf_op jit(solution)/shard_map/ppermute | solution.py:1019
  105.9 11.0 %collective-permute-start.12 = (bf16[80,512]{1,0:T(8,128)(2,1)}, bf16[80,512]{1,0:T(8,128)(2,1)}, u32[]{:S(2)}, u32[]{:S(2)}) collective-permute-start(bf16[80,512]{1,0:T(8,128)(2,1)} %get-tuple-element.129), channel_id=1, source_target_pairs={{0,24},{4,28},{8,16},{12,20},{16,8},{20,12},{24,0},{28,4},{1,25},{... | collective-permute-start | bytes 245768 | tf_op jit(solution)/shard_map/ppermute | solution.py:1019
  108.3 11.1 %collective-permute-start.14 = (bf16[64,512]{1,0:T(8,128)(2,1)}, bf16[64,512]{1,0:T(8,128)(2,1)}, u32[]{:S(2)}, u32[]{:S(2)}) collective-permute-start(bf16[64,512]{1,0:T(8,128)(2,1)} %get-tuple-element.136.refs_1_), channel_id=1, source_target_pairs={{0,8},{4,12},{8,0},{12,4},{16,24},{20,28},{24,16},{28,20},{1,9},{5... | collective-permute-start | bytes 196616 | tf_op jit(solution)/shard_map/ppermute | solution.py:1019
  113.2 6.3 %collective-permute-start.13 = (bf16[64,512]{1,0:T(8,128)(2,1)}, bf16[64,512]{1,0:T(8,128)(2,1)}, u32[]{:S(2)}, u32[]{:S(2)}) collective-permute-start(bf16[64,512]{1,0:T(8,128)(2,1)} %get-tuple-element.136.refs_1_), channel_id=1, source_target_pairs={{0,4},{4,0},{8,12},{12,8},{16,20},{20,16},{24,28},{28,24},{1,5},{5... | collective-permute-start | bytes 196616 | tf_op jit(solution)/shard_map/ppermute | solution.py:1019
  114.9 8.3 %collective-permute-start.19 = (bf16[64,512]{1,0:T(8,128)(2,1)}, bf16[64,512]{1,0:T(8,128)(2,1)}, u32[]{:S(2)}, u32[]{:S(2)}) collective-permute-start(bf16[64,512]{1,0:T(8,128)(2,1)} %collective-permute-done.18.refs_7_), channel_id=1, source_target_pairs={{0,4},{4,0},{8,12},{12,8},{16,20},{20,16},{24,28},{28,24},{1,5},{5... | collective-permute-start | bytes 196616 | tf_op jit(solution)/shard_map/ppermute | solution.py:1019
  115.3 8.3 %collective-permute-start.17 = (bf16[64,512]{1,0:T(8,128)(2,1)}, bf16[64,512]{1,0:T(8,128)(2,1)}, u32[]{:S(2)}, u32[]{:S(2)}) collective-permute-start(bf16[64,512]{1,0:T(8,128)(2,1)} %collective-permute-done.16.refs_5_), channel_id=1, source_target_pairs={{0,4},{4,0},{8,12},{12,8},{16,20},{20,16},{24,28},{28,24},{1,5},{5... | collective-permute-start | bytes 196616 | tf_op jit(solution)/shard_map/ppermute | solution.py:1019
  118.7 6.6 %collective-permute-start.25 = (bf16[64,512]{1,0:T(8,128)(2,1)}, bf16[64,512]{1,0:T(8,128)(2,1)}, u32[]{:S(2)}, u32[]{:S(2)}) collective-permute-start(bf16[64,512]{1,0:T(8,128)(2,1)} %get-tuple-element.137.refs_9_), channel_id=1, source_target_pairs={{0,24},{4,28},{8,16},{12,20},{16,8},{20,12},{24,0},{28,4},{1,25},{... | collective-permute-start | bytes 196616 | tf_op jit(solution)/shard_map/ppermute | solution.py:1019
  119.4 6.9 %collective-permute-start.23 = (bf16[64,512]{1,0:T(8,128)(2,1)}, bf16[64,512]{1,0:T(8,128)(2,1)}, u32[]{:S(2)}, u32[]{:S(2)}) collective-permute-start(bf16[64,512]{1,0:T(8,128)(2,1)} %get-tuple-element.137.refs_9_), channel_id=1, source_target_pairs={{0,16},{4,20},{8,24},{12,28},{16,0},{20,4},{24,8},{28,12},{1,17},{... | collective-permute-start | bytes 196616 | tf_op jit(solution)/shard_map/ppermute | solution.py:1019
  119.5 7.8 %collective-permute-start.21 = (bf16[64,512]{1,0:T(8,128)(2,1)}, bf16[64,512]{1,0:T(8,128)(2,1)}, u32[]{:S(2)}, u32[]{:S(2)}) collective-permute-start(bf16[64,512]{1,0:T(8,128)(2,1)} %get-tuple-element.137.refs_9_), channel_id=1, source_target_pairs={{0,8},{4,12},{8,0},{12,4},{16,24},{20,28},{24,16},{28,20},{1,9},{5... | collective-permute-start | bytes 196616 | tf_op jit(solution)/shard_map/ppermute | solution.py:1019
  123.2 8.7 %collective-permute-start.15 = (bf16[64,512]{1,0:T(8,128)(2,1)}, bf16[64,512]{1,0:T(8,128)(2,1)}, u32[]{:S(2)}, u32[]{:S(2)}) collective-permute-start(bf16[64,512]{1,0:T(8,128)(2,1)} %collective-permute-done.14.refs_3_), channel_id=1, source_target_pairs={{0,4},{4,0},{8,12},{12,8},{16,20},{20,16},{24,28},{28,24},{1,5},{5... | collective-permute-start | bytes 196616 | tf_op jit(solution)/shard_map/ppermute | solution.py:1019
  123.6 8.4 %collective-permute-start.20 = (bf16[64,512]{1,0:T(8,128)(2,1)}, bf16[64,512]{1,0:T(8,128)(2,1)}, u32[]{:S(2)}, u32[]{:S(2)}) collective-permute-start(bf16[64,512]{1,0:T(8,128)(2,1)} %get-tuple-element.137.refs_9_), channel_id=1, source_target_pairs={{0,4},{4,0},{8,12},{12,8},{16,20},{20,16},{24,28},{28,24},{1,5},{5... | collective-permute-start | bytes 196616 | tf_op jit(solution)/shard_map/ppermute | solution.py:1019
  125.3 6.7 %collective-permute-start.26 = (bf16[64,512]{1,0:T(8,128)(2,1)}, bf16[64,512]{1,0:T(8,128)(2,1)}, u32[]{:S(2)}, u32[]{:S(2)}) collective-permute-start(bf16[64,512]{1,0:T(8,128)(2,1)} %collective-permute-done.25.refs_15_), channel_id=1, source_target_pairs={{0,4},{4,0},{8,12},{12,8},{16,20},{20,16},{24,28},{28,24},{1,5},{5... | collective-permute-start | bytes 196616 | tf_op jit(solution)/shard_map/ppermute | solution.py:1019
  126.3 5.6 %collective-permute-start.24 = (bf16[64,512]{1,0:T(8,128)(2,1)}, bf16[64,512]{1,0:T(8,128)(2,1)}, u32[]{:S(2)}, u32[]{:S(2)}) collective-permute-start(bf16[64,512]{1,0:T(8,128)(2,1)} %collective-permute-done.23.refs_13_), channel_id=1, source_target_pairs={{0,4},{4,0},{8,12},{12,8},{16,20},{20,16},{24,28},{28,24},{1,5},{5... | collective-permute-start | bytes 196616 | tf_op jit(solution)/shard_map/ppermute | solution.py:1019
  127.3 4.6 %collective-permute-start.22 = (bf16[64,512]{1,0:T(8,128)(2,1)}, bf16[64,512]{1,0:T(8,128)(2,1)}, u32[]{:S(2)}, u32[]{:S(2)}) collective-permute-start(bf16[64,512]{1,0:T(8,128)(2,1)} %collective-permute-done.21.refs_11_), channel_id=1, source_target_pairs={{0,4},{4,0},{8,12},{12,8},{16,20},{20,16},{24,28},{28,24},{1,5},{5... | collective-permute-start | bytes 196616 | tf_op jit(solution)/shard_map/ppermute | solution.py:1019

commit v6 on v5

--- a/solution.py
+++ b/solution.py
@@ -16,6 +16,7 @@
 PARAM_ROWS = 32
 OWN_MEAN = 16
 VMEM_BYTES = 64 * 1024 * 1024
+SMALL_VMEM_BYTES = 24 * 1024 * 1024
 
 GAIN, SHIFT, SKIP, BIAS_LINEAR, BIAS_GATE = range(5)
 RATE_RE, RATE_IM, GAMMA = range(3)
@@ -201,6 +202,45 @@
     def finish(self):
         for copy in self.copies:
             copy.wait()
+
+
+class Resident:
+    def __init__(self, ref):
+        self.ref = ref
+
+    def wait(self, piece=None):
+        return self.ref
+
+    def send(self, start=None, size=None, source=None):
+        if source is not None and start is None:
+            self.ref[...] = source[...]
+        elif source is not None:
+            self.ref[start : start + size, :] = source[...]
+
+
+def call_small(kernel, outs, scratch, args, name, sent=False):
+    def body(*refs):
+        count, results = len(args), len(outs)
+        ins, refs = [Resident(ref) for ref in refs[:count]], refs[count:]
+        if not sent:
+            kernel(None, ins, [Resident(ref) for ref in refs[:results]], *refs[results:])
+            return
+        targets, copied, scratch_refs = refs[:results], refs[results], refs[results + 1 :]
+        departures = [Departure(target, None, copied, place * LAYERS) for place, target in enumerate(targets)]
+        kernel(None, ins, departures, *scratch_refs)
+        for departure in departures:
+            departure.finish()
+
+    return pl.pallas_call(
+        body,
+        out_shape=tuple(outs),
+        in_specs=[pl.BlockSpec(memory_space=pltpu.VMEM)] * len(args),
+        out_specs=tuple(pl.BlockSpec(memory_space=pl.ANY if sent else pltpu.VMEM) for _ in outs),
+        scratch_shapes=([pltpu.SemaphoreType.DMA((LAYERS * len(outs),))] if sent else []) + list(scratch),
+        compiler_params=pltpu.CompilerParams(vmem_limit_bytes=SMALL_VMEM_BYTES),
+        cost_estimate=pl.CostEstimate(flops=0, bytes_accessed=0, transcendentals=0),
+        name=name,
+    )(*args)
 
 
 def call(kernel, outs, scratch, args, name, pieces=None, axes=None, bare=(), late=(), order=None, flops=0):
@@ -387,26 +427,27 @@
 
 def skip_sums(pre_grad_ref, normed_ref, quarter, small_ref):
     own = lanes_at(quarter, 128)
-
-    def inner(rows, index, carry):
-        return carry + folded(pre_grad_ref[rows, own].astype(F32) * normed_ref[rows, own].astype(F32))
-
-    small_ref[3:4, 0:128] = column_sum(for_rows(0, pre_grad_ref.shape[0], 16, inner, jnp.zeros((8, 128), F32), unroll=4))
+    value = jnp.zeros((8, 128), F32)
+    for rows, _ in blocks_of(0, pre_grad_ref.shape[0]):
+        value += folded(pre_grad_ref[rows, own].astype(F32) * normed_ref[rows, own].astype(F32))
+    small_ref[3:4, 0:128] = column_sum(value)
 
 
 def bias_sums(grad_gated_ref, quarter, small_ref):
-    own, far = lanes_at(quarter, 128), lanes_at(quarter + 4, 128)
-
-    def inner(rows, index, carry):
-        return (
-            carry[0] + folded(grad_gated_ref[rows, own].astype(F32)),
-            carry[1] + folded(grad_gated_ref[rows, far].astype(F32)),
-        )
-
-    zero = jnp.zeros((8, 128), F32)
-    one, two = for_rows(0, grad_gated_ref.shape[0], 16, inner, (zero, zero), unroll=4)
-    small_ref[4:5, 0:128] = column_sum(one)
-    small_ref[5:6, 0:128] = column_sum(two)
+    for place in range(2):
+        lanes = lanes_at(quarter + 4 * place, 128)
+        value = jnp.zeros((8, 128), F32)
+        for rows, _ in blocks_of(0, grad_gated_ref.shape[0]):
+            value += folded(grad_gated_ref[rows, lanes].astype(F32))
+        small_ref[4 + place : 5 + place, 0:128] = column_sum(value)
+
+
+def together(*parts):
+    def run():
+        for part in parts:
+            part()
+
+    return run
 
 
 def adjoint_phase(low_ref, im_lane, drive_own_ref, state, first_row, length, grad_state_ref, grad_driven_ref, small_ref, reverse, beside):
@@ -462,6 +503,16 @@
         grads_ref[2 * half + place * half : 2 * half + (place + 1) * half, :] = got.astype(LOW)
 
     return [functools.partial(product, 0, low_re, 1.0), functools.partial(product, 1, low_im, -1.0)]
+
+
+def beside_sweep(products, grad_gated_ref, pre_grad_ref, normed_ref, quarter, small_ref):
+    first, second, third, fourth = products
+    return (
+        together(first, functools.partial(bias_sums, grad_gated_ref, quarter, small_ref)),
+        together(second, functools.partial(skip_sums, pre_grad_ref, normed_ref, quarter, small_ref)),
+        third,
+        fourth,
+    )
 
 
 def input_products(grads_ref, grad_driven_ref, normed_ref, states):
@@ -529,6 +580,10 @@
         whole.send(first, size, source=value.ref.at[layer])
 
 
+def total_kernel(length_ref, ins, outs):
+    outs[0].ref[...] = total_rows(ins[0].ref)
+
+
 def cotangent_kernel(length_ref, ins, outs, held_ref):
     x, b, c, w = ins
     whole, later = outs
@@ -552,7 +607,7 @@
 
 
 def start_kernel(length_ref, ins, outs, stats_ref, stream_ref, drive_ref, pre_ref, held_ref, b_ref, c_ref, w_ref, low_ref):
-    sums, tokens, *parts = ins
+    all_stats, tokens, parts = ins[:4], ins[4], ins[5:]
     feature, state_out, norm, normed, drive_own, low_own, stream, linear_out, gate_out, slope, active, b_out, c_out, w_out, spread = outs
     length, quarter = length_ref[0], own_quarter()
     total, full = active.ref.shape
@@ -580,12 +635,8 @@
             state_out.ref[first : first + 1, lanes] = modulus * jnp.cos(angle)
             state_out.ref[first + 1 : first + 2, lanes] = modulus * jnp.sin(angle)
             state_out.ref[first + 2 : first + 3, lanes] = jnp.exp(logs[first + 2 : first + 3, :])
-    sums_ref = sums.wait()
-    for place in range(4):
-        value = sums_ref[place, :, :]
-        for other in range(1, sums_ref.shape[0] // 4):
-            value += sums_ref[other * 4 + place, :, :]
-        stats_ref[:, place * width : (place + 1) * width] = value
+    for place, stats in enumerate(all_stats):
+        stats_ref[:, lanes_at(quarter ^ place, width)] = stats.wait()[...]
     centre, inv_dev = norm_rows(stats_ref[0:2, :], stats_ref[2:3, :])
     norm.ref[...] = jnp.zeros_like(norm.ref)
     norm.ref[0:1, :] = centre
@@ -742,13 +793,14 @@
         pre_grad_piece(piece, pre_ref, slope_ref, pre_grad_ref)
         drive_ref[piece, :] = dot(pre_grad_ref[piece, :], c_ref[...], NT)
     small_ref[...] = jnp.zeros_like(small_ref)
-    bias_sums(grad_gated_ref, quarter, small_ref)
-    skip_sums(pre_grad_ref, normed_ref, quarter, small_ref)
     to_feature_rows(lambda rows, index: stream.ref[rows, own] + mixed_ref[rows, own], order_ref, result, steps)
     adjoint_phase(
         low_ref, states, drive_own_ref, state, 5, length, drive_ref, grad_driven_ref, small_ref, False,
-        glu_products(grads_ref, 2 * width, grad_gated_ref, active_ref, quarter)
-        + output_products(grads_ref, lambda: low_ref[:, 0:128], lambda: low_ref[:, states : states + 128], pre_grad_ref, states),
+        beside_sweep(
+            glu_products(grads_ref, 2 * width, grad_gated_ref, active_ref, quarter)
+            + output_products(grads_ref, lambda: low_ref[:, 0:128], lambda: low_ref[:, states : states + 128], pre_grad_ref, states),
+            grad_gated_ref, pre_grad_ref, normed_ref, quarter, small_ref,
+        ),
     )
     scale = inv_dev * gain
     for piece in pieces_of(total):
@@ -816,12 +868,13 @@
     up_out.send()
     for value in (normed, active, low, drive_own):
         value.wait()
-    bias_sums(grad_gated_ref, quarter, small_ref)
-    skip_sums(pre_grad_ref, normed.ref, quarter, small_ref)
     adjoint_phase(
         low.ref, 128, drive_own.ref, state, 2, length, grad_state_ref, grad_driven_ref, small_ref, True,
-        glu_products(grads_ref, 2 * width, grad_gated_ref, active.ref, quarter)
-        + output_products(grads_ref, lambda: low.ref[:, :128], lambda: low.ref[:, 128:], pre_grad_ref, state.shape[1]),
+        beside_sweep(
+            glu_products(grads_ref, 2 * width, grad_gated_ref, active.ref, quarter)
+            + output_products(grads_ref, lambda: low.ref[:, :128], lambda: low.ref[:, 128:], pre_grad_ref, state.shape[1]),
+            grad_gated_ref, pre_grad_ref, normed.ref, quarter, small_ref,
+        ),
     )
     b.wait()
     x.wait()
@@ -872,8 +925,7 @@
 
 
 def pair_kernel(length_ref, ins, outs, sum_ref, pack_ref):
-    kept, other, *last = ins
-    back, *outs = outs
+    kept, other = ins
     for value in ins:
         value.wait()
     half = kept.ref.shape[0] - 16
@@ -887,25 +939,24 @@
     for place, out in enumerate(outs):
         out.send(0, share, source=sum_ref.at[rows_at((lax.axis_index("dp") >> 1) ^ place, share)])
         out.send(share, 16, source=pack_ref)
-    for piece in range(0, share, 16):
-        at = slice(piece, piece + 16)
-        back.ref[at, :] = (last[0].ref[at, :].astype(F32) + last[1].ref[at, :].astype(F32)).astype(LOW)
 
 
 def share_kernel(length_ref, ins, outs):
+    *blocks, kept, other = ins
     out, small = outs
-    share = out.ref.shape[0]
+    share = kept.ref.shape[0]
     for value in ins:
         value.wait()
     for piece in range(0, share, 16):
         at = slice(piece, piece + 16)
-        value = ins[0].ref[at, :].astype(F32)
-        for block in ins[1:]:
+        value = blocks[0].ref[at, :].astype(F32)
+        for block in blocks[1:]:
             value += block.ref[at, :].astype(F32)
         out.ref[at, :] = value.astype(LOW)
-    out.send()
-    value = ins[0].ref[share:, :].astype(F32)
-    for block in ins[1:]:
+        value = kept.ref[at, :].astype(F32) + other.ref[at, :].astype(F32)
+        out.ref[share + piece : share + piece + 16, :] = value.astype(LOW)
+    value = blocks[0].ref[share:, :].astype(F32)
+    for block in blocks[1:]:
         value += block.ref[share:, :].astype(F32)
     small.ref[...] = value[0:8, :] + value[8:16, :]
 
@@ -953,18 +1004,17 @@
 
 
 def widen_kernel(length_ref, ins, outs, held_ref):
-    half = outs[0].ref.shape[1]
-    groups = len(ins) // 2
-    share = ins[0].ref.shape[0]
+    half = outs[0].target.shape[1]
+    groups = len(ins)
+    share = ins[0].ref.shape[0] // 2
     stages = groups.bit_length() - 1
-    for layer, values in ((1, ins[:groups]), (0, ins[groups:])):
-        for place, value in enumerate(values):
-            value.wait()
+    for layer in (1, 0):
+        for place, value in enumerate(ins):
             owner = lax.axis_index("dp") ^ place
             at = (owner & 1) * (groups // 2) + (owner >> 1)
             if layer == 1:
                 at = sum((owner >> stage & 1) << (stages - 1 - stage) for stage in range(stages))
-            held_ref[layer, rows_at(at, share), :] = value.ref[...].astype(F32)
+            held_ref[layer, rows_at(at, share), :] = value.ref[layer * share : (layer + 1) * share, :].astype(F32)
         for out, first, size in zip(outs, (0, half, 2 * half), (half, half, 2 * half)):
             out.send(layer, 1, source=held_ref.at[pl.ds(layer, 1), pl.ds(first, size)])
 
@@ -1021,13 +1071,12 @@
     def add(halves, stage):
         kept, other = halves
         rows = kept.shape[0]
-        return call(
+        return call_small(
             functools.partial(add_kernel, stage=stage + 1),
             (shape(rows // 2, full, dtype=LOW),) * 2,
             [pltpu.VMEM((rows, full), LOW)],
-            (lengths, kept, other),
+            (kept, other),
             "add",
-            bare=(0, 1),
         )
 
 
@@ -1037,7 +1086,7 @@
         enter_kernel,
         (
             shape(total, width),
-            shape(dp_size * state_size, 8, width),
+            shape(dp_size, 8, width),
             shape(6 * width + PARAM_ROWS, full, dtype=LOW),
         ),
         [pltpu.VMEM((total, width), F32), pltpu.VMEM((PARAM_ROWS, width), F32)],
@@ -1048,9 +1097,8 @@
         late=(9, 10, 11),
     )
     near, far = swap(first, 1, sharers), swap(first, 2, sharers)
-    sums = across(sums, ("dp", "state"))
-    if sharers > 1:
-        sums = sums.reshape(dp_size * 4, sharers, 8, width)[:, 0]
+    (stats,) = call_small(total_kernel, (shape(8, width),), [], (across(sums, "dp"),), "total")
+    stats_near, stats_far = swap(stats, 1, sharers), swap(stats, 2, sharers)
     cotangent, tokens = lax.optimization_barrier((cotangent, tokens))
     up_own, later = call(
         cotangent_kernel,
@@ -1065,8 +1113,9 @@
         axes={1: 1},
         late=(2, 3, 4),
     )
-    near, far, sums, later = lax.optimization_barrier((near, far, sums, later))
+    near, far, stats_near, stats_far, later = lax.optimization_barrier((near, far, stats_near, stats_far, later))
     parts = (first, near, far, swap(far, 1, sharers))
+    all_stats = (stats, stats_near, stats_far, swap(stats_far, 1, sharers))
     later_far = swap(later, 2, sharers)
     feature, state, norm0, normed0, drive0, low0, stream1, linear0, gate0, slope0, active0, b_all, c_all, w_all, sums1 = call(
         start_kernel,
@@ -1098,9 +1147,9 @@
             pltpu.VMEM((2 * full, full), LOW),
             pltpu.VMEM((total, 2 * states), LOW),
         ],
-        (lengths, sums, tokens, *parts),
+        (lengths, *all_stats, tokens, *parts),
         "start",
-        pieces={2: piece} | {place: width for place in (3, 4, 5, 6)},
+        pieces={5: piece} | {place: width for place in (6, 7, 8, 9)},
         order=(4, 5),
         bare=(11, 12, 13),
         flops=1e9,
@@ -1142,7 +1191,7 @@
         (lengths, sums1, norm0, feature, state, stream1, up_own, *later_parts),
         "middle",
         pieces={5: piece} | {place: width for place in (7, 8, 9, 10)},
-        late=(6, 7, 8, 9, 10),
+        late=(6,),
         bare=(4, 5),
         flops=1e9,
     )
@@ -1186,28 +1235,24 @@
             halves1[1] = exchange(halves1[1], 1 << stage)
         if stage < stages - 1:
             halves1 = list(add(halves1, stage))
-    back1, *blocks = call(
+    kept0, *halves1 = lax.optimization_barrier((kept0, *halves1))
+    blocks = call_small(
         pair_kernel,
-        (shape(share, full, dtype=LOW),) + (shape(share + 16, full, dtype=LOW),) * (dp_size // 2),
+        (shape(share + 16, full, dtype=LOW),) * (dp_size // 2),
         [pltpu.VMEM((2 * width, full), LOW), pltpu.VMEM((16, full), LOW)],
-        (lengths, kept0, sent0, *halves1),
+        (kept0, sent0),
         "pair",
-        bare=tuple(range(1, 1 + dp_size // 2)),
     )
     blocks = [blocks[0]] + [exchange(blocks[place], 2 * place) for place in range(1, dp_size // 2)]
-    back0, small0 = call(
+    back, small0 = call_small(
         share_kernel,
-        (shape(share, full, dtype=LOW), shape(8, full)),
+        (shape(2 * share, full, dtype=LOW), shape(8, full)),
         [],
-        (lengths, *blocks),
+        (*blocks, *halves1),
         "share",
     )
-
-    def to_all(value):
-        got = [value] + [exchange(value, place) for place in range(2, dp_size, 2)]
-        return [each for first in got for each in (first, exchange(first, 1))]
-
-    backs = to_all(back1) + to_all(back0)
+    backs = [back] + [exchange(back, place) for place in range(2, dp_size, 2)]
+    backs = [each for first in backs for each in (first, exchange(first, 1))]
     grad_nu, grad_theta, grad_gamma, grad_skip, grad_bias, grad_gain, grad_shift, grad_inputs = call(
         finish_kernel,
         (
@@ -1224,13 +1269,13 @@
         (lengths, small0, bn1, norm0, feature, nu_log, theta_log, up0, grad0, tokens),
         "finish",
     )
-    grad_b, grad_c, grad_glu = call(
+    grad_b, grad_c, grad_glu = call_small(
         widen_kernel,
         (shape(LAYERS, width, full), shape(LAYERS, width, full), shape(LAYERS, 2 * width, full)),
         [pltpu.VMEM((LAYERS, 4 * width, full), F32)],
-        (lengths, *backs),
+        tuple(backs),
         "widen",
-        bare=(0, 1, 2),
+        sent=True,
     )
     grad_b = grad_b.reshape(LAYERS, 2, own_states, full)
     grad_c = grad_c.reshape(LAYERS, 2, own_states, full)

time: 135 us -> 129 us (0.956)
  blocking collectives: 0 us -> 12.5 us
  starting transfers between devices: 43.4 us -> 32.4 us
  Pallas kernels: 53.2 us -> 47.4 us
  waiting for transfers between devices: 36.6 us -> 30.9 us
  local copies, waits for them, and re-layouts: 0 us -> 4.06 us
    all_to_all x0 -> x1, blocking collectives: none -> 12.5 us  [across(): return lax.all_to_all(value, axes, 0, 0, tiled=True)]
    all_to_all x3 -> x2, waiting for transfers between devices: 17.1 us -> 5.34 us  [across(): return lax.all_to_all(value, axes, 0, 0, tiled=True)]
    pallas_call x11 -> x6, Pallas kernels: 53.2 us -> 41.6 us  [call(): pl.pallas_call(body, out_shape=tuple(outs), in_specs=[pl.BlockSpec(memory...]
    ppermute x21 -> x14, starting transfers between devices: 24.6 us -> 16.7 us  [exchange(): return lax.ppermute(value, 'dp', [(i, i ^ bit) for i in range(dp_size)])]
    pallas_call x0 -> x6, Pallas kernels: none -> 5.81 us  [call_small(): pl.pallas_call(body, out_shape=tuple(outs), in_specs=[pl.BlockSpec(memory...]
    ppermute x21 -> x14, waiting for transfers between devices: 12.4 us -> 17.8 us  [exchange(): return lax.ppermute(value, 'dp', [(i, i ^ bit) for i in range(dp_size)])]
    all_to_all x3 -> x2, starting transfers between devices: 14.2 us -> 10 us  [across(): return lax.all_to_all(value, axes, 0, 0, tiled=True)]
    unnamed x0 -> x10, local copies, waits for them, and re-layouts: none -> 4.06 us
  transfers between devices with their start and end apart: 30 -> 25, of which waited for: 11 -> 15; matrix products, arithmetic and copies ran while one was open for 0% -> 0% of each run, Pallas kernels for 23% -> 21%
where the time goes in v6:
time: 129 us
  Pallas kernels  47.4 us (37%)
  starting transfers between devices  32.4 us (25%)
  waiting for transfers between devices  30.9 us (24%)
  blocking collectives  12.5 us (10%)
  local copies, waits for them, and re-layouts  4.06 us (3%)
  between operations  1.6 us (1%)
    pallas_call x6, Pallas kernels, call(): pl.pallas_call(body, out_shape=tuple(outs), in_specs=[pl.BlockSpec(memory...  41.6 us
    ppermute x14, waiting for transfers between devices, exchange(): return lax.ppermute(value, 'dp', [(i, i ^ bit) for i in range(dp_size)])  17.8 us
    ppermute x14, starting transfers between devices, exchange(): return lax.ppermute(value, 'dp', [(i, i ^ bit) for i in range(dp_size)])  16.7 us
    all_to_all x1, blocking collectives, across(): return lax.all_to_all(value, axes, 0, 0, tiled=True)  12.5 us
    all_to_all x2, starting transfers between devices, across(): return lax.all_to_all(value, axes, 0, 0, tiled=True)  10 us
    ppermute x9, waiting for transfers between devices, swap(): return lax.ppermute(value, 'state', pairs)  7.77 us
    pallas_call x6, Pallas kernels, call_small(): pl.pallas_call(body, out_shape=tuple(outs), in_specs=[pl.BlockSpec(memory...  5.81 us
    ppermute x9, starting transfers between devices, swap(): return lax.ppermute(value, 'state', pairs)  5.59 us
  transfers between devices with their start and end apart: 25, of which 15 were waited for; matrix products, arithmetic and copies ran while one was open for 0% of the time, Pallas kernels for 21%

profile of v6, /device:TPU:0, one launch (start us, length us, event | category | flops | bytes accessed | tf_op | source)
XLA Modules:
  0.0 128.8 jit_solution(1656328366098469788)
XLA Ops:
  1.3 3.3 %enter.1 = (f32[1024,128]{1,0:T(8,128)}, f32[8,8,128]{2,1,0:T(8,128)}, bf16[800,512]{1,0:T(8,128)(2,1)}) custom-call(s32[1]{0:T(128)S(6)} %copy.25.refs_0_, f32[128,1024]{1,0:T(8,128)} %bitcast.16, f32[2,128]{1,0:T(2,128)} %refs_2_.1, f32[2,128]{1,0:T(2,128)} %refs_3_.1, f32[2,128]{1,0:T(2,128)} %refs_4_.1, f32[2,2,128]{2,1,0:T(2,128)} %refs_5_.2, ...), custom_call_target="tpu_custom_call" | custom-call | tf_op jit(solution)/shard_map/enter/pallas_call | solution.py:288
  4.6 3.0 %collective-permute-start.1 = (bf16[800,512]{1,0:T(8,128)(2,1)}, bf16[800,512]{1,0:T(8,128)(2,1)}, u32[]{:S(2)}, u32[]{:S(2)}) collective-permute-start(bf16[800,512]{1,0:T(8,128)(2,1)} %get-tuple-element.82.refs_6_), channel_id=1, source_target_pairs={{0,2},{1,3},{2,0},{3,1},{4,6},{5,7},{6,4},{7,5},{8,10},{9,11},{10,... | collective-permute-start | bytes 2457608 | tf_op jit(solution)/shard_map/ppermute | solution.py:1028
  7.6 12.5 %all_to_all.15.refs_0_ = f32[8,8,128]{2,1,0:T(8,128)S(1)} all-to-all(f32[8,8,128]{2,1,0:T(8,128)} %get-tuple-element.83), channel_id=1, replica_groups=mesh['dp'=8,'state'=4] {'dp'}, dimensions={0} | all-to-all | bytes 65536 | tf_op jit(solution)/shard_map/all_to_all | solution.py:1032
  20.1 0.6 total.1.refs_1_
  20.7 0.5 collective-permute-start.3
  21.3 2.9 %cotangent.1 = (f32[1024,128]{1,0:T(8,128)}, bf16[768,512]{1,0:T(8,128)(2,1)}) custom-call(s32[1]{0:T(128)S(6)} %copy.25.refs_0_, f32[128,1024]{1,0:T(8,128)} %bitcast.17, bf16[2,128,512]{2,1,0:T(8,128)(2,1)} %bitcast.13, bf16[2,128,512]{2,1,0:T(8,128)(2,1)} %bitcast.15, bf16[2,256,512]{2,1,0:T(8,128)(2,1)} %bitcast.11), custom_call_target="tpu_custom_call" | custom-call | tf_op jit(solution)/shard_map/cotangent/pallas_call | solution.py:288
  24.1 2.1 %collective-permute-done.3.refs_3_ = f32[8,128]{1,0:T(8,128)} collective-permute-done((f32[8,128]{1,0:T(8,128)}, f32[8,128]{1,0:T(8,128)}, u32[]{:S(2)}, u32[]{:S(2)}) %collective-permute-start.3) | collective-permute-done | bytes 4128 | tf_op jit(solution)/shard_map/ppermute | solution.py:1028
  26.3 1.8 %collective-permute-start.4 = (bf16[768,512]{1,0:T(8,128)(2,1)}, bf16[768,512]{1,0:T(8,128)(2,1)}, u32[]{:S(2)}, u32[]{:S(2)}) collective-permute-start(bf16[768,512]{1,0:T(8,128)(2,1)} %get-tuple-element.87.refs_7_), channel_id=1, source_target_pairs={{0,2},{1,3},{2,0},{3,1},{4,6},{5,7},{6,4},{7,5},{8,10},{9,11},{10,... | collective-permute-start | bytes 2359304 | tf_op jit(solution)/shard_map/ppermute | solution.py:1028
  28.3 1.3 %collective-permute-done.5.refs_4_ = f32[8,128]{1,0:T(8,128)} collective-permute-done((f32[8,128]{1,0:T(8,128)}, f32[8,128]{1,0:T(8,128)}, u32[]{:S(2)}, u32[]{:S(2)}) %collective-permute-start.5) | collective-permute-done | bytes 4128 | tf_op jit(solution)/shard_map/ppermute | solution.py:1028
  29.7 9.4 %start.1 = (f32[32,512]{1,0:T(8,128)}, f32[8,256]{1,0:T(8,128)}, f32[8,512]{1,0:T(8,128)}, bf16[1024,512]{1,0:T(8,128)(2,1)}, f32[1024,256]{1,0:T(8,128)}, /*ind...) custom-call(s32[1]{0:T(128)S(6)} %copy.25.refs_0_, ...), custom_call_target="tpu_custom_call" | custom-call | flops 1000000000 | tf_op jit(solution)/shard_map/start/pallas_call | solution.py:288
  39.1 5.9 %all-to-all-start.1 = ((f32[8,8,128]{2,1,0:T(8,128)}), f32[8,8,128]{2,1,0:T(8,128)}, u32[]{:S(2)}, u32[]{:S(2)}) async-start(f32[8,8,128]{2,1,0:T(8,128)} %get-tuple-element.93), calls=%async_computation.1 | async-start | bytes 65536 | tf_op jit(solution)/shard_map/all_to_all | solution.py:1032
  44.9 1.7 %collective-permute-done.4.refs_9_ = bf16[768,512]{1,0:T(8,128)(2,1)} collective-permute-done((bf16[768,512]{1,0:T(8,128)(2,1)}, bf16[768,512]{1,0:T(8,128)(2,1)}, u32[]{:S(2)}, u32[]{:S(2)}) %collective-permute-start.4) | collective-permute-done | bytes 786464 | tf_op jit(solution)/shard_map/ppermute | solution.py:1028
  46.6 5.1 %all-to-all-done.1.refs_1_ = f32[8,8,128]{2,1,0:T(8,128)} async-done(((f32[8,8,128]{2,1,0:T(8,128)}), f32[8,8,128]{2,1,0:T(8,128)}, u32[]{:S(2)}, u32[]{:S(2)}) %all-to-all-start.1) | async-done | bytes 32800 | tf_op jit(solution)/shard_map/all_to_all | solution.py:1032
  51.7 2.6 %collective-permute-done.8.refs_10_ = bf16[768,512]{1,0:T(8,128)(2,1)} collective-permute-done((bf16[768,512]{1,0:T(8,128)(2,1)}, bf16[768,512]{1,0:T(8,128)(2,1)}, u32[]{:S(2)}, u32[]{:S(2)}) %collective-permute-start.8) | collective-permute-done | bytes 786464 | tf_op jit(solution)/shard_map/ppermute | solution.py:1028
  54.3 13.4 %middle.1 = (f32[128,1024]{1,0:T(8,128)}, f32[1024,512]{1,0:T(8,128)}, f32[8,16,128]{2,1,0:T(8,128)}, f32[8,512]{1,0:T(8,128)}, bf16[256,512]{1,0:T(8,128)(2,1)}, /*index=5*/bf16[256,512]{1,0:T(8,128)(2,1)}) custom-call(s32[1]{0:T(128)S(6)} %copy.25.refs_0_, f32[8,8,128]{2,1,0:T(8,128)} %all-to-all-done.1.refs_1_, ...), custom_call_target="tpu_custom_call" | custom-call | flops 1000000000 | tf_op jit(solution)/shard_map/middle/pallas_call | solution.py:288
  67.8 0.5 collective-permute-start.9
  68.3 4.2 %all-to-all-start.2 = ((f32[8,16,128]{2,1,0:T(8,128)}), f32[8,16,128]{2,1,0:T(8,128)}, u32[]{:S(2)}, u32[]{:S(2)}) async-start(f32[8,16,128]{2,1,0:T(8,128)} %get-tuple-element.102), calls=%async_computation.2 | async-start | bytes 131072 | tf_op jit(solution)/shard_map/all_to_all | solution.py:1032
  72.5 4.1 %collective-permute-done.9.refs_1_ = bf16[256,512]{1,0:T(8,128)(2,1)S(1)} collective-permute-done((bf16[256,512]{1,0:T(8,128)(2,1)}, bf16[256,512]{1,0:T(8,128)(2,1)S(1)}, u32[]{:S(2)}, u32[]{:S(2)}) %collective-permute-start.9) | collective-permute-done | bytes 262176 | tf_op jit(solution)/shard_map/ppermute | solution.py:1069
  76.6 0.9 copy-done.1
  77.5 0.8 add.2
  78.3 0.6 copy-done.2
  79.4 9.0 %last.1 = (bf16[272,512]{1,0:T(8,128)(2,1)}, bf16[272,512]{1,0:T(8,128)(2,1)}, f32[1024,128]{1,0:T(8,128)}, f32[1024,128]{1,0:T(8,128)}) custom-call(s32[1]{0:T(128)S(6)} %copy.25.refs_0_, f32[8,16,128]{2,1,0:T(8,128)} %all-to-all-done.2.refs_1_.refs_2_, f32[8,512]{1,0:T(8,128)} %get-tuple-element.110.refs_2_, f32[32,512]{1,0:T(8,128)} %get-tuple-element.96.refs_3_.refs_4_, ...), custom_call_target="tpu_custom_call" | custom-call | flops 99999997952 | tf_op jit(solution)/shard_map/last/pallas_call | solution.py:288
  88.5 1.1 collective-permute-start.12
  89.5 0.9 copy-done.3
  90.4 0.9 add.3
  91.4 0.8 collective-permute-start.11
  92.2 4.5 %collective-permute-done.11.refs_5_ = bf16[64,512]{1,0:T(8,128)(2,1)S(1)} collective-permute-done((bf16[64,512]{1,0:T(8,128)(2,1)S(1)}, bf16[64,512]{1,0:T(8,128)(2,1)S(1)}, u32[]{:S(2)}, u32[]{:S(2)}) %collective-permute-start.11) | collective-permute-done | bytes 65568 | tf_op jit(solution)/shard_map/ppermute | solution.py:1069
  96.6 1.0 copy-done
  97.7 1.3 %collective-permute-start.13 = (bf16[80,512]{1,0:T(8,128)(2,1)S(1)}, bf16[80,512]{1,0:T(8,128)(2,1)S(1)}, u32[]{:S(2)}, u32[]{:S(2)}) collective-permute-start(bf16[80,512]{1,0:T(8,128)(2,1)S(1)} %get-tuple-element.132), channel_id=1, source_target_pairs={{0,8},{4,12},{8,0},{12,4},{16,24},{20,28},{24,16},{28,20},{1,9},{5... | collective-permute-start | bytes 245768 | tf_op jit(solution)/shard_map/ppermute | solution.py:1069
  99.0 1.1 collective-permute-start.14
  100.1 2.0 %collective-permute-start.15 = (bf16[80,512]{1,0:T(8,128)(2,1)S(1)}, bf16[80,512]{1,0:T(8,128)(2,1)S(1)}, u32[]{:S(2)}, u32[]{:S(2)}) collective-permute-start(bf16[80,512]{1,0:T(8,128)(2,1)S(1)} %get-tuple-element.134), channel_id=1, source_target_pairs={{0,24},{4,28},{8,16},{12,20},{16,8},{20,12},{24,0},{28,4},{1,25},{... | collective-permute-start | bytes 245768 | tf_op jit(solution)/shard_map/ppermute | solution.py:1069
  102.1 1.3 collective-permute-done.13.refs_1_
  103.4 1.8 %collective-permute-done.14.refs_2_ = bf16[80,512]{1,0:T(8,128)(2,1)S(1)} collective-permute-done((bf16[80,512]{1,0:T(8,128)(2,1)S(1)}, bf16[80,512]{1,0:T(8,128)(2,1)S(1)}, u32[]{:S(2)}, u32[]{:S(2)}) %collective-permute-start.14) | collective-permute-done | bytes 81952 | tf_op jit(solution)/shard_map/ppermute | solution.py:1069
  105.2 1.2 collective-permute-done.15.refs_3_
  106.5 0.7 share.1
  107.2 0.6 copy-done.4
  107.8 1.9 %collective-permute-start.21 = (bf16[128,512]{1,0:T(8,128)(2,1)}, bf16[128,512]{1,0:T(8,128)(2,1)}, u32[]{:S(2)}, u32[]{:S(2)}) collective-permute-start(bf16[128,512]{1,0:T(8,128)(2,1)} %get-tuple-element.143.refs_0_), channel_id=1, source_target_pairs={{0,24},{4,28},{8,16},{12,20},{16,8},{20,12},{24,0},{28,4},{1,25},{... | collective-permute-start | bytes 393224 | tf_op jit(solution)/shard_map/ppermute | solution.py:1069
  109.7 0.6 collective-permute-start.19
  110.3 1.8 %collective-permute-start.17 = (bf16[128,512]{1,0:T(8,128)(2,1)}, bf16[128,512]{1,0:T(8,128)(2,1)}, u32[]{:S(2)}, u32[]{:S(2)}) collective-permute-start(bf16[128,512]{1,0:T(8,128)(2,1)} %get-tuple-element.143.refs_0_), channel_id=1, source_target_pairs={{0,8},{4,12},{8,0},{12,4},{16,24},{20,28},{24,16},{28,20},{1,9},{5... | collective-permute-start | bytes 393224 | tf_op jit(solution)/shard_map/ppermute | solution.py:1069
  112.2 1.6 %collective-permute-start.16 = (bf16[128,512]{1,0:T(8,128)(2,1)}, bf16[128,512]{1,0:T(8,128)(2,1)}, u32[]{:S(2)}, u32[]{:S(2)}) collective-permute-start(bf16[128,512]{1,0:T(8,128)(2,1)} %get-tuple-element.143.refs_0_), channel_id=1, source_target_pairs={{0,4},{4,0},{8,12},{12,8},{16,20},{20,16},{24,28},{28,24},{1,5},{5... | collective-permute-start | bytes 393224 | tf_op jit(solution)/shard_map/ppermute | solution.py:1069
  113.8 1.2 collective-permute-done.21.refs_6_
  115.0 1.7 %collective-permute-start.22 = (bf16[128,512]{1,0:T(8,128)(2,1)}, bf16[128,512]{1,0:T(8,128)(2,1)}, u32[]{:S(2)}, u32[]{:S(2)}) collective-permute-start(bf16[128,512]{1,0:T(8,128)(2,1)} %collective-permute-done.21.refs_6_), channel_id=1, source_target_pairs={{0,4},{4,0},{8,12},{12,8},{16,20},{20,16},{24,28},{28,24},{1,5},{5... | collective-permute-start | bytes 393224 | tf_op jit(solution)/shard_map/ppermute | solution.py:1069
  116.7 2.0 %collective-permute-done.19.refs_4_ = bf16[128,512]{1,0:T(8,128)(2,1)} collective-permute-done((bf16[128,512]{1,0:T(8,128)(2,1)}, bf16[128,512]{1,0:T(8,128)(2,1)}, u32[]{:S(2)}, u32[]{:S(2)}) %collective-permute-start.19) | collective-permute-done | bytes 131104 | tf_op jit(solution)/shard_map/ppermute | solution.py:1069
  118.7 1.2 collective-permute-start.20
  119.9 0.8 collective-permute-start.18
  120.7 3.6 %finish.1 = (f32[2,64]{1,0:T(2,128)}, f32[2,64]{1,0:T(2,128)}, f32[2,64]{1,0:T(2,128)}, f32[2,128]{1,0:T(2,128)}, f32[2,2,128]{2,1,0:T(2,128)}, /*index=5*/f32[2...) custom-call(s32[1]{0:T(128)S(6)} %copy.25.refs_0_, f32[8,512]{1,0:T(8,128)} %copy-done.4, ...), custom_call_target="tpu_custom_call" | custom-call | tf_op jit(solution)/shard_map/finish/pallas_call | solution.py:288
  124.5 1.4 %collective-permute-done.18.refs_3_ = bf16[128,512]{1,0:T(8,128)(2,1)} collective-permute-done((bf16[128,512]{1,0:T(8,128)(2,1)}, bf16[128,512]{1,0:T(8,128)(2,1)}, u32[]{:S(2)}, u32[]{:S(2)}) %collective-permute-start.18) | collective-permute-done | bytes 131104 | tf_op jit(solution)/shard_map/ppermute | solution.py:1069
  125.9 2.7 %widen.1 = (f32[2,128,512]{2,1,0:T(8,128)}, f32[2,128,512]{2,1,0:T(8,128)}, f32[2,256,512]{2,1,0:T(8,128)}) custom-call(bf16[128,512]{1,0:T(8,128)(2,1)} %get-tuple-element.143.refs_0_, bf16[128,512]{1,0:T(8,128)(2,1)} %collective-permute-done.16.refs_1_, bf16[128,512]{1,0:T(8,128)(2,1)} %collective-permute-done.17.refs_2_, ...), custom_call_target="tpu_custom_call" | custom-call | tf_op jit(solution)/shard_map/widen/pallas_call | solution.py:234
  (25 shorter events, 1.1 us)
Async XLA Ops:
  4.6 21.7 %collective-permute-start.1 = (bf16[800,512]{1,0:T(8,128)(2,1)}, bf16[800,512]{1,0:T(8,128)(2,1)}, u32[]{:S(2)}, u32[]{:S(2)}) collective-permute-start(bf16[800,512]{1,0:T(8,128)(2,1)} %get-tuple-element.82.refs_6_), channel_id=1, source_target_pairs={{0,2},{1,3},{2,0},{3,1},{4,6},{5,7},{6,4},{7,5},{8,10},{9,11},{10,... | collective-permute-start | bytes 2457608 | tf_op jit(solution)/shard_map/ppermute | solution.py:1028
  7.6 18.7 %collective-permute-start = (bf16[800,512]{1,0:T(8,128)(2,1)}, bf16[800,512]{1,0:T(8,128)(2,1)}, u32[]{:S(2)}, u32[]{:S(2)}) collective-permute-start(bf16[800,512]{1,0:T(8,128)(2,1)} %get-tuple-element.82.refs_6_), channel_id=1, source_target_pairs={{0,1},{1,0},{2,3},{3,2},{4,5},{5,4},{6,7},{7,6},{8,9},{9,8},{10,11... | collective-permute-start | bytes 2457608 | tf_op jit(solution)/shard_map/ppermute | solution.py:1028
  20.7 5.5 %collective-permute-start.3 = (f32[8,128]{1,0:T(8,128)}, f32[8,128]{1,0:T(8,128)}, u32[]{:S(2)}, u32[]{:S(2)}) collective-permute-start(f32[8,128]{1,0:T(8,128)} %total.1.refs_1_), channel_id=1, source_target_pairs={{0,2},{1,3},{2,0},{3,1},{4,6},{5,7},{6,4},{7,5},{8,10},{9,11},{10,... | collective-permute-start | bytes 12296 | tf_op jit(solution)/shard_map/ppermute | solution.py:1028
  21.3 5.0 %collective-permute-start.2 = (f32[8,128]{1,0:T(8,128)}, f32[8,128]{1,0:T(8,128)}, u32[]{:S(2)}, u32[]{:S(2)}) collective-permute-start(f32[8,128]{1,0:T(8,128)} %total.1.refs_1_), channel_id=1, source_target_pairs={{0,1},{1,0},{2,3},{3,2},{4,5},{5,4},{6,7},{7,6},{8,9},{9,8},{10,11... | collective-permute-start | bytes 12296 | tf_op jit(solution)/shard_map/ppermute | solution.py:1028
  26.3 3.4 %collective-permute-start.6 = (bf16[800,512]{1,0:T(8,128)(2,1)}, bf16[800,512]{1,0:T(8,128)(2,1)}, u32[]{:S(2)}, u32[]{:S(2)}) collective-permute-start(bf16[800,512]{1,0:T(8,128)(2,1)} %collective-permute-done.1.refs_8_), channel_id=1, source_target_pairs={{0,1},{1,0},{2,3},{3,2},{4,5},{5,4},{6,7},{7,6},{8,9},{9,8},{10,11... | collective-permute-start | bytes 2457608 | tf_op jit(solution)/shard_map/ppermute | solution.py:1028
  26.3 20.3 %collective-permute-start.4 = (bf16[768,512]{1,0:T(8,128)(2,1)}, bf16[768,512]{1,0:T(8,128)(2,1)}, u32[]{:S(2)}, u32[]{:S(2)}) collective-permute-start(bf16[768,512]{1,0:T(8,128)(2,1)} %get-tuple-element.87.refs_7_), channel_id=1, source_target_pairs={{0,2},{1,3},{2,0},{3,1},{4,6},{5,7},{6,4},{7,5},{8,10},{9,11},{10,... | collective-permute-start | bytes 2359304 | tf_op jit(solution)/shard_map/ppermute | solution.py:1028
  28.2 1.5 %collective-permute-start.5 = (f32[8,128]{1,0:T(8,128)}, f32[8,128]{1,0:T(8,128)}, u32[]{:S(2)}, u32[]{:S(2)}) collective-permute-start(f32[8,128]{1,0:T(8,128)} %collective-permute-done.3.refs_3_), channel_id=1, source_target_pairs={{0,1},{1,0},{2,3},{3,2},{4,5},{5,4},{6,7},{7,6},{8,9},{9,8},{10,11... | collective-permute-start | bytes 12296 | tf_op jit(solution)/shard_map/ppermute | solution.py:1028
  39.1 12.6 %all-to-all-start.1 = ((f32[8,8,128]{2,1,0:T(8,128)}), f32[8,8,128]{2,1,0:T(8,128)}, u32[]{:S(2)}, u32[]{:S(2)}) async-start(f32[8,8,128]{2,1,0:T(8,128)} %get-tuple-element.93), calls=%async_computation.1 | async-start | bytes 65536 | tf_op jit(solution)/shard_map/all_to_all | solution.py:1032
  44.9 6.8 %collective-permute-start.7 = (bf16[768,512]{1,0:T(8,128)(2,1)}, bf16[768,512]{1,0:T(8,128)(2,1)}, u32[]{:S(2)}, u32[]{:S(2)}) collective-permute-start(bf16[768,512]{1,0:T(8,128)(2,1)} %get-tuple-element.87.refs_7_), channel_id=1, source_target_pairs={{0,1},{1,0},{2,3},{3,2},{4,5},{5,4},{6,7},{7,6},{8,9},{9,8},{10,11... | collective-permute-start | bytes 2359304 | tf_op jit(solution)/shard_map/ppermute | solution.py:1028
  51.7 2.6 %collective-permute-start.8 = (bf16[768,512]{1,0:T(8,128)(2,1)}, bf16[768,512]{1,0:T(8,128)(2,1)}, u32[]{:S(2)}, u32[]{:S(2)}) collective-permute-start(bf16[768,512]{1,0:T(8,128)(2,1)} %collective-permute-done.4.refs_9_), channel_id=1, source_target_pairs={{0,1},{1,0},{2,3},{3,2},{4,5},{5,4},{6,7},{7,6},{8,9},{9,8},{10,11... | collective-permute-start | bytes 2359304 | tf_op jit(solution)/shard_map/ppermute | solution.py:1028
  67.8 8.8 %collective-permute-start.9 = (bf16[256,512]{1,0:T(8,128)(2,1)}, bf16[256,512]{1,0:T(8,128)(2,1)S(1)}, u32[]{:S(2)}, u32[]{:S(2)}) collective-permute-start(bf16[256,512]{1,0:T(8,128)(2,1)} %get-tuple-element.104), channel_id=1, source_target_pairs={{0,4},{4,0},{8,12},{12,8},{16,20},{20,16},{24,28},{28,24},{1,5},{5... | collective-permute-start | bytes 786440 | tf_op jit(solution)/shard_map/ppermute | solution.py:1069
  68.3 10.9 %all-to-all-start.2 = ((f32[8,16,128]{2,1,0:T(8,128)}), f32[8,16,128]{2,1,0:T(8,128)}, u32[]{:S(2)}, u32[]{:S(2)}) async-start(f32[8,16,128]{2,1,0:T(8,128)} %get-tuple-element.102), calls=%async_computation.2 | async-start | bytes 131072 | tf_op jit(solution)/shard_map/all_to_all | solution.py:1032
  76.6 1.0 copy-start.1
  78.3 0.6 copy-start.2
  79.2 9.3 %collective-permute-start.10 = (bf16[128,512]{1,0:T(8,128)(2,1)}, bf16[128,512]{1,0:T(8,128)(2,1)}, u32[]{:S(2)}, u32[]{:S(2)}) collective-permute-start(bf16[128,512]{1,0:T(8,128)(2,1)} %get-tuple-element.108), channel_id=1, source_target_pairs={{0,8},{4,12},{8,0},{12,4},{16,24},{20,28},{24,16},{28,20},{1,9},{5... | collective-permute-start | bytes 393224 | tf_op jit(solution)/shard_map/ppermute | solution.py:1069
  88.5 8.2 %collective-permute-start.12 = (bf16[272,512]{1,0:T(8,128)(2,1)}, bf16[272,512]{1,0:T(8,128)(2,1)S(1)}, u32[]{:S(2)}, u32[]{:S(2)}) collective-permute-start(bf16[272,512]{1,0:T(8,128)(2,1)} %get-tuple-element.130), channel_id=1, source_target_pairs={{0,4},{4,0},{8,12},{12,8},{16,20},{20,16},{24,28},{28,24},{1,5},{5... | collective-permute-start | bytes 835592 | tf_op jit(solution)/shard_map/ppermute | solution.py:1069
  89.5 0.9 copy-start.3
  91.4 5.2 %collective-permute-start.11 = (bf16[64,512]{1,0:T(8,128)(2,1)S(1)}, bf16[64,512]{1,0:T(8,128)(2,1)S(1)}, u32[]{:S(2)}, u32[]{:S(2)}) collective-permute-start(bf16[64,512]{1,0:T(8,128)(2,1)S(1)} %get-tuple-element.128), channel_id=1, source_target_pairs={{0,16},{4,20},{8,24},{12,28},{16,0},{20,4},{24,8},{28,12},{1,17},{... | collective-permute-start | bytes 196616 | tf_op jit(solution)/shard_map/ppermute | solution.py:1069
  96.6 1.0 copy-start
  97.7 5.7 %collective-permute-start.13 = (bf16[80,512]{1,0:T(8,128)(2,1)S(1)}, bf16[80,512]{1,0:T(8,128)(2,1)S(1)}, u32[]{:S(2)}, u32[]{:S(2)}) collective-permute-start(bf16[80,512]{1,0:T(8,128)(2,1)S(1)} %get-tuple-element.132), channel_id=1, source_target_pairs={{0,8},{4,12},{8,0},{12,4},{16,24},{20,28},{24,16},{28,20},{1,9},{5... | collective-permute-start | bytes 245768 | tf_op jit(solution)/shard_map/ppermute | solution.py:1069
  99.0 6.2 %collective-permute-start.14 = (bf16[80,512]{1,0:T(8,128)(2,1)S(1)}, bf16[80,512]{1,0:T(8,128)(2,1)S(1)}, u32[]{:S(2)}, u32[]{:S(2)}) collective-permute-start(bf16[80,512]{1,0:T(8,128)(2,1)S(1)} %get-tuple-element.133), channel_id=1, source_target_pairs={{0,16},{4,20},{8,24},{12,28},{16,0},{20,4},{24,8},{28,12},{1,17},{... | collective-permute-start | bytes 245768 | tf_op jit(solution)/shard_map/ppermute | solution.py:1069
  100.1 6.3 %collective-permute-start.15 = (bf16[80,512]{1,0:T(8,128)(2,1)S(1)}, bf16[80,512]{1,0:T(8,128)(2,1)S(1)}, u32[]{:S(2)}, u32[]{:S(2)}) collective-permute-start(bf16[80,512]{1,0:T(8,128)(2,1)S(1)} %get-tuple-element.134), channel_id=1, source_target_pairs={{0,24},{4,28},{8,16},{12,20},{16,8},{20,12},{24,0},{28,4},{1,25},{... | collective-permute-start | bytes 245768 | tf_op jit(solution)/shard_map/ppermute | solution.py:1069
  107.2 0.6 copy-start.4
  107.8 7.3 %collective-permute-start.21 = (bf16[128,512]{1,0:T(8,128)(2,1)}, bf16[128,512]{1,0:T(8,128)(2,1)}, u32[]{:S(2)}, u32[]{:S(2)}) collective-permute-start(bf16[128,512]{1,0:T(8,128)(2,1)} %get-tuple-element.143.refs_0_), channel_id=1, source_target_pairs={{0,24},{4,28},{8,16},{12,20},{16,8},{20,12},{24,0},{28,4},{1,25},{... | collective-permute-start | bytes 393224 | tf_op jit(solution)/shard_map/ppermute | solution.py:1069
  109.7 9.0 %collective-permute-start.19 = (bf16[128,512]{1,0:T(8,128)(2,1)}, bf16[128,512]{1,0:T(8,128)(2,1)}, u32[]{:S(2)}, u32[]{:S(2)}) collective-permute-start(bf16[128,512]{1,0:T(8,128)(2,1)} %get-tuple-element.143.refs_0_), channel_id=1, source_target_pairs={{0,16},{4,20},{8,24},{12,28},{16,0},{20,4},{24,8},{28,12},{1,17},{... | collective-permute-start | bytes 393224 | tf_op jit(solution)/shard_map/ppermute | solution.py:1069
  110.3 9.6 %collective-permute-start.17 = (bf16[128,512]{1,0:T(8,128)(2,1)}, bf16[128,512]{1,0:T(8,128)(2,1)}, u32[]{:S(2)}, u32[]{:S(2)}) collective-permute-start(bf16[128,512]{1,0:T(8,128)(2,1)} %get-tuple-element.143.refs_0_), channel_id=1, source_target_pairs={{0,8},{4,12},{8,0},{12,4},{16,24},{20,28},{24,16},{28,20},{1,9},{5... | collective-permute-start | bytes 393224 | tf_op jit(solution)/shard_map/ppermute | solution.py:1069
  112.2 12.1 %collective-permute-start.16 = (bf16[128,512]{1,0:T(8,128)(2,1)}, bf16[128,512]{1,0:T(8,128)(2,1)}, u32[]{:S(2)}, u32[]{:S(2)}) collective-permute-start(bf16[128,512]{1,0:T(8,128)(2,1)} %get-tuple-element.143.refs_0_), channel_id=1, source_target_pairs={{0,4},{4,0},{8,12},{12,8},{16,20},{20,16},{24,28},{28,24},{1,5},{5... | collective-permute-start | bytes 393224 | tf_op jit(solution)/shard_map/ppermute | solution.py:1069
  115.0 9.3 %collective-permute-start.22 = (bf16[128,512]{1,0:T(8,128)(2,1)}, bf16[128,512]{1,0:T(8,128)(2,1)}, u32[]{:S(2)}, u32[]{:S(2)}) collective-permute-start(bf16[128,512]{1,0:T(8,128)(2,1)} %collective-permute-done.21.refs_6_), channel_id=1, source_target_pairs={{0,4},{4,0},{8,12},{12,8},{16,20},{20,16},{24,28},{28,24},{1,5},{5... | collective-permute-start | bytes 393224 | tf_op jit(solution)/shard_map/ppermute | solution.py:1069
  118.7 5.9 %collective-permute-start.20 = (bf16[128,512]{1,0:T(8,128)(2,1)}, bf16[128,512]{1,0:T(8,128)(2,1)}, u32[]{:S(2)}, u32[]{:S(2)}) collective-permute-start(bf16[128,512]{1,0:T(8,128)(2,1)} %collective-permute-done.19.refs_4_), channel_id=1, source_target_pairs={{0,4},{4,0},{8,12},{12,8},{16,20},{20,16},{24,28},{28,24},{1,5},{5... | collective-permute-start | bytes 393224 | tf_op jit(solution)/shard_map/ppermute | solution.py:1069
  119.9 6.1 %collective-permute-start.18 = (bf16[128,512]{1,0:T(8,128)(2,1)}, bf16[128,512]{1,0:T(8,128)(2,1)}, u32[]{:S(2)}, u32[]{:S(2)}) collective-permute-start(bf16[128,512]{1,0:T(8,128)(2,1)} %collective-permute-done.17.refs_2_), channel_id=1, source_target_pairs={{0,4},{4,0},{8,12},{12,8},{16,20},{20,16},{24,28},{28,24},{1,5},{5... | collective-permute-start | bytes 393224 | tf_op jit(solution)/shard_map/ppermute | solution.py:1069

commit v7 on v6

--- a/solution.py
+++ b/solution.py
@@ -16,7 +16,7 @@
 PARAM_ROWS = 32
 OWN_MEAN = 16
 VMEM_BYTES = 64 * 1024 * 1024
-SMALL_VMEM_BYTES = 24 * 1024 * 1024
+SMALL_VMEM_BYTES = 8 * 1024 * 1024
 
 GAIN, SHIFT, SKIP, BIAS_LINEAR, BIAS_GATE = range(5)
 RATE_RE, RATE_IM, GAMMA = range(3)
@@ -218,10 +218,10 @@
             self.ref[start : start + size, :] = source[...]
 
 
-def call_small(kernel, outs, scratch, args, name, sent=False):
+def call_small(kernel, outs, scratch, args, name, sent=False, into=()):
     def body(*refs):
         count, results = len(args), len(outs)
-        ins, refs = [Resident(ref) for ref in refs[:count]], refs[count:]
+        ins, refs = [Resident(ref) for ref in refs[:count]], refs[count + len(into) :]
         if not sent:
             kernel(None, ins, [Resident(ref) for ref in refs[:results]], *refs[results:])
             return
@@ -234,13 +234,14 @@
     return pl.pallas_call(
         body,
         out_shape=tuple(outs),
-        in_specs=[pl.BlockSpec(memory_space=pltpu.VMEM)] * len(args),
+        in_specs=[pl.BlockSpec(memory_space=pltpu.VMEM)] * len(args) + [pl.BlockSpec(memory_space=pl.ANY)] * len(into),
         out_specs=tuple(pl.BlockSpec(memory_space=pl.ANY if sent else pltpu.VMEM) for _ in outs),
+        input_output_aliases={len(args) + place: place for place in range(len(into))},
         scratch_shapes=([pltpu.SemaphoreType.DMA((LAYERS * len(outs),))] if sent else []) + list(scratch),
         compiler_params=pltpu.CompilerParams(vmem_limit_bytes=SMALL_VMEM_BYTES),
         cost_estimate=pl.CostEstimate(flops=0, bytes_accessed=0, transcendentals=0),
         name=name,
-    )(*args)
+    )(*args, *into)
 
 
 def call(kernel, outs, scratch, args, name, pieces=None, axes=None, bare=(), late=(), order=None, flops=0):
@@ -646,32 +647,32 @@
         out.send()
 
     each = total // PIECES
-
-    def normal(rows, index, carry):
-        keep = keep_rows(index, 16, steps, length)
-        there = pl.ds(pl.multiple_of(index * 16 % each, 16), 16)
-        for place, part_ref in enumerate(rows_refs):
-            lanes = lanes_at(quarter ^ place, width)
-            if place == 0:
-                value = tokens.ref[rows, :]
-            else:
-                value = part_ref[there, lanes_at(index * 16 // each, width)].astype(F32)
-                value = value + feature.ref[OWN_MEAN : OWN_MEAN + 1, lanes]
-            stream_ref[rows, lanes] = value
-            z = (value - norm.ref[0:1, lanes]) * norm.ref[1:2, lanes]
-            z = z * feature.ref[GAIN : GAIN + 1, lanes] + feature.ref[SHIFT : SHIFT + 1, lanes]
-            normed.ref[rows, lanes] = jnp.where(keep, z, 0.0).astype(LOW)
-        return carry
-
-    for piece in range(PIECES):
-        tokens.wait(piece)
-        for_rows(piece * total // PIECES, (piece + 1) * total // PIECES, 16, normal)
-        normed.send_piece(piece)
     assemble_states([part.wait(0).at[0:width] for part in parts], b_ref)
     b_out.send(source=b_ref)
     state = state_out.ref[...]
     states = state.shape[1]
-    drive_phase(normed.ref, b_ref, drive_ref, state[2 + GAMMA : 3 + GAMMA, :])
+    gamma = state[2 + GAMMA : 3 + GAMMA, :]
+    gammas = jnp.concatenate([gamma, gamma], axis=1)
+    rows_of = []
+    for place in range(4):
+        lanes = lanes_at(quarter ^ place, width)
+        rows_of.append((lanes, feature.ref[OWN_MEAN : OWN_MEAN + 1, lanes], norm.ref[0:1, lanes], norm.ref[1:2, lanes],
+                        feature.ref[GAIN : GAIN + 1, lanes], feature.ref[SHIFT : SHIFT + 1, lanes]))
+    for at, piece in enumerate(pieces_of(total)):
+        tokens.wait(at)
+        for rows, index in blocks_of(piece.start, piece.stop):
+            keep = keep_rows(index, 16, steps, length)
+            there = slice(rows.start % each, rows.start % each + 16)
+            for place, (lanes, mean, middle, inverse, gain, shift) in enumerate(rows_of):
+                if place == 0:
+                    value = tokens.ref[rows, :]
+                else:
+                    value = rows_refs[place][there, at * width : (at + 1) * width].astype(F32) + mean
+                stream_ref[rows, lanes] = value
+                z = (value - middle) * inverse * gain + shift
+                normed.ref[rows, lanes] = jnp.where(keep, z, 0.0).astype(LOW)
+        normed.send_piece(at)
+        drive_ref[piece, :] = dot(normed.ref[piece, :], b_ref[...], NT) * gammas
     assemble_output([part.wait(1).at[width : 2 * width] for part in parts], c_ref)
     c_out.send(source=c_ref)
     store = store_states(low_ref, drive_own.ref)
@@ -719,7 +720,7 @@
 def middle_kernel(
     length_ref, ins, outs,
     small_ref, b_ref, c_ref, w_ref, normed_ref, drive_ref, drive_own_ref, low_ref, slope_ref, active_ref, held_ref, pre_ref, mixed_ref,
-    order_ref, up_ref, grad_gated_ref, pre_grad_ref, grad_driven_ref, grads_ref,
+    up_ref, grad_gated_ref, pre_grad_ref, grad_driven_ref, grads_ref,
 ):
     sums, norm0, feature_in, state_in, stream, up_own = ins[:6]
     parts = ins[6:]
@@ -763,11 +764,8 @@
     up_own.wait()
     own = lanes_at(quarter, width)
 
-    def spread_up(rows, index, carry):
+    for rows, _ in blocks_of(0, total):
         up_ref[rows, own] = up_own.ref[rows, :]
-        return carry
-
-    for_rows(0, total, 16, spread_up, unroll=4)
     for place, piece in enumerate(pieces_of(total)):
         for other in range(1, 4):
             lanes = lanes_at(quarter ^ other, width)
@@ -793,7 +791,9 @@
         pre_grad_piece(piece, pre_ref, slope_ref, pre_grad_ref)
         drive_ref[piece, :] = dot(pre_grad_ref[piece, :], c_ref[...], NT)
     small_ref[...] = jnp.zeros_like(small_ref)
-    to_feature_rows(lambda rows, index: stream.ref[rows, own] + mixed_ref[rows, own], order_ref, result, steps)
+    for rows, _ in blocks_of(0, total):
+        result.ref[rows, :] = stream.ref[rows, own] + mixed_ref[rows, own]
+    result.send()
     adjoint_phase(
         low_ref, states, drive_own_ref, state, 5, length, drive_ref, grad_driven_ref, small_ref, False,
         beside_sweep(
@@ -843,8 +843,6 @@
     for place, piece in enumerate(pieces_of(total)):
         for value in (stream, base, gate, linear):
             value.wait(place)
-        if place == 0:
-            w.wait()
         for rows, index in blocks_of(piece.start, piece.stop):
             keep = keep_rows(index, 16, steps, length)
             up = base.ref[rows, :] - jnp.where(keep, level + (stream.ref[rows, :] - centre) * tilt, 0.0)
@@ -852,6 +850,8 @@
             up = jnp.where(keep, up, 0.0)
             grad_gated_ref[rows, :full] = (up * gate.ref[rows, :].astype(F32)).astype(LOW)
             grad_gated_ref[rows, full:] = (up * linear.ref[rows, :].astype(F32)).astype(LOW)
+        if place == 0:
+            w.wait()
         held_ref[piece, :] = dot(grad_gated_ref[piece, :], w.ref[...], NN)
     for value in (slope, c):
         value.wait()
@@ -914,14 +914,8 @@
         out.send(source=source_ref.at[rows_at(which, half)])
 
 
-def add_kernel(length_ref, ins, outs, sum_ref, stage):
-    kept, other = ins
-    kept.wait()
-    other.wait()
-    for piece in range(0, kept.ref.shape[0], 16):
-        at = slice(piece, piece + 16)
-        sum_ref[at, :] = (kept.ref[at, :].astype(F32) + other.ref[at, :].astype(F32)).astype(LOW)
-    send_halves(sum_ref, outs, stage)
+def add_kernel(length_ref, ins, outs):
+    outs[0].ref[...] = (ins[0].ref[...].astype(F32) + ins[1].ref[...].astype(F32)).astype(LOW)
 
 
 def pair_kernel(length_ref, ins, outs, sum_ref, pack_ref):
@@ -942,33 +936,25 @@
 
 
 def share_kernel(length_ref, ins, outs):
-    *blocks, kept, other = ins
     out, small = outs
-    share = kept.ref.shape[0]
-    for value in ins:
-        value.wait()
-    for piece in range(0, share, 16):
-        at = slice(piece, piece + 16)
-        value = blocks[0].ref[at, :].astype(F32)
-        for block in blocks[1:]:
-            value += block.ref[at, :].astype(F32)
-        out.ref[at, :] = value.astype(LOW)
-        value = kept.ref[at, :].astype(F32) + other.ref[at, :].astype(F32)
-        out.ref[share + piece : share + piece + 16, :] = value.astype(LOW)
-    value = blocks[0].ref[share:, :].astype(F32)
-    for block in blocks[1:]:
-        value += block.ref[share:, :].astype(F32)
-    small.ref[...] = value[0:8, :] + value[8:16, :]
+    share = out.ref.shape[0]
+    value = ins[0].ref[...].astype(F32)
+    for block in ins[1:]:
+        value += block.ref[...].astype(F32)
+    out.ref[...] = value[:share, :].astype(LOW)
+    small.ref[...] = value[share : share + 8, :] + value[share + 8 :, :]
 
 
 def finish_kernel(length_ref, ins, outs, held_ref, order_ref):
-    small0, bn1, norm0, feature, nu, theta, up, grad, x = ins
-    nu_out, theta_out, gamma_out, skip_out, bias_out, gain_out, shift_out, out = outs
+    small0, bn1, norm0, feature, nu, theta, result, up, grad, x = ins
+    nu_out, theta_out, gamma_out, skip_out, bias_out, gain_out, shift_out, result_out, out = outs
     length, quarter = length_ref[0], own_quarter()
     total, width = up.ref.shape
     steps = total // CHUNKS
     own = lanes_at(quarter, width)
     states = nu_out.ref.shape[1]
+    result.wait()
+    to_feature_rows(lambda rows, index: result.ref[rows, :], order_ref, result_out, steps)
     for value in ins:
         value.wait()
     whole = total_rows(bn1.ref)
@@ -1003,20 +989,27 @@
     to_feature_rows(load, order_ref, out, steps)
 
 
-def widen_kernel(length_ref, ins, outs, held_ref):
+def send_wide(layer, outs, held_ref):
     half = outs[0].target.shape[1]
+    for out, first, size in zip(outs, (0, half, 2 * half), (half, half, 2 * half)):
+        out.send(layer, 1, source=held_ref.at[pl.ds(0, 1), pl.ds(first, size)])
+
+
+def widen1_kernel(length_ref, ins, outs, held_ref):
+    half = ins[0].ref.shape[0]
+    mine = lax.axis_index("dp") & 1
+    for which, value in ((mine, ins[0]), (1 - mine, ins[1])):
+        held_ref[0, rows_at(which, half), :] = value.ref[...].astype(F32)
+    send_wide(1, outs, held_ref)
+
+
+def widen0_kernel(length_ref, ins, outs, held_ref):
     groups = len(ins)
-    share = ins[0].ref.shape[0] // 2
-    stages = groups.bit_length() - 1
-    for layer in (1, 0):
-        for place, value in enumerate(ins):
-            owner = lax.axis_index("dp") ^ place
-            at = (owner & 1) * (groups // 2) + (owner >> 1)
-            if layer == 1:
-                at = sum((owner >> stage & 1) << (stages - 1 - stage) for stage in range(stages))
-            held_ref[layer, rows_at(at, share), :] = value.ref[layer * share : (layer + 1) * share, :].astype(F32)
-        for out, first, size in zip(outs, (0, half, 2 * half), (half, half, 2 * half)):
-            out.send(layer, 1, source=held_ref.at[pl.ds(layer, 1), pl.ds(first, size)])
+    share = ins[0].ref.shape[0]
+    for place, value in enumerate(ins):
+        owner = lax.axis_index("dp") ^ place
+        held_ref[0, rows_at((owner & 1) * (groups // 2) + (owner >> 1), share), :] = value.ref[...].astype(F32)
+    send_wide(0, outs, held_ref)
 
 
 def shape(*dims, dtype=F32):
@@ -1068,17 +1061,8 @@
     def exchange(value, bit):
         return lax.ppermute(value, "dp", [(i, i ^ bit) for i in range(dp_size)])
 
-    def add(halves, stage):
-        kept, other = halves
-        rows = kept.shape[0]
-        return call_small(
-            functools.partial(add_kernel, stage=stage + 1),
-            (shape(rows // 2, full, dtype=LOW),) * 2,
-            [pltpu.VMEM((rows, full), LOW)],
-            (kept, other),
-            "add",
-        )
-
+    def add(one, other):
+        return call_small(add_kernel, (shape(*one.shape, dtype=LOW),), [], (one, other), "add")[0]
 
     b_weight, c_weight = b_weight.reshape(LAYERS, width, full), c_weight.reshape(LAYERS, width, full)
     glu_weight = glu_weight.reshape(LAYERS, 2 * width, full)
@@ -1113,10 +1097,10 @@
         axes={1: 1},
         late=(2, 3, 4),
     )
+    later_far = swap(later, 2, sharers)
     near, far, stats_near, stats_far, later = lax.optimization_barrier((near, far, stats_near, stats_far, later))
     parts = (first, near, far, swap(far, 1, sharers))
     all_stats = (stats, stats_near, stats_far, swap(stats_far, 1, sharers))
-    later_far = swap(later, 2, sharers)
     feature, state, norm0, normed0, drive0, low0, stream1, linear0, gate0, slope0, active0, b_all, c_all, w_all, sums1 = call(
         start_kernel,
         (
@@ -1152,15 +1136,15 @@
         pieces={5: piece} | {place: width for place in (6, 7, 8, 9)},
         order=(4, 5),
         bare=(11, 12, 13),
-        flops=1e9,
+        flops=0,
     )
     sums1 = across(sums1, "dp")
     later_far, sums1 = lax.optimization_barrier((later_far, sums1))
     later_parts = (later, swap(later, 1, sharers), later_far, swap(later_far, 1, sharers))
-    result, base, bn1, norm1, *halves1 = call(
+    result_rows, base, bn1, norm1, *halves1 = call(
         middle_kernel,
         (
-            shape(width, total),
+            shape(total, width),
             shape(total, full),
             shape(dp_size, 16, width),
             shape(8, full),
@@ -1181,7 +1165,6 @@
             pltpu.VMEM((total, 2 * full), F32),
             pltpu.VMEM((total, full), F32),
             pltpu.VMEM((total, full), F32),
-            pltpu.VMEM((total, width), F32),
             pltpu.VMEM((total, full), F32),
             pltpu.VMEM((total, 2 * full), LOW),
             pltpu.VMEM((total, full), LOW),
@@ -1196,10 +1179,9 @@
         flops=1e9,
     )
     bn1 = across(bn1, "dp")
-    halves1[1] = exchange(halves1[1], 1)
-    halves1 = list(add(halves1, 0))
-    bn1, *halves1 = lax.optimization_barrier((bn1, *halves1))
-    halves1[1] = exchange(halves1[1], 2)
+    half1 = add(halves1[0], exchange(halves1[1], 1))
+    bn1, half1 = lax.optimization_barrier((bn1, half1))
+    other1 = exchange(half1, 1 << (stages - 1))
     kept0, sent0, up0, grad0 = call(
         last_kernel,
         (
@@ -1228,14 +1210,13 @@
         late=tuple(range(11, 19)),
         flops=1e11,
     )
-    *halves1, kept0, sent0 = lax.optimization_barrier((*halves1, kept0, sent0))
+    other1, kept0 = lax.optimization_barrier((other1, kept0))
     sent0 = exchange(sent0, 1)
-    for stage in range(1, stages):
-        if stage > 1:
-            halves1[1] = exchange(halves1[1], 1 << stage)
-        if stage < stages - 1:
-            halves1 = list(add(halves1, stage))
-    kept0, *halves1 = lax.optimization_barrier((kept0, *halves1))
+    half1 = add(half1, other1)
+    kept0, half1 = lax.optimization_barrier((kept0, half1))
+    for stage in reversed(range(2, stages - 1)):
+        half1 = add(half1, exchange(half1, 1 << stage))
+    other1 = exchange(half1, 2)
     blocks = call_small(
         pair_kernel,
         (shape(share + 16, full, dtype=LOW),) * (dp_size // 2),
@@ -1244,16 +1225,17 @@
         "pair",
     )
     blocks = [blocks[0]] + [exchange(blocks[place], 2 * place) for place in range(1, dp_size // 2)]
+    other1, *blocks = lax.optimization_barrier((other1, *blocks))
+    half1 = add(half1, other1)
+    blocks[0], half1 = lax.optimization_barrier((blocks[0], half1))
+    other1 = exchange(half1, 1)
     back, small0 = call_small(
-        share_kernel,
-        (shape(2 * share, full, dtype=LOW), shape(8, full)),
-        [],
-        (*blocks, *halves1),
-        "share",
+        share_kernel, (shape(share, full, dtype=LOW), shape(8, full)), [], tuple(blocks), "share"
     )
+    small0, other1 = lax.optimization_barrier((small0, other1))
     backs = [back] + [exchange(back, place) for place in range(2, dp_size, 2)]
     backs = [each for first in backs for each in (first, exchange(first, 1))]
-    grad_nu, grad_theta, grad_gamma, grad_skip, grad_bias, grad_gain, grad_shift, grad_inputs = call(
+    grad_nu, grad_theta, grad_gamma, grad_skip, grad_bias, grad_gain, grad_shift, result, grad_inputs = call(
         finish_kernel,
         (
             shape(LAYERS, own_states),
@@ -1264,19 +1246,16 @@
             shape(LAYERS, width),
             shape(LAYERS, width),
             shape(width, total),
+            shape(width, total),
         ),
         [pltpu.VMEM((32, full), F32), pltpu.VMEM((total, width), F32)],
-        (lengths, small0, bn1, norm0, feature, nu_log, theta_log, up0, grad0, tokens),
+        (lengths, small0, bn1, norm0, feature, nu_log, theta_log, result_rows, up0, grad0, tokens),
         "finish",
     )
-    grad_b, grad_c, grad_glu = call_small(
-        widen_kernel,
-        (shape(LAYERS, width, full), shape(LAYERS, width, full), shape(LAYERS, 2 * width, full)),
-        [pltpu.VMEM((LAYERS, 4 * width, full), F32)],
-        tuple(backs),
-        "widen",
-        sent=True,
-    )
+    wide = (shape(LAYERS, width, full), shape(LAYERS, width, full), shape(LAYERS, 2 * width, full))
+    held = [pltpu.VMEM((1, 4 * width, full), F32)]
+    grads = call_small(widen1_kernel, wide, held, (half1, other1), "widen1", sent=True)
+    grad_b, grad_c, grad_glu = call_small(widen0_kernel, wide, held, tuple(backs), "widen0", sent=True, into=tuple(grads))
     grad_b = grad_b.reshape(LAYERS, 2, own_states, full)
     grad_c = grad_c.reshape(LAYERS, 2, own_states, full)
     grad_glu = grad_glu.reshape(LAYERS, 2, width, full)

time: 129 us -> 126 us (0.977)
  local copies, waits for them, and re-layouts: 4.06 us -> 1.91 us
    unnamed x10 -> x6, local copies, waits for them, and re-layouts: 4.06 us -> 1.91 us
    ppermute x14 -> x15, starting transfers between devices: 16.7 us -> 15.7 us  [exchange(): return lax.ppermute(value, 'dp', [(i, i ^ bit) for i in range(dp_size)])]
    pallas_call x6 -> x8, Pallas kernels: 5.81 us -> 6.53 us  [call_small(): pl.pallas_call(body, out_shape=tuple(outs), in_specs=[pl.BlockSpec(memory...]
    ppermute x14 -> x15, waiting for transfers between devices: 17.8 us -> 17.1 us  [exchange(): return lax.ppermute(value, 'dp', [(i, i ^ bit) for i in range(dp_size)])]
  transfers between devices with their start and end apart: 25 -> 26, of which waited for: 15 -> 12; matrix products, arithmetic and copies ran while one was open for 0% -> 0% of each run, Pallas kernels for 21% -> 23%
where the time goes in v7:
time: 126 us
  Pallas kernels  47.7 us (38%)
  starting transfers between devices  31.4 us (25%)
  waiting for transfers between devices  30.8 us (24%)
  blocking collectives  12.5 us (10%)
  local copies, waits for them, and re-layouts  1.91 us (2%)
  between operations  1.64 us (1%)
    pallas_call x6, Pallas kernels, call(): pl.pallas_call(body, out_shape=tuple(outs), in_specs=[pl.BlockSpec(memory...  41.2 us
    ppermute x15, waiting for transfers between devices, exchange(): return lax.ppermute(value, 'dp', [(i, i ^ bit) for i in range(dp_size)])  17.1 us
    ppermute x15, starting transfers between devices, exchange(): return lax.ppermute(value, 'dp', [(i, i ^ bit) for i in range(dp_size)])  15.7 us
    all_to_all x1, blocking collectives, across(): return lax.all_to_all(value, axes, 0, 0, tiled=True)  12.5 us
    all_to_all x2, starting transfers between devices, across(): return lax.all_to_all(value, axes, 0, 0, tiled=True)  10 us
    ppermute x9, waiting for transfers between devices, swap(): return lax.ppermute(value, 'state', pairs)  7.83 us
    pallas_call x8, Pallas kernels, call_small(): pl.pallas_call(body, out_shape=tuple(outs), in_specs=[pl.BlockSpec(memory...  6.53 us
    all_to_all x2, waiting for transfers between devices, across(): return lax.all_to_all(value, axes, 0, 0, tiled=True)  5.91 us
  transfers between devices with their start and end apart: 26, of which 12 were waited for; matrix products, arithmetic and copies ran while one was open for 0% of the time, Pallas kernels for 23%

profile of v7, /device:TPU:0, one launch (start us, length us, event | category | flops | bytes accessed | tf_op | source)
XLA Modules:
  0.0 125.9 jit_solution(1598018337527211618)
XLA Ops:
  1.3 3.3 %enter.1 = (f32[1024,128]{1,0:T(8,128)}, f32[8,8,128]{2,1,0:T(8,128)}, bf16[800,512]{1,0:T(8,128)(2,1)}) custom-call(s32[1]{0:T(128)S(6)} %copy.31.refs_0_, f32[128,1024]{1,0:T(8,128)} %bitcast.19, f32[2,128]{1,0:T(2,128)} %refs_2_.1, f32[2,128]{1,0:T(2,128)} %refs_3_.1, f32[2,128]{1,0:T(2,128)} %refs_4_.1, f32[2,2,128]{2,1,0:T(2,128)} %refs_5_.2, ...), custom_call_target="tpu_custom_call" | custom-call | tf_op jit(solution)/shard_map/enter/pallas_call | solution.py:289
  4.6 3.0 %collective-permute-start.2 = (bf16[800,512]{1,0:T(8,128)(2,1)}, bf16[800,512]{1,0:T(8,128)(2,1)}, u32[]{:S(2)}, u32[]{:S(2)}) collective-permute-start(bf16[800,512]{1,0:T(8,128)(2,1)} %get-tuple-element.91.refs_6_), channel_id=1, source_target_pairs={{0,2},{1,3},{2,0},{3,1},{4,6},{5,7},{6,4},{7,5},{8,10},{9,11},{10,... | collective-permute-start | bytes 2457608 | tf_op jit(solution)/shard_map/ppermute | solution.py:1021
  7.6 12.5 %all_to_all.15.refs_0_ = f32[8,8,128]{2,1,0:T(8,128)S(1)} all-to-all(f32[8,8,128]{2,1,0:T(8,128)} %get-tuple-element.90), channel_id=1, replica_groups=mesh['dp'=8,'state'=4] {'dp'}, dimensions={0} | all-to-all | bytes 65536 | tf_op jit(solution)/shard_map/all_to_all | solution.py:1025
  20.1 0.6 total.1.refs_1_
  20.7 0.5 collective-permute-start.4
  21.3 2.9 %cotangent.1 = (f32[1024,128]{1,0:T(8,128)}, bf16[768,512]{1,0:T(8,128)(2,1)}) custom-call(s32[1]{0:T(128)S(6)} %copy.31.refs_0_, f32[128,1024]{1,0:T(8,128)} %bitcast.20, bf16[2,128,512]{2,1,0:T(8,128)(2,1)} %bitcast.14, bf16[2,128,512]{2,1,0:T(8,128)(2,1)} %bitcast.16, bf16[2,256,512]{2,1,0:T(8,128)(2,1)} %bitcast.11), custom_call_target="tpu_custom_call" | custom-call | tf_op jit(solution)/shard_map/cotangent/pallas_call | solution.py:289
  24.2 2.1 %collective-permute-done.4.refs_3_ = f32[8,128]{1,0:T(8,128)} collective-permute-done((f32[8,128]{1,0:T(8,128)}, f32[8,128]{1,0:T(8,128)}, u32[]{:S(2)}, u32[]{:S(2)}) %collective-permute-start.4) | collective-permute-done | bytes 4128 | tf_op jit(solution)/shard_map/ppermute | solution.py:1021
  26.3 0.1 collective-permute-start.6
  26.4 1.8 %collective-permute-start = (bf16[768,512]{1,0:T(8,128)(2,1)}, bf16[768,512]{1,0:T(8,128)(2,1)}, u32[]{:S(2)}, u32[]{:S(2)}) collective-permute-start(bf16[768,512]{1,0:T(8,128)(2,1)} %get-tuple-element.104.refs_7_), channel_id=1, source_target_pairs={{0,2},{1,3},{2,0},{3,1},{4,6},{5,7},{6,4},{7,5},{8,10},{9,11},{10,... | collective-permute-start | bytes 2359304 | tf_op jit(solution)/shard_map/ppermute | solution.py:1021
  28.2 0.2 collective-permute-start.5
  28.3 1.3 %collective-permute-done.5.refs_4_ = f32[8,128]{1,0:T(8,128)} collective-permute-done((f32[8,128]{1,0:T(8,128)}, f32[8,128]{1,0:T(8,128)}, u32[]{:S(2)}, u32[]{:S(2)}) %collective-permute-start.5) | collective-permute-done | bytes 4128 | tf_op jit(solution)/shard_map/ppermute | solution.py:1021
  29.7 9.3 %start.1 = (f32[32,512]{1,0:T(8,128)}, f32[8,256]{1,0:T(8,128)}, f32[8,512]{1,0:T(8,128)}, bf16[1024,512]{1,0:T(8,128)(2,1)}, f32[1024,256]{1,0:T(8,128)}, /*ind...) custom-call(s32[1]{0:T(128)S(6)} %copy.31.refs_0_, ...), custom_call_target="tpu_custom_call" | custom-call | tf_op jit(solution)/shard_map/start/pallas_call | solution.py:289
  39.0 5.8 %all-to-all-start.1 = ((f32[8,8,128]{2,1,0:T(8,128)}), f32[8,8,128]{2,1,0:T(8,128)}, u32[]{:S(2)}, u32[]{:S(2)}) async-start(f32[8,8,128]{2,1,0:T(8,128)} %get-tuple-element.97), calls=%async_computation.1 | async-start | bytes 65536 | tf_op jit(solution)/shard_map/all_to_all | solution.py:1025
  44.9 1.7 %collective-permute-done.refs_9_ = bf16[768,512]{1,0:T(8,128)(2,1)} collective-permute-done((bf16[768,512]{1,0:T(8,128)(2,1)}, bf16[768,512]{1,0:T(8,128)(2,1)}, u32[]{:S(2)}, u32[]{:S(2)}) %collective-permute-start) | collective-permute-done | bytes 786464 | tf_op jit(solution)/shard_map/ppermute | solution.py:1021
  46.6 5.0 %all-to-all-done.1.refs_1_ = f32[8,8,128]{2,1,0:T(8,128)} async-done(((f32[8,8,128]{2,1,0:T(8,128)}), f32[8,8,128]{2,1,0:T(8,128)}, u32[]{:S(2)}, u32[]{:S(2)}) %all-to-all-start.1) | async-done | bytes 32800 | tf_op jit(solution)/shard_map/all_to_all | solution.py:1025
  51.7 2.6 %collective-permute-done.8.refs_10_ = bf16[768,512]{1,0:T(8,128)(2,1)} collective-permute-done((bf16[768,512]{1,0:T(8,128)(2,1)}, bf16[768,512]{1,0:T(8,128)(2,1)}, u32[]{:S(2)}, u32[]{:S(2)}) %collective-permute-start.8) | collective-permute-done | bytes 786464 | tf_op jit(solution)/shard_map/ppermute | solution.py:1021
  54.3 12.7 %middle.1 = (f32[1024,128]{1,0:T(8,128)}, f32[1024,512]{1,0:T(8,128)}, f32[8,16,128]{2,1,0:T(8,128)}, f32[8,512]{1,0:T(8,128)}, bf16[256,512]{1,0:T(8,128)(2,1)}, /*index=5*/bf16[256,512]{1,0:T(8,128)(2,1)}) custom-call(s32[1]{0:T(128)S(6)} %copy.31.refs_0_, f32[8,8,128]{2,1,0:T(8,128)} %all-to-all-done.1.refs_1_, ...), custom_call_target="tpu_custom_call" | custom-call | flops 1000000000 | tf_op jit(solution)/shard_map/middle/pallas_call | solution.py:289
  67.0 0.5 collective-permute-start.9
  67.5 4.2 %all-to-all-start.2 = ((f32[8,16,128]{2,1,0:T(8,128)}), f32[8,16,128]{2,1,0:T(8,128)}, u32[]{:S(2)}, u32[]{:S(2)}) async-start(f32[8,16,128]{2,1,0:T(8,128)} %get-tuple-element.106), calls=%async_computation.2 | async-start | bytes 131072 | tf_op jit(solution)/shard_map/all_to_all | solution.py:1025
  71.7 4.1 %collective-permute-done.9.refs_1_ = bf16[256,512]{1,0:T(8,128)(2,1)S(1)} collective-permute-done((bf16[256,512]{1,0:T(8,128)(2,1)}, bf16[256,512]{1,0:T(8,128)(2,1)S(1)}, u32[]{:S(2)}, u32[]{:S(2)}) %collective-permute-start.9) | collective-permute-done | bytes 262176 | tf_op jit(solution)/shard_map/ppermute | solution.py:1062
  75.8 0.9 copy-done.1
  76.8 0.8 add.3.refs_0_
  77.5 0.9 all-to-all-done.2.refs_1_.refs_2_
  78.4 0.5 collective-permute-start.10
  78.9 9.0 %last.1 = (bf16[272,512]{1,0:T(8,128)(2,1)}, bf16[272,512]{1,0:T(8,128)(2,1)}, f32[1024,128]{1,0:T(8,128)}, f32[1024,128]{1,0:T(8,128)}) custom-call(s32[1]{0:T(128)S(6)} %copy.31.refs_0_, f32[8,16,128]{2,1,0:T(8,128)} %all-to-all-done.2.refs_1_.refs_2_, f32[8,512]{1,0:T(8,128)} %get-tuple-element.111.refs_2_, f32[32,512]{1,0:T(8,128)} %get-tuple-element.100.refs_3_.refs_4_, ...), custom_call_target="tpu_custom_call" | custom-call | flops 99999997952 | tf_op jit(solution)/shard_map/last/pallas_call | solution.py:289
  87.9 0.5 collective-permute-start.12
  88.3 3.5 %collective-permute-done.10.refs_1_ = bf16[256,512]{1,0:T(8,128)(2,1)} collective-permute-done((bf16[256,512]{1,0:T(8,128)(2,1)}, bf16[256,512]{1,0:T(8,128)(2,1)}, u32[]{:S(2)}, u32[]{:S(2)}) %collective-permute-start.10) | collective-permute-done | bytes 262176 | tf_op jit(solution)/shard_map/ppermute | solution.py:1062
  91.8 1.1 add.4.refs_0_
  93.0 2.4 %collective-permute-done.12.refs_1_ = bf16[272,512]{1,0:T(8,128)(2,1)S(1)} collective-permute-done((bf16[272,512]{1,0:T(8,128)(2,1)}, bf16[272,512]{1,0:T(8,128)(2,1)S(1)}, u32[]{:S(2)}, u32[]{:S(2)}) %collective-permute-start.12) | collective-permute-done | bytes 278560 | tf_op jit(solution)/shard_map/ppermute | solution.py:1062
  95.4 1.0 copy-done
  96.4 0.1 pair.1
  96.5 0.5 collective-permute-start.13
  97.0 2.0 %collective-permute-start.14 = (bf16[80,512]{1,0:T(8,128)(2,1)S(1)}, bf16[80,512]{1,0:T(8,128)(2,1)S(1)}, u32[]{:S(2)}, u32[]{:S(2)}) collective-permute-start(bf16[80,512]{1,0:T(8,128)(2,1)S(1)} %get-tuple-element.131), channel_id=1, source_target_pairs={{0,16},{4,20},{8,24},{12,28},{16,0},{20,4},{24,8},{28,12},{1,17},{... | collective-permute-start | bytes 245768 | tf_op jit(solution)/shard_map/ppermute | solution.py:1062
  99.0 1.9 %collective-permute-start.15 = (bf16[80,512]{1,0:T(8,128)(2,1)S(1)}, bf16[80,512]{1,0:T(8,128)(2,1)S(1)}, u32[]{:S(2)}, u32[]{:S(2)}) collective-permute-start(bf16[80,512]{1,0:T(8,128)(2,1)S(1)} %get-tuple-element.132), channel_id=1, source_target_pairs={{0,24},{4,28},{8,16},{12,20},{16,8},{20,12},{24,0},{28,4},{1,25},{... | collective-permute-start | bytes 245768 | tf_op jit(solution)/shard_map/ppermute | solution.py:1062
  100.9 5.6 %collective-permute-done.13.refs_1_ = bf16[80,512]{1,0:T(8,128)(2,1)S(1)} collective-permute-done((bf16[80,512]{1,0:T(8,128)(2,1)S(1)}, bf16[80,512]{1,0:T(8,128)(2,1)S(1)}, u32[]{:S(2)}, u32[]{:S(2)}) %collective-permute-start.13) | collective-permute-done | bytes 81952 | tf_op jit(solution)/shard_map/ppermute | solution.py:1062
  106.6 0.7 collective-permute-start.16
  107.3 0.7 share.1
  108.0 2.3 %collective-permute-start.22 = (bf16[64,512]{1,0:T(8,128)(2,1)}, bf16[64,512]{1,0:T(8,128)(2,1)}, u32[]{:S(2)}, u32[]{:S(2)}) collective-permute-start(bf16[64,512]{1,0:T(8,128)(2,1)} %get-tuple-element.149.refs_0_), channel_id=1, source_target_pairs={{0,24},{4,28},{8,16},{12,20},{16,8},{20,12},{24,0},{28,4},{1,25},{... | collective-permute-start | bytes 196616 | tf_op jit(solution)/shard_map/ppermute | solution.py:1062
  110.2 2.1 %collective-permute-start.18 = (bf16[64,512]{1,0:T(8,128)(2,1)}, bf16[64,512]{1,0:T(8,128)(2,1)}, u32[]{:S(2)}, u32[]{:S(2)}) collective-permute-start(bf16[64,512]{1,0:T(8,128)(2,1)} %get-tuple-element.149.refs_0_), channel_id=1, source_target_pairs={{0,8},{4,12},{8,0},{12,4},{16,24},{20,28},{24,16},{28,20},{1,9},{5... | collective-permute-start | bytes 196616 | tf_op jit(solution)/shard_map/ppermute | solution.py:1062
  112.4 1.4 %collective-permute-start.17 = (bf16[64,512]{1,0:T(8,128)(2,1)}, bf16[64,512]{1,0:T(8,128)(2,1)}, u32[]{:S(2)}, u32[]{:S(2)}) collective-permute-start(bf16[64,512]{1,0:T(8,128)(2,1)} %get-tuple-element.149.refs_0_), channel_id=1, source_target_pairs={{0,4},{4,0},{8,12},{12,8},{16,20},{20,16},{24,28},{28,24},{1,5},{5... | collective-permute-start | bytes 196616 | tf_op jit(solution)/shard_map/ppermute | solution.py:1062
  113.7 1.2 collective-permute-done.22.refs_6_
  114.9 1.2 collective-permute-start.23
  116.2 0.3 collective-permute-done.20.refs_4_
  116.4 1.6 %collective-permute-start.21 = (bf16[64,512]{1,0:T(8,128)(2,1)}, bf16[64,512]{1,0:T(8,128)(2,1)}, u32[]{:S(2)}, u32[]{:S(2)}) collective-permute-start(bf16[64,512]{1,0:T(8,128)(2,1)} %collective-permute-done.20.refs_4_), channel_id=1, source_target_pairs={{0,4},{4,0},{8,12},{12,8},{16,20},{20,16},{24,28},{28,24},{1,5},{5... | collective-permute-start | bytes 196616 | tf_op jit(solution)/shard_map/ppermute | solution.py:1062
  118.0 0.5 collective-permute-start.19
  118.5 1.1 widen1.1
  119.6 4.0 %finish.1 = (f32[2,64]{1,0:T(2,128)}, f32[2,64]{1,0:T(2,128)}, f32[2,64]{1,0:T(2,128)}, f32[2,128]{1,0:T(2,128)}, f32[2,2,128]{2,1,0:T(2,128)}, /*index=5*/f32[2...) custom-call(s32[1]{0:T(128)S(6)} %copy.31.refs_0_, f32[8,512]{1,0:T(8,128)} %copy-done.2, ...), custom_call_target="tpu_custom_call" | custom-call | tf_op jit(solution)/shard_map/finish/pallas_call | solution.py:289
  123.6 2.2 %widen0.1 = (f32[2,128,512]{2,1,0:T(8,128)}, f32[2,128,512]{2,1,0:T(8,128)}, f32[2,256,512]{2,1,0:T(8,128)}) custom-call(bf16[64,512]{1,0:T(8,128)(2,1)} %get-tuple-element.149.refs_0_, bf16[64,512]{1,0:T(8,128)(2,1)} %collective-permute-done.17.refs_1_, ...), custom_call_target="tpu_custom_call", output_to_operand_aliasing={{0}: (8, {}), {1}: (9, {}), {2}: (10, {})} | custom-call | tf_op jit(solution)/shard_map/widen0/pallas_call | solution.py:234
  (25 shorter events, 0.2 us)
Async XLA Ops:
  4.6 21.7 %collective-permute-start.2 = (bf16[800,512]{1,0:T(8,128)(2,1)}, bf16[800,512]{1,0:T(8,128)(2,1)}, u32[]{:S(2)}, u32[]{:S(2)}) collective-permute-start(bf16[800,512]{1,0:T(8,128)(2,1)} %get-tuple-element.91.refs_6_), channel_id=1, source_target_pairs={{0,2},{1,3},{2,0},{3,1},{4,6},{5,7},{6,4},{7,5},{8,10},{9,11},{10,... | collective-permute-start | bytes 2457608 | tf_op jit(solution)/shard_map/ppermute | solution.py:1021
  7.6 18.7 %collective-permute-start.1 = (bf16[800,512]{1,0:T(8,128)(2,1)}, bf16[800,512]{1,0:T(8,128)(2,1)}, u32[]{:S(2)}, u32[]{:S(2)}) collective-permute-start(bf16[800,512]{1,0:T(8,128)(2,1)} %get-tuple-element.91.refs_6_), channel_id=1, source_target_pairs={{0,1},{1,0},{2,3},{3,2},{4,5},{5,4},{6,7},{7,6},{8,9},{9,8},{10,11... | collective-permute-start | bytes 2457608 | tf_op jit(solution)/shard_map/ppermute | solution.py:1021
  20.7 5.5 %collective-permute-start.4 = (f32[8,128]{1,0:T(8,128)}, f32[8,128]{1,0:T(8,128)}, u32[]{:S(2)}, u32[]{:S(2)}) collective-permute-start(f32[8,128]{1,0:T(8,128)} %total.1.refs_1_), channel_id=1, source_target_pairs={{0,2},{1,3},{2,0},{3,1},{4,6},{5,7},{6,4},{7,5},{8,10},{9,11},{10,... | collective-permute-start | bytes 12296 | tf_op jit(solution)/shard_map/ppermute | solution.py:1021
  21.3 5.0 %collective-permute-start.3 = (f32[8,128]{1,0:T(8,128)}, f32[8,128]{1,0:T(8,128)}, u32[]{:S(2)}, u32[]{:S(2)}) collective-permute-start(f32[8,128]{1,0:T(8,128)} %total.1.refs_1_), channel_id=1, source_target_pairs={{0,1},{1,0},{2,3},{3,2},{4,5},{5,4},{6,7},{7,6},{8,9},{9,8},{10,11... | collective-permute-start | bytes 12296 | tf_op jit(solution)/shard_map/ppermute | solution.py:1021
  26.3 3.4 %collective-permute-start.6 = (bf16[800,512]{1,0:T(8,128)(2,1)}, bf16[800,512]{1,0:T(8,128)(2,1)}, u32[]{:S(2)}, u32[]{:S(2)}) collective-permute-start(bf16[800,512]{1,0:T(8,128)(2,1)} %collective-permute-done.2.refs_8_), channel_id=1, source_target_pairs={{0,1},{1,0},{2,3},{3,2},{4,5},{5,4},{6,7},{7,6},{8,9},{9,8},{10,11... | collective-permute-start | bytes 2457608 | tf_op jit(solution)/shard_map/ppermute | solution.py:1021
  26.4 20.3 %collective-permute-start = (bf16[768,512]{1,0:T(8,128)(2,1)}, bf16[768,512]{1,0:T(8,128)(2,1)}, u32[]{:S(2)}, u32[]{:S(2)}) collective-permute-start(bf16[768,512]{1,0:T(8,128)(2,1)} %get-tuple-element.104.refs_7_), channel_id=1, source_target_pairs={{0,2},{1,3},{2,0},{3,1},{4,6},{5,7},{6,4},{7,5},{8,10},{9,11},{10,... | collective-permute-start | bytes 2359304 | tf_op jit(solution)/shard_map/ppermute | solution.py:1021
  28.2 1.5 %collective-permute-start.5 = (f32[8,128]{1,0:T(8,128)}, f32[8,128]{1,0:T(8,128)}, u32[]{:S(2)}, u32[]{:S(2)}) collective-permute-start(f32[8,128]{1,0:T(8,128)} %collective-permute-done.4.refs_3_), channel_id=1, source_target_pairs={{0,1},{1,0},{2,3},{3,2},{4,5},{5,4},{6,7},{7,6},{8,9},{9,8},{10,11... | collective-permute-start | bytes 12296 | tf_op jit(solution)/shard_map/ppermute | solution.py:1021
  39.0 12.6 %all-to-all-start.1 = ((f32[8,8,128]{2,1,0:T(8,128)}), f32[8,8,128]{2,1,0:T(8,128)}, u32[]{:S(2)}, u32[]{:S(2)}) async-start(f32[8,8,128]{2,1,0:T(8,128)} %get-tuple-element.97), calls=%async_computation.1 | async-start | bytes 65536 | tf_op jit(solution)/shard_map/all_to_all | solution.py:1025
  44.9 6.8 %collective-permute-start.7 = (bf16[768,512]{1,0:T(8,128)(2,1)}, bf16[768,512]{1,0:T(8,128)(2,1)}, u32[]{:S(2)}, u32[]{:S(2)}) collective-permute-start(bf16[768,512]{1,0:T(8,128)(2,1)} %get-tuple-element.104.refs_7_), channel_id=1, source_target_pairs={{0,1},{1,0},{2,3},{3,2},{4,5},{5,4},{6,7},{7,6},{8,9},{9,8},{10,11... | collective-permute-start | bytes 2359304 | tf_op jit(solution)/shard_map/ppermute | solution.py:1021
  51.7 2.6 %collective-permute-start.8 = (bf16[768,512]{1,0:T(8,128)(2,1)}, bf16[768,512]{1,0:T(8,128)(2,1)}, u32[]{:S(2)}, u32[]{:S(2)}) collective-permute-start(bf16[768,512]{1,0:T(8,128)(2,1)} %collective-permute-done.refs_9_), channel_id=1, source_target_pairs={{0,1},{1,0},{2,3},{3,2},{4,5},{5,4},{6,7},{7,6},{8,9},{9,8},{10,11... | collective-permute-start | bytes 2359304 | tf_op jit(solution)/shard_map/ppermute | solution.py:1021
  67.0 8.8 %collective-permute-start.9 = (bf16[256,512]{1,0:T(8,128)(2,1)}, bf16[256,512]{1,0:T(8,128)(2,1)S(1)}, u32[]{:S(2)}, u32[]{:S(2)}) collective-permute-start(bf16[256,512]{1,0:T(8,128)(2,1)} %get-tuple-element.108), channel_id=1, source_target_pairs={{0,4},{4,0},{8,12},{12,8},{16,20},{20,16},{24,28},{28,24},{1,5},{5... | collective-permute-start | bytes 786440 | tf_op jit(solution)/shard_map/ppermute | solution.py:1062
  67.5 10.9 %all-to-all-start.2 = ((f32[8,16,128]{2,1,0:T(8,128)}), f32[8,16,128]{2,1,0:T(8,128)}, u32[]{:S(2)}, u32[]{:S(2)}) async-start(f32[8,16,128]{2,1,0:T(8,128)} %get-tuple-element.106), calls=%async_computation.2 | async-start | bytes 131072 | tf_op jit(solution)/shard_map/all_to_all | solution.py:1025
  75.8 1.0 copy-start.1
  78.4 13.4 %collective-permute-start.10 = (bf16[256,512]{1,0:T(8,128)(2,1)}, bf16[256,512]{1,0:T(8,128)(2,1)}, u32[]{:S(2)}, u32[]{:S(2)}) collective-permute-start(bf16[256,512]{1,0:T(8,128)(2,1)} %add.3.refs_0_), channel_id=1, source_target_pairs={{0,16},{4,20},{8,24},{12,28},{16,0},{20,4},{24,8},{28,12},{1,17},{... | collective-permute-start | bytes 786440 | tf_op jit(solution)/shard_map/ppermute | solution.py:1062
  87.9 7.5 %collective-permute-start.12 = (bf16[272,512]{1,0:T(8,128)(2,1)}, bf16[272,512]{1,0:T(8,128)(2,1)S(1)}, u32[]{:S(2)}, u32[]{:S(2)}) collective-permute-start(bf16[272,512]{1,0:T(8,128)(2,1)} %get-tuple-element.128), channel_id=1, source_target_pairs={{0,4},{4,0},{8,12},{12,8},{16,20},{20,16},{24,28},{28,24},{1,5},{5... | collective-permute-start | bytes 835592 | tf_op jit(solution)/shard_map/ppermute | solution.py:1062
  92.9 13.6 %collective-permute-start.11 = (bf16[256,512]{1,0:T(8,128)(2,1)S(1)}, bf16[256,512]{1,0:T(8,128)(2,1)S(1)}, u32[]{:S(2)}, u32[]{:S(2)}) collective-permute-start(bf16[256,512]{1,0:T(8,128)(2,1)S(1)} %add.4.refs_0_), channel_id=1, source_target_pairs={{0,8},{4,12},{8,0},{12,4},{16,24},{20,28},{24,16},{28,20},{1,9},{5... | collective-permute-start | bytes 786440 | tf_op jit(solution)/shard_map/ppermute | solution.py:1062
  95.4 1.0 copy-start
  96.5 10.0 %collective-permute-start.13 = (bf16[80,512]{1,0:T(8,128)(2,1)S(1)}, bf16[80,512]{1,0:T(8,128)(2,1)S(1)}, u32[]{:S(2)}, u32[]{:S(2)}) collective-permute-start(bf16[80,512]{1,0:T(8,128)(2,1)S(1)} %get-tuple-element.130), channel_id=1, source_target_pairs={{0,8},{4,12},{8,0},{12,4},{16,24},{20,28},{24,16},{28,20},{1,9},{5... | collective-permute-start | bytes 245768 | tf_op jit(solution)/shard_map/ppermute | solution.py:1062
  97.0 9.5 %collective-permute-start.14 = (bf16[80,512]{1,0:T(8,128)(2,1)S(1)}, bf16[80,512]{1,0:T(8,128)(2,1)S(1)}, u32[]{:S(2)}, u32[]{:S(2)}) collective-permute-start(bf16[80,512]{1,0:T(8,128)(2,1)S(1)} %get-tuple-element.131), channel_id=1, source_target_pairs={{0,16},{4,20},{8,24},{12,28},{16,0},{20,4},{24,8},{28,12},{1,17},{... | collective-permute-start | bytes 245768 | tf_op jit(solution)/shard_map/ppermute | solution.py:1062
  99.0 7.5 %collective-permute-start.15 = (bf16[80,512]{1,0:T(8,128)(2,1)S(1)}, bf16[80,512]{1,0:T(8,128)(2,1)S(1)}, u32[]{:S(2)}, u32[]{:S(2)}) collective-permute-start(bf16[80,512]{1,0:T(8,128)(2,1)S(1)} %get-tuple-element.132), channel_id=1, source_target_pairs={{0,24},{4,28},{8,16},{12,20},{16,8},{20,12},{24,0},{28,4},{1,25},{... | collective-permute-start | bytes 245768 | tf_op jit(solution)/shard_map/ppermute | solution.py:1062
  106.6 11.9 %collective-permute-start.16 = (bf16[256,512]{1,0:T(8,128)(2,1)S(1)}, bf16[256,512]{1,0:T(8,128)(2,1)S(1)}, u32[]{:S(2)}, u32[]{:S(2)}) collective-permute-start(bf16[256,512]{1,0:T(8,128)(2,1)S(1)} %add.5.refs_0_), channel_id=1, source_target_pairs={{0,4},{4,0},{8,12},{12,8},{16,20},{20,16},{24,28},{28,24},{1,5},{5... | collective-permute-start | bytes 786440 | tf_op jit(solution)/shard_map/ppermute | solution.py:1062
  108.0 11.6 %copy-start.2 = (f32[8,512]{1,0:T(8,128)}, f32[8,512]{1,0:T(8,128)S(1)}, u32[]{:S(2)}) copy-start(f32[8,512]{1,0:T(8,128)S(1)} %get-tuple-element.141.refs_1_) | copy-start | bytes 49156
  108.0 7.0 %collective-permute-start.22 = (bf16[64,512]{1,0:T(8,128)(2,1)}, bf16[64,512]{1,0:T(8,128)(2,1)}, u32[]{:S(2)}, u32[]{:S(2)}) collective-permute-start(bf16[64,512]{1,0:T(8,128)(2,1)} %get-tuple-element.149.refs_0_), channel_id=1, source_target_pairs={{0,24},{4,28},{8,16},{12,20},{16,8},{20,12},{24,0},{28,4},{1,25},{... | collective-permute-start | bytes 196616 | tf_op jit(solution)/shard_map/ppermute | solution.py:1062
  110.2 6.2 %collective-permute-start.20 = (bf16[64,512]{1,0:T(8,128)(2,1)}, bf16[64,512]{1,0:T(8,128)(2,1)}, u32[]{:S(2)}, u32[]{:S(2)}) collective-permute-start(bf16[64,512]{1,0:T(8,128)(2,1)} %get-tuple-element.149.refs_0_), channel_id=1, source_target_pairs={{0,16},{4,20},{8,24},{12,28},{16,0},{20,4},{24,8},{28,12},{1,17},{... | collective-permute-start | bytes 196616 | tf_op jit(solution)/shard_map/ppermute | solution.py:1062
  110.2 7.7 %collective-permute-start.18 = (bf16[64,512]{1,0:T(8,128)(2,1)}, bf16[64,512]{1,0:T(8,128)(2,1)}, u32[]{:S(2)}, u32[]{:S(2)}) collective-permute-start(bf16[64,512]{1,0:T(8,128)(2,1)} %get-tuple-element.149.refs_0_), channel_id=1, source_target_pairs={{0,8},{4,12},{8,0},{12,4},{16,24},{20,28},{24,16},{28,20},{1,9},{5... | collective-permute-start | bytes 196616 | tf_op jit(solution)/shard_map/ppermute | solution.py:1062
  112.4 11.2 %collective-permute-start.17 = (bf16[64,512]{1,0:T(8,128)(2,1)}, bf16[64,512]{1,0:T(8,128)(2,1)}, u32[]{:S(2)}, u32[]{:S(2)}) collective-permute-start(bf16[64,512]{1,0:T(8,128)(2,1)} %get-tuple-element.149.refs_0_), channel_id=1, source_target_pairs={{0,4},{4,0},{8,12},{12,8},{16,20},{20,16},{24,28},{28,24},{1,5},{5... | collective-permute-start | bytes 196616 | tf_op jit(solution)/shard_map/ppermute | solution.py:1062
  114.9 8.6 %collective-permute-start.23 = (bf16[64,512]{1,0:T(8,128)(2,1)}, bf16[64,512]{1,0:T(8,128)(2,1)}, u32[]{:S(2)}, u32[]{:S(2)}) collective-permute-start(bf16[64,512]{1,0:T(8,128)(2,1)} %collective-permute-done.22.refs_6_), channel_id=1, source_target_pairs={{0,4},{4,0},{8,12},{12,8},{16,20},{20,16},{24,28},{28,24},{1,5},{5... | collective-permute-start | bytes 196616 | tf_op jit(solution)/shard_map/ppermute | solution.py:1062
  116.4 7.1 %collective-permute-start.21 = (bf16[64,512]{1,0:T(8,128)(2,1)}, bf16[64,512]{1,0:T(8,128)(2,1)}, u32[]{:S(2)}, u32[]{:S(2)}) collective-permute-start(bf16[64,512]{1,0:T(8,128)(2,1)} %collective-permute-done.20.refs_4_), channel_id=1, source_target_pairs={{0,4},{4,0},{8,12},{12,8},{16,20},{20,16},{24,28},{28,24},{1,5},{5... | collective-permute-start | bytes 196616 | tf_op jit(solution)/shard_map/ppermute | solution.py:1062
  118.0 5.6 %collective-permute-start.19 = (bf16[64,512]{1,0:T(8,128)(2,1)}, bf16[64,512]{1,0:T(8,128)(2,1)}, u32[]{:S(2)}, u32[]{:S(2)}) collective-permute-start(bf16[64,512]{1,0:T(8,128)(2,1)} %collective-permute-done.18.refs_2_), channel_id=1, source_target_pairs={{0,4},{4,0},{8,12},{12,8},{16,20},{20,16},{24,28},{28,24},{1,5},{5... | collective-permute-start | bytes 196616 | tf_op jit(solution)/shard_map/ppermute | solution.py:1062

commit v8 on v7

--- a/solution.py
+++ b/solution.py
@@ -244,7 +244,7 @@
     )(*args, *into)
 
 
-def call(kernel, outs, scratch, args, name, pieces=None, axes=None, bare=(), late=(), order=None, flops=0):
+def call(kernel, outs, scratch, args, name, pieces=None, axes=None, bare=(), late=(), order=None, flops=0, vmem=VMEM_BYTES):
     pieces, axes = pieces or {}, axes or {}
     along = [axes.get(place, 0) for place in range(1, len(args))]
     sizes = [pieces.get(place, args[place].shape[axis]) for place, axis in enumerate(along, 1)]
@@ -298,7 +298,7 @@
             pltpu.SemaphoreType.DMA((slots * len(outs),)),
             *scratch,
         ],
-        compiler_params=pltpu.CompilerParams(vmem_limit_bytes=VMEM_BYTES),
+        compiler_params=pltpu.CompilerParams(vmem_limit_bytes=vmem),
         cost_estimate=pl.CostEstimate(flops=int(flops), bytes_accessed=0, transcendentals=0),
         name=name,
     )(*args)
@@ -936,12 +936,15 @@
 
 
 def share_kernel(length_ref, ins, outs):
-    out, small = outs
-    share = out.ref.shape[0]
-    value = ins[0].ref[...].astype(F32)
-    for block in ins[1:]:
+    half, *blocks = ins
+    out, both, small = outs
+    share, rows = out.ref.shape[0], half.ref.shape[0]
+    value = blocks[0].ref[...].astype(F32)
+    for block in blocks[1:]:
         value += block.ref[...].astype(F32)
     out.ref[...] = value[:share, :].astype(LOW)
+    both.ref[0:rows, :] = half.ref[...]
+    both.ref[rows:, :] = value[:share, :].astype(LOW)
     small.ref[...] = value[share : share + 8, :] + value[share + 8 :, :]
 
 
@@ -999,7 +1002,7 @@
     half = ins[0].ref.shape[0]
     mine = lax.axis_index("dp") & 1
     for which, value in ((mine, ins[0]), (1 - mine, ins[1])):
-        held_ref[0, rows_at(which, half), :] = value.ref[...].astype(F32)
+        held_ref[0, rows_at(which, half), :] = value.ref[0:half, :].astype(F32)
     send_wide(1, outs, held_ref)
 
 
@@ -1008,7 +1011,8 @@
     share = ins[0].ref.shape[0]
     for place, value in enumerate(ins):
         owner = lax.axis_index("dp") ^ place
-        held_ref[0, rows_at((owner & 1) * (groups // 2) + (owner >> 1), share), :] = value.ref[...].astype(F32)
+        first = value.ref.shape[0] - share
+        held_ref[0, rows_at((owner & 1) * (groups // 2) + (owner >> 1), share), :] = value.ref[first:, :].astype(F32)
     send_wide(0, outs, held_ref)
 
 
@@ -1227,14 +1231,19 @@
     blocks = [blocks[0]] + [exchange(blocks[place], 2 * place) for place in range(1, dp_size // 2)]
     other1, *blocks = lax.optimization_barrier((other1, *blocks))
     half1 = add(half1, other1)
-    blocks[0], half1 = lax.optimization_barrier((blocks[0], half1))
-    other1 = exchange(half1, 1)
-    back, small0 = call_small(
-        share_kernel, (shape(share, full, dtype=LOW), shape(8, full)), [], tuple(blocks), "share"
+    back, both, small0 = call_small(
+        share_kernel,
+        (shape(share, full, dtype=LOW), shape(2 * width + share, full, dtype=LOW), shape(8, full)),
+        [],
+        (half1, *blocks),
+        "share",
     )
-    small0, other1 = lax.optimization_barrier((small0, other1))
-    backs = [back] + [exchange(back, place) for place in range(2, dp_size, 2)]
-    backs = [each for first in backs for each in (first, exchange(first, 1))]
+    neighbour = exchange(both, 1)
+    small0, neighbour = lax.optimization_barrier((small0, neighbour))
+    backs = [back, neighbour]
+    for place in range(2, dp_size, 2):
+        backs += [exchange(back, place)]
+        backs += [exchange(backs[-1], 1)]
     grad_nu, grad_theta, grad_gamma, grad_skip, grad_bias, grad_gain, grad_shift, result, grad_inputs = call(
         finish_kernel,
         (
@@ -1251,10 +1260,12 @@
         [pltpu.VMEM((32, full), F32), pltpu.VMEM((total, width), F32)],
         (lengths, small0, bn1, norm0, feature, nu_log, theta_log, result_rows, up0, grad0, tokens),
         "finish",
+        late=(1, 2, 3, 4, 5, 6),
+        vmem=16 * 1024 * 1024,
     )
     wide = (shape(LAYERS, width, full), shape(LAYERS, width, full), shape(LAYERS, 2 * width, full))
     held = [pltpu.VMEM((1, 4 * width, full), F32)]
-    grads = call_small(widen1_kernel, wide, held, (half1, other1), "widen1", sent=True)
+    grads = call_small(widen1_kernel, wide, held, (half1, neighbour), "widen1", sent=True)
     grad_b, grad_c, grad_glu = call_small(widen0_kernel, wide, held, tuple(backs), "widen0", sent=True, into=tuple(grads))
     grad_b = grad_b.reshape(LAYERS, 2, own_states, full)
     grad_c = grad_c.reshape(LAYERS, 2, own_states, full)

time: 126 us -> 124 us (0.984)
  Pallas kernels: 47.7 us -> 45.3 us
  starting transfers between devices: 31.4 us -> 30 us
    pallas_call x8, Pallas kernels: 6.53 us -> 4.88 us  [call_small(): pl.pallas_call(body, out_shape=tuple(outs), in_specs=[pl.BlockSpec(memory...]
    ppermute x15 -> x14, starting transfers between devices: 15.7 us -> 14.4 us  [exchange(): return lax.ppermute(value, 'dp', [(i, i ^ bit) for i in range(dp_size)])]
    ppermute x15 -> x14, waiting for transfers between devices: 17.1 us -> 18.1 us  [exchange(): return lax.ppermute(value, 'dp', [(i, i ^ bit) for i in range(dp_size)])]
  transfers between devices with their start and end apart: 26 -> 25, of which waited for: 12 -> 12; matrix products, arithmetic and copies ran while one was open for 0% -> 0% of each run, Pallas kernels for 23% -> 23%
where the time goes in v8:
time: 124 us; the launch traced here: 123 us
  Pallas kernels  45.3 us (37%)
  waiting for transfers between devices  31.8 us (26%)
  starting transfers between devices  30 us (24%)
  blocking collectives  12.5 us (10%)
  local copies, waits for them, and re-layouts  1.94 us (2%)
  between operations  1.73 us (1%)
    pallas_call x6, Pallas kernels, call(): pl.pallas_call(body, out_shape=tuple(outs), in_specs=[pl.BlockSpec(memory...  40.4 us
    ppermute x14, waiting for transfers between devices, exchange(): return lax.ppermute(value, 'dp', [(i, i ^ bit) for i in range(dp_size)])  18.1 us
    ppermute x14, starting transfers between devices, exchange(): return lax.ppermute(value, 'dp', [(i, i ^ bit) for i in range(dp_size)])  14.4 us
    all_to_all x1, blocking collectives, across(): return lax.all_to_all(value, axes, 0, 0, tiled=True)  12.5 us
    all_to_all x2, starting transfers between devices, across(): return lax.all_to_all(value, axes, 0, 0, tiled=True)  10 us
    ppermute x9, waiting for transfers between devices, swap(): return lax.ppermute(value, 'state', pairs)  7.83 us
    all_to_all x2, waiting for transfers between devices, across(): return lax.all_to_all(value, axes, 0, 0, tiled=True)  5.93 us
    ppermute x9, starting transfers between devices, swap(): return lax.ppermute(value, 'state', pairs)  5.59 us
  transfers between devices with their start and end apart: 25, of which 12 were waited for; matrix products, arithmetic and copies ran while one was open for 0% of the time, Pallas kernels for 23%

profile of v8, /device:TPU:0, one launch (start us, length us, event | category | flops | bytes accessed | tf_op | source)
XLA Modules:
  0.0 123.3 jit_solution(6526541960024262891)
XLA Ops:
  1.3 3.3 %enter.1 = (f32[1024,128]{1,0:T(8,128)}, f32[8,8,128]{2,1,0:T(8,128)}, bf16[800,512]{1,0:T(8,128)(2,1)}) custom-call(s32[1]{0:T(128)S(6)} %copy.31.refs_0_, f32[128,1024]{1,0:T(8,128)} %bitcast.17, f32[2,128]{1,0:T(2,128)} %refs_2_.1, f32[2,128]{1,0:T(2,128)} %refs_3_.1, f32[2,128]{1,0:T(2,128)} %refs_4_.1, f32[2,2,128]{2,1,0:T(2,128)} %refs_5_.2, ...), custom_call_target="tpu_custom_call" | custom-call | tf_op jit(solution)/shard_map/enter/pallas_call | solution.py:289
  4.6 3.0 %collective-permute-start.2 = (bf16[800,512]{1,0:T(8,128)(2,1)}, bf16[800,512]{1,0:T(8,128)(2,1)}, u32[]{:S(2)}, u32[]{:S(2)}) collective-permute-start(bf16[800,512]{1,0:T(8,128)(2,1)} %get-tuple-element.90.refs_6_), channel_id=1, source_target_pairs={{0,2},{1,3},{2,0},{3,1},{4,6},{5,7},{6,4},{7,5},{8,10},{9,11},{10,... | collective-permute-start | bytes 2457608 | tf_op jit(solution)/shard_map/ppermute | solution.py:1025
  7.6 12.5 %all_to_all.15.refs_0_ = f32[8,8,128]{2,1,0:T(8,128)S(1)} all-to-all(f32[8,8,128]{2,1,0:T(8,128)} %get-tuple-element.89), channel_id=1, replica_groups=mesh['dp'=8,'state'=4] {'dp'}, dimensions={0} | all-to-all | bytes 65536 | tf_op jit(solution)/shard_map/all_to_all | solution.py:1029
  20.1 0.6 total.1.refs_1_
  20.7 0.5 collective-permute-start.4
  21.3 2.9 %cotangent.1 = (f32[1024,128]{1,0:T(8,128)}, bf16[768,512]{1,0:T(8,128)(2,1)}) custom-call(s32[1]{0:T(128)S(6)} %copy.31.refs_0_, f32[128,1024]{1,0:T(8,128)} %bitcast.18, bf16[2,128,512]{2,1,0:T(8,128)(2,1)} %bitcast.14, bf16[2,128,512]{2,1,0:T(8,128)(2,1)} %bitcast.16, bf16[2,256,512]{2,1,0:T(8,128)(2,1)} %bitcast.11), custom_call_target="tpu_custom_call" | custom-call | tf_op jit(solution)/shard_map/cotangent/pallas_call | solution.py:289
  24.1 2.1 %collective-permute-done.4.refs_3_ = f32[8,128]{1,0:T(8,128)} collective-permute-done((f32[8,128]{1,0:T(8,128)}, f32[8,128]{1,0:T(8,128)}, u32[]{:S(2)}, u32[]{:S(2)}) %collective-permute-start.4) | collective-permute-done | bytes 4128 | tf_op jit(solution)/shard_map/ppermute | solution.py:1025
  26.3 0.1 collective-permute-start.6
  26.4 1.8 %collective-permute-start = (bf16[768,512]{1,0:T(8,128)(2,1)}, bf16[768,512]{1,0:T(8,128)(2,1)}, u32[]{:S(2)}, u32[]{:S(2)}) collective-permute-start(bf16[768,512]{1,0:T(8,128)(2,1)} %get-tuple-element.103.refs_7_), channel_id=1, source_target_pairs={{0,2},{1,3},{2,0},{3,1},{4,6},{5,7},{6,4},{7,5},{8,10},{9,11},{10,... | collective-permute-start | bytes 2359304 | tf_op jit(solution)/shard_map/ppermute | solution.py:1025
  28.2 0.2 collective-permute-start.5
  28.3 1.3 %collective-permute-done.5.refs_4_ = f32[8,128]{1,0:T(8,128)} collective-permute-done((f32[8,128]{1,0:T(8,128)}, f32[8,128]{1,0:T(8,128)}, u32[]{:S(2)}, u32[]{:S(2)}) %collective-permute-start.5) | collective-permute-done | bytes 4128 | tf_op jit(solution)/shard_map/ppermute | solution.py:1025
  29.7 9.3 %start.1 = (f32[32,512]{1,0:T(8,128)}, f32[8,256]{1,0:T(8,128)}, f32[8,512]{1,0:T(8,128)}, bf16[1024,512]{1,0:T(8,128)(2,1)}, f32[1024,256]{1,0:T(8,128)}, /*ind...) custom-call(s32[1]{0:T(128)S(6)} %copy.31.refs_0_, ...), custom_call_target="tpu_custom_call" | custom-call | tf_op jit(solution)/shard_map/start/pallas_call | solution.py:289
  39.0 5.9 %all-to-all-start.1 = ((f32[8,8,128]{2,1,0:T(8,128)}), f32[8,8,128]{2,1,0:T(8,128)}, u32[]{:S(2)}, u32[]{:S(2)}) async-start(f32[8,8,128]{2,1,0:T(8,128)} %get-tuple-element.96), calls=%async_computation.1 | async-start | bytes 65536 | tf_op jit(solution)/shard_map/all_to_all | solution.py:1029
  44.9 1.7 %collective-permute-done.refs_9_ = bf16[768,512]{1,0:T(8,128)(2,1)} collective-permute-done((bf16[768,512]{1,0:T(8,128)(2,1)}, bf16[768,512]{1,0:T(8,128)(2,1)}, u32[]{:S(2)}, u32[]{:S(2)}) %collective-permute-start) | collective-permute-done | bytes 786464 | tf_op jit(solution)/shard_map/ppermute | solution.py:1025
  46.6 5.0 %all-to-all-done.1.refs_1_ = f32[8,8,128]{2,1,0:T(8,128)} async-done(((f32[8,8,128]{2,1,0:T(8,128)}), f32[8,8,128]{2,1,0:T(8,128)}, u32[]{:S(2)}, u32[]{:S(2)}) %all-to-all-start.1) | async-done | bytes 32800 | tf_op jit(solution)/shard_map/all_to_all | solution.py:1029
  51.7 2.6 %collective-permute-done.8.refs_10_ = bf16[768,512]{1,0:T(8,128)(2,1)} collective-permute-done((bf16[768,512]{1,0:T(8,128)(2,1)}, bf16[768,512]{1,0:T(8,128)(2,1)}, u32[]{:S(2)}, u32[]{:S(2)}) %collective-permute-start.8) | collective-permute-done | bytes 786464 | tf_op jit(solution)/shard_map/ppermute | solution.py:1025
  54.3 12.7 %middle.1 = (f32[1024,128]{1,0:T(8,128)}, f32[1024,512]{1,0:T(8,128)}, f32[8,16,128]{2,1,0:T(8,128)}, f32[8,512]{1,0:T(8,128)}, bf16[256,512]{1,0:T(8,128)(2,1)}, /*index=5*/bf16[256,512]{1,0:T(8,128)(2,1)}) custom-call(s32[1]{0:T(128)S(6)} %copy.31.refs_0_, f32[8,8,128]{2,1,0:T(8,128)} %all-to-all-done.1.refs_1_, ...), custom_call_target="tpu_custom_call" | custom-call | flops 1000000000 | tf_op jit(solution)/shard_map/middle/pallas_call | solution.py:289
  67.0 0.5 collective-permute-start.9
  67.5 4.2 %all-to-all-start.2 = ((f32[8,16,128]{2,1,0:T(8,128)}), f32[8,16,128]{2,1,0:T(8,128)}, u32[]{:S(2)}, u32[]{:S(2)}) async-start(f32[8,16,128]{2,1,0:T(8,128)} %get-tuple-element.105), calls=%async_computation.2 | async-start | bytes 131072 | tf_op jit(solution)/shard_map/all_to_all | solution.py:1029
  71.7 4.1 %collective-permute-done.9.refs_1_ = bf16[256,512]{1,0:T(8,128)(2,1)S(1)} collective-permute-done((bf16[256,512]{1,0:T(8,128)(2,1)}, bf16[256,512]{1,0:T(8,128)(2,1)S(1)}, u32[]{:S(2)}, u32[]{:S(2)}) %collective-permute-start.9) | collective-permute-done | bytes 262176 | tf_op jit(solution)/shard_map/ppermute | solution.py:1066
  75.8 0.9 copy-done.6
  76.8 0.8 add.3.refs_0_
  77.5 0.9 all-to-all-done.2.refs_1_.refs_2_
  78.4 0.5 collective-permute-start.10
  78.9 9.0 %last.1 = (bf16[272,512]{1,0:T(8,128)(2,1)}, bf16[272,512]{1,0:T(8,128)(2,1)}, f32[1024,128]{1,0:T(8,128)}, f32[1024,128]{1,0:T(8,128)}) custom-call(s32[1]{0:T(128)S(6)} %copy.31.refs_0_, f32[8,16,128]{2,1,0:T(8,128)} %all-to-all-done.2.refs_1_.refs_2_, f32[8,512]{1,0:T(8,128)} %get-tuple-element.110.refs_2_, f32[32,512]{1,0:T(8,128)} %get-tuple-element.99.refs_3_.refs_4_, ...), custom_call_target="tpu_custom_call" | custom-call | flops 99999997952 | tf_op jit(solution)/shard_map/last/pallas_call | solution.py:289
  88.0 0.5 collective-permute-start.12
  88.4 3.4 %collective-permute-done.10.refs_1_ = bf16[256,512]{1,0:T(8,128)(2,1)} collective-permute-done((bf16[256,512]{1,0:T(8,128)(2,1)}, bf16[256,512]{1,0:T(8,128)(2,1)}, u32[]{:S(2)}, u32[]{:S(2)}) %collective-permute-start.10) | collective-permute-done | bytes 262176 | tf_op jit(solution)/shard_map/ppermute | solution.py:1066
  91.9 1.1 add.4.refs_0_
  92.9 0.1 collective-permute-start.11
  93.0 2.5 %collective-permute-done.12.refs_1_ = bf16[272,512]{1,0:T(8,128)(2,1)S(1)} collective-permute-done((bf16[272,512]{1,0:T(8,128)(2,1)}, bf16[272,512]{1,0:T(8,128)(2,1)S(1)}, u32[]{:S(2)}, u32[]{:S(2)}) %collective-permute-start.12) | collective-permute-done | bytes 278560 | tf_op jit(solution)/shard_map/ppermute | solution.py:1066
  95.5 1.0 copy-done.4
  96.5 0.1 pair.1
  96.6 0.5 collective-permute-start.13
  97.1 2.0 %collective-permute-start.14 = (bf16[80,512]{1,0:T(8,128)(2,1)S(1)}, bf16[80,512]{1,0:T(8,128)(2,1)S(1)}, u32[]{:S(2)}, u32[]{:S(2)}) collective-permute-start(bf16[80,512]{1,0:T(8,128)(2,1)S(1)} %get-tuple-element.130), channel_id=1, source_target_pairs={{0,16},{4,20},{8,24},{12,28},{16,0},{20,4},{24,8},{28,12},{1,17},{... | collective-permute-start | bytes 245768 | tf_op jit(solution)/shard_map/ppermute | solution.py:1066
  99.1 1.9 %collective-permute-start.15 = (bf16[80,512]{1,0:T(8,128)(2,1)S(1)}, bf16[80,512]{1,0:T(8,128)(2,1)S(1)}, u32[]{:S(2)}, u32[]{:S(2)}) collective-permute-start(bf16[80,512]{1,0:T(8,128)(2,1)S(1)} %get-tuple-element.131), channel_id=1, source_target_pairs={{0,24},{4,28},{8,16},{12,20},{16,8},{20,12},{24,0},{28,4},{1,25},{... | collective-permute-start | bytes 245768 | tf_op jit(solution)/shard_map/ppermute | solution.py:1066
  101.0 5.5 %collective-permute-done.13.refs_2_ = bf16[80,512]{1,0:T(8,128)(2,1)S(1)} collective-permute-done((bf16[80,512]{1,0:T(8,128)(2,1)S(1)}, bf16[80,512]{1,0:T(8,128)(2,1)S(1)}, u32[]{:S(2)}, u32[]{:S(2)}) %collective-permute-start.13) | collective-permute-done | bytes 81952 | tf_op jit(solution)/shard_map/ppermute | solution.py:1066
  106.6 0.7 collective-permute-start.16
  107.4 2.3 %collective-permute-start.21 = (bf16[64,512]{1,0:T(8,128)(2,1)S(1)}, bf16[64,512]{1,0:T(8,128)(2,1)S(1)}, u32[]{:S(2)}, u32[]{:S(2)}) collective-permute-start(bf16[64,512]{1,0:T(8,128)(2,1)S(1)} %get-tuple-element.147.refs_0_), channel_id=1, source_target_pairs={{0,24},{4,28},{8,16},{12,20},{16,8},{20,12},{24,0},{28,4},{1,25},{... | collective-permute-start | bytes 196616 | tf_op jit(solution)/shard_map/ppermute | solution.py:1066
  109.7 0.3 collective-permute-start.19
  110.0 1.8 %collective-permute-start.17 = (bf16[64,512]{1,0:T(8,128)(2,1)S(1)}, bf16[64,512]{1,0:T(8,128)(2,1)S(1)}, u32[]{:S(2)}, u32[]{:S(2)}) collective-permute-start(bf16[64,512]{1,0:T(8,128)(2,1)S(1)} %get-tuple-element.147.refs_0_), channel_id=1, source_target_pairs={{0,8},{4,12},{8,0},{12,4},{16,24},{20,28},{24,16},{28,20},{1,9},{5... | collective-permute-start | bytes 196616 | tf_op jit(solution)/shard_map/ppermute | solution.py:1066
  111.8 2.2 %collective-permute-done.21.refs_6_ = bf16[64,512]{1,0:T(8,128)(2,1)S(1)} collective-permute-done((bf16[64,512]{1,0:T(8,128)(2,1)S(1)}, bf16[64,512]{1,0:T(8,128)(2,1)S(1)}, u32[]{:S(2)}, u32[]{:S(2)}) %collective-permute-start.21) | collective-permute-done | bytes 65568 | tf_op jit(solution)/shard_map/ppermute | solution.py:1066
  114.0 1.2 %collective-permute-start.22 = (bf16[64,512]{1,0:T(8,128)(2,1)S(1)}, bf16[64,512]{1,0:T(8,128)(2,1)S(1)}, u32[]{:S(2)}, u32[]{:S(2)}) collective-permute-start(bf16[64,512]{1,0:T(8,128)(2,1)S(1)} %collective-permute-done.21.refs_6_), channel_id=1, source_target_pairs={{0,4},{4,0},{8,12},{12,8},{16,20},{20,16},{24,28},{28,24},{1,5},{5... | collective-permute-start | bytes 196616 | tf_op jit(solution)/shard_map/ppermute | solution.py:1066
  115.2 0.3 collective-permute-done.19.refs_4_
  115.6 1.6 %collective-permute-start.20 = (bf16[64,512]{1,0:T(8,128)(2,1)S(1)}, bf16[64,512]{1,0:T(8,128)(2,1)S(1)}, u32[]{:S(2)}, u32[]{:S(2)}) collective-permute-start(bf16[64,512]{1,0:T(8,128)(2,1)S(1)} %collective-permute-done.19.refs_4_), channel_id=1, source_target_pairs={{0,4},{4,0},{8,12},{12,8},{16,20},{20,16},{24,28},{28,24},{1,5},{5... | collective-permute-start | bytes 196616 | tf_op jit(solution)/shard_map/ppermute | solution.py:1066
  117.1 0.5 collective-permute-start.18
  117.6 1.1 widen1.1
  118.8 3.2 %finish.1 = (f32[2,64]{1,0:T(2,128)}, f32[2,64]{1,0:T(2,128)}, f32[2,64]{1,0:T(2,128)}, f32[2,128]{1,0:T(2,128)}, f32[2,2,128]{2,1,0:T(2,128)}, /*index=5*/f32[2...) custom-call(s32[1]{0:T(128)S(6)} %copy.31.refs_0_, f32[8,512]{1,0:T(8,128)S(1)} %get-tuple-element.139.refs_1_, ...), custom_call_target="tpu_custom_call" | custom-call | tf_op jit(solution)/shard_map/finish/pallas_call | solution.py:289
  122.0 1.1 widen0.1
  (37 shorter events, 0.2 us)
Async XLA Ops:
  4.6 21.7 %collective-permute-start.2 = (bf16[800,512]{1,0:T(8,128)(2,1)}, bf16[800,512]{1,0:T(8,128)(2,1)}, u32[]{:S(2)}, u32[]{:S(2)}) collective-permute-start(bf16[800,512]{1,0:T(8,128)(2,1)} %get-tuple-element.90.refs_6_), channel_id=1, source_target_pairs={{0,2},{1,3},{2,0},{3,1},{4,6},{5,7},{6,4},{7,5},{8,10},{9,11},{10,... | collective-permute-start | bytes 2457608 | tf_op jit(solution)/shard_map/ppermute | solution.py:1025
  7.6 18.7 %collective-permute-start.1 = (bf16[800,512]{1,0:T(8,128)(2,1)}, bf16[800,512]{1,0:T(8,128)(2,1)}, u32[]{:S(2)}, u32[]{:S(2)}) collective-permute-start(bf16[800,512]{1,0:T(8,128)(2,1)} %get-tuple-element.90.refs_6_), channel_id=1, source_target_pairs={{0,1},{1,0},{2,3},{3,2},{4,5},{5,4},{6,7},{7,6},{8,9},{9,8},{10,11... | collective-permute-start | bytes 2457608 | tf_op jit(solution)/shard_map/ppermute | solution.py:1025
  20.7 5.5 %collective-permute-start.4 = (f32[8,128]{1,0:T(8,128)}, f32[8,128]{1,0:T(8,128)}, u32[]{:S(2)}, u32[]{:S(2)}) collective-permute-start(f32[8,128]{1,0:T(8,128)} %total.1.refs_1_), channel_id=1, source_target_pairs={{0,2},{1,3},{2,0},{3,1},{4,6},{5,7},{6,4},{7,5},{8,10},{9,11},{10,... | collective-permute-start | bytes 12296 | tf_op jit(solution)/shard_map/ppermute | solution.py:1025
  21.3 5.0 %collective-permute-start.3 = (f32[8,128]{1,0:T(8,128)}, f32[8,128]{1,0:T(8,128)}, u32[]{:S(2)}, u32[]{:S(2)}) collective-permute-start(f32[8,128]{1,0:T(8,128)} %total.1.refs_1_), channel_id=1, source_target_pairs={{0,1},{1,0},{2,3},{3,2},{4,5},{5,4},{6,7},{7,6},{8,9},{9,8},{10,11... | collective-permute-start | bytes 12296 | tf_op jit(solution)/shard_map/ppermute | solution.py:1025
  26.3 3.4 %collective-permute-start.6 = (bf16[800,512]{1,0:T(8,128)(2,1)}, bf16[800,512]{1,0:T(8,128)(2,1)}, u32[]{:S(2)}, u32[]{:S(2)}) collective-permute-start(bf16[800,512]{1,0:T(8,128)(2,1)} %collective-permute-done.2.refs_8_), channel_id=1, source_target_pairs={{0,1},{1,0},{2,3},{3,2},{4,5},{5,4},{6,7},{7,6},{8,9},{9,8},{10,11... | collective-permute-start | bytes 2457608 | tf_op jit(solution)/shard_map/ppermute | solution.py:1025
  26.4 20.3 %collective-permute-start = (bf16[768,512]{1,0:T(8,128)(2,1)}, bf16[768,512]{1,0:T(8,128)(2,1)}, u32[]{:S(2)}, u32[]{:S(2)}) collective-permute-start(bf16[768,512]{1,0:T(8,128)(2,1)} %get-tuple-element.103.refs_7_), channel_id=1, source_target_pairs={{0,2},{1,3},{2,0},{3,1},{4,6},{5,7},{6,4},{7,5},{8,10},{9,11},{10,... | collective-permute-start | bytes 2359304 | tf_op jit(solution)/shard_map/ppermute | solution.py:1025
  28.2 1.5 %collective-permute-start.5 = (f32[8,128]{1,0:T(8,128)}, f32[8,128]{1,0:T(8,128)}, u32[]{:S(2)}, u32[]{:S(2)}) collective-permute-start(f32[8,128]{1,0:T(8,128)} %collective-permute-done.4.refs_3_), channel_id=1, source_target_pairs={{0,1},{1,0},{2,3},{3,2},{4,5},{5,4},{6,7},{7,6},{8,9},{9,8},{10,11... | collective-permute-start | bytes 12296 | tf_op jit(solution)/shard_map/ppermute | solution.py:1025
  39.0 12.6 %all-to-all-start.1 = ((f32[8,8,128]{2,1,0:T(8,128)}), f32[8,8,128]{2,1,0:T(8,128)}, u32[]{:S(2)}, u32[]{:S(2)}) async-start(f32[8,8,128]{2,1,0:T(8,128)} %get-tuple-element.96), calls=%async_computation.1 | async-start | bytes 65536 | tf_op jit(solution)/shard_map/all_to_all | solution.py:1029
  44.9 6.8 %collective-permute-start.7 = (bf16[768,512]{1,0:T(8,128)(2,1)}, bf16[768,512]{1,0:T(8,128)(2,1)}, u32[]{:S(2)}, u32[]{:S(2)}) collective-permute-start(bf16[768,512]{1,0:T(8,128)(2,1)} %get-tuple-element.103.refs_7_), channel_id=1, source_target_pairs={{0,1},{1,0},{2,3},{3,2},{4,5},{5,4},{6,7},{7,6},{8,9},{9,8},{10,11... | collective-permute-start | bytes 2359304 | tf_op jit(solution)/shard_map/ppermute | solution.py:1025
  51.7 2.6 %collective-permute-start.8 = (bf16[768,512]{1,0:T(8,128)(2,1)}, bf16[768,512]{1,0:T(8,128)(2,1)}, u32[]{:S(2)}, u32[]{:S(2)}) collective-permute-start(bf16[768,512]{1,0:T(8,128)(2,1)} %collective-permute-done.refs_9_), channel_id=1, source_target_pairs={{0,1},{1,0},{2,3},{3,2},{4,5},{5,4},{6,7},{7,6},{8,9},{9,8},{10,11... | collective-permute-start | bytes 2359304 | tf_op jit(solution)/shard_map/ppermute | solution.py:1025
  67.0 8.8 %collective-permute-start.9 = (bf16[256,512]{1,0:T(8,128)(2,1)}, bf16[256,512]{1,0:T(8,128)(2,1)S(1)}, u32[]{:S(2)}, u32[]{:S(2)}) collective-permute-start(bf16[256,512]{1,0:T(8,128)(2,1)} %get-tuple-element.107), channel_id=1, source_target_pairs={{0,4},{4,0},{8,12},{12,8},{16,20},{20,16},{24,28},{28,24},{1,5},{5... | collective-permute-start | bytes 786440 | tf_op jit(solution)/shard_map/ppermute | solution.py:1066
  67.5 10.9 %all-to-all-start.2 = ((f32[8,16,128]{2,1,0:T(8,128)}), f32[8,16,128]{2,1,0:T(8,128)}, u32[]{:S(2)}, u32[]{:S(2)}) async-start(f32[8,16,128]{2,1,0:T(8,128)} %get-tuple-element.105), calls=%async_computation.2 | async-start | bytes 131072 | tf_op jit(solution)/shard_map/all_to_all | solution.py:1029
  75.8 1.0 copy-start.6
  78.4 13.4 %collective-permute-start.10 = (bf16[256,512]{1,0:T(8,128)(2,1)}, bf16[256,512]{1,0:T(8,128)(2,1)}, u32[]{:S(2)}, u32[]{:S(2)}) collective-permute-start(bf16[256,512]{1,0:T(8,128)(2,1)} %add.3.refs_0_), channel_id=1, source_target_pairs={{0,16},{4,20},{8,24},{12,28},{16,0},{20,4},{24,8},{28,12},{1,17},{... | collective-permute-start | bytes 786440 | tf_op jit(solution)/shard_map/ppermute | solution.py:1066
  87.9 30.8 %copy-start = (f32[1024,128]{1,0:T(8,128)S(1)}, f32[1024,128]{1,0:T(8,128)}, u32[]{:S(2)}) copy-start(f32[1024,128]{1,0:T(8,128)} %get-tuple-element.93.refs_5_.refs_18_.refs_10_) | copy-start | bytes 1572868
  87.9 30.8 %copy-start.1 = (f32[1024,128]{1,0:T(8,128)S(1)}, f32[1024,128]{1,0:T(8,128)}, u32[]{:S(2)}) copy-start(f32[1024,128]{1,0:T(8,128)} %get-tuple-element.140.refs_7_) | copy-start | bytes 1572868
  88.0 30.8 %copy-start.2 = (f32[1024,128]{1,0:T(8,128)S(1)}, f32[1024,128]{1,0:T(8,128)}, u32[]{:S(2)}) copy-start(f32[1024,128]{1,0:T(8,128)} %get-tuple-element.141.refs_8_) | copy-start | bytes 1572868
  88.0 30.8 %copy-start.3 = (f32[1024,128]{1,0:T(8,128)S(1)}, f32[1024,128]{1,0:T(8,128)}, u32[]{:S(2)}) copy-start(f32[1024,128]{1,0:T(8,128)} %get-tuple-element.142.refs_9_) | copy-start | bytes 1572868
  88.0 7.5 %collective-permute-start.12 = (bf16[272,512]{1,0:T(8,128)(2,1)}, bf16[272,512]{1,0:T(8,128)(2,1)S(1)}, u32[]{:S(2)}, u32[]{:S(2)}) collective-permute-start(bf16[272,512]{1,0:T(8,128)(2,1)} %get-tuple-element.127), channel_id=1, source_target_pairs={{0,4},{4,0},{8,12},{12,8},{16,20},{20,16},{24,28},{28,24},{1,5},{5... | collective-permute-start | bytes 835592 | tf_op jit(solution)/shard_map/ppermute | solution.py:1066
  92.9 13.6 %collective-permute-start.11 = (bf16[256,512]{1,0:T(8,128)(2,1)S(1)}, bf16[256,512]{1,0:T(8,128)(2,1)S(1)}, u32[]{:S(2)}, u32[]{:S(2)}) collective-permute-start(bf16[256,512]{1,0:T(8,128)(2,1)S(1)} %add.4.refs_0_), channel_id=1, source_target_pairs={{0,8},{4,12},{8,0},{12,4},{16,24},{20,28},{24,16},{28,20},{1,9},{5... | collective-permute-start | bytes 786440 | tf_op jit(solution)/shard_map/ppermute | solution.py:1066
  95.5 1.0 copy-start.4
  96.4 22.3 %copy-start.5 = (f32[32,512]{1,0:T(8,128)S(1)}, f32[32,512]{1,0:T(8,128)}, u32[]{:S(2)}) copy-start(f32[32,512]{1,0:T(8,128)} %get-tuple-element.99.refs_3_.refs_4_) | copy-start | bytes 196612
  96.4 22.3 %copy-start.7 = (f32[8,512]{1,0:T(8,128)S(1)}, f32[8,512]{1,0:T(8,128)}, u32[]{:S(2)}) copy-start(f32[8,512]{1,0:T(8,128)} %get-tuple-element.98.refs_2_.refs_5_.refs_3_) | copy-start | bytes 49156
  96.5 22.3 %copy-start.8 = (f32[2,64]{1,0:T(2,128)S(1)}, f32[2,64]{1,0:T(2,128)}, u32[]{:S(2)}) copy-start(f32[2,64]{1,0:T(2,128)} %refs_5_.3) | copy-start | bytes 1540
  96.5 22.3 %copy-start.9 = (f32[2,64]{1,0:T(2,128)S(1)}, f32[2,64]{1,0:T(2,128)}, u32[]{:S(2)}) copy-start(f32[2,64]{1,0:T(2,128)} %refs_6_.3) | copy-start | bytes 1540
  96.6 9.9 %collective-permute-start.13 = (bf16[80,512]{1,0:T(8,128)(2,1)S(1)}, bf16[80,512]{1,0:T(8,128)(2,1)S(1)}, u32[]{:S(2)}, u32[]{:S(2)}) collective-permute-start(bf16[80,512]{1,0:T(8,128)(2,1)S(1)} %get-tuple-element.129), channel_id=1, source_target_pairs={{0,8},{4,12},{8,0},{12,4},{16,24},{20,28},{24,16},{28,20},{1,9},{5... | collective-permute-start | bytes 245768 | tf_op jit(solution)/shard_map/ppermute | solution.py:1066
  97.1 9.4 %collective-permute-start.14 = (bf16[80,512]{1,0:T(8,128)(2,1)S(1)}, bf16[80,512]{1,0:T(8,128)(2,1)S(1)}, u32[]{:S(2)}, u32[]{:S(2)}) collective-permute-start(bf16[80,512]{1,0:T(8,128)(2,1)S(1)} %get-tuple-element.130), channel_id=1, source_target_pairs={{0,16},{4,20},{8,24},{12,28},{16,0},{20,4},{24,8},{28,12},{1,17},{... | collective-permute-start | bytes 245768 | tf_op jit(solution)/shard_map/ppermute | solution.py:1066
  99.1 7.4 %collective-permute-start.15 = (bf16[80,512]{1,0:T(8,128)(2,1)S(1)}, bf16[80,512]{1,0:T(8,128)(2,1)S(1)}, u32[]{:S(2)}, u32[]{:S(2)}) collective-permute-start(bf16[80,512]{1,0:T(8,128)(2,1)S(1)} %get-tuple-element.131), channel_id=1, source_target_pairs={{0,24},{4,28},{8,16},{12,20},{16,8},{20,12},{24,0},{28,4},{1,25},{... | collective-permute-start | bytes 245768 | tf_op jit(solution)/shard_map/ppermute | solution.py:1066
  106.6 10.9 %collective-permute-start.16 = (bf16[320,512]{1,0:T(8,128)(2,1)S(1)}, bf16[320,512]{1,0:T(8,128)(2,1)S(1)}, u32[]{:S(2)}, u32[]{:S(2)}) collective-permute-start(bf16[320,512]{1,0:T(8,128)(2,1)S(1)} %get-tuple-element.138), channel_id=1, source_target_pairs={{0,4},{4,0},{8,12},{12,8},{16,20},{20,16},{24,28},{28,24},{1,5},{5... | collective-permute-start | bytes 983048 | tf_op jit(solution)/shard_map/ppermute | solution.py:1066
  107.4 6.6 %collective-permute-start.21 = (bf16[64,512]{1,0:T(8,128)(2,1)S(1)}, bf16[64,512]{1,0:T(8,128)(2,1)S(1)}, u32[]{:S(2)}, u32[]{:S(2)}) collective-permute-start(bf16[64,512]{1,0:T(8,128)(2,1)S(1)} %get-tuple-element.147.refs_0_), channel_id=1, source_target_pairs={{0,24},{4,28},{8,16},{12,20},{16,8},{20,12},{24,0},{28,4},{1,25},{... | collective-permute-start | bytes 196616 | tf_op jit(solution)/shard_map/ppermute | solution.py:1066
  109.7 5.9 %collective-permute-start.19 = (bf16[64,512]{1,0:T(8,128)(2,1)S(1)}, bf16[64,512]{1,0:T(8,128)(2,1)S(1)}, u32[]{:S(2)}, u32[]{:S(2)}) collective-permute-start(bf16[64,512]{1,0:T(8,128)(2,1)S(1)} %get-tuple-element.147.refs_0_), channel_id=1, source_target_pairs={{0,16},{4,20},{8,24},{12,28},{16,0},{20,4},{24,8},{28,12},{1,17},{... | collective-permute-start | bytes 196616 | tf_op jit(solution)/shard_map/ppermute | solution.py:1066
  110.0 7.2 %collective-permute-start.17 = (bf16[64,512]{1,0:T(8,128)(2,1)S(1)}, bf16[64,512]{1,0:T(8,128)(2,1)S(1)}, u32[]{:S(2)}, u32[]{:S(2)}) collective-permute-start(bf16[64,512]{1,0:T(8,128)(2,1)S(1)} %get-tuple-element.147.refs_0_), channel_id=1, source_target_pairs={{0,8},{4,12},{8,0},{12,4},{16,24},{20,28},{24,16},{28,20},{1,9},{5... | collective-permute-start | bytes 196616 | tf_op jit(solution)/shard_map/ppermute | solution.py:1066
  114.0 8.0 %collective-permute-start.22 = (bf16[64,512]{1,0:T(8,128)(2,1)S(1)}, bf16[64,512]{1,0:T(8,128)(2,1)S(1)}, u32[]{:S(2)}, u32[]{:S(2)}) collective-permute-start(bf16[64,512]{1,0:T(8,128)(2,1)S(1)} %collective-permute-done.21.refs_6_), channel_id=1, source_target_pairs={{0,4},{4,0},{8,12},{12,8},{16,20},{20,16},{24,28},{28,24},{1,5},{5... | collective-permute-start | bytes 196616 | tf_op jit(solution)/shard_map/ppermute | solution.py:1066
  115.6 6.4 %collective-permute-start.20 = (bf16[64,512]{1,0:T(8,128)(2,1)S(1)}, bf16[64,512]{1,0:T(8,128)(2,1)S(1)}, u32[]{:S(2)}, u32[]{:S(2)}) collective-permute-start(bf16[64,512]{1,0:T(8,128)(2,1)S(1)} %collective-permute-done.19.refs_4_), channel_id=1, source_target_pairs={{0,4},{4,0},{8,12},{12,8},{16,20},{20,16},{24,28},{28,24},{1,5},{5... | collective-permute-start | bytes 196616 | tf_op jit(solution)/shard_map/ppermute | solution.py:1066
  117.1 4.8 %collective-permute-start.18 = (bf16[64,512]{1,0:T(8,128)(2,1)S(1)}, bf16[64,512]{1,0:T(8,128)(2,1)S(1)}, u32[]{:S(2)}, u32[]{:S(2)}) collective-permute-start(bf16[64,512]{1,0:T(8,128)(2,1)S(1)} %collective-permute-done.17.refs_2_), channel_id=1, source_target_pairs={{0,4},{4,0},{8,12},{12,8},{16,20},{20,16},{24,28},{28,24},{1,5},{5... | collective-permute-start | bytes 196616 | tf_op jit(solution)/shard_map/ppermute | solution.py:1066

commit v9 on v8

--- a/solution.py
+++ b/solution.py
@@ -496,32 +496,34 @@
     return [functools.partial(product, place) for place in range(2)]
 
 
-def output_products(grads_ref, low_re, low_im, pre_grad_ref, states):
-    half = states // 4
-
-    def product(place, low, sign):
-        got = sign * dot(low(), pre_grad_ref[...], TN)[:half, :]
-        grads_ref[2 * half + place * half : 2 * half + (place + 1) * half, :] = got.astype(LOW)
-
-    return [functools.partial(product, 0, low_re, 1.0), functools.partial(product, 1, low_im, -1.0)]
+def pack_own(source_ref, im_lane, packed_ref):
+    lane = lax.broadcasted_iota(jnp.int32, (16, 128), 1)
+    for rows, _ in blocks_of(0, source_ref.shape[0]):
+        re = source_ref[rows, 0:128].astype(F32)
+        im = source_ref[rows, im_lane : im_lane + 128].astype(F32)
+        packed_ref[rows, :] = jnp.where(lane < 64, re, pltpu.roll(im, 64, 1)).astype(LOW)
+
+
+def output_product(grads_ref, packed_ref, pre_grad_ref):
+    got = dot(packed_ref[...], pre_grad_ref[...], TN)
+    half = got.shape[0] // 2
+    grads_ref[2 * half : 3 * half, :] = got[:half, :].astype(LOW)
+    grads_ref[3 * half : 4 * half, :] = -got[half:, :].astype(LOW)
 
 
 def beside_sweep(products, grad_gated_ref, pre_grad_ref, normed_ref, quarter, small_ref):
-    first, second, third, fourth = products
     return (
-        together(first, functools.partial(bias_sums, grad_gated_ref, quarter, small_ref)),
-        together(second, functools.partial(skip_sums, pre_grad_ref, normed_ref, quarter, small_ref)),
-        third,
-        fourth,
+        *products,
+        together(
+            functools.partial(bias_sums, grad_gated_ref, quarter, small_ref),
+            functools.partial(skip_sums, pre_grad_ref, normed_ref, quarter, small_ref),
+        ),
     )
 
 
-def input_products(grads_ref, grad_driven_ref, normed_ref, states):
-    half = states // 4
-    for place in range(2):
-        lanes = slice(place * states, place * states + 128)
-        got = dot(grad_driven_ref[:, lanes], normed_ref[...], TN)[:half, :]
-        grads_ref[place * half : (place + 1) * half, :] = got.astype(LOW)
+def input_product(grads_ref, packed_ref, normed_ref):
+    got = dot(packed_ref[...], normed_ref[...], TN)
+    grads_ref[0 : got.shape[0], :] = got.astype(LOW)
 
 
 def enter_kernel(length_ref, ins, outs, held_ref, params_ref):
@@ -720,7 +722,7 @@
 def middle_kernel(
     length_ref, ins, outs,
     small_ref, b_ref, c_ref, w_ref, normed_ref, drive_ref, drive_own_ref, low_ref, slope_ref, active_ref, held_ref, pre_ref, mixed_ref,
-    up_ref, grad_gated_ref, pre_grad_ref, grad_driven_ref, grads_ref,
+    up_ref, grad_gated_ref, pre_grad_ref, grad_driven_ref, grads_ref, packed_ref,
 ):
     sums, norm0, feature_in, state_in, stream, up_own = ins[:6]
     parts = ins[6:]
@@ -773,6 +775,7 @@
     bias_linear = feature[5 + BIAS_LINEAR : 6 + BIAS_LINEAR, :]
     bias_gate = feature[5 + BIAS_GATE : 6 + BIAS_GATE, :]
     pre_products(low_ref, c_ref, pre_ref)
+    pack_own(low_ref, states, packed_ref)
     for piece in pieces_of(total):
         pre_piece(piece, pre_ref, normed_ref, skip, active_ref, slope_ref)
         held_ref[piece, :] = dot(active_ref[piece, :], w_ref[...], NT)
@@ -798,13 +801,14 @@
         low_ref, states, drive_own_ref, state, 5, length, drive_ref, grad_driven_ref, small_ref, False,
         beside_sweep(
             glu_products(grads_ref, 2 * width, grad_gated_ref, active_ref, quarter)
-            + output_products(grads_ref, lambda: low_ref[:, 0:128], lambda: low_ref[:, states : states + 128], pre_grad_ref, states),
+            + [functools.partial(output_product, grads_ref, packed_ref, pre_grad_ref)],
             grad_gated_ref, pre_grad_ref, normed_ref, quarter, small_ref,
         ),
     )
     scale = inv_dev * gain
     for piece in pieces_of(total):
         pre_ref[piece, :] = dot(grad_driven_ref[piece, :], b_ref[...], NN)
+    pack_own(grad_driven_ref, states, packed_ref)
     plain, scaled = jnp.zeros((8, full), F32), jnp.zeros((8, full), F32)
     for place, piece in enumerate(pieces_of(total)):
         for rows, _ in blocks_of(piece.start, piece.stop):
@@ -814,16 +818,16 @@
             plain += folded(grad)
             scaled += folded(grad * z)
         base.send_piece(place)
-    input_products(grads_ref, grad_driven_ref, normed_ref, states)
+    input_product(grads_ref, packed_ref, normed_ref)
     sent = narrowed([column_sum(plain), column_sum(scaled)], width)
     spread_rows(jnp.concatenate([sent, small_ref[:, 0:width]], axis=0), spread)
     send_halves(grads_ref, shares, 0)
 
 
 def last_kernel(
-    length_ref, ins, outs, held_ref, grad_state_ref, grad_gated_ref, pre_grad_ref, grad_driven_ref, small_ref, up_ref, grads_ref, pack_ref, low_ref
+    length_ref, ins, outs, held_ref, grad_state_ref, grad_gated_ref, pre_grad_ref, grad_driven_ref, small_ref, up_ref, grads_ref, pack_ref, low_ref, packed_ref
 ):
-    (sums, norm1, feature_in, state_in, norm0, stream, base, gate, linear, w, slope, c, normed, active, low, drive_own, b, x) = ins
+    (sums, norm1, feature_in, state_in, norm0, stream, base, gate, linear, w, slope, c, low, normed, active, drive_own, b, x) = ins
     kept, sent, up_out, grad_out = outs
     length, quarter = length_ref[0], own_quarter()
     total, full = stream.ref.shape
@@ -853,8 +857,9 @@
         if place == 0:
             w.wait()
         held_ref[piece, :] = dot(grad_gated_ref[piece, :], w.ref[...], NN)
-    for value in (slope, c):
+    for value in (slope, c, low):
         value.wait()
+    pack_own(low.ref, 128, packed_ref)
     for piece in pieces_of(total):
         pre_grad_piece(piece, held_ref, slope.ref, pre_grad_ref)
         grad_state_ref[piece, :] = dot(pre_grad_ref[piece, :], c.ref[...], NT)
@@ -872,14 +877,15 @@
         low.ref, 128, drive_own.ref, state, 2, length, grad_state_ref, grad_driven_ref, small_ref, True,
         beside_sweep(
             glu_products(grads_ref, 2 * width, grad_gated_ref, active.ref, quarter)
-            + output_products(grads_ref, lambda: low.ref[:, :128], lambda: low.ref[:, 128:], pre_grad_ref, state.shape[1]),
+            + [functools.partial(output_product, grads_ref, packed_ref, pre_grad_ref)],
             grad_gated_ref, pre_grad_ref, normed.ref, quarter, small_ref,
         ),
     )
     b.wait()
     x.wait()
     held_ref[:, :width] = dot(grad_driven_ref[...], b.ref[:, own], NN)
-    input_products(grads_ref, grad_driven_ref, normed.ref, state.shape[1])
+    pack_own(grad_driven_ref, state.shape[1], packed_ref)
+    input_product(grads_ref, packed_ref, normed.ref)
     zero = jnp.zeros((8, width), F32)
     centre0, inv_dev0 = norm0.wait()[0:1, own], norm0.ref[1:2, own]
     skip = feature[SKIP : SKIP + 1, own]
@@ -1174,6 +1180,7 @@
             pltpu.VMEM((total, full), LOW),
             pltpu.VMEM((total, 2 * states), LOW),
             pltpu.VMEM((4 * width, full), LOW),
+            pltpu.VMEM((total, width), LOW),
         ],
         (lengths, sums1, norm0, feature, state, stream1, up_own, *later_parts),
         "middle",
@@ -1205,8 +1212,9 @@
             pltpu.VMEM((4 * width, full), LOW),
             pltpu.VMEM((16, full), F32),
             pltpu.VMEM((16, full), LOW),
+            pltpu.VMEM((total, width), LOW),
         ],
-        (lengths, bn1, norm1, feature, state, norm0, stream1, base, gate0, linear0, w_all, slope0, c_all, normed0, active0, low0,
+        (lengths, bn1, norm1, feature, state, norm0, stream1, base, gate0, linear0, w_all, slope0, c_all, low0, normed0, active0,
          drive0, b_all, tokens),
         "last",
         bare=(0, 1),

time: 124 us -> 124 us (level)
  transfers between devices with their start and end apart: 25 -> 25, of which waited for: 12 -> 12; matrix products, arithmetic and copies ran while one was open for 0% -> 0% of each run, Pallas kernels for 23% -> 22%
where the time goes in v9:
time: 124 us; the launch traced here: 123 us
  Pallas kernels  44.9 us (36%)
  waiting for transfers between devices  32.1 us (26%)
  starting transfers between devices  30 us (24%)
  blocking collectives  12.5 us (10%)
  local copies, waits for them, and re-layouts  1.94 us (2%)
  between operations  1.73 us (1%)
    pallas_call x6, Pallas kernels, call(): pl.pallas_call(body, out_shape=tuple(outs), in_specs=[pl.BlockSpec(memory...  40 us
    ppermute x14, waiting for transfers between devices, exchange(): return lax.ppermute(value, 'dp', [(i, i ^ bit) for i in range(dp_size)])  18.3 us
    ppermute x14, starting transfers between devices, exchange(): return lax.ppermute(value, 'dp', [(i, i ^ bit) for i in range(dp_size)])  14.4 us
    all_to_all x1, blocking collectives, across(): return lax.all_to_all(value, axes, 0, 0, tiled=True)  12.5 us
    all_to_all x2, starting transfers between devices, across(): return lax.all_to_all(value, axes, 0, 0, tiled=True)  10 us
    ppermute x9, waiting for transfers between devices, swap(): return lax.ppermute(value, 'state', pairs)  7.83 us
    all_to_all x2, waiting for transfers between devices, across(): return lax.all_to_all(value, axes, 0, 0, tiled=True)  5.91 us
    ppermute x9, starting transfers between devices, swap(): return lax.ppermute(value, 'state', pairs)  5.59 us
  transfers between devices with their start and end apart: 25, of which 12 were waited for; matrix products, arithmetic and copies ran while one was open for 0% of the time, Pallas kernels for 22%

profile of v9, /device:TPU:0, one launch (start us, length us, event | category | flops | bytes accessed | tf_op | source)
XLA Modules:
  0.0 123.2 jit_solution(13397367172248141256)
XLA Ops:
  1.3 3.3 %enter.1 = (f32[1024,128]{1,0:T(8,128)}, f32[8,8,128]{2,1,0:T(8,128)}, bf16[800,512]{1,0:T(8,128)(2,1)}) custom-call(s32[1]{0:T(128)S(6)} %copy.31.refs_0_, f32[128,1024]{1,0:T(8,128)} %bitcast.17, f32[2,128]{1,0:T(2,128)} %refs_2_.1, f32[2,128]{1,0:T(2,128)} %refs_3_.1, f32[2,128]{1,0:T(2,128)} %refs_4_.1, f32[2,2,128]{2,1,0:T(2,128)} %refs_5_.2, ...), custom_call_target="tpu_custom_call" | custom-call | tf_op jit(solution)/shard_map/enter/pallas_call | solution.py:289
  4.6 3.0 %collective-permute-start.2 = (bf16[800,512]{1,0:T(8,128)(2,1)}, bf16[800,512]{1,0:T(8,128)(2,1)}, u32[]{:S(2)}, u32[]{:S(2)}) collective-permute-start(bf16[800,512]{1,0:T(8,128)(2,1)} %get-tuple-element.90.refs_6_), channel_id=1, source_target_pairs={{0,2},{1,3},{2,0},{3,1},{4,6},{5,7},{6,4},{7,5},{8,10},{9,11},{10,... | collective-permute-start | bytes 2457608 | tf_op jit(solution)/shard_map/ppermute | solution.py:1031
  7.6 12.5 %all_to_all.15.refs_0_ = f32[8,8,128]{2,1,0:T(8,128)S(1)} all-to-all(f32[8,8,128]{2,1,0:T(8,128)} %get-tuple-element.89), channel_id=1, replica_groups=mesh['dp'=8,'state'=4] {'dp'}, dimensions={0} | all-to-all | bytes 65536 | tf_op jit(solution)/shard_map/all_to_all | solution.py:1035
  20.1 0.6 total.1.refs_1_
  20.7 0.5 collective-permute-start.4
  21.3 2.9 %cotangent.1 = (f32[1024,128]{1,0:T(8,128)}, bf16[768,512]{1,0:T(8,128)(2,1)}) custom-call(s32[1]{0:T(128)S(6)} %copy.31.refs_0_, f32[128,1024]{1,0:T(8,128)} %bitcast.18, bf16[2,128,512]{2,1,0:T(8,128)(2,1)} %bitcast.14, bf16[2,128,512]{2,1,0:T(8,128)(2,1)} %bitcast.16, bf16[2,256,512]{2,1,0:T(8,128)(2,1)} %bitcast.11), custom_call_target="tpu_custom_call" | custom-call | tf_op jit(solution)/shard_map/cotangent/pallas_call | solution.py:289
  24.1 2.1 %collective-permute-done.4.refs_3_ = f32[8,128]{1,0:T(8,128)} collective-permute-done((f32[8,128]{1,0:T(8,128)}, f32[8,128]{1,0:T(8,128)}, u32[]{:S(2)}, u32[]{:S(2)}) %collective-permute-start.4) | collective-permute-done | bytes 4128 | tf_op jit(solution)/shard_map/ppermute | solution.py:1031
  26.3 0.1 collective-permute-start.6
  26.4 1.8 %collective-permute-start = (bf16[768,512]{1,0:T(8,128)(2,1)}, bf16[768,512]{1,0:T(8,128)(2,1)}, u32[]{:S(2)}, u32[]{:S(2)}) collective-permute-start(bf16[768,512]{1,0:T(8,128)(2,1)} %get-tuple-element.103.refs_7_), channel_id=1, source_target_pairs={{0,2},{1,3},{2,0},{3,1},{4,6},{5,7},{6,4},{7,5},{8,10},{9,11},{10,... | collective-permute-start | bytes 2359304 | tf_op jit(solution)/shard_map/ppermute | solution.py:1031
  28.2 0.2 collective-permute-start.5
  28.3 1.3 %collective-permute-done.5.refs_4_ = f32[8,128]{1,0:T(8,128)} collective-permute-done((f32[8,128]{1,0:T(8,128)}, f32[8,128]{1,0:T(8,128)}, u32[]{:S(2)}, u32[]{:S(2)}) %collective-permute-start.5) | collective-permute-done | bytes 4128 | tf_op jit(solution)/shard_map/ppermute | solution.py:1031
  29.7 9.3 %start.1 = (f32[32,512]{1,0:T(8,128)}, f32[8,256]{1,0:T(8,128)}, f32[8,512]{1,0:T(8,128)}, bf16[1024,512]{1,0:T(8,128)(2,1)}, f32[1024,256]{1,0:T(8,128)}, /*ind...) custom-call(s32[1]{0:T(128)S(6)} %copy.31.refs_0_, ...), custom_call_target="tpu_custom_call" | custom-call | tf_op jit(solution)/shard_map/start/pallas_call | solution.py:289
  39.0 5.9 %all-to-all-start.1 = ((f32[8,8,128]{2,1,0:T(8,128)}), f32[8,8,128]{2,1,0:T(8,128)}, u32[]{:S(2)}, u32[]{:S(2)}) async-start(f32[8,8,128]{2,1,0:T(8,128)} %get-tuple-element.96), calls=%async_computation.1 | async-start | bytes 65536 | tf_op jit(solution)/shard_map/all_to_all | solution.py:1035
  44.9 1.7 %collective-permute-done.refs_9_ = bf16[768,512]{1,0:T(8,128)(2,1)} collective-permute-done((bf16[768,512]{1,0:T(8,128)(2,1)}, bf16[768,512]{1,0:T(8,128)(2,1)}, u32[]{:S(2)}, u32[]{:S(2)}) %collective-permute-start) | collective-permute-done | bytes 786464 | tf_op jit(solution)/shard_map/ppermute | solution.py:1031
  46.6 5.0 %all-to-all-done.1.refs_1_ = f32[8,8,128]{2,1,0:T(8,128)} async-done(((f32[8,8,128]{2,1,0:T(8,128)}), f32[8,8,128]{2,1,0:T(8,128)}, u32[]{:S(2)}, u32[]{:S(2)}) %all-to-all-start.1) | async-done | bytes 32800 | tf_op jit(solution)/shard_map/all_to_all | solution.py:1035
  51.7 2.6 %collective-permute-done.8.refs_10_ = bf16[768,512]{1,0:T(8,128)(2,1)} collective-permute-done((bf16[768,512]{1,0:T(8,128)(2,1)}, bf16[768,512]{1,0:T(8,128)(2,1)}, u32[]{:S(2)}, u32[]{:S(2)}) %collective-permute-start.8) | collective-permute-done | bytes 786464 | tf_op jit(solution)/shard_map/ppermute | solution.py:1031
  54.3 12.7 %middle.1 = (f32[1024,128]{1,0:T(8,128)}, f32[1024,512]{1,0:T(8,128)}, f32[8,16,128]{2,1,0:T(8,128)}, f32[8,512]{1,0:T(8,128)}, bf16[256,512]{1,0:T(8,128)(2,1)}, /*index=5*/bf16[256,512]{1,0:T(8,128)(2,1)}) custom-call(s32[1]{0:T(128)S(6)} %copy.31.refs_0_, f32[8,8,128]{2,1,0:T(8,128)} %all-to-all-done.1.refs_1_, ...), custom_call_target="tpu_custom_call" | custom-call | flops 1000000000 | tf_op jit(solution)/shard_map/middle/pallas_call | solution.py:289
  67.0 0.5 collective-permute-start.9
  67.5 4.2 %all-to-all-start.2 = ((f32[8,16,128]{2,1,0:T(8,128)}), f32[8,16,128]{2,1,0:T(8,128)}, u32[]{:S(2)}, u32[]{:S(2)}) async-start(f32[8,16,128]{2,1,0:T(8,128)} %get-tuple-element.105), calls=%async_computation.2 | async-start | bytes 131072 | tf_op jit(solution)/shard_map/all_to_all | solution.py:1035
  71.7 4.1 %collective-permute-done.9.refs_1_ = bf16[256,512]{1,0:T(8,128)(2,1)S(1)} collective-permute-done((bf16[256,512]{1,0:T(8,128)(2,1)}, bf16[256,512]{1,0:T(8,128)(2,1)S(1)}, u32[]{:S(2)}, u32[]{:S(2)}) %collective-permute-start.9) | collective-permute-done | bytes 262176 | tf_op jit(solution)/shard_map/ppermute | solution.py:1072
  75.8 0.9 copy-done.6
  76.8 0.8 add.3.refs_0_
  77.6 0.9 all-to-all-done.2.refs_1_.refs_2_
  78.4 0.5 collective-permute-start.10
  78.9 8.6 %last.1 = (bf16[272,512]{1,0:T(8,128)(2,1)}, bf16[272,512]{1,0:T(8,128)(2,1)}, f32[1024,128]{1,0:T(8,128)}, f32[1024,128]{1,0:T(8,128)}) custom-call(s32[1]{0:T(128)S(6)} %copy.31.refs_0_, f32[8,16,128]{2,1,0:T(8,128)} %all-to-all-done.2.refs_1_.refs_2_, f32[8,512]{1,0:T(8,128)} %get-tuple-element.110.refs_2_, f32[32,512]{1,0:T(8,128)} %get-tuple-element.99.refs_3_.refs_4_, ...), custom_call_target="tpu_custom_call" | custom-call | flops 99999997952 | tf_op jit(solution)/shard_map/last/pallas_call | solution.py:289
  87.6 0.5 collective-permute-start.12
  88.1 3.8 %collective-permute-done.10.refs_1_ = bf16[256,512]{1,0:T(8,128)(2,1)} collective-permute-done((bf16[256,512]{1,0:T(8,128)(2,1)}, bf16[256,512]{1,0:T(8,128)(2,1)}, u32[]{:S(2)}, u32[]{:S(2)}) %collective-permute-start.10) | collective-permute-done | bytes 262176 | tf_op jit(solution)/shard_map/ppermute | solution.py:1072
  91.9 1.1 add.4.refs_0_
  93.0 0.1 collective-permute-start.11
  93.1 2.0 %collective-permute-done.12.refs_1_ = bf16[272,512]{1,0:T(8,128)(2,1)S(1)} collective-permute-done((bf16[272,512]{1,0:T(8,128)(2,1)}, bf16[272,512]{1,0:T(8,128)(2,1)S(1)}, u32[]{:S(2)}, u32[]{:S(2)}) %collective-permute-start.12) | collective-permute-done | bytes 278560 | tf_op jit(solution)/shard_map/ppermute | solution.py:1072
  95.1 1.0 copy-done.4
  96.1 0.1 pair.1
  96.2 0.5 collective-permute-start.13
  96.7 2.0 %collective-permute-start.14 = (bf16[80,512]{1,0:T(8,128)(2,1)S(1)}, bf16[80,512]{1,0:T(8,128)(2,1)S(1)}, u32[]{:S(2)}, u32[]{:S(2)}) collective-permute-start(bf16[80,512]{1,0:T(8,128)(2,1)S(1)} %get-tuple-element.130), channel_id=1, source_target_pairs={{0,16},{4,20},{8,24},{12,28},{16,0},{20,4},{24,8},{28,12},{1,17},{... | collective-permute-start | bytes 245768 | tf_op jit(solution)/shard_map/ppermute | solution.py:1072
  98.7 1.9 %collective-permute-start.15 = (bf16[80,512]{1,0:T(8,128)(2,1)S(1)}, bf16[80,512]{1,0:T(8,128)(2,1)S(1)}, u32[]{:S(2)}, u32[]{:S(2)}) collective-permute-start(bf16[80,512]{1,0:T(8,128)(2,1)S(1)} %get-tuple-element.131), channel_id=1, source_target_pairs={{0,24},{4,28},{8,16},{12,20},{16,8},{20,12},{24,0},{28,4},{1,25},{... | collective-permute-start | bytes 245768 | tf_op jit(solution)/shard_map/ppermute | solution.py:1072
  100.6 5.9 %collective-permute-done.13.refs_2_ = bf16[80,512]{1,0:T(8,128)(2,1)S(1)} collective-permute-done((bf16[80,512]{1,0:T(8,128)(2,1)S(1)}, bf16[80,512]{1,0:T(8,128)(2,1)S(1)}, u32[]{:S(2)}, u32[]{:S(2)}) %collective-permute-start.13) | collective-permute-done | bytes 81952 | tf_op jit(solution)/shard_map/ppermute | solution.py:1072
  106.6 0.1 add.5.refs_0_
  106.7 0.7 collective-permute-start.16
  107.4 2.2 %collective-permute-start.21 = (bf16[64,512]{1,0:T(8,128)(2,1)S(1)}, bf16[64,512]{1,0:T(8,128)(2,1)S(1)}, u32[]{:S(2)}, u32[]{:S(2)}) collective-permute-start(bf16[64,512]{1,0:T(8,128)(2,1)S(1)} %get-tuple-element.147.refs_0_), channel_id=1, source_target_pairs={{0,24},{4,28},{8,16},{12,20},{16,8},{20,12},{24,0},{28,4},{1,25},{... | collective-permute-start | bytes 196616 | tf_op jit(solution)/shard_map/ppermute | solution.py:1072
  109.6 2.2 %collective-permute-start.17 = (bf16[64,512]{1,0:T(8,128)(2,1)S(1)}, bf16[64,512]{1,0:T(8,128)(2,1)S(1)}, u32[]{:S(2)}, u32[]{:S(2)}) collective-permute-start(bf16[64,512]{1,0:T(8,128)(2,1)S(1)} %get-tuple-element.147.refs_0_), channel_id=1, source_target_pairs={{0,8},{4,12},{8,0},{12,4},{16,24},{20,28},{24,16},{28,20},{1,9},{5... | collective-permute-start | bytes 196616 | tf_op jit(solution)/shard_map/ppermute | solution.py:1072
  111.8 2.2 %collective-permute-done.21.refs_6_ = bf16[64,512]{1,0:T(8,128)(2,1)S(1)} collective-permute-done((bf16[64,512]{1,0:T(8,128)(2,1)S(1)}, bf16[64,512]{1,0:T(8,128)(2,1)S(1)}, u32[]{:S(2)}, u32[]{:S(2)}) %collective-permute-start.21) | collective-permute-done | bytes 65568 | tf_op jit(solution)/shard_map/ppermute | solution.py:1072
  114.0 1.2 %collective-permute-start.22 = (bf16[64,512]{1,0:T(8,128)(2,1)S(1)}, bf16[64,512]{1,0:T(8,128)(2,1)S(1)}, u32[]{:S(2)}, u32[]{:S(2)}) collective-permute-start(bf16[64,512]{1,0:T(8,128)(2,1)S(1)} %collective-permute-done.21.refs_6_), channel_id=1, source_target_pairs={{0,4},{4,0},{8,12},{12,8},{16,20},{20,16},{24,28},{28,24},{1,5},{5... | collective-permute-start | bytes 196616 | tf_op jit(solution)/shard_map/ppermute | solution.py:1072
  115.3 0.2 collective-permute-done.19.refs_4_
  115.4 1.5 %collective-permute-start.20 = (bf16[64,512]{1,0:T(8,128)(2,1)S(1)}, bf16[64,512]{1,0:T(8,128)(2,1)S(1)}, u32[]{:S(2)}, u32[]{:S(2)}) collective-permute-start(bf16[64,512]{1,0:T(8,128)(2,1)S(1)} %collective-permute-done.19.refs_4_), channel_id=1, source_target_pairs={{0,4},{4,0},{8,12},{12,8},{16,20},{20,16},{24,28},{28,24},{1,5},{5... | collective-permute-start | bytes 196616 | tf_op jit(solution)/shard_map/ppermute | solution.py:1072
  116.9 0.5 collective-permute-start.18
  117.5 1.1 widen1.1
  118.7 3.2 %finish.1 = (f32[2,64]{1,0:T(2,128)}, f32[2,64]{1,0:T(2,128)}, f32[2,64]{1,0:T(2,128)}, f32[2,128]{1,0:T(2,128)}, f32[2,2,128]{2,1,0:T(2,128)}, /*index=5*/f32[2...) custom-call(s32[1]{0:T(128)S(6)} %copy.31.refs_0_, f32[8,512]{1,0:T(8,128)S(1)} %get-tuple-element.139.refs_1_, ...), custom_call_target="tpu_custom_call" | custom-call | tf_op jit(solution)/shard_map/finish/pallas_call | solution.py:289
  121.9 1.1 widen0.1
  (37 shorter events, 0.1 us)
Async XLA Ops:
  4.6 21.7 %collective-permute-start.2 = (bf16[800,512]{1,0:T(8,128)(2,1)}, bf16[800,512]{1,0:T(8,128)(2,1)}, u32[]{:S(2)}, u32[]{:S(2)}) collective-permute-start(bf16[800,512]{1,0:T(8,128)(2,1)} %get-tuple-element.90.refs_6_), channel_id=1, source_target_pairs={{0,2},{1,3},{2,0},{3,1},{4,6},{5,7},{6,4},{7,5},{8,10},{9,11},{10,... | collective-permute-start | bytes 2457608 | tf_op jit(solution)/shard_map/ppermute | solution.py:1031
  7.6 18.7 %collective-permute-start.1 = (bf16[800,512]{1,0:T(8,128)(2,1)}, bf16[800,512]{1,0:T(8,128)(2,1)}, u32[]{:S(2)}, u32[]{:S(2)}) collective-permute-start(bf16[800,512]{1,0:T(8,128)(2,1)} %get-tuple-element.90.refs_6_), channel_id=1, source_target_pairs={{0,1},{1,0},{2,3},{3,2},{4,5},{5,4},{6,7},{7,6},{8,9},{9,8},{10,11... | collective-permute-start | bytes 2457608 | tf_op jit(solution)/shard_map/ppermute | solution.py:1031
  20.7 5.5 %collective-permute-start.4 = (f32[8,128]{1,0:T(8,128)}, f32[8,128]{1,0:T(8,128)}, u32[]{:S(2)}, u32[]{:S(2)}) collective-permute-start(f32[8,128]{1,0:T(8,128)} %total.1.refs_1_), channel_id=1, source_target_pairs={{0,2},{1,3},{2,0},{3,1},{4,6},{5,7},{6,4},{7,5},{8,10},{9,11},{10,... | collective-permute-start | bytes 12296 | tf_op jit(solution)/shard_map/ppermute | solution.py:1031
  21.3 5.0 %collective-permute-start.3 = (f32[8,128]{1,0:T(8,128)}, f32[8,128]{1,0:T(8,128)}, u32[]{:S(2)}, u32[]{:S(2)}) collective-permute-start(f32[8,128]{1,0:T(8,128)} %total.1.refs_1_), channel_id=1, source_target_pairs={{0,1},{1,0},{2,3},{3,2},{4,5},{5,4},{6,7},{7,6},{8,9},{9,8},{10,11... | collective-permute-start | bytes 12296 | tf_op jit(solution)/shard_map/ppermute | solution.py:1031
  26.3 3.4 %collective-permute-start.6 = (bf16[800,512]{1,0:T(8,128)(2,1)}, bf16[800,512]{1,0:T(8,128)(2,1)}, u32[]{:S(2)}, u32[]{:S(2)}) collective-permute-start(bf16[800,512]{1,0:T(8,128)(2,1)} %collective-permute-done.2.refs_8_), channel_id=1, source_target_pairs={{0,1},{1,0},{2,3},{3,2},{4,5},{5,4},{6,7},{7,6},{8,9},{9,8},{10,11... | collective-permute-start | bytes 2457608 | tf_op jit(solution)/shard_map/ppermute | solution.py:1031
  26.4 20.3 %collective-permute-start = (bf16[768,512]{1,0:T(8,128)(2,1)}, bf16[768,512]{1,0:T(8,128)(2,1)}, u32[]{:S(2)}, u32[]{:S(2)}) collective-permute-start(bf16[768,512]{1,0:T(8,128)(2,1)} %get-tuple-element.103.refs_7_), channel_id=1, source_target_pairs={{0,2},{1,3},{2,0},{3,1},{4,6},{5,7},{6,4},{7,5},{8,10},{9,11},{10,... | collective-permute-start | bytes 2359304 | tf_op jit(solution)/shard_map/ppermute | solution.py:1031
  28.2 1.5 %collective-permute-start.5 = (f32[8,128]{1,0:T(8,128)}, f32[8,128]{1,0:T(8,128)}, u32[]{:S(2)}, u32[]{:S(2)}) collective-permute-start(f32[8,128]{1,0:T(8,128)} %collective-permute-done.4.refs_3_), channel_id=1, source_target_pairs={{0,1},{1,0},{2,3},{3,2},{4,5},{5,4},{6,7},{7,6},{8,9},{9,8},{10,11... | collective-permute-start | bytes 12296 | tf_op jit(solution)/shard_map/ppermute | solution.py:1031
  39.0 12.6 %all-to-all-start.1 = ((f32[8,8,128]{2,1,0:T(8,128)}), f32[8,8,128]{2,1,0:T(8,128)}, u32[]{:S(2)}, u32[]{:S(2)}) async-start(f32[8,8,128]{2,1,0:T(8,128)} %get-tuple-element.96), calls=%async_computation.1 | async-start | bytes 65536 | tf_op jit(solution)/shard_map/all_to_all | solution.py:1035
  44.9 6.8 %collective-permute-start.7 = (bf16[768,512]{1,0:T(8,128)(2,1)}, bf16[768,512]{1,0:T(8,128)(2,1)}, u32[]{:S(2)}, u32[]{:S(2)}) collective-permute-start(bf16[768,512]{1,0:T(8,128)(2,1)} %get-tuple-element.103.refs_7_), channel_id=1, source_target_pairs={{0,1},{1,0},{2,3},{3,2},{4,5},{5,4},{6,7},{7,6},{8,9},{9,8},{10,11... | collective-permute-start | bytes 2359304 | tf_op jit(solution)/shard_map/ppermute | solution.py:1031
  51.7 2.6 %collective-permute-start.8 = (bf16[768,512]{1,0:T(8,128)(2,1)}, bf16[768,512]{1,0:T(8,128)(2,1)}, u32[]{:S(2)}, u32[]{:S(2)}) collective-permute-start(bf16[768,512]{1,0:T(8,128)(2,1)} %collective-permute-done.refs_9_), channel_id=1, source_target_pairs={{0,1},{1,0},{2,3},{3,2},{4,5},{5,4},{6,7},{7,6},{8,9},{9,8},{10,11... | collective-permute-start | bytes 2359304 | tf_op jit(solution)/shard_map/ppermute | solution.py:1031
  67.0 8.9 %collective-permute-start.9 = (bf16[256,512]{1,0:T(8,128)(2,1)}, bf16[256,512]{1,0:T(8,128)(2,1)S(1)}, u32[]{:S(2)}, u32[]{:S(2)}) collective-permute-start(bf16[256,512]{1,0:T(8,128)(2,1)} %get-tuple-element.107), channel_id=1, source_target_pairs={{0,4},{4,0},{8,12},{12,8},{16,20},{20,16},{24,28},{28,24},{1,5},{5... | collective-permute-start | bytes 786440 | tf_op jit(solution)/shard_map/ppermute | solution.py:1072
  67.5 10.9 %all-to-all-start.2 = ((f32[8,16,128]{2,1,0:T(8,128)}), f32[8,16,128]{2,1,0:T(8,128)}, u32[]{:S(2)}, u32[]{:S(2)}) async-start(f32[8,16,128]{2,1,0:T(8,128)} %get-tuple-element.105), calls=%async_computation.2 | async-start | bytes 131072 | tf_op jit(solution)/shard_map/all_to_all | solution.py:1035
  75.8 1.0 copy-start.6
  78.4 13.4 %collective-permute-start.10 = (bf16[256,512]{1,0:T(8,128)(2,1)}, bf16[256,512]{1,0:T(8,128)(2,1)}, u32[]{:S(2)}, u32[]{:S(2)}) collective-permute-start(bf16[256,512]{1,0:T(8,128)(2,1)} %add.3.refs_0_), channel_id=1, source_target_pairs={{0,16},{4,20},{8,24},{12,28},{16,0},{20,4},{24,8},{28,12},{1,17},{... | collective-permute-start | bytes 786440 | tf_op jit(solution)/shard_map/ppermute | solution.py:1072
  87.6 31.0 %copy-start = (f32[1024,128]{1,0:T(8,128)S(1)}, f32[1024,128]{1,0:T(8,128)}, u32[]{:S(2)}) copy-start(f32[1024,128]{1,0:T(8,128)} %get-tuple-element.93.refs_5_.refs_18_.refs_10_) | copy-start | bytes 1572868
  87.6 31.0 %copy-start.1 = (f32[1024,128]{1,0:T(8,128)S(1)}, f32[1024,128]{1,0:T(8,128)}, u32[]{:S(2)}) copy-start(f32[1024,128]{1,0:T(8,128)} %get-tuple-element.140.refs_7_) | copy-start | bytes 1572868
  87.6 31.0 %copy-start.2 = (f32[1024,128]{1,0:T(8,128)S(1)}, f32[1024,128]{1,0:T(8,128)}, u32[]{:S(2)}) copy-start(f32[1024,128]{1,0:T(8,128)} %get-tuple-element.141.refs_8_) | copy-start | bytes 1572868
  87.6 31.0 %copy-start.3 = (f32[1024,128]{1,0:T(8,128)S(1)}, f32[1024,128]{1,0:T(8,128)}, u32[]{:S(2)}) copy-start(f32[1024,128]{1,0:T(8,128)} %get-tuple-element.142.refs_9_) | copy-start | bytes 1572868
  87.6 7.5 %collective-permute-start.12 = (bf16[272,512]{1,0:T(8,128)(2,1)}, bf16[272,512]{1,0:T(8,128)(2,1)S(1)}, u32[]{:S(2)}, u32[]{:S(2)}) collective-permute-start(bf16[272,512]{1,0:T(8,128)(2,1)} %get-tuple-element.127), channel_id=1, source_target_pairs={{0,4},{4,0},{8,12},{12,8},{16,20},{20,16},{24,28},{28,24},{1,5},{5... | collective-permute-start | bytes 835592 | tf_op jit(solution)/shard_map/ppermute | solution.py:1072
  93.0 13.6 %collective-permute-start.11 = (bf16[256,512]{1,0:T(8,128)(2,1)S(1)}, bf16[256,512]{1,0:T(8,128)(2,1)S(1)}, u32[]{:S(2)}, u32[]{:S(2)}) collective-permute-start(bf16[256,512]{1,0:T(8,128)(2,1)S(1)} %add.4.refs_0_), channel_id=1, source_target_pairs={{0,8},{4,12},{8,0},{12,4},{16,24},{20,28},{24,16},{28,20},{1,9},{5... | collective-permute-start | bytes 786440 | tf_op jit(solution)/shard_map/ppermute | solution.py:1072
  95.1 1.0 copy-start.4
  96.1 22.6 %copy-start.5 = (f32[32,512]{1,0:T(8,128)S(1)}, f32[32,512]{1,0:T(8,128)}, u32[]{:S(2)}) copy-start(f32[32,512]{1,0:T(8,128)} %get-tuple-element.99.refs_3_.refs_4_) | copy-start | bytes 196612
  96.1 22.6 %copy-start.7 = (f32[8,512]{1,0:T(8,128)S(1)}, f32[8,512]{1,0:T(8,128)}, u32[]{:S(2)}) copy-start(f32[8,512]{1,0:T(8,128)} %get-tuple-element.98.refs_2_.refs_5_.refs_3_) | copy-start | bytes 49156
  96.1 22.6 %copy-start.8 = (f32[2,64]{1,0:T(2,128)S(1)}, f32[2,64]{1,0:T(2,128)}, u32[]{:S(2)}) copy-start(f32[2,64]{1,0:T(2,128)} %refs_5_.3) | copy-start | bytes 1540
  96.1 22.6 %copy-start.9 = (f32[2,64]{1,0:T(2,128)S(1)}, f32[2,64]{1,0:T(2,128)}, u32[]{:S(2)}) copy-start(f32[2,64]{1,0:T(2,128)} %refs_6_.3) | copy-start | bytes 1540
  96.2 10.4 %collective-permute-start.13 = (bf16[80,512]{1,0:T(8,128)(2,1)S(1)}, bf16[80,512]{1,0:T(8,128)(2,1)S(1)}, u32[]{:S(2)}, u32[]{:S(2)}) collective-permute-start(bf16[80,512]{1,0:T(8,128)(2,1)S(1)} %get-tuple-element.129), channel_id=1, source_target_pairs={{0,8},{4,12},{8,0},{12,4},{16,24},{20,28},{24,16},{28,20},{1,9},{5... | collective-permute-start | bytes 245768 | tf_op jit(solution)/shard_map/ppermute | solution.py:1072
  96.7 9.8 %collective-permute-start.14 = (bf16[80,512]{1,0:T(8,128)(2,1)S(1)}, bf16[80,512]{1,0:T(8,128)(2,1)S(1)}, u32[]{:S(2)}, u32[]{:S(2)}) collective-permute-start(bf16[80,512]{1,0:T(8,128)(2,1)S(1)} %get-tuple-element.130), channel_id=1, source_target_pairs={{0,16},{4,20},{8,24},{12,28},{16,0},{20,4},{24,8},{28,12},{1,17},{... | collective-permute-start | bytes 245768 | tf_op jit(solution)/shard_map/ppermute | solution.py:1072
  98.7 7.8 %collective-permute-start.15 = (bf16[80,512]{1,0:T(8,128)(2,1)S(1)}, bf16[80,512]{1,0:T(8,128)(2,1)S(1)}, u32[]{:S(2)}, u32[]{:S(2)}) collective-permute-start(bf16[80,512]{1,0:T(8,128)(2,1)S(1)} %get-tuple-element.131), channel_id=1, source_target_pairs={{0,24},{4,28},{8,16},{12,20},{16,8},{20,12},{24,0},{28,4},{1,25},{... | collective-permute-start | bytes 245768 | tf_op jit(solution)/shard_map/ppermute | solution.py:1072
  106.7 10.8 %collective-permute-start.16 = (bf16[320,512]{1,0:T(8,128)(2,1)S(1)}, bf16[320,512]{1,0:T(8,128)(2,1)S(1)}, u32[]{:S(2)}, u32[]{:S(2)}) collective-permute-start(bf16[320,512]{1,0:T(8,128)(2,1)S(1)} %get-tuple-element.138), channel_id=1, source_target_pairs={{0,4},{4,0},{8,12},{12,8},{16,20},{20,16},{24,28},{28,24},{1,5},{5... | collective-permute-start | bytes 983048 | tf_op jit(solution)/shard_map/ppermute | solution.py:1072
  107.4 6.6 %collective-permute-start.21 = (bf16[64,512]{1,0:T(8,128)(2,1)S(1)}, bf16[64,512]{1,0:T(8,128)(2,1)S(1)}, u32[]{:S(2)}, u32[]{:S(2)}) collective-permute-start(bf16[64,512]{1,0:T(8,128)(2,1)S(1)} %get-tuple-element.147.refs_0_), channel_id=1, source_target_pairs={{0,24},{4,28},{8,16},{12,20},{16,8},{20,12},{24,0},{28,4},{1,25},{... | collective-permute-start | bytes 196616 | tf_op jit(solution)/shard_map/ppermute | solution.py:1072
  109.6 5.9 %collective-permute-start.19 = (bf16[64,512]{1,0:T(8,128)(2,1)S(1)}, bf16[64,512]{1,0:T(8,128)(2,1)S(1)}, u32[]{:S(2)}, u32[]{:S(2)}) collective-permute-start(bf16[64,512]{1,0:T(8,128)(2,1)S(1)} %get-tuple-element.147.refs_0_), channel_id=1, source_target_pairs={{0,16},{4,20},{8,24},{12,28},{16,0},{20,4},{24,8},{28,12},{1,17},{... | collective-permute-start | bytes 196616 | tf_op jit(solution)/shard_map/ppermute | solution.py:1072
  109.6 7.4 %collective-permute-start.17 = (bf16[64,512]{1,0:T(8,128)(2,1)S(1)}, bf16[64,512]{1,0:T(8,128)(2,1)S(1)}, u32[]{:S(2)}, u32[]{:S(2)}) collective-permute-start(bf16[64,512]{1,0:T(8,128)(2,1)S(1)} %get-tuple-element.147.refs_0_), channel_id=1, source_target_pairs={{0,8},{4,12},{8,0},{12,4},{16,24},{20,28},{24,16},{28,20},{1,9},{5... | collective-permute-start | bytes 196616 | tf_op jit(solution)/shard_map/ppermute | solution.py:1072
  114.0 7.8 %collective-permute-start.22 = (bf16[64,512]{1,0:T(8,128)(2,1)S(1)}, bf16[64,512]{1,0:T(8,128)(2,1)S(1)}, u32[]{:S(2)}, u32[]{:S(2)}) collective-permute-start(bf16[64,512]{1,0:T(8,128)(2,1)S(1)} %collective-permute-done.21.refs_6_), channel_id=1, source_target_pairs={{0,4},{4,0},{8,12},{12,8},{16,20},{20,16},{24,28},{28,24},{1,5},{5... | collective-permute-start | bytes 196616 | tf_op jit(solution)/shard_map/ppermute | solution.py:1072
  115.4 6.4 %collective-permute-start.20 = (bf16[64,512]{1,0:T(8,128)(2,1)S(1)}, bf16[64,512]{1,0:T(8,128)(2,1)S(1)}, u32[]{:S(2)}, u32[]{:S(2)}) collective-permute-start(bf16[64,512]{1,0:T(8,128)(2,1)S(1)} %collective-permute-done.19.refs_4_), channel_id=1, source_target_pairs={{0,4},{4,0},{8,12},{12,8},{16,20},{20,16},{24,28},{28,24},{1,5},{5... | collective-permute-start | bytes 196616 | tf_op jit(solution)/shard_map/ppermute | solution.py:1072
  116.9 4.9 %collective-permute-start.18 = (bf16[64,512]{1,0:T(8,128)(2,1)S(1)}, bf16[64,512]{1,0:T(8,128)(2,1)S(1)}, u32[]{:S(2)}, u32[]{:S(2)}) collective-permute-start(bf16[64,512]{1,0:T(8,128)(2,1)S(1)} %collective-permute-done.17.refs_2_), channel_id=1, source_target_pairs={{0,4},{4,0},{8,12},{12,8},{16,20},{20,16},{24,28},{28,24},{1,5},{5... | collective-permute-start | bytes 196616 | tf_op jit(solution)/shard_map/ppermute | solution.py:1072
